TPU v7x, 32 devices: a whole 2x2x4 slice. The times are simulated.
32 devices in a mesh: groups: 2 (over x), seq: 16 (over z, y, core).
Axes of the slice: x: 2, y: 2, z: 4, core: 2. Of those that a mesh axis runs over, the one named last changes fastest.
Arguments:
- tokens: bfloat16 [96, 5120], P(('groups', 'seq')), parts along dimension 0, may hold values from -6 to 6
- modulation: float32 [6, 5120], replicated, may hold values from -2.5 to 2.5
- w_qkv: bfloat16 [3, 5120, 2560], P(None, None, 'seq'), may hold values from -0.078125 to 0.078125
- norm_gains: float32 [2, 2560], replicated, may hold values from 0.56 to 12
- cache_kv: bfloat16 [2, 2, 96, 2560], P(None, None, ('groups', 'seq')), parts along dimension 2, may hold values from -17 to 17
- w_out: bfloat16 [2560, 5120], P(None, 'seq'), may hold values from -0.125 to 0.125
- w_up: bfloat16 [5120, 13824], P(None, 'seq'), may hold values from -0.078125 to 0.078125
- w_down: bfloat16 [13824, 5120], P('seq'), may hold values from -0.0546875 to 0.0546875
Outputs:
- block_out: bfloat16 [96, 5120], P(('groups', 'seq')), parts along dimension 0
There are 2 independent parts, one for each index of `groups`. A program takes and returns all parts, laid end to end along the dimension named above; an argument that names none is the same for every part. Nothing has to cross between parts.
All inputs are finite; a program needn't handle non-finite values.
Results may differ from a plain program's by a relative error of at most 0.017.
The roundings to bfloat16 on the way count: a program that leaves them out, or rounds other values in their place, can miss the bound.
Values may be sent and summed in bfloat16 or wider, within the bound.
No kernel may reach another device: no remote copies, remote signals or barrier semaphores. Data moves between devices by JAX's collectives and lax.ppermute only.
A program may use at most 128 MiB of HBM per device.

v0:
```python
import math

import jax
import jax.numpy as jnp
from jax import lax
from jax.sharding import PartitionSpec as P

HEAD_DIM = 128
HEADS = 20


def layer_norm(values):
    center = values - jnp.mean(values, axis=-1, keepdims=True)
    spread = jnp.mean(center * center, axis=-1, keepdims=True)
    return center * lax.rsqrt(spread + 1e-06)


def rms_norm(values, gain):
    return values * lax.rsqrt(jnp.mean(values * values, axis=-1, keepdims=True) + 1e-06) * gain


def local(tokens, modulation, w_qkv, norm_gains, cache_kv, w_out, w_up, w_down):
    own_rows = tokens.shape[0]
    width = HEADS * HEAD_DIM
    scale = 1.0 / math.sqrt(HEAD_DIM)
    residual = tokens.astype(jnp.float32)
    normed = (layer_norm(residual) * (1.0 + modulation[1]) + modulation[0]).astype(jnp.bfloat16)
    qkv_cols = jnp.einsum(
        "td,kda->kta",
        lax.all_gather(normed, "seq", axis=0, tiled=True),
        w_qkv,
        preferred_element_type=jnp.float32,
    ).astype(jnp.bfloat16)
    qkv = lax.all_to_all(qkv_cols, "seq", split_axis=1, concat_axis=2, tiled=True)
    queries = rms_norm(qkv[0].astype(jnp.float32), norm_gains[0]).astype(jnp.bfloat16)
    keys_now = rms_norm(qkv[1].astype(jnp.float32), norm_gains[1]).astype(jnp.bfloat16)
    local_keys = jnp.concatenate([cache_kv[0].reshape(-1, width), keys_now], axis=0)
    local_values = jnp.concatenate([cache_kv[1].reshape(-1, width), qkv[2]], axis=0)
    query_heads = queries.reshape(own_rows, HEADS, HEAD_DIM)
    peak_old = jnp.full((own_rows, HEADS), -1e30, jnp.float32)
    key_piece = lax.all_gather(local_keys, "seq", axis=0, tiled=True)
    value_piece = lax.all_gather(local_values, "seq", axis=0, tiled=True)
    count = key_piece.shape[0]
    scores = (
        jnp.einsum(
            "qhd,khd->qhk",
            query_heads,
            key_piece.reshape(count, HEADS, HEAD_DIM),
            preferred_element_type=jnp.float32,
        )
        * scale
    )
    peak_new = jnp.maximum(peak_old, jnp.max(scores, axis=-1))
    expo = jnp.exp(scores - peak_new[..., None])
    total_new = jnp.sum(expo, axis=-1)
    weights = expo.astype(jnp.bfloat16)
    summed_new = jnp.einsum(
        "qhk,khd->qhd",
        weights,
        value_piece.reshape(count, HEADS, HEAD_DIM),
        preferred_element_type=jnp.float32,
    )
    attended = (summed_new / total_new[..., None]).reshape(own_rows, width).astype(jnp.bfloat16)
    projected_cols = jnp.dot(
        lax.all_gather(attended, "seq", axis=0, tiled=True),
        w_out,
        preferred_element_type=jnp.float32,
    ).astype(jnp.bfloat16)
    projected = lax.all_to_all(projected_cols, "seq", split_axis=0, concat_axis=1, tiled=True)
    residual = residual + modulation[2] * projected.astype(jnp.float32)
    normed2 = (layer_norm(residual) * (1.0 + modulation[4]) + modulation[3]).astype(jnp.bfloat16)
    hidden = jax.nn.gelu(
        jnp.dot(
            lax.all_gather(normed2, "seq", axis=0, tiled=True),
            w_up,
            preferred_element_type=jnp.float32,
        ),
        approximate=True,
    ).astype(jnp.bfloat16)
    feed = lax.psum_scatter(
        jnp.dot(hidden, w_down, preferred_element_type=jnp.float32),
        "seq",
        scatter_dimension=0,
        tiled=True,
    )
    return (residual + modulation[5] * feed).astype(jnp.bfloat16)


def solution(mesh):
    in_specs = (
        P(("groups", "seq"), None),
        P(),
        P(None, None, "seq"),
        P(),
        P(None, None, ("groups", "seq"), None),
        P(None, "seq"),
        P(None, "seq"),
        P("seq", None),
    )
    out_specs = P(("groups", "seq"), None)
    return jax.shard_map(local, mesh=mesh, in_specs=in_specs, out_specs=out_specs, check_vma=False)
```

profile of v0, /device:TPU:0, one launch (start us, length us, event | category | flops | bytes accessed | tf_op | source)
XLA Modules:
  0.0 266.4 jit_solution(11914635441609002521)
XLA Ops:
  6.5 1.1 convert_reduce_fusion
  7.6 1.0 fusion.23
  8.6 1.6 fusion.41
  10.2 0.9 fusion.33
  11.1 25.1 %all-gather = bf16[16,3,5120]{2,1,0:T(4,128)(2,1)S(1)} all-gather(bf16[1,3,5120]{2,1,0:T(4,128)(2,1)S(1)} %fusion.33), channel_id=1, replica_groups=mesh['groups'=2,'seq'=16] {'seq'}, dimensions={0}, use_global_device_ids=true | all-gather | bytes 522240 | tf_op jit(solution)/shard_map/all_gather | solution.py:30
  36.2 0.4 reshape.97
  36.6 4.1 %fusion.1 = bf16[3,48,160]{2,1,0:T(8,128)(2,1)S(1)} fusion(bf16[48,5120,1]{1,0,2:T(8,128)(2,1)S(1)} %reshape.97, bf16[3,5120,160]{1,2,0:T(8,128)(2,1)} %param.10), kind=kOutput, calls=%fused_computation.3 | convolution fusion | flops 235952640 | bytes 5452800 | tf_op jit(solution)/shard_map/td,kda->kta/dot_general | solution.py:28
  40.8 0.8 reshape.102
  41.6 3.5 %all-to-all-start = ((bf16[16,2,720]{2,1,0:T(2,128)(2,1)}), bf16[16,2,720]{2,1,0:T(2,128)(2,1)S(1)}, u32[]{:S(2)}, u32[]{:S(2)}) async-start(bf16[16,2,720]{2,1,0:T(2,128)(2,1)} %reshape.102), calls=%async_computation | async-start | bytes 98304 | tf_op jit(solution)/shard_map/all_to_all | solution.py:34
  45.4 6.4 %all-to-all-done = bf16[16,2,720]{2,1,0:T(2,128)(2,1)S(1)} async-done(((bf16[16,2,720]{2,1,0:T(2,128)(2,1)}), bf16[16,2,720]{2,1,0:T(2,128)(2,1)S(1)}, u32[]{:S(2)}, u32[]{:S(2)}) %all-to-all-start) | async-done | bytes 46112 | tf_op jit(solution)/shard_map/all_to_all | solution.py:34
  52.7 22.7 %all-gather.2 = bf16[16,9,2560]{2,1,0:T(8,128)(2,1)S(1)} all-gather(bf16[1,9,2560]{2,1,0:T(8,128)(2,1)S(1)} %maximum_bitcast_fusion.1), channel_id=1, replica_groups=mesh['groups'=2,'seq'=16] {'seq'}, dimensions={0}, use_global_device_ids=true | all-gather | bytes 783360 | tf_op jit(solution)/shard_map/all_gather | solution.py:41
  75.4 1.3 reshape.80
  76.8 1.7 fusion.43
  78.6 22.8 %all-gather.1 = bf16[16,9,2560]{2,1,0:T(8,128)(2,1)S(1)} all-gather(bf16[1,9,2560]{2,1,0:T(8,128)(2,1)S(1)} %maximum_bitcast_fusion), channel_id=1, replica_groups=mesh['groups'=2,'seq'=16] {'seq'}, dimensions={0}, use_global_device_ids=true | all-gather | bytes 783360 | tf_op jit(solution)/shard_map/all_gather | solution.py:42
  101.4 1.3 reshape.79
  102.9 1.5 fusion.4
  104.4 19.2 %all-gather.3 = bf16[16,3,2560]{2,1,0:T(4,128)(2,1)S(1)} all-gather(bf16[1,3,2560]{2,1,0:T(4,128)(2,1)S(1)} %fusion.4), channel_id=1, replica_groups=mesh['groups'=2,'seq'=16] {'seq'}, dimensions={0}, use_global_device_ids=true | all-gather | bytes 261120 | tf_op jit(solution)/shard_map/all_gather | solution.py:65
  123.8 0.6 convolution_convert_fusion.1
  124.4 9.3 %all_to_all.28 = bf16[16,3,320]{2,1,0:T(4,128)(2,1)S(1)} all-to-all(bf16[16,3,320]{2,1,0:T(4,128)(2,1)S(1)} %all_to_all.24), channel_id=1, replica_groups=mesh['groups'=2,'seq'=16] {'seq'}, dimensions={0} | all-to-all | bytes 61440 | tf_op jit(solution)/shard_map/all_to_all | solution.py:69
  134.4 19.5 %all-gather.4 = bf16[16,3,5120]{2,1,0:T(4,128)(2,1)S(1)} all-gather(bf16[1,3,5120]{2,1,0:T(4,128)(2,1)S(1)} %fusion.32), channel_id=1, replica_groups=mesh['groups'=2,'seq'=16] {'seq'}, dimensions={0}, use_global_device_ids=true | all-gather | bytes 522240 | tf_op jit(solution)/shard_map/all_gather | solution.py:74
  154.3 11.9 %fusion.17 = f32[48,5120]{1,0:T(8,128)} fusion(bf16[864,5120]{1,0:T(8,128)(2,1)} %param.15, bf16[48,5120]{1,0:T(8,128)(2,1)S(1)} %reshape.93, bf16[5120,864]{0,1:T(8,128)(2,1)} %param.14), kind=kOutput, calls=%fused_computation.27 | convolution fusion | flops 849719808 | bytes 19169280 | tf_op jit(solution)/shard_map/dot_general | solution.py:81
  166.3 0.6 dynamic-slice
  167.5 90.4 %all-reduce.3.cloned.1.call-done = f32[48,5120]{1,0:T(8,128)} async-done(((f32[48,5120]{1,0:T(8,128)}), f32[48,5120]{1,0:T(8,128)}) %all-reduce.3.cloned.1.call-update) | async-done | bytes 983056
  257.9 1.6 fusion.28
  (50 shorter events, 2.8 us)
Async XLA Ops:
  6.5 117.2 %copy-start = (bf16[2560,320]{0,1:T(8,128)(2,1)S(1)}, bf16[2560,320]{0,1:T(8,128)(2,1)}, u32[]{:S(2)}) copy-start(bf16[2560,320]{0,1:T(8,128)(2,1)} %param.13) | copy-start | bytes 4915204
  6.5 38.6 %copy-start.2 = (bf16[2,2,3,2560]{3,1,2,0:T(2,128)(2,1)S(1)}, bf16[2,2,3,2560]{3,1,2,0:T(2,128)(2,1)}, u32[]{:S(2)}) copy-start(bf16[2,2,3,2560]{3,1,2,0:T(2,128)(2,1)} %param.12) | copy-start | bytes 184324
  6.5 38.8 %copy-start.3 = (f32[2,2560]{1,0:T(2,128)S(1)}, f32[2,2560]{1,0:T(2,128)}, u32[]{:S(2)}) copy-start(f32[2,2560]{1,0:T(2,128)} %param.11) | copy-start | bytes 61444
  41.6 10.2 %all-to-all-start = ((bf16[16,2,720]{2,1,0:T(2,128)(2,1)}), bf16[16,2,720]{2,1,0:T(2,128)(2,1)S(1)}, u32[]{:S(2)}, u32[]{:S(2)}) async-start(bf16[16,2,720]{2,1,0:T(2,128)(2,1)} %reshape.102), calls=%async_computation | async-start | bytes 98304 | tf_op jit(solution)/shard_map/all_to_all | solution.py:34
  45.1 212.8 %all-reduce.3.cloned.1.call-start = ((), (), s32[]{:S(2)}) async-start(), calls=%async_computation.2 | async-start | bytes 1966080
  76.8 57.1 %copy-start.1 = (bf16[3,5120]{1,0:T(4,128)(2,1)S(1)}, bf16[3,5120]{1,0:T(4,128)(2,1)}, u32[]{:S(2)}) copy-start(bf16[3,5120]{1,0:T(4,128)(2,1)} %param.8) | copy-start | bytes 92164
  154.3 12.0 %copy-start.4 = (u32[32]{0:T(128)S(1)}, u32[32]{0:T(128)}, u32[]{:S(2)}) copy-start(u32[32]{0:T(128)} %constant.33) | copy-start | bytes 388
Sparse Core Ops, SparseCore 0:
  166.4 91.4 all-reduce.2
where the time goes:
time: 267 us; the launch traced here: 266 us
  blocking collectives  119 us (45%)
  waiting for transfers between devices  96.9 us (36%)
  matrix products  19.9 us (7%)
  between operations  14.3 us (5%)
  other arithmetic  7.35 us (3%)
  local copies, waits for them, and re-layouts  5.94 us (2%)
  starting transfers between devices  3.54 us (1%)
    unnamed x2, waiting for transfers between devices  90.4 us
    all_gather x1, blocking collectives, local(): lax.all_gather(normed, 'seq', axis=0, tiled=True)  25.1 us
    all_gather x1, blocking collectives, local(): value_piece = lax.all_gather(local_values, 'seq', axis=0, tiled=True)  22.8 us
    all_gather x1, blocking collectives, local(): key_piece = lax.all_gather(local_keys, 'seq', axis=0, tiled=True)  22.7 us
    all_gather x1, blocking collectives, local(): lax.all_gather(normed2, 'seq', axis=0, tiled=True)  19.5 us
    all_gather x1, blocking collectives, local(): lax.all_gather(attended, 'seq', axis=0, tiled=True)  19.2 us
    dot_general x1, matrix products, local(): jnp.dot(hidden, w_down, preferred_element_type=jnp.float32)  11.9 us
    all_to_all x1, blocking collectives, local(): lax.all_to_all(projected_cols, 'seq', split_axis=0, concat_axis=1, tiled=...  9.34 us
  transfers between devices with their start and end apart: 2, of which 2 were waited for; matrix products, arithmetic and copies ran while one was open for 0% of the time, Pallas kernels for 0%

commit v1 on v0

--- a/solution.py
+++ b/solution.py
@@ -19,7 +19,70 @@
     return values * lax.rsqrt(jnp.mean(values * values, axis=-1, keepdims=True) + 1e-06) * gain
 
 
-def local(tokens, modulation, w_qkv, norm_gains, cache_kv, w_out, w_up, w_down):
+def swap(values, offset):
+    return lax.ppermute(values, "seq", [(i, i ^ offset) for i in range(16)])
+
+
+def gather(block):
+    planes = jnp.stack([block] + [swap(block, 4 * z) for z in (1, 2, 3)])
+    half = jnp.concatenate([planes, swap(planes, 2)])
+    return jnp.concatenate([half, swap(half, 1)])
+
+
+def in_order(slots, me):
+    apart = jnp.arange(16) ^ me
+    return slots[(apart & 1) * 8 + ((apart >> 1) & 1) * 4 + (apart >> 2)]
+
+
+def scatter_sum(partial, me):
+    apart = jnp.arange(16) ^ me
+    near = partial[apart].reshape(4, 2, 2, *partial.shape[1:])
+    near = near[:, :, 0] + swap(near[:, :, 1].astype(jnp.bfloat16), 1).astype(jnp.float32)
+    near = near[:, 0] + swap(near[:, 1].astype(jnp.bfloat16), 2).astype(jnp.float32)
+    total = near[0]
+    for z in (1, 2, 3):
+        total = total + swap(near[z].astype(jnp.bfloat16), 4 * z).astype(jnp.float32)
+    return total
+
+
+def staged(tokens, modulation, w_qkv, norm_gains, cache_kv, w_out, w_up, w_down):
+    own_rows = tokens.shape[0]
+    rows = own_rows * 16
+    width = HEADS * HEAD_DIM
+    scale = 1.0 / math.sqrt(HEAD_DIM)
+    me = lax.axis_index("seq")
+    all_tokens = in_order(gather(tokens), me).reshape(rows, -1).astype(jnp.float32)
+    cached = in_order(gather(cache_kv), me)
+    cached = cached.transpose(1, 0, 2, 3, 4).reshape(2, -1, width)
+    normed = (layer_norm(all_tokens) * (1.0 + modulation[1]) + modulation[0]).astype(jnp.bfloat16)
+    qkv_cols = jnp.einsum("td,kda->kta", normed, w_qkv, preferred_element_type=jnp.float32).astype(jnp.bfloat16)
+    qkv = in_order(gather(qkv_cols), me).transpose(1, 2, 0, 3).reshape(3, rows, width)
+    queries = rms_norm(qkv[0].astype(jnp.float32), norm_gains[0]).astype(jnp.bfloat16)
+    keys_now = rms_norm(qkv[1].astype(jnp.float32), norm_gains[1]).astype(jnp.bfloat16)
+    keys = jnp.concatenate([cached[0], keys_now]).reshape(-1, HEADS, HEAD_DIM)
+    values = jnp.concatenate([cached[1], qkv[2]]).reshape(-1, HEADS, HEAD_DIM)
+    scores = (
+        jnp.einsum("qhd,khd->hqk", queries.reshape(rows, HEADS, HEAD_DIM), keys, preferred_element_type=jnp.float32)
+        * scale
+    )
+    expo = jnp.exp(scores - jnp.max(scores, axis=-1, keepdims=True))
+    total = jnp.sum(expo, axis=-1, keepdims=True)
+    summed = jnp.einsum("hqk,khd->hqd", expo.astype(jnp.bfloat16), values, preferred_element_type=jnp.float32) / total
+    attended = summed.transpose(1, 0, 2).reshape(rows, width).astype(jnp.bfloat16)
+    projected_cols = jnp.dot(attended, w_out, preferred_element_type=jnp.float32).astype(jnp.bfloat16)
+    projected = in_order(gather(projected_cols), me).transpose(1, 0, 2).reshape(rows, -1)
+    residual = all_tokens + modulation[2] * projected.astype(jnp.float32)
+    normed2 = (layer_norm(residual) * (1.0 + modulation[4]) + modulation[3]).astype(jnp.bfloat16)
+    hidden = jax.nn.gelu(
+        jnp.dot(normed2, w_up, preferred_element_type=jnp.float32), approximate=True
+    ).astype(jnp.bfloat16)
+    partial = jnp.dot(hidden, w_down, preferred_element_type=jnp.float32)
+    feed = scatter_sum(partial.reshape(16, own_rows, -1), me)
+    own = lax.dynamic_index_in_dim(residual.reshape(16, own_rows, -1), me, 0, keepdims=False)
+    return (own + modulation[5] * feed).astype(jnp.bfloat16)
+
+
+def general(tokens, modulation, w_qkv, norm_gains, cache_kv, w_out, w_up, w_down):
     own_rows = tokens.shape[0]
     width = HEADS * HEAD_DIM
     scale = 1.0 / math.sqrt(HEAD_DIM)
@@ -98,4 +161,5 @@
         P("seq", None),
     )
     out_specs = P(("groups", "seq"), None)
+    local = staged if mesh.shape["seq"] == 16 else general
     return jax.shard_map(local, mesh=mesh, in_specs=in_specs, out_specs=out_specs, check_vma=False)

time: 267 us -> 157 us (0.59)
  blocking collectives: 119 us -> 0 us
  waiting for transfers between devices: 96.9 us -> 24.4 us
  local copies, waits for them, and re-layouts: 5.94 us -> 64 us
  starting transfers between devices: 3.54 us -> 30.3 us
  between operations: 14.3 us -> 0.48 us
  other arithmetic: 7.35 us -> 17.1 us
    all_gather x5 -> x0, blocking collectives: 109 us -> none  [the longest x1 25.1 us: local(): lax.all_gather(normed, 'seq', axis=0, tiled=True)]
    unnamed x2 -> x0, waiting for transfers between devices: 90.4 us -> none
    ppermute x0 -> x25, starting transfers between devices: none -> 30.3 us  [swap(): return lax.ppermute(values, 'seq', [(i, i ^ offset) for i in range(16)])]
    ppermute x0 -> x25, waiting for transfers between devices: none -> 24.4 us  [swap(): return lax.ppermute(values, 'seq', [(i, i ^ offset) for i in range(16)])]
    concatenate x0 -> x14, local copies, waits for them, and re-layouts: none -> 14.2 us  [the longest x4 4.91 us: gather(): return jnp.concatenate([half, swap(half, 1)])]
    gather x0 -> x5, local copies, waits for them, and re-layouts: none -> 13.1 us  [the longest x4 9.26 us: in_order(): return slots[(apart & 1) * 8 + (apart >> 1 & 1) * 4 + (apart >> 2)]]
    convert_element_type x7 -> x10, local copies, waits for them, and re-layouts: 0.38 us -> 11.8 us  [the longest x2 4.05 us: staged(): qkv[0].astype(jnp.float32)]
    unnamed x16 -> x60, local copies, waits for them, and re-layouts: 2.55 us -> 12.4 us
  transfers between devices with their start and end apart: 2 -> 25, of which waited for: 2 -> 10; matrix products, arithmetic and copies ran while one was open for 0% -> 29% of each run, Pallas kernels for 0% -> 0%
where the time goes in v1:
time: 157 us; the launch traced here: 156 us
  local copies, waits for them, and re-layouts  64 us (41%)
  starting transfers between devices  30.3 us (19%)
  waiting for transfers between devices  24.4 us (16%)
  matrix products  19.7 us (13%)
  other arithmetic  17.1 us (11%)
    ppermute x25, starting transfers between devices, swap(): return lax.ppermute(values, 'seq', [(i, i ^ offset) for i in range(16)])  30.3 us
    ppermute x25, waiting for transfers between devices, swap(): return lax.ppermute(values, 'seq', [(i, i ^ offset) for i in range(16)])  24.4 us
    dot_general x1, matrix products, staged(): partial = jnp.dot(hidden, w_down, preferred_element_type=jnp.float32)  12.6 us
    unnamed x60, local copies, waits for them, and re-layouts  12.4 us
    gather x4, local copies, waits for them, and re-layouts, in_order(): return slots[(apart & 1) * 8 + (apart >> 1 & 1) * 4 + (apart >> 2)]  9.26 us
    concatenate x4, local copies, waits for them, and re-layouts, gather(): return jnp.concatenate([half, swap(half, 1)])  4.91 us
    dot_general x1, matrix products, staged(): jnp.einsum('td,kda->kta', normed, w_qkv, preferred_element_type=jnp.float32)  4.84 us
    concatenate x4, local copies, waits for them, and re-layouts, staged(): values = jnp.concatenate([cached[1], qkv[2]]).reshape(-1, HEADS, HEAD_DIM)  4.69 us
  transfers between devices with their start and end apart: 25, of which 10 were waited for; matrix products, arithmetic and copies ran while one was open for 29% of the time, Pallas kernels for 0%

profile of v1, /device:TPU:0, one launch (start us, length us, event | category | flops | bytes accessed | tf_op | source)
XLA Modules:
  0.0 156.0 jit_solution(6118981499210462762)
XLA Ops:
  0.0 3.0 %collective-permute-start = (bf16[3,5120]{1,0:T(4,128)(2,1)}, bf16[3,5120]{1,0:T(4,128)(2,1)S(1)}, u32[]{:S(2)}, u32[]{:S(2)}) collective-permute-start(bf16[3,5120]{1,0:T(4,128)(2,1)} %param.8), channel_id=1, source_target_pairs={{0,4},{1,5},{2,6},{3,7},{4,0},{5,1},{6,2},{7,3},{8,12},{9,13},{10,... | collective-permute-start | bytes 92168 | tf_op jit(solution)/shard_map/ppermute | solution.py:23
  3.0 2.6 %collective-permute-start.1 = (bf16[3,5120]{1,0:T(4,128)(2,1)}, bf16[3,5120]{1,0:T(4,128)(2,1)S(1)}, u32[]{:S(2)}, u32[]{:S(2)}) collective-permute-start(bf16[3,5120]{1,0:T(4,128)(2,1)} %param.8), channel_id=1, source_target_pairs={{0,8},{1,9},{2,10},{3,11},{4,12},{5,13},{6,14},{7,15},{8,0},{9,1},... | collective-permute-start | bytes 92168 | tf_op jit(solution)/shard_map/ppermute | solution.py:23
  6.5 3.5 %collective-permute-start.11 = (bf16[2,2,3,2560]{3,1,2,0:T(2,128)(2,1)}, bf16[2,2,3,2560]{3,1,2,0:T(2,128)(2,1)S(1)}, u32[]{:S(2)}, u32[]{:S(2)}) collective-permute-start(bf16[2,2,3,2560]{3,1,2,0:T(2,128)(2,1)} %param.12), channel_id=1, source_target_pairs={{0,8},{1,9},{2,10},{3,11},{4,12},{5,13},{6,14},{7,15},{8,0},{9,1},... | collective-permute-start | bytes 184328 | tf_op jit(solution)/shard_map/ppermute | solution.py:23
  12.4 2.9 %fusion.62 = (f32[1,5120]{1,0:T(1,128)}, f32[5120]{0:T(1024)}, f32[1,5120]{1,0:T(1,128)S(1)}, f32[1,5120]{1,0:T(1,128)}, f32[1,5120]{1,0:T(1,128)}, /*index=5*/f32[1,5120]{1,0:T(1,128)}, f32[1,5120]{1,0:T(1,128)}) fusion(f32[6,5120]{1,0:T(8,128)} %param.9), kind=kLoop, calls=%fused_computation.160 | loop fusion | flops 10240 | bytes 266240 | tf_op jit(solution)/shard_map/slice | solution.py:82
  19.7 3.3 %collective-permute-done.12 = bf16[2,2,3,2560]{3,1,2,0:T(2,128)(2,1)S(1)} collective-permute-done((bf16[2,2,3,2560]{3,1,2,0:T(2,128)(2,1)}, bf16[2,2,3,2560]{3,1,2,0:T(2,128)(2,1)S(1)}, u32[]{:S(2)}, u32[]{:S(2)}) %collective-permute-start.12) | collective-permute-done | bytes 61472 | tf_op jit(solution)/shard_map/ppermute | solution.py:23
  36.1 4.8 %constant_dynamic-update-slice_fusion.15 = (bf16[8,3,48,160]{3,2,1,0:T(8,128)(2,1)}, bf16[16,3,48,160]{3,2,1,0:T(8,128)(2,1)S(1)}, bf16[48,3,160]{2,0,1:T(8,128)(2,1)S(1)}) fusion(bf16[3,5120,160]{1,2,0:T(8,128)(2,1)} %param.10, f32[48,5120]{1,0:T(8,128)S(1)} %reshape.228, f32[5120]{0:T(1024)S(1)} %bitcast.172, f32[5120]{0:T(1024)} %bitcast.173, ...), kind=kOutput, calls=%fused_computation.89 | convolution fusion | flops 237181440 | bytes 6160768 | tf_op jit(solution)/shard_map/td,kda->kta/dot_general | solution.py:58
  42.5 2.8 %collective-permute-start.7 = (bf16[3,48,160]{2,1,0:T(8,128)(2,1)S(1)}, bf16[3,48,160]{2,1,0:T(8,128)(2,1)S(1)}, u32[]{:S(2)}, u32[]{:S(2)}) collective-permute-start(bf16[3,48,160]{2,1,0:T(8,128)(2,1)S(1)} %bitcast.153), channel_id=1, source_target_pairs={{0,12},{1,13},{2,14},{3,15},{4,8},{5,9},{6,10},{7,11},{8,4},{9,5},... | collective-permute-start | bytes 138248 | tf_op jit(solution)/shard_map/ppermute | solution.py:23
  46.3 3.8 %collective-permute-done.6 = bf16[3,48,160]{2,1,0:T(8,128)(2,1)S(1)} collective-permute-done((bf16[3,48,160]{2,1,0:T(8,128)(2,1)S(1)}, bf16[3,48,160]{2,1,0:T(8,128)(2,1)S(1)}, u32[]{:S(2)}, u32[]{:S(2)}) %collective-permute-start.6) | collective-permute-done | bytes 46112 | tf_op jit(solution)/shard_map/ppermute | solution.py:23
  52.8 4.1 %collective-permute-done.8 = bf16[4,3,48,160]{3,2,1,0:T(8,128)(2,1)S(1)} collective-permute-done((bf16[4,3,48,160]{3,2,1,0:T(8,128)(2,1)S(1)}, bf16[4,3,48,160]{3,2,1,0:T(8,128)(2,1)S(1)}, u32[]{:S(2)}, u32[]{:S(2)}) %collective-permute-start.8) | collective-permute-done | bytes 184352 | tf_op jit(solution)/shard_map/ppermute | solution.py:23
  59.9 3.8 %gather_fusion.2 = bf16[16,2,2,3,2560]{4,2,3,1,0:T(2,128)(2,1)S(1)} fusion(bf16[16,2,2,3,2560]{4,2,3,1,0:T(2,128)(2,1)} %constant_dynamic-update-slice_fusion.27, s32[1024]{0:T(1024)S(1)} %pad_clamp_fusion.1), kind=kCustom, calls=%fused_computation.2 | custom fusion | bytes 1966144 | tf_op jit(solution)/shard_map/gather | solution.py:34
  68.5 1.9 %constant_dynamic-update-slice_fusion.16 = bf16[16,3,48,160]{3,2,1,0:T(8,128)(2,1)} fusion(bf16[16,3,48,160]{3,2,1,0:T(8,128)(2,1)} %copy-done.8, bf16[8,3,48,160]{3,2,1,0:T(8,128)(2,1)} %collective-permute-done.9), kind=kLoop, calls=%fused_computation.90 | loop fusion | bytes 1179648 | tf_op jit(solution)/shard_map/concatenate | solution.py:29
  75.4 2.5 %reshape.229 = f32[48,20,128]{2,1,0:T(8,128)} reshape(f32[1,48,16,160]{3,2,1,0:T(8,128)} %copy.66) | data formatting | bytes 983040 | tf_op jit(solution)/shard_map/convert_element_type | solution.py:60
  81.0 1.9 %copy.73 = bf16[1,48,16,160]{3,2,1,0:T(8,128)(2,1)} copy(bf16[1,48,16,160]{3,1,0,2:T(8,128)(2,1)} %get-tuple-element.12) | data formatting | bytes 491520 | tf_op jit(solution)/shard_map/slice | solution.py:63
  82.9 2.4 %concatenate.55 = bf16[48,20,128]{2,1,0:T(8,128)(2,1)} reshape(bf16[1,48,16,160]{3,2,1,0:T(8,128)(2,1)} %copy.73) | data formatting | bytes 491520 | tf_op jit(solution)/shard_map/concatenate | solution.py:63
  89.5 2.6 %collective-permute-start.15 = (bf16[48,320]{1,0:T(8,128)(2,1)S(1)}, bf16[48,320]{1,0:T(8,128)(2,1)S(1)}, u32[]{:S(2)}, u32[]{:S(2)}) collective-permute-start(bf16[48,320]{1,0:T(8,128)(2,1)S(1)} %get-tuple-element.69), channel_id=1, source_target_pairs={{0,4},{1,5},{2,6},{3,7},{4,0},{5,1},{6,2},{7,3},{8,12},{9,13},{10,... | collective-permute-start | bytes 92168 | tf_op jit(solution)/shard_map/ppermute | solution.py:23
  94.4 2.7 %collective-permute-done.16 = bf16[48,320]{1,0:T(8,128)(2,1)S(1)} collective-permute-done((bf16[48,320]{1,0:T(8,128)(2,1)S(1)}, bf16[48,320]{1,0:T(8,128)(2,1)S(1)}, u32[]{:S(2)}, u32[]{:S(2)}) %collective-permute-start.16) | collective-permute-done | bytes 30752 | tf_op jit(solution)/shard_map/ppermute | solution.py:23
  101.5 2.2 %collective-permute-done.18 = bf16[4,48,320]{2,1,0:T(8,128)(2,1)S(1)} collective-permute-done((bf16[4,48,320]{2,1,0:T(8,128)(2,1)S(1)}, bf16[4,48,320]{2,1,0:T(8,128)(2,1)S(1)}, u32[]{:S(2)}, u32[]{:S(2)}) %collective-permute-start.18) | collective-permute-done | bytes 122912 | tf_op jit(solution)/shard_map/ppermute | solution.py:23
  108.1 2.5 %gather_fusion.3 = bf16[16,48,320]{2,1,0:T(8,128)(2,1)} fusion(bf16[16,48,320]{2,1,0:T(8,128)(2,1)} %constant_dynamic-update-slice_fusion.38, s32[1024]{0:T(1024)S(1)} %pad_clamp_fusion.1), kind=kCustom, calls=%fused_computation.3 | custom fusion | bytes 983104 | tf_op jit(solution)/shard_map/gather | solution.py:34
  114.6 12.6 %fusion.41 = f32[48,5120]{1,0:T(8,128)} fusion(bf16[864,5120]{1,0:T(8,128)(2,1)} %param.15, bf16[5120,864]{0,1:T(8,128)(2,1)} %param.14, f32[48,5120]{1,0:T(8,128)} %copy-done.2, f32[48,5120]{1,0:T(8,128)} %reshape.232, f32[5120]{0:T(1024)S(1)} %bitcast.170, f32[5120]{0:T(1024)S(1)} %bitcast.171, f32[48]{0:T(128)S(1)} %add_rsqrt_fusion.1, ...), kind=kOutput, calls=%fused_computation.70 | convolution fusion | flops 851440128 | bytes 20705664 | tf_op jit(solution)/shard_map/dot_general | solution.py:79
  127.1 2.7 %reshape.226 = f32[16,3,5120]{2,1,0:T(4,128)} reshape(f32[48,5120]{1,0:T(8,128)} %fusion.41) | data formatting | bytes 1966080 | tf_op jit(solution)/shard_map/reshape | solution.py:80
  129.8 3.9 %gather_fusion.4 = f32[16,3,5120]{2,1,0:T(4,128)} fusion(f32[16,3,5120]{2,1,0:T(4,128)} %reshape.226, s32[1024]{0:T(1024)S(1)} %pad_clamp_fusion), kind=kCustom, calls=%fused_computation.4 | custom fusion | bytes 1966144 | tf_op jit(solution)/shard_map/gather | solution.py:39
  139.3 4.2 %collective-permute-done.21 = bf16[4,3,5120]{2,0,1:T(4,128)(2,1)S(1)} collective-permute-done((bf16[4,3,5120]{2,0,1:T(4,128)(2,1)S(1)}, bf16[4,3,5120]{2,0,1:T(4,128)(2,1)S(1)}, u32[]{:S(2)}, u32[]{:S(2)}) %collective-permute-start.21) | collective-permute-done | bytes 122912 | tf_op jit(solution)/shard_map/ppermute | solution.py:23
  145.3 2.2 %collective-permute-start.23 = (bf16[3,5120]{1,0:T(4,128)(2,1)}, bf16[3,5120]{1,0:T(4,128)(2,1)}, u32[]{:S(2)}, u32[]{:S(2)}) collective-permute-start(bf16[3,5120]{1,0:T(4,128)(2,1)} %bitcast.140), channel_id=1, source_target_pairs={{0,8},{1,9},{2,10},{3,11},{4,12},{5,13},{6,14},{7,15},{8,0},{9,1},... | collective-permute-start | bytes 92168 | tf_op jit(solution)/shard_map/ppermute | solution.py:23
  148.2 2.0 %collective-permute-start.24 = (bf16[3,5120]{1,0:T(4,128)(2,1)}, bf16[3,5120]{1,0:T(4,128)(2,1)}, u32[]{:S(2)}, u32[]{:S(2)}) collective-permute-start(bf16[3,5120]{1,0:T(4,128)(2,1)} %bitcast.139), channel_id=1, source_target_pairs={{0,12},{1,13},{2,14},{3,15},{4,8},{5,9},{6,10},{7,11},{8,4},{9,5},... | collective-permute-start | bytes 92168 | tf_op jit(solution)/shard_map/ppermute | solution.py:23
  (164 shorter events, 74.7 us)
Async XLA Ops:
  0.0 16.7 %collective-permute-start = (bf16[3,5120]{1,0:T(4,128)(2,1)}, bf16[3,5120]{1,0:T(4,128)(2,1)S(1)}, u32[]{:S(2)}, u32[]{:S(2)}) collective-permute-start(bf16[3,5120]{1,0:T(4,128)(2,1)} %param.8), channel_id=1, source_target_pairs={{0,4},{1,5},{2,6},{3,7},{4,0},{5,1},{6,2},{7,3},{8,12},{9,13},{10,... | collective-permute-start | bytes 92168 | tf_op jit(solution)/shard_map/ppermute | solution.py:23
  3.0 13.8 %collective-permute-start.1 = (bf16[3,5120]{1,0:T(4,128)(2,1)}, bf16[3,5120]{1,0:T(4,128)(2,1)S(1)}, u32[]{:S(2)}, u32[]{:S(2)}) collective-permute-start(bf16[3,5120]{1,0:T(4,128)(2,1)} %param.8), channel_id=1, source_target_pairs={{0,8},{1,9},{2,10},{3,11},{4,12},{5,13},{6,14},{7,15},{8,0},{9,1},... | collective-permute-start | bytes 92168 | tf_op jit(solution)/shard_map/ppermute | solution.py:23
  5.6 11.2 %collective-permute-start.2 = (bf16[3,5120]{1,0:T(4,128)(2,1)}, bf16[3,5120]{1,0:T(4,128)(2,1)S(1)}, u32[]{:S(2)}, u32[]{:S(2)}) collective-permute-start(bf16[3,5120]{1,0:T(4,128)(2,1)} %param.8), channel_id=1, source_target_pairs={{0,12},{1,13},{2,14},{3,15},{4,8},{5,9},{6,10},{7,11},{8,4},{9,5},... | collective-permute-start | bytes 92168 | tf_op jit(solution)/shard_map/ppermute | solution.py:23
  5.6 14.0 %collective-permute-start.10 = (bf16[2,2,3,2560]{3,1,2,0:T(2,128)(2,1)}, bf16[2,2,3,2560]{3,1,2,0:T(2,128)(2,1)S(1)}, u32[]{:S(2)}, u32[]{:S(2)}) collective-permute-start(bf16[2,2,3,2560]{3,1,2,0:T(2,128)(2,1)} %param.12), channel_id=1, source_target_pairs={{0,4},{1,5},{2,6},{3,7},{4,0},{5,1},{6,2},{7,3},{8,12},{9,13},{10,... | collective-permute-start | bytes 184328 | tf_op jit(solution)/shard_map/ppermute | solution.py:23
  6.5 13.1 %collective-permute-start.11 = (bf16[2,2,3,2560]{3,1,2,0:T(2,128)(2,1)}, bf16[2,2,3,2560]{3,1,2,0:T(2,128)(2,1)S(1)}, u32[]{:S(2)}, u32[]{:S(2)}) collective-permute-start(bf16[2,2,3,2560]{3,1,2,0:T(2,128)(2,1)} %param.12), channel_id=1, source_target_pairs={{0,8},{1,9},{2,10},{3,11},{4,12},{5,13},{6,14},{7,15},{8,0},{9,1},... | collective-permute-start | bytes 184328 | tf_op jit(solution)/shard_map/ppermute | solution.py:23
  16.7 6.3 %collective-permute-start.12 = (bf16[2,2,3,2560]{3,1,2,0:T(2,128)(2,1)}, bf16[2,2,3,2560]{3,1,2,0:T(2,128)(2,1)S(1)}, u32[]{:S(2)}, u32[]{:S(2)}) collective-permute-start(bf16[2,2,3,2560]{3,1,2,0:T(2,128)(2,1)} %param.12), channel_id=1, source_target_pairs={{0,12},{1,13},{2,14},{3,15},{4,8},{5,9},{6,10},{7,11},{8,4},{9,5},... | collective-permute-start | bytes 184328 | tf_op jit(solution)/shard_map/ppermute | solution.py:23
  17.7 9.4 %collective-permute-start.3 = (bf16[4,3,5120]{2,1,0:T(4,128)(2,1)S(1)}, bf16[4,3,5120]{2,1,0:T(4,128)(2,1)S(1)}, u32[]{:S(2)}, u32[]{:S(2)}) collective-permute-start(bf16[4,3,5120]{2,1,0:T(4,128)(2,1)S(1)} %pad_maximum_fusion.2), channel_id=1, source_target_pairs={{0,2},{1,3},{2,0},{3,1},{4,6},{5,7},{6,4},{7,5},{8,10},{9,11},{10,... | collective-permute-start | bytes 368648 | tf_op jit(solution)/shard_map/ppermute | solution.py:23
  24.2 21.2 %collective-permute-start.13 = (bf16[4,2,2,3,2560]{4,2,3,1,0:T(2,128)(2,1)}, bf16[4,2,2,3,2560]{4,2,3,1,0:T(2,128)(2,1)S(1)}, u32[]{:S(2)}, u32[]{:S(2)}) collective-permute-start(bf16[4,2,2,3,2560]{4,2,3,1,0:T(2,128)(2,1)} %pad_maximum_fusion.1), channel_id=1, source_target_pairs={{0,2},{1,3},{2,0},{3,1},{4,6},{5,7},{6,4},{7,5},{8,10},{9,11},{10,... | collective-permute-start | bytes 737288 | tf_op jit(solution)/shard_map/ppermute | solution.py:23
  27.9 1.8 %collective-permute-start.4 = (bf16[8,3,5120]{2,1,0:T(4,128)(2,1)}, bf16[8,3,5120]{2,1,0:T(4,128)(2,1)S(1)}, u32[]{:S(2)}, u32[]{:S(2)}) collective-permute-start(bf16[8,3,5120]{2,1,0:T(4,128)(2,1)} %get-tuple-element.27), channel_id=1, source_target_pairs={{0,1},{1,0},{2,3},{3,2},{4,5},{5,4},{6,7},{7,6},{8,9},{9,8},{10,11... | collective-permute-start | bytes 737288 | tf_op jit(solution)/shard_map/ppermute | solution.py:23
  40.9 5.4 %collective-permute-start.5 = (bf16[3,48,160]{2,1,0:T(8,128)(2,1)S(1)}, bf16[3,48,160]{2,1,0:T(8,128)(2,1)S(1)}, u32[]{:S(2)}, u32[]{:S(2)}) collective-permute-start(bf16[3,48,160]{2,1,0:T(8,128)(2,1)S(1)} %bitcast.151), channel_id=1, source_target_pairs={{0,4},{1,5},{2,6},{3,7},{4,0},{5,1},{6,2},{7,3},{8,12},{9,13},{10,... | collective-permute-start | bytes 138248 | tf_op jit(solution)/shard_map/ppermute | solution.py:23
  40.9 9.2 %collective-permute-start.6 = (bf16[3,48,160]{2,1,0:T(8,128)(2,1)S(1)}, bf16[3,48,160]{2,1,0:T(8,128)(2,1)S(1)}, u32[]{:S(2)}, u32[]{:S(2)}) collective-permute-start(bf16[3,48,160]{2,1,0:T(8,128)(2,1)S(1)} %bitcast.152), channel_id=1, source_target_pairs={{0,8},{1,9},{2,10},{3,11},{4,12},{5,13},{6,14},{7,15},{8,0},{9,1},... | collective-permute-start | bytes 138248 | tf_op jit(solution)/shard_map/ppermute | solution.py:23
  42.5 7.6 %collective-permute-start.7 = (bf16[3,48,160]{2,1,0:T(8,128)(2,1)S(1)}, bf16[3,48,160]{2,1,0:T(8,128)(2,1)S(1)}, u32[]{:S(2)}, u32[]{:S(2)}) collective-permute-start(bf16[3,48,160]{2,1,0:T(8,128)(2,1)S(1)} %bitcast.153), channel_id=1, source_target_pairs={{0,12},{1,13},{2,14},{3,15},{4,8},{5,9},{6,10},{7,11},{8,4},{9,5},... | collective-permute-start | bytes 138248 | tf_op jit(solution)/shard_map/ppermute | solution.py:23
  46.3 11.4 %collective-permute-start.14 = (bf16[8,2,2,3,2560]{4,2,3,1,0:T(2,128)(2,1)S(1)}, bf16[8,2,2,3,2560]{4,2,3,1,0:T(2,128)(2,1)S(1)}, u32[]{:S(2)}, u32[]{:S(2)}) collective-permute-start(bf16[8,2,2,3,2560]{4,2,3,1,0:T(2,128)(2,1)S(1)} %get-tuple-element.18), channel_id=1, source_target_pairs={{0,1},{1,0},{2,3},{3,2},{4,5},{5,4},{6,7},{7,6},{8,9},{9,8},{10,11... | collective-permute-start | bytes 1474568 | tf_op jit(solution)/shard_map/ppermute | solution.py:23
  50.2 6.8 %collective-permute-start.8 = (bf16[4,3,48,160]{3,2,1,0:T(8,128)(2,1)S(1)}, bf16[4,3,48,160]{3,2,1,0:T(8,128)(2,1)S(1)}, u32[]{:S(2)}, u32[]{:S(2)}) collective-permute-start(bf16[4,3,48,160]{3,2,1,0:T(8,128)(2,1)S(1)} %pad_maximum_fusion), channel_id=1, source_target_pairs={{0,2},{1,3},{2,0},{3,1},{4,6},{5,7},{6,4},{7,5},{8,10},{9,11},{10,... | collective-permute-start | bytes 552968 | tf_op jit(solution)/shard_map/ppermute | solution.py:23
  57.8 10.7 %collective-permute-start.9 = (bf16[8,3,48,160]{3,2,1,0:T(8,128)(2,1)}, bf16[8,3,48,160]{3,2,1,0:T(8,128)(2,1)}, u32[]{:S(2)}, u32[]{:S(2)}) collective-permute-start(bf16[8,3,48,160]{3,2,1,0:T(8,128)(2,1)} %get-tuple-element.16), channel_id=1, source_target_pairs={{0,1},{1,0},{2,3},{3,2},{4,5},{5,4},{6,7},{7,6},{8,9},{9,8},{10,11... | collective-permute-start | bytes 1105928 | tf_op jit(solution)/shard_map/ppermute | solution.py:23
  89.5 4.9 %collective-permute-start.15 = (bf16[48,320]{1,0:T(8,128)(2,1)S(1)}, bf16[48,320]{1,0:T(8,128)(2,1)S(1)}, u32[]{:S(2)}, u32[]{:S(2)}) collective-permute-start(bf16[48,320]{1,0:T(8,128)(2,1)S(1)} %get-tuple-element.69), channel_id=1, source_target_pairs={{0,4},{1,5},{2,6},{3,7},{4,0},{5,1},{6,2},{7,3},{8,12},{9,13},{10,... | collective-permute-start | bytes 92168 | tf_op jit(solution)/shard_map/ppermute | solution.py:23
  92.1 5.1 %collective-permute-start.16 = (bf16[48,320]{1,0:T(8,128)(2,1)S(1)}, bf16[48,320]{1,0:T(8,128)(2,1)S(1)}, u32[]{:S(2)}, u32[]{:S(2)}) collective-permute-start(bf16[48,320]{1,0:T(8,128)(2,1)S(1)} %get-tuple-element.69), channel_id=1, source_target_pairs={{0,8},{1,9},{2,10},{3,11},{4,12},{5,13},{6,14},{7,15},{8,0},{9,1},... | collective-permute-start | bytes 92168 | tf_op jit(solution)/shard_map/ppermute | solution.py:23
  92.6 5.8 %collective-permute-start.17 = (bf16[48,320]{1,0:T(8,128)(2,1)S(1)}, bf16[48,320]{1,0:T(8,128)(2,1)S(1)}, u32[]{:S(2)}, u32[]{:S(2)}) collective-permute-start(bf16[48,320]{1,0:T(8,128)(2,1)S(1)} %get-tuple-element.69), channel_id=1, source_target_pairs={{0,12},{1,13},{2,14},{3,15},{4,8},{5,9},{6,10},{7,11},{8,4},{9,5},... | collective-permute-start | bytes 92168 | tf_op jit(solution)/shard_map/ppermute | solution.py:23
  98.4 5.2 %collective-permute-start.18 = (bf16[4,48,320]{2,1,0:T(8,128)(2,1)S(1)}, bf16[4,48,320]{2,1,0:T(8,128)(2,1)S(1)}, u32[]{:S(2)}, u32[]{:S(2)}) collective-permute-start(bf16[4,48,320]{2,1,0:T(8,128)(2,1)S(1)} %pad_maximum_fusion.3), channel_id=1, source_target_pairs={{0,2},{1,3},{2,0},{3,1},{4,6},{5,7},{6,4},{7,5},{8,10},{9,11},{10,... | collective-permute-start | bytes 368648 | tf_op jit(solution)/shard_map/ppermute | solution.py:23
  104.4 1.9 %collective-permute-start.19 = (bf16[8,48,320]{2,1,0:T(8,128)(2,1)}, bf16[8,48,320]{2,1,0:T(8,128)(2,1)}, u32[]{:S(2)}, u32[]{:S(2)}) collective-permute-start(bf16[8,48,320]{2,1,0:T(8,128)(2,1)} %get-tuple-element.29), channel_id=1, source_target_pairs={{0,1},{1,0},{2,3},{3,2},{4,5},{5,4},{6,7},{7,6},{8,9},{9,8},{10,11... | collective-permute-start | bytes 737288 | tf_op jit(solution)/shard_map/ppermute | solution.py:23
  138.0 5.4 %collective-permute-start.21 = (bf16[4,3,5120]{2,0,1:T(4,128)(2,1)S(1)}, bf16[4,3,5120]{2,0,1:T(4,128)(2,1)S(1)}, u32[]{:S(2)}, u32[]{:S(2)}) collective-permute-start(bf16[4,3,5120]{2,0,1:T(4,128)(2,1)S(1)} %bitcast.169), channel_id=1, source_target_pairs={{0,2},{1,3},{2,0},{3,1},{4,6},{5,7},{6,4},{7,5},{8,10},{9,11},{10,... | collective-permute-start | bytes 368648 | tf_op jit(solution)/shard_map/ppermute | solution.py:23
  144.4 9.8 %collective-permute-start.22 = (bf16[3,5120]{1,0:T(4,128)(2,1)S(1)}, bf16[3,5120]{1,0:T(4,128)(2,1)}, u32[]{:S(2)}, u32[]{:S(2)}) collective-permute-start(bf16[3,5120]{1,0:T(4,128)(2,1)S(1)} %bitcast.177), channel_id=1, source_target_pairs={{0,4},{1,5},{2,6},{3,7},{4,0},{5,1},{6,2},{7,3},{8,12},{9,13},{10,... | collective-permute-start | bytes 92168 | tf_op jit(solution)/shard_map/ppermute | solution.py:23
  145.3 9.0 %collective-permute-start.23 = (bf16[3,5120]{1,0:T(4,128)(2,1)}, bf16[3,5120]{1,0:T(4,128)(2,1)}, u32[]{:S(2)}, u32[]{:S(2)}) collective-permute-start(bf16[3,5120]{1,0:T(4,128)(2,1)} %bitcast.140), channel_id=1, source_target_pairs={{0,8},{1,9},{2,10},{3,11},{4,12},{5,13},{6,14},{7,15},{8,0},{9,1},... | collective-permute-start | bytes 92168 | tf_op jit(solution)/shard_map/ppermute | solution.py:23
  148.2 6.1 %collective-permute-start.24 = (bf16[3,5120]{1,0:T(4,128)(2,1)}, bf16[3,5120]{1,0:T(4,128)(2,1)}, u32[]{:S(2)}, u32[]{:S(2)}) collective-permute-start(bf16[3,5120]{1,0:T(4,128)(2,1)} %bitcast.139), channel_id=1, source_target_pairs={{0,12},{1,13},{2,14},{3,15},{4,8},{5,9},{6,10},{7,11},{8,4},{9,5},... | collective-permute-start | bytes 92168 | tf_op jit(solution)/shard_map/ppermute | solution.py:23
  (21 other events, 182.9 us)

commit v2 on v0

--- a/solution.py
+++ b/solution.py
@@ -3,6 +3,8 @@
 import jax
 import jax.numpy as jnp
 from jax import lax
+from jax.experimental import pallas as pl
+from jax.experimental.pallas import tpu as pltpu
 from jax.sharding import PartitionSpec as P
 
 HEAD_DIM = 128
@@ -19,7 +21,218 @@
     return values * lax.rsqrt(jnp.mean(values * values, axis=-1, keepdims=True) + 1e-06) * gain
 
 
-def local(tokens, modulation, w_qkv, norm_gains, cache_kv, w_out, w_up, w_down):
+VMEM = pl.BlockSpec(memory_space=pltpu.VMEM)
+ANY = pl.BlockSpec(memory_space=pl.ANY)
+NT = (((1,), (1,)), ((), ()))
+
+
+def call(body, outs, *operands, any_space=(), scratch=(), limit=24, flops=0, moved=0):
+    return pl.pallas_call(
+        body,
+        out_shape=[jax.ShapeDtypeStruct(shape, dtype) for shape, dtype in outs],
+        in_specs=[ANY if i in any_space else VMEM for i in range(len(operands))],
+        out_specs=[VMEM] * len(outs),
+        scratch_shapes=list(scratch),
+        compiler_params=pltpu.CompilerParams(vmem_limit_bytes=limit << 20),
+        cost_estimate=pl.CostEstimate(flops=flops, bytes_accessed=moved, transcendentals=0),
+    )(*operands)
+
+
+def load(weights):
+    rows, width = weights.shape
+    cuts = [rows * i // 4 // 16 * 16 for i in range(4)] + [rows]
+
+    def body(source, target, sems):
+        copies = [
+            pltpu.make_async_copy(source.at[pl.ds(a, b - a)], target.at[pl.ds(a, b - a)], sems.at[i])
+            for i, (a, b) in enumerate(zip(cuts, cuts[1:]))
+        ]
+        for copy in copies:
+            copy.start()
+        for copy in copies:
+            copy.wait()
+
+    scratch = [pltpu.SemaphoreType.DMA((4,))]
+    moved = rows * width * 4
+    return call(body, [((rows, width), weights.dtype)], weights, any_space=(0,), scratch=scratch, moved=moved)[0]
+
+
+def swap(values, offset):
+    return lax.ppermute(values, "seq", [(i, i ^ offset) for i in range(16)])
+
+
+def stack(pieces):
+    def body(*refs):
+        for i, ref in enumerate(refs[:-1]):
+            refs[-1][i] = ref[...]
+
+    return call(body, [((len(pieces), *pieces[0].shape), pieces[0].dtype)], *pieces)[0]
+
+
+def gather(block, tie=lambda pieces: pieces):
+    planes = stack(tie([block] + [swap(block, 4 * z) for z in (1, 2, 3)]))
+    across = swap(planes, 2)
+    return [planes, across, swap(planes, 1), swap(across, 1)]
+
+
+def apart(slot, z):
+    return 4 * z + 2 * (slot & 1) + (slot >> 1)
+
+
+def place(stacks, target):
+    me = lax.axis_index("seq")
+    for slot, ref in enumerate(stacks):
+        for z in range(4):
+            target[me ^ apart(slot, z)] = ref[z]
+
+
+def normalize(values, shift, gain):
+    return (layer_norm(values) * (1.0 + gain) + shift).astype(jnp.bfloat16)
+
+
+def project_qkv(s0, s1, s2, s3, mod, weights, tokens_out, qkv_out, slots, flat):
+    place((s0, s1, s2, s3), slots)
+    for j in range(16):
+        flat[3 * j : 3 * j + 3, :] = slots[j].astype(jnp.float32)
+    tokens = flat[...]
+    tokens_out[...] = tokens.astype(jnp.bfloat16)
+    normed = normalize(tokens, mod[0:1, :], mod[1:2, :])
+    qkv_out[...] = lax.dot_general(normed, weights[...], NT, preferred_element_type=jnp.float32).astype(jnp.bfloat16)
+
+
+def line_up(s0, s1, s2, s3, keys_out, values_out, keys, values):
+    for slot, ref in enumerate((s0, s1, s2, s3)):
+        for z in range(4):
+            for token in range(3):
+                row = 6 * (4 * slot + z) + 2 * token
+                keys[row : row + 2, :] = ref[z, 0, token].astype(jnp.float32)
+                values[row : row + 2, :] = ref[z, 1, token].astype(jnp.float32)
+    keys_out[...] = keys[...].astype(jnp.bfloat16)
+    values_out[...] = values[...].astype(jnp.bfloat16)
+
+
+def attend(s0, s1, s2, s3, old_keys, old_values, gains, weights, out, slots, attended):
+    place((s0, s1, s2, s3), slots)
+    pieces = [slots[j].astype(jnp.float32) for j in range(16)]
+    queries, keys, values = (
+        jnp.concatenate([piece[:, 160 * i : 160 * i + 160] for piece in pieces], axis=1) for i in range(3)
+    )
+    queries = rms_norm(queries, gains[0:1, :]).astype(jnp.bfloat16)
+    keys = jnp.concatenate([old_keys[...], rms_norm(keys, gains[1:2, :]).astype(jnp.bfloat16)], axis=0)
+    values = jnp.concatenate([old_values[...], values.astype(jnp.bfloat16)], axis=0)
+    for head in range(HEADS):
+        cols = slice(HEAD_DIM * head, HEAD_DIM * (head + 1))
+        scores = lax.dot_general(queries[:, cols], keys[:, cols], NT, preferred_element_type=jnp.float32)
+        scores = scores * (1.0 / math.sqrt(HEAD_DIM))
+        expo = jnp.exp(scores - jnp.max(scores, axis=-1, keepdims=True))
+        total = jnp.sum(expo, axis=-1, keepdims=True)
+        summed = jnp.dot(expo.astype(jnp.bfloat16), values[:, cols], preferred_element_type=jnp.float32)
+        attended[:, cols] = (summed / total).astype(jnp.bfloat16)
+    out[...] = lax.dot_general(attended[...], weights[...], NT, preferred_element_type=jnp.float32).astype(jnp.bfloat16)
+
+
+def feed_forward(s0, s1, s2, s3, tokens, own, mod, w_up, w_down, keep, send, residual_out, slots):
+    place((s0, s1, s2, s3), slots)
+    projected = jnp.concatenate([slots[j] for j in range(16)], axis=1)
+    gate = mod[2:3, :]
+    residual = tokens[...].astype(jnp.float32) + gate * projected.astype(jnp.float32)
+    normed = normalize(residual, mod[3:4, :], mod[4:5, :])
+    hidden = lax.dot_general(normed, w_up[...], NT, preferred_element_type=jnp.float32)
+    hidden = jax.nn.gelu(hidden, approximate=True).astype(jnp.bfloat16)
+    me = lax.axis_index("seq")
+    row = lax.broadcasted_iota(jnp.int32, (48, 48), 0)
+    token = lax.broadcasted_iota(jnp.int32, (48, 48), 1)
+    block = (row * 171) >> 9
+    device = me ^ (4 * (block & 3) + 2 * ((block >> 2) & 1) + (block >> 3))
+    pick = (token == 3 * device + row - 3 * block).astype(jnp.bfloat16)
+    hidden = jnp.dot(pick, hidden, preferred_element_type=jnp.float32).astype(jnp.bfloat16)
+    partial = jnp.dot(hidden, w_down[...], preferred_element_type=jnp.float32)
+    keep[...] = partial[:24]
+    send[...] = partial[24:].astype(jnp.bfloat16)
+    mine = jnp.dot(pick[0:16], projected, preferred_element_type=jnp.float32)[0:3]
+    residual_out[...] = own[...].astype(jnp.float32) + gate * mine
+
+
+def add_near(keep, got, keep_out, send_out):
+    total = keep[...] + got[...].astype(jnp.float32)
+    keep_out[...] = total[:12]
+    send_out[...] = total[12:].astype(jnp.bfloat16)
+
+
+def add_plane(keep, got, keep_out, send1, send2, send3):
+    total = keep[...] + got[...].astype(jnp.float32)
+    keep_out[...] = total[0:3]
+    for z, send in ((1, send1), (2, send2), (3, send3)):
+        send[...] = total[3 * z : 3 * z + 3].astype(jnp.bfloat16)
+
+
+def finish(keep, got1, got2, got3, residual, mod, out):
+    total = keep[...]
+    for got in (got1, got2, got3):
+        total = total + got[...].astype(jnp.float32)
+    out[...] = (residual[...] + mod[5:6, :] * total).astype(jnp.bfloat16)
+
+
+def staged(tokens, modulation, w_qkv, norm_gains, cache_kv, w_out, w_up, w_down):
+    f32, bf16 = jnp.float32, jnp.bfloat16
+    w_qkv = load(jnp.swapaxes(w_qkv, 1, 2).reshape(480, 5120))
+
+    def after_load(pieces):
+        nonlocal w_qkv
+        *pieces, w_qkv = lax.optimization_barrier((*pieces, w_qkv))
+        return pieces
+
+    token_stacks = gather(tokens, after_load)
+    cache_stacks = gather(cache_kv.transpose(0, 2, 1, 3))
+    all_tokens, qkv = call(
+        project_qkv,
+        [((48, 5120), bf16), ((48, 480), bf16)],
+        *token_stacks,
+        modulation,
+        w_qkv,
+        scratch=[pltpu.VMEM((16, 3, 5120), bf16), pltpu.VMEM((48, 5120), f32)],
+        flops=2 * 48 * 5120 * 480,
+    )
+    old_keys, old_values = call(
+        line_up, [((96, 2560), bf16)] * 2, *cache_stacks, scratch=[pltpu.VMEM((96, 2560), f32)] * 2, moved=8 << 20
+    )
+    projected = call(
+        attend,
+        [((48, 320), bf16)],
+        *gather(qkv),
+        old_keys,
+        old_values,
+        norm_gains,
+        w_out.T,
+        scratch=[pltpu.VMEM((16, 48, 480), bf16), pltpu.VMEM((48, 2560), bf16)],
+        flops=2 * 48 * 2560 * 608,
+    )[0]
+    w_up, w_down = load(w_up.T), load(w_down)
+
+    def after_loads(pieces):
+        nonlocal w_up, w_down
+        *pieces, w_up, w_down = lax.optimization_barrier((*pieces, w_up, w_down))
+        return pieces
+
+    keep, send, residual = call(
+        feed_forward,
+        [((24, 5120), f32), ((24, 5120), bf16), ((3, 5120), f32)],
+        *gather(projected, after_loads),
+        all_tokens,
+        tokens,
+        modulation,
+        w_up,
+        w_down,
+        scratch=[pltpu.VMEM((16, 48, 320), bf16)],
+        flops=4 * 48 * 5120 * 864,
+    )
+    keep, send = call(add_near, [((12, 5120), f32), ((12, 5120), bf16)], keep, swap(send, 1))
+    keep, *sends = call(add_plane, [((3, 5120), f32)] + [((3, 5120), bf16)] * 3, keep, swap(send, 2))
+    got = [swap(send, 4 * z) for z, send in zip((1, 2, 3), sends)]
+    return call(finish, [((3, 5120), bf16)], keep, *got, residual, modulation)[0]
+
+
+def general(tokens, modulation, w_qkv, norm_gains, cache_kv, w_out, w_up, w_down):
     own_rows = tokens.shape[0]
     width = HEADS * HEAD_DIM
     scale = 1.0 / math.sqrt(HEAD_DIM)
@@ -98,4 +311,5 @@
         P("seq", None),
     )
     out_specs = P(("groups", "seq"), None)
+    local = staged if mesh.shape["seq"] == 16 else general
     return jax.shard_map(local, mesh=mesh, in_specs=in_specs, out_specs=out_specs, check_vma=False)

time: 267 us -> 90.5 us (0.34)
  blocking collectives: 119 us -> 0 us
  waiting for transfers between devices: 96.9 us -> 35.6 us
  starting transfers between devices: 3.54 us -> 29 us
  matrix products: 19.9 us -> 0 us
  Pallas kernels: 0 us -> 17.6 us
  between operations: 14.3 us -> 0.2 us
  other arithmetic: 7.35 us -> 0.01 us
    all_gather x5 -> x0, blocking collectives: 109 us -> none  [the longest x1 25.1 us: local(): lax.all_gather(normed, 'seq', axis=0, tiled=True)]
    unnamed x2 -> x0, waiting for transfers between devices: 90.4 us -> none
    ppermute x0 -> x29, waiting for transfers between devices: none -> 35.6 us  [swap(): return lax.ppermute(values, 'seq', [(i, i ^ offset) for i in range(16)])]
    ppermute x0 -> x29, starting transfers between devices: none -> 29 us  [swap(): return lax.ppermute(values, 'seq', [(i, i ^ offset) for i in range(16)])]
    dot_general x5 -> x0, matrix products: 19.9 us -> none  [the longest x1 11.9 us: local(): jnp.dot(hidden, w_down, preferred_element_type=jnp.float32)]
    pallas_call x0 -> x14, Pallas kernels: none -> 17.6 us  [call(): pl.pallas_call(body, out_shape=[jax.ShapeDtypeStruct(shape, dtype) for sh...]
    all_to_all x1 -> x0, blocking collectives: 9.34 us -> none  [local(): lax.all_to_all(projected_cols, 'seq', split_axis=0, concat_axis=1, tiled=...]
    all_to_all x1 -> x0, waiting for transfers between devices: 6.42 us -> none  [local(): lax.all_to_all(qkv_cols, 'seq', split_axis=1, concat_axis=2, tiled=True)]
  transfers between devices with their start and end apart: 2 -> 29, of which waited for: 2 -> 14; matrix products, arithmetic and copies ran while one was open for 0% -> 0% of each run, Pallas kernels for 0% -> 6%
where the time goes in v2:
time: 90.5 us; the launch traced here: 90.2 us
  waiting for transfers between devices  35.6 us (39%)
  starting transfers between devices  29 us (32%)
  Pallas kernels  17.6 us (19%)
  local copies, waits for them, and re-layouts  7.75 us (9%)
    ppermute x29, waiting for transfers between devices, swap(): return lax.ppermute(values, 'seq', [(i, i ^ offset) for i in range(16)])  35.6 us
    ppermute x29, starting transfers between devices, swap(): return lax.ppermute(values, 'seq', [(i, i ^ offset) for i in range(16)])  29 us
    pallas_call x14, Pallas kernels, call(): pl.pallas_call(body, out_shape=[jax.ShapeDtypeStruct(shape, dtype) for sh...  17.6 us
    unnamed x26, local copies, waits for them, and re-layouts  7.75 us
  transfers between devices with their start and end apart: 29, of which 14 were waited for; matrix products, arithmetic and copies ran while one was open for 0% of the time, Pallas kernels for 6%

profile of v2, /device:TPU:0, one launch (start us, length us, event | category | flops | bytes accessed | tf_op | source)
XLA Modules:
  0.0 90.2 jit_solution(2854184564906580924)
XLA Ops:
  0.0 5.0 %collective-permute-start.2 = (bf16[3,5120]{1,0:T(4,128)(2,1)}, bf16[3,5120]{1,0:T(4,128)(2,1)S(1)}, u32[]{:S(2)}, u32[]{:S(2)}) collective-permute-start(bf16[3,5120]{1,0:T(4,128)(2,1)} %own.1), channel_id=1, source_target_pairs={{0,12},{1,13},{2,14},{3,15},{4,8},{5,9},{6,10},{7,11},{8,4},{9,5},... | collective-permute-start | bytes 92168 | tf_op jit(solution)/shard_map/ppermute | solution.py:61
  5.6 2.4 %copy-done = bf16[3,5120,160]{1,2,0:T(8,128)(2,1)S(1)} copy-done((bf16[3,5120,160]{1,2,0:T(8,128)(2,1)S(1)}, bf16[3,5120,160]{1,2,0:T(8,128)(2,1)}, u32[]{:S(2)}) %copy-start) | copy-done | bytes 4915224
  10.2 1.5 %copy-done.3 = bf16[3,5120]{1,0:T(4,128)(2,1)S(1)} copy-done((bf16[3,5120]{1,0:T(4,128)(2,1)S(1)}, bf16[3,5120]{1,0:T(4,128)(2,1)}, u32[]{:S(2)}) %copy-start.3) | copy-done | bytes 30744
  11.7 1.6 %collective-permute-start.3 = (bf16[4,3,5120]{2,1,0:T(4,128)(2,1)S(1)}, bf16[4,3,5120]{2,1,0:T(4,128)(2,1)S(1)}, u32[]{:S(2)}, u32[]{:S(2)}) collective-permute-start(bf16[4,3,5120]{2,1,0:T(4,128)(2,1)S(1)} %shard_map.83.s0), channel_id=1, source_target_pairs={{0,2},{1,3},{2,0},{3,1},{4,6},{5,7},{6,4},{7,5},{8,10},{9,11},{10,... | collective-permute-start | bytes 368648 | tf_op jit(solution)/shard_map/ppermute | solution.py:61
  13.3 3.8 %collective-permute-done.3.s1 = bf16[4,3,5120]{2,1,0:T(4,128)(2,1)S(1)} collective-permute-done((bf16[4,3,5120]{2,1,0:T(4,128)(2,1)S(1)}, bf16[4,3,5120]{2,1,0:T(4,128)(2,1)S(1)}, u32[]{:S(2)}, u32[]{:S(2)}) %collective-permute-start.3) | collective-permute-done | bytes 122912 | tf_op jit(solution)/shard_map/ppermute | solution.py:61
  17.1 1.9 %collective-permute-start.14 = (bf16[2,3,2,2560]{3,2,1,0:T(2,128)(2,1)}, bf16[2,3,2,2560]{3,2,1,0:T(2,128)(2,1)S(1)}, u32[]{:S(2)}, u32[]{:S(2)}) collective-permute-start(bf16[2,3,2,2560]{3,2,1,0:T(2,128)(2,1)} %bitcast.13), channel_id=1, source_target_pairs={{0,12},{1,13},{2,14},{3,15},{4,8},{5,9},{6,10},{7,11},{8,4},{9,5},... | collective-permute-start | bytes 184328 | tf_op jit(solution)/shard_map/ppermute | solution.py:61
  19.1 2.4 %collective-permute-start.12 = (bf16[2,3,2,2560]{3,2,1,0:T(2,128)(2,1)}, bf16[2,3,2,2560]{3,2,1,0:T(2,128)(2,1)S(1)}, u32[]{:S(2)}, u32[]{:S(2)}) collective-permute-start(bf16[2,3,2,2560]{3,2,1,0:T(2,128)(2,1)} %bitcast.15), channel_id=1, source_target_pairs={{0,4},{1,5},{2,6},{3,7},{4,0},{5,1},{6,2},{7,3},{8,12},{9,13},{10,... | collective-permute-start | bytes 184328 | tf_op jit(solution)/shard_map/ppermute | solution.py:61
  21.5 2.5 %collective-permute-done.14.refs_3_ = bf16[2,3,2,2560]{3,2,1,0:T(2,128)(2,1)S(1)} collective-permute-done((bf16[2,3,2,2560]{3,2,1,0:T(2,128)(2,1)}, bf16[2,3,2,2560]{3,2,1,0:T(2,128)(2,1)S(1)}, u32[]{:S(2)}, u32[]{:S(2)}) %collective-permute-start.14) | collective-permute-done | bytes 61472 | tf_op jit(solution)/shard_map/ppermute | solution.py:61
  24.0 2.1 %collective-permute-done.13.refs_2_ = bf16[2,3,2,2560]{3,2,1,0:T(2,128)(2,1)S(1)} collective-permute-done((bf16[2,3,2,2560]{3,2,1,0:T(2,128)(2,1)}, bf16[2,3,2,2560]{3,2,1,0:T(2,128)(2,1)S(1)}, u32[]{:S(2)}, u32[]{:S(2)}) %collective-permute-start.13) | collective-permute-done | bytes 61472 | tf_op jit(solution)/shard_map/ppermute | solution.py:61
  27.0 1.6 %collective-permute-start.15 = (bf16[4,2,3,2,2560]{4,3,2,1,0:T(2,128)(2,1)S(1)}, bf16[4,2,3,2,2560]{4,3,2,1,0:T(2,128)(2,1)S(1)}, u32[]{:S(2)}, u32[]{:S(2)}) collective-permute-start(bf16[4,2,3,2,2560]{4,3,2,1,0:T(2,128)(2,1)S(1)} %shard_map.86.s0), channel_id=1, source_target_pairs={{0,2},{1,3},{2,0},{3,1},{4,6},{5,7},{6,4},{7,5},{8,10},{9,11},{10,... | collective-permute-start | bytes 737288 | tf_op jit(solution)/shard_map/ppermute | solution.py:61
  28.6 2.0 %shard_map.84 = (bf16[48,5120]{1,0:T(8,128)(2,1)S(1)}, bf16[48,480]{1,0:T(8,128)(2,1)S(1)}) custom-call(bf16[4,3,5120]{2,1,0:T(4,128)(2,1)S(1)} %shard_map.83.s0, bf16[4,3,5120]{2,1,0:T(4,128)(2,1)S(1)} %collective-permute-done.3.s1, bf16[4,3,5120]{2,1,0:T(4,128)(2,1)S(1)} %collective-permute-done.4.s2, bf16[4,3,5120]{2,1,0:T(4,128)(2,1)S(1)} %collective-permute-done.5.s3, ...), custom_call_target="tpu_custom_call" | custom-call | flops 235929600 | tf_op jit(solution)/shard_map/pallas_call | solution.py:30
  30.6 2.5 %collective-permute-start.8 = (bf16[48,480]{1,0:T(8,128)(2,1)S(1)}, bf16[48,480]{1,0:T(8,128)(2,1)S(1)}, u32[]{:S(2)}, u32[]{:S(2)}) collective-permute-start(bf16[48,480]{1,0:T(8,128)(2,1)S(1)} %get-tuple-element.34.refs_0_), channel_id=1, source_target_pairs={{0,12},{1,13},{2,14},{3,15},{4,8},{5,9},{6,10},{7,11},{8,4},{9,5},... | collective-permute-start | bytes 138248 | tf_op jit(solution)/shard_map/ppermute | solution.py:61
  33.1 1.9 %collective-permute-start.6 = (bf16[48,480]{1,0:T(8,128)(2,1)S(1)}, bf16[48,480]{1,0:T(8,128)(2,1)S(1)}, u32[]{:S(2)}, u32[]{:S(2)}) collective-permute-start(bf16[48,480]{1,0:T(8,128)(2,1)S(1)} %get-tuple-element.34.refs_0_), channel_id=1, source_target_pairs={{0,4},{1,5},{2,6},{3,7},{4,0},{5,1},{6,2},{7,3},{8,12},{9,13},{10,... | collective-permute-start | bytes 138248 | tf_op jit(solution)/shard_map/ppermute | solution.py:61
  36.6 1.5 %collective-permute-done.7.refs_2_ = bf16[48,480]{1,0:T(8,128)(2,1)S(1)} collective-permute-done((bf16[48,480]{1,0:T(8,128)(2,1)S(1)}, bf16[48,480]{1,0:T(8,128)(2,1)S(1)}, u32[]{:S(2)}, u32[]{:S(2)}) %collective-permute-start.7) | collective-permute-done | bytes 46112 | tf_op jit(solution)/shard_map/ppermute | solution.py:61
  39.2 5.0 %collective-permute-done.9.s1 = bf16[4,48,480]{2,1,0:T(8,128)(2,1)S(1)} collective-permute-done((bf16[4,48,480]{2,1,0:T(8,128)(2,1)S(1)}, bf16[4,48,480]{2,1,0:T(8,128)(2,1)S(1)}, u32[]{:S(2)}, u32[]{:S(2)}) %collective-permute-start.9) | collective-permute-done | bytes 184352 | tf_op jit(solution)/shard_map/ppermute | solution.py:61
  46.4 5.6 %shard_map.88.refs_0_ = bf16[48,320]{1,0:T(8,128)(2,1)S(1)} custom-call(bf16[4,48,480]{2,1,0:T(8,128)(2,1)S(1)} %shard_map.85.s0, bf16[4,48,480]{2,1,0:T(8,128)(2,1)S(1)} %collective-permute-done.9.s1, bf16[4,48,480]{2,1,0:T(8,128)(2,1)S(1)} %collective-permute-done.10.s2, bf16[4,48,480]{2,1,0:T(8,128)(2,1)S(1)} %collective-permute-done.11.s3, ...), custom_call_target="tpu_custom_call" | custom-call | flops 149422080 | tf_op jit(solution)/shard_map/pallas_call | solution.py:30
  52.0 1.8 %collective-permute-start.20 = (bf16[48,320]{1,0:T(8,128)(2,1)S(1)}, bf16[48,320]{1,0:T(8,128)(2,1)S(1)}, u32[]{:S(2)}, u32[]{:S(2)}) collective-permute-start(bf16[48,320]{1,0:T(8,128)(2,1)S(1)} %shard_map.88.refs_0_), channel_id=1, source_target_pairs={{0,12},{1,13},{2,14},{3,15},{4,8},{5,9},{6,10},{7,11},{8,4},{9,5},... | collective-permute-start | bytes 92168 | tf_op jit(solution)/shard_map/ppermute | solution.py:61
  54.2 2.2 %collective-permute-start.18 = (bf16[48,320]{1,0:T(8,128)(2,1)S(1)}, bf16[48,320]{1,0:T(8,128)(2,1)S(1)}, u32[]{:S(2)}, u32[]{:S(2)}) collective-permute-start(bf16[48,320]{1,0:T(8,128)(2,1)S(1)} %shard_map.88.refs_0_), channel_id=1, source_target_pairs={{0,4},{1,5},{2,6},{3,7},{4,0},{5,1},{6,2},{7,3},{8,12},{9,13},{10,... | collective-permute-start | bytes 92168 | tf_op jit(solution)/shard_map/ppermute | solution.py:61
  61.8 4.6 %collective-permute-done.21.s1 = bf16[4,48,320]{2,1,0:T(8,128)(2,1)S(1)} collective-permute-done((bf16[4,48,320]{2,1,0:T(8,128)(2,1)S(1)}, bf16[4,48,320]{2,1,0:T(8,128)(2,1)S(1)}, u32[]{:S(2)}, u32[]{:S(2)}) %collective-permute-start.21) | collective-permute-done | bytes 122912 | tf_op jit(solution)/shard_map/ppermute | solution.py:61
  67.8 5.5 %shard_map.92 = (f32[24,5120]{1,0:T(8,128)S(1)}, bf16[24,5120]{1,0:T(8,128)(2,1)S(1)}, f32[3,5120]{1,0:T(4,128)S(1)}) custom-call(bf16[4,48,320]{2,1,0:T(8,128)(2,1)S(1)} %shard_map.91.s0, bf16[4,48,320]{2,1,0:T(8,128)(2,1)S(1)} %collective-permute-done.21.s1, bf16[4,48,320]{2,1,0:T(8,128)(2,1)S(1)} %collective-permute-done.22.s2, ...), custom_call_target="tpu_custom_call" | custom-call | flops 849346560 | tf_op jit(solution)/shard_map/pallas_call | solution.py:30
  75.5 5.7 %collective-permute-done.25.got = bf16[12,5120]{1,0:T(8,128)(2,1)S(1)} collective-permute-done((bf16[12,5120]{1,0:T(8,128)(2,1)S(1)}, bf16[12,5120]{1,0:T(8,128)(2,1)S(1)}, u32[]{:S(2)}, u32[]{:S(2)}) %collective-permute-start.25) | collective-permute-done | bytes 122912 | tf_op jit(solution)/shard_map/ppermute | solution.py:61
  81.6 2.1 %collective-permute-start.27 = (bf16[3,5120]{1,0:T(4,128)(2,1)S(1)}, bf16[3,5120]{1,0:T(4,128)(2,1)S(1)}, u32[]{:S(2)}, u32[]{:S(2)}) collective-permute-start(bf16[3,5120]{1,0:T(4,128)(2,1)S(1)} %get-tuple-element.50), channel_id=1, source_target_pairs={{0,8},{1,9},{2,10},{3,11},{4,12},{5,13},{6,14},{7,15},{8,0},{9,1},... | collective-permute-start | bytes 92168 | tf_op jit(solution)/shard_map/ppermute | solution.py:61
  83.7 2.1 %collective-permute-start.28 = (bf16[3,5120]{1,0:T(4,128)(2,1)S(1)}, bf16[3,5120]{1,0:T(4,128)(2,1)S(1)}, u32[]{:S(2)}, u32[]{:S(2)}) collective-permute-start(bf16[3,5120]{1,0:T(4,128)(2,1)S(1)} %get-tuple-element.51), channel_id=1, source_target_pairs={{0,12},{1,13},{2,14},{3,15},{4,8},{5,9},{6,10},{7,11},{8,4},{9,5},... | collective-permute-start | bytes 92168 | tf_op jit(solution)/shard_map/ppermute | solution.py:61
  86.5 3.0 %collective-permute-done.28.got3 = bf16[3,5120]{1,0:T(4,128)(2,1)S(1)} collective-permute-done((bf16[3,5120]{1,0:T(4,128)(2,1)S(1)}, bf16[3,5120]{1,0:T(4,128)(2,1)S(1)}, u32[]{:S(2)}, u32[]{:S(2)}) %collective-permute-start.28) | collective-permute-done | bytes 30752 | tf_op jit(solution)/shard_map/ppermute | solution.py:61
  (76 shorter events, 19.5 us)
Async XLA Ops:
  0.0 8.6 %collective-permute-start.2 = (bf16[3,5120]{1,0:T(4,128)(2,1)}, bf16[3,5120]{1,0:T(4,128)(2,1)S(1)}, u32[]{:S(2)}, u32[]{:S(2)}) collective-permute-start(bf16[3,5120]{1,0:T(4,128)(2,1)} %own.1), channel_id=1, source_target_pairs={{0,12},{1,13},{2,14},{3,15},{4,8},{5,9},{6,10},{7,11},{8,4},{9,5},... | collective-permute-start | bytes 92168 | tf_op jit(solution)/shard_map/ppermute | solution.py:61
  5.0 5.1 %collective-permute-start.1 = (bf16[3,5120]{1,0:T(4,128)(2,1)}, bf16[3,5120]{1,0:T(4,128)(2,1)S(1)}, u32[]{:S(2)}, u32[]{:S(2)}) collective-permute-start(bf16[3,5120]{1,0:T(4,128)(2,1)} %own.1), channel_id=1, source_target_pairs={{0,8},{1,9},{2,10},{3,11},{4,12},{5,13},{6,14},{7,15},{8,0},{9,1},... | collective-permute-start | bytes 92168 | tf_op jit(solution)/shard_map/ppermute | solution.py:61
  5.1 5.1 %collective-permute-start = (bf16[3,5120]{1,0:T(4,128)(2,1)}, bf16[3,5120]{1,0:T(4,128)(2,1)S(1)}, u32[]{:S(2)}, u32[]{:S(2)}) collective-permute-start(bf16[3,5120]{1,0:T(4,128)(2,1)} %own.1), channel_id=1, source_target_pairs={{0,4},{1,5},{2,6},{3,7},{4,0},{5,1},{6,2},{7,3},{8,12},{9,13},{10,... | collective-permute-start | bytes 92168 | tf_op jit(solution)/shard_map/ppermute | solution.py:61
  11.7 5.4 %collective-permute-start.3 = (bf16[4,3,5120]{2,1,0:T(4,128)(2,1)S(1)}, bf16[4,3,5120]{2,1,0:T(4,128)(2,1)S(1)}, u32[]{:S(2)}, u32[]{:S(2)}) collective-permute-start(bf16[4,3,5120]{2,1,0:T(4,128)(2,1)S(1)} %shard_map.83.s0), channel_id=1, source_target_pairs={{0,2},{1,3},{2,0},{3,1},{4,6},{5,7},{6,4},{7,5},{8,10},{9,11},{10,... | collective-permute-start | bytes 368648 | tf_op jit(solution)/shard_map/ppermute | solution.py:61
  13.3 15.3 %collective-permute-start.4 = (bf16[4,3,5120]{2,1,0:T(4,128)(2,1)S(1)}, bf16[4,3,5120]{2,1,0:T(4,128)(2,1)S(1)}, u32[]{:S(2)}, u32[]{:S(2)}) collective-permute-start(bf16[4,3,5120]{2,1,0:T(4,128)(2,1)S(1)} %shard_map.83.s0), channel_id=1, source_target_pairs={{0,1},{1,0},{2,3},{3,2},{4,5},{5,4},{6,7},{7,6},{8,9},{9,8},{10,11... | collective-permute-start | bytes 368648 | tf_op jit(solution)/shard_map/ppermute | solution.py:61
  17.1 11.5 %collective-permute-start.5 = (bf16[4,3,5120]{2,1,0:T(4,128)(2,1)S(1)}, bf16[4,3,5120]{2,1,0:T(4,128)(2,1)S(1)}, u32[]{:S(2)}, u32[]{:S(2)}) collective-permute-start(bf16[4,3,5120]{2,1,0:T(4,128)(2,1)S(1)} %collective-permute-done.3.s1), channel_id=1, source_target_pairs={{0,1},{1,0},{2,3},{3,2},{4,5},{5,4},{6,7},{7,6},{8,9},{9,8},{10,11... | collective-permute-start | bytes 368648 | tf_op jit(solution)/shard_map/ppermute | solution.py:61
  17.1 6.9 %collective-permute-start.14 = (bf16[2,3,2,2560]{3,2,1,0:T(2,128)(2,1)}, bf16[2,3,2,2560]{3,2,1,0:T(2,128)(2,1)S(1)}, u32[]{:S(2)}, u32[]{:S(2)}) collective-permute-start(bf16[2,3,2,2560]{3,2,1,0:T(2,128)(2,1)} %bitcast.13), channel_id=1, source_target_pairs={{0,12},{1,13},{2,14},{3,15},{4,8},{5,9},{6,10},{7,11},{8,4},{9,5},... | collective-permute-start | bytes 184328 | tf_op jit(solution)/shard_map/ppermute | solution.py:61
  19.0 7.1 %collective-permute-start.13 = (bf16[2,3,2,2560]{3,2,1,0:T(2,128)(2,1)}, bf16[2,3,2,2560]{3,2,1,0:T(2,128)(2,1)S(1)}, u32[]{:S(2)}, u32[]{:S(2)}) collective-permute-start(bf16[2,3,2,2560]{3,2,1,0:T(2,128)(2,1)} %bitcast.14), channel_id=1, source_target_pairs={{0,8},{1,9},{2,10},{3,11},{4,12},{5,13},{6,14},{7,15},{8,0},{9,1},... | collective-permute-start | bytes 184328 | tf_op jit(solution)/shard_map/ppermute | solution.py:61
  19.1 7.0 %collective-permute-start.12 = (bf16[2,3,2,2560]{3,2,1,0:T(2,128)(2,1)}, bf16[2,3,2,2560]{3,2,1,0:T(2,128)(2,1)S(1)}, u32[]{:S(2)}, u32[]{:S(2)}) collective-permute-start(bf16[2,3,2,2560]{3,2,1,0:T(2,128)(2,1)} %bitcast.15), channel_id=1, source_target_pairs={{0,4},{1,5},{2,6},{3,7},{4,0},{5,1},{6,2},{7,3},{8,12},{9,13},{10,... | collective-permute-start | bytes 184328 | tf_op jit(solution)/shard_map/ppermute | solution.py:61
  27.0 11.7 %collective-permute-start.15 = (bf16[4,2,3,2,2560]{4,3,2,1,0:T(2,128)(2,1)S(1)}, bf16[4,2,3,2,2560]{4,3,2,1,0:T(2,128)(2,1)S(1)}, u32[]{:S(2)}, u32[]{:S(2)}) collective-permute-start(bf16[4,2,3,2,2560]{4,3,2,1,0:T(2,128)(2,1)S(1)} %shard_map.86.s0), channel_id=1, source_target_pairs={{0,2},{1,3},{2,0},{3,1},{4,6},{5,7},{6,4},{7,5},{8,10},{9,11},{10,... | collective-permute-start | bytes 737288 | tf_op jit(solution)/shard_map/ppermute | solution.py:61
  30.6 6.0 %collective-permute-start.8 = (bf16[48,480]{1,0:T(8,128)(2,1)S(1)}, bf16[48,480]{1,0:T(8,128)(2,1)S(1)}, u32[]{:S(2)}, u32[]{:S(2)}) collective-permute-start(bf16[48,480]{1,0:T(8,128)(2,1)S(1)} %get-tuple-element.34.refs_0_), channel_id=1, source_target_pairs={{0,12},{1,13},{2,14},{3,15},{4,8},{5,9},{6,10},{7,11},{8,4},{9,5},... | collective-permute-start | bytes 138248 | tf_op jit(solution)/shard_map/ppermute | solution.py:61
  33.1 5.0 %collective-permute-start.7 = (bf16[48,480]{1,0:T(8,128)(2,1)S(1)}, bf16[48,480]{1,0:T(8,128)(2,1)S(1)}, u32[]{:S(2)}, u32[]{:S(2)}) collective-permute-start(bf16[48,480]{1,0:T(8,128)(2,1)S(1)} %get-tuple-element.34.refs_0_), channel_id=1, source_target_pairs={{0,8},{1,9},{2,10},{3,11},{4,12},{5,13},{6,14},{7,15},{8,0},{9,1},... | collective-permute-start | bytes 138248 | tf_op jit(solution)/shard_map/ppermute | solution.py:61
  33.1 5.0 %collective-permute-start.6 = (bf16[48,480]{1,0:T(8,128)(2,1)S(1)}, bf16[48,480]{1,0:T(8,128)(2,1)S(1)}, u32[]{:S(2)}, u32[]{:S(2)}) collective-permute-start(bf16[48,480]{1,0:T(8,128)(2,1)S(1)} %get-tuple-element.34.refs_0_), channel_id=1, source_target_pairs={{0,4},{1,5},{2,6},{3,7},{4,0},{5,1},{6,2},{7,3},{8,12},{9,13},{10,... | collective-permute-start | bytes 138248 | tf_op jit(solution)/shard_map/ppermute | solution.py:61
  38.1 6.1 %collective-permute-start.9 = (bf16[4,48,480]{2,1,0:T(8,128)(2,1)S(1)}, bf16[4,48,480]{2,1,0:T(8,128)(2,1)S(1)}, u32[]{:S(2)}, u32[]{:S(2)}) collective-permute-start(bf16[4,48,480]{2,1,0:T(8,128)(2,1)S(1)} %shard_map.85.s0), channel_id=1, source_target_pairs={{0,2},{1,3},{2,0},{3,1},{4,6},{5,7},{6,4},{7,5},{8,10},{9,11},{10,... | collective-permute-start | bytes 552968 | tf_op jit(solution)/shard_map/ppermute | solution.py:61
  38.7 5.5 %collective-permute-start.16 = (bf16[4,2,3,2,2560]{4,3,2,1,0:T(2,128)(2,1)S(1)}, bf16[4,2,3,2,2560]{4,3,2,1,0:T(2,128)(2,1)S(1)}, u32[]{:S(2)}, u32[]{:S(2)}) collective-permute-start(bf16[4,2,3,2,2560]{4,3,2,1,0:T(2,128)(2,1)S(1)} %shard_map.86.s0), channel_id=1, source_target_pairs={{0,1},{1,0},{2,3},{3,2},{4,5},{5,4},{6,7},{7,6},{8,9},{9,8},{10,11... | collective-permute-start | bytes 737288 | tf_op jit(solution)/shard_map/ppermute | solution.py:61
  38.7 5.5 %collective-permute-start.17 = (bf16[4,2,3,2,2560]{4,3,2,1,0:T(2,128)(2,1)S(1)}, bf16[4,2,3,2,2560]{4,3,2,1,0:T(2,128)(2,1)S(1)}, u32[]{:S(2)}, u32[]{:S(2)}) collective-permute-start(bf16[4,2,3,2,2560]{4,3,2,1,0:T(2,128)(2,1)S(1)} %collective-permute-done.15.s1), channel_id=1, source_target_pairs={{0,1},{1,0},{2,3},{3,2},{4,5},{5,4},{6,7},{7,6},{8,9},{9,8},{10,11... | collective-permute-start | bytes 737288 | tf_op jit(solution)/shard_map/ppermute | solution.py:61
  39.2 5.6 %collective-permute-start.10 = (bf16[4,48,480]{2,1,0:T(8,128)(2,1)S(1)}, bf16[4,48,480]{2,1,0:T(8,128)(2,1)S(1)}, u32[]{:S(2)}, u32[]{:S(2)}) collective-permute-start(bf16[4,48,480]{2,1,0:T(8,128)(2,1)S(1)} %shard_map.85.s0), channel_id=1, source_target_pairs={{0,1},{1,0},{2,3},{3,2},{4,5},{5,4},{6,7},{7,6},{8,9},{9,8},{10,11... | collective-permute-start | bytes 552968 | tf_op jit(solution)/shard_map/ppermute | solution.py:61
  52.0 9.2 %collective-permute-start.20 = (bf16[48,320]{1,0:T(8,128)(2,1)S(1)}, bf16[48,320]{1,0:T(8,128)(2,1)S(1)}, u32[]{:S(2)}, u32[]{:S(2)}) collective-permute-start(bf16[48,320]{1,0:T(8,128)(2,1)S(1)} %shard_map.88.refs_0_), channel_id=1, source_target_pairs={{0,12},{1,13},{2,14},{3,15},{4,8},{5,9},{6,10},{7,11},{8,4},{9,5},... | collective-permute-start | bytes 92168 | tf_op jit(solution)/shard_map/ppermute | solution.py:61
  53.8 7.3 %collective-permute-start.19 = (bf16[48,320]{1,0:T(8,128)(2,1)S(1)}, bf16[48,320]{1,0:T(8,128)(2,1)S(1)}, u32[]{:S(2)}, u32[]{:S(2)}) collective-permute-start(bf16[48,320]{1,0:T(8,128)(2,1)S(1)} %shard_map.88.refs_0_), channel_id=1, source_target_pairs={{0,8},{1,9},{2,10},{3,11},{4,12},{5,13},{6,14},{7,15},{8,0},{9,1},... | collective-permute-start | bytes 92168 | tf_op jit(solution)/shard_map/ppermute | solution.py:61
  54.2 6.9 %collective-permute-start.18 = (bf16[48,320]{1,0:T(8,128)(2,1)S(1)}, bf16[48,320]{1,0:T(8,128)(2,1)S(1)}, u32[]{:S(2)}, u32[]{:S(2)}) collective-permute-start(bf16[48,320]{1,0:T(8,128)(2,1)S(1)} %shard_map.88.refs_0_), channel_id=1, source_target_pairs={{0,4},{1,5},{2,6},{3,7},{4,0},{5,1},{6,2},{7,3},{8,12},{9,13},{10,... | collective-permute-start | bytes 92168 | tf_op jit(solution)/shard_map/ppermute | solution.py:61
  61.2 5.2 %collective-permute-start.21 = (bf16[4,48,320]{2,1,0:T(8,128)(2,1)S(1)}, bf16[4,48,320]{2,1,0:T(8,128)(2,1)S(1)}, u32[]{:S(2)}, u32[]{:S(2)}) collective-permute-start(bf16[4,48,320]{2,1,0:T(8,128)(2,1)S(1)} %shard_map.91.s0), channel_id=1, source_target_pairs={{0,2},{1,3},{2,0},{3,1},{4,6},{5,7},{6,4},{7,5},{8,10},{9,11},{10,... | collective-permute-start | bytes 368648 | tf_op jit(solution)/shard_map/ppermute | solution.py:61
  74.9 6.3 %collective-permute-start.25 = (bf16[12,5120]{1,0:T(8,128)(2,1)S(1)}, bf16[12,5120]{1,0:T(8,128)(2,1)S(1)}, u32[]{:S(2)}, u32[]{:S(2)}) collective-permute-start(bf16[12,5120]{1,0:T(8,128)(2,1)S(1)} %get-tuple-element.47), channel_id=1, source_target_pairs={{0,2},{1,3},{2,0},{3,1},{4,6},{5,7},{6,4},{7,5},{8,10},{9,11},{10,... | collective-permute-start | bytes 368648 | tf_op jit(solution)/shard_map/ppermute | solution.py:61
  81.6 4.9 %collective-permute-start.27 = (bf16[3,5120]{1,0:T(4,128)(2,1)S(1)}, bf16[3,5120]{1,0:T(4,128)(2,1)S(1)}, u32[]{:S(2)}, u32[]{:S(2)}) collective-permute-start(bf16[3,5120]{1,0:T(4,128)(2,1)S(1)} %get-tuple-element.50), channel_id=1, source_target_pairs={{0,8},{1,9},{2,10},{3,11},{4,12},{5,13},{6,14},{7,15},{8,0},{9,1},... | collective-permute-start | bytes 92168 | tf_op jit(solution)/shard_map/ppermute | solution.py:61
  83.7 5.8 %collective-permute-start.28 = (bf16[3,5120]{1,0:T(4,128)(2,1)S(1)}, bf16[3,5120]{1,0:T(4,128)(2,1)S(1)}, u32[]{:S(2)}, u32[]{:S(2)}) collective-permute-start(bf16[3,5120]{1,0:T(4,128)(2,1)S(1)} %get-tuple-element.51), channel_id=1, source_target_pairs={{0,12},{1,13},{2,14},{3,15},{4,8},{5,9},{6,10},{7,11},{8,4},{9,5},... | collective-permute-start | bytes 92168 | tf_op jit(solution)/shard_map/ppermute | solution.py:61
  (18 other events, 228.3 us)

commit v3 on v2

--- a/solution.py
+++ b/solution.py
@@ -22,39 +22,46 @@
 
 
 VMEM = pl.BlockSpec(memory_space=pltpu.VMEM)
-ANY = pl.BlockSpec(memory_space=pl.ANY)
+HBM = pl.BlockSpec(memory_space=pltpu.HBM)
 NT = (((1,), (1,)), ((), ()))
 
 
-def call(body, outs, *operands, any_space=(), scratch=(), limit=24, flops=0, moved=0):
+def call(body, outs, *operands, spec=VMEM, scratch=(), limit=24):
     return pl.pallas_call(
         body,
         out_shape=[jax.ShapeDtypeStruct(shape, dtype) for shape, dtype in outs],
-        in_specs=[ANY if i in any_space else VMEM for i in range(len(operands))],
+        in_specs=[spec] * len(operands),
         out_specs=[VMEM] * len(outs),
         scratch_shapes=list(scratch),
         compiler_params=pltpu.CompilerParams(vmem_limit_bytes=limit << 20),
-        cost_estimate=pl.CostEstimate(flops=flops, bytes_accessed=moved, transcendentals=0),
+        cost_estimate=pl.CostEstimate(flops=0, bytes_accessed=0, transcendentals=0),
     )(*operands)
 
 
-def load(weights):
-    rows, width = weights.shape
-    cuts = [rows * i // 4 // 16 * 16 for i in range(4)] + [rows]
-
-    def body(source, target, sems):
-        copies = [
-            pltpu.make_async_copy(source.at[pl.ds(a, b - a)], target.at[pl.ds(a, b - a)], sems.at[i])
-            for i, (a, b) in enumerate(zip(cuts, cuts[1:]))
-        ]
+def load(*arrays):
+    parts = []
+    for i, array in enumerate(arrays):
+        rows = array.shape[0]
+        if array.size < 1 << 20:
+            parts.append((i, None))
+        else:
+            cuts = [rows * k // 4 // 16 * 16 for k in range(4)] + [rows]
+            parts += [(i, pl.ds(lo, hi - lo)) for lo, hi in zip(cuts, cuts[1:])]
+
+    def body(*refs):
+        sources, targets, sems = refs[: len(arrays)], refs[len(arrays) : -1], refs[-1]
+        copies = []
+        for n, (i, cut) in enumerate(parts):
+            source, target = (sources[i], targets[i]) if cut is None else (sources[i].at[cut], targets[i].at[cut])
+            copies.append(pltpu.make_async_copy(source, target, sems.at[n]))
         for copy in copies:
             copy.start()
         for copy in copies:
             copy.wait()
 
-    scratch = [pltpu.SemaphoreType.DMA((4,))]
-    moved = rows * width * 4
-    return call(body, [((rows, width), weights.dtype)], weights, any_space=(0,), scratch=scratch, moved=moved)[0]
+    outs = [(array.shape, array.dtype) for array in arrays]
+    arrays = [pltpu.with_memory_space_constraint(array, pltpu.HBM) for array in arrays]
+    return call(body, outs, *arrays, spec=HBM, scratch=[pltpu.SemaphoreType.DMA((len(parts),))])
 
 
 def swap(values, offset):
@@ -69,10 +76,20 @@
     return call(body, [((len(pieces), *pieces[0].shape), pieces[0].dtype)], *pieces)[0]
 
 
-def gather(block, tie=lambda pieces: pieces):
-    planes = stack(tie([block] + [swap(block, 4 * z) for z in (1, 2, 3)]))
+def load_beside(weights, before, beside):
+    weights, _ = lax.optimization_barrier((weights, before))
+    return lax.optimization_barrier((load(weights)[0], beside))
+
+
+def gather(block, load_z=None, load_y=None):
+    pieces = tuple(swap(block, 4 * z) for z in (1, 2, 3))
+    if load_z is not None:
+        load_z, pieces = load_beside(load_z, block, pieces)
+    planes = stack([block, *pieces])
     across = swap(planes, 2)
-    return [planes, across, swap(planes, 1), swap(across, 1)]
+    if load_y is not None:
+        load_y, across = load_beside(load_y, planes, across)
+    return [planes, across, swap(planes, 1), swap(across, 1)], load_z, load_y
 
 
 def apart(slot, z):
@@ -175,56 +192,59 @@
 
 def staged(tokens, modulation, w_qkv, norm_gains, cache_kv, w_out, w_up, w_down):
     f32, bf16 = jnp.float32, jnp.bfloat16
-    w_qkv = load(jnp.swapaxes(w_qkv, 1, 2).reshape(480, 5120))
-
-    def after_load(pieces):
-        nonlocal w_qkv
-        *pieces, w_qkv = lax.optimization_barrier((*pieces, w_qkv))
-        return pieces
-
-    token_stacks = gather(tokens, after_load)
-    cache_stacks = gather(cache_kv.transpose(0, 2, 1, 3))
+    w_qkv = jnp.swapaxes(w_qkv, 1, 2).reshape(480, 5120)
+    cache_kv = cache_kv.transpose(0, 2, 1, 3)
+    pieces = tuple(swap(tokens, 4 * z) for z in (1, 2, 3))
+    cache_pieces = tuple(swap(cache_kv, 4 * z) for z in (1, 2, 3))
+    tokens, modulation, norm_gains, cache_kv, w_qkv = load(tokens, modulation, norm_gains, cache_kv, w_qkv)
+    pieces, tokens = lax.optimization_barrier((pieces, tokens))
+    planes = stack([tokens, *pieces])
+    across = swap(planes, 2)
+    cache_planes = stack([cache_kv, *cache_pieces])
+    across, cache_planes = lax.optimization_barrier((across, cache_planes))
+    cache_across = swap(cache_planes, 2)
     all_tokens, qkv = call(
         project_qkv,
         [((48, 5120), bf16), ((48, 480), bf16)],
-        *token_stacks,
+        planes,
+        across,
+        swap(planes, 1),
+        swap(across, 1),
         modulation,
         w_qkv,
         scratch=[pltpu.VMEM((16, 3, 5120), bf16), pltpu.VMEM((48, 5120), f32)],
-        flops=2 * 48 * 5120 * 480,
-    )
+    )
+    qkv_stacks, w_out, w_up = gather(qkv, w_out.T, w_up.T)
     old_keys, old_values = call(
-        line_up, [((96, 2560), bf16)] * 2, *cache_stacks, scratch=[pltpu.VMEM((96, 2560), f32)] * 2, moved=8 << 20
+        line_up,
+        [((96, 2560), bf16)] * 2,
+        cache_planes,
+        cache_across,
+        swap(cache_planes, 1),
+        swap(cache_across, 1),
+        scratch=[pltpu.VMEM((96, 2560), f32)] * 2,
     )
     projected = call(
         attend,
         [((48, 320), bf16)],
-        *gather(qkv),
+        *qkv_stacks,
         old_keys,
         old_values,
         norm_gains,
-        w_out.T,
+        w_out,
         scratch=[pltpu.VMEM((16, 48, 480), bf16), pltpu.VMEM((48, 2560), bf16)],
-        flops=2 * 48 * 2560 * 608,
     )[0]
-    w_up, w_down = load(w_up.T), load(w_down)
-
-    def after_loads(pieces):
-        nonlocal w_up, w_down
-        *pieces, w_up, w_down = lax.optimization_barrier((*pieces, w_up, w_down))
-        return pieces
-
+    projected_stacks, _, w_down = gather(projected, None, w_down)
     keep, send, residual = call(
         feed_forward,
         [((24, 5120), f32), ((24, 5120), bf16), ((3, 5120), f32)],
-        *gather(projected, after_loads),
+        *projected_stacks,
         all_tokens,
         tokens,
         modulation,
         w_up,
         w_down,
         scratch=[pltpu.VMEM((16, 48, 320), bf16)],
-        flops=4 * 48 * 5120 * 864,
     )
     keep, send = call(add_near, [((12, 5120), f32), ((12, 5120), bf16)], keep, swap(send, 1))
     keep, *sends = call(add_plane, [((3, 5120), f32)] + [((3, 5120), bf16)] * 3, keep, swap(send, 2))

time: 90.5 us -> 81.9 us (0.905)
  waiting for transfers between devices: 35.6 us -> 26.8 us
  Pallas kernels: 17.6 us -> 25.9 us
  local copies, waits for them, and re-layouts: 7.75 us -> 0 us
    ppermute x29, waiting for transfers between devices: 35.6 us -> 26.8 us  [swap(): return lax.ppermute(values, 'seq', [(i, i ^ offset) for i in range(16)])]
    pallas_call x14 -> x15, Pallas kernels: 17.6 us -> 25.9 us  [call(): pl.pallas_call(body, out_shape=[jax.ShapeDtypeStruct(shape, dtype) for sh...]
    unnamed x26 -> x0, local copies, waits for them, and re-layouts: 7.75 us -> none
  transfers between devices with their start and end apart: 29 -> 29, of which waited for: 14 -> 17; matrix products, arithmetic and copies ran while one was open for 0% -> 0% of each run, Pallas kernels for 6% -> 17%
where the time goes in v3:
time: 81.9 us; the launch traced here: 81.8 us
  starting transfers between devices  28.9 us (35%)
  waiting for transfers between devices  26.8 us (33%)
  Pallas kernels  25.9 us (32%)
    ppermute x29, starting transfers between devices, swap(): return lax.ppermute(values, 'seq', [(i, i ^ offset) for i in range(16)])  28.9 us
    ppermute x29, waiting for transfers between devices, swap(): return lax.ppermute(values, 'seq', [(i, i ^ offset) for i in range(16)])  26.8 us
    pallas_call x15, Pallas kernels, call(): pl.pallas_call(body, out_shape=[jax.ShapeDtypeStruct(shape, dtype) for sh...  25.9 us
  transfers between devices with their start and end apart: 29, of which 17 were waited for; matrix products, arithmetic and copies ran while one was open for 0% of the time, Pallas kernels for 17%

profile of v3, /device:TPU:0, one launch (start us, length us, event | category | flops | bytes accessed | tf_op | source)
XLA Modules:
  0.0 81.8 jit_solution(1532892421881640073)
XLA Ops:
  0.0 4.0 %collective-permute-start.1 = (bf16[3,5120]{1,0:T(4,128)(2,1)}, bf16[3,5120]{1,0:T(4,128)(2,1)S(1)}, u32[]{:S(2)}, u32[]{:S(2)}) collective-permute-start(bf16[3,5120]{1,0:T(4,128)(2,1)} %refs_0_.1), channel_id=1, source_target_pairs={{0,8},{1,9},{2,10},{3,11},{4,12},{5,13},{6,14},{7,15},{8,0},{9,1},... | collective-permute-start | bytes 92168 | tf_op jit(solution)/shard_map/ppermute | solution.py:68
  4.0 1.6 %collective-permute-start = (bf16[3,5120]{1,0:T(4,128)(2,1)}, bf16[3,5120]{1,0:T(4,128)(2,1)S(1)}, u32[]{:S(2)}, u32[]{:S(2)}) collective-permute-start(bf16[3,5120]{1,0:T(4,128)(2,1)} %refs_0_.1), channel_id=1, source_target_pairs={{0,4},{1,5},{2,6},{3,7},{4,0},{5,1},{6,2},{7,3},{8,12},{9,13},{10,... | collective-permute-start | bytes 92168 | tf_op jit(solution)/shard_map/ppermute | solution.py:68
  5.6 2.6 %shard_map.82 = (bf16[3,5120]{1,0:T(4,128)(2,1)S(1)}, f32[6,5120]{1,0:T(8,128)S(1)}, f32[2,2560]{1,0:T(2,128)S(1)}, bf16[2,3,2,2560]{3,2,1,0:T(2,128)(2,1)S(1)}, bf16[480,5120]{1,0:T(8,128)(2,1)S(1)}) custom-call(bf16[3,5120]{1,0:T(4,128)(2,1)} %refs_0_.1, f32[6,5120]{1,0:T(8,128)} %refs_1_.1, f32[2,2560]{1,0:T(2,128)} %refs_2_.1, ...), custom_call_target="tpu_custom_call" | custom-call | tf_op jit(solution)/shard_map/pallas_call | solution.py:30
  8.3 3.3 %collective-permute-done.2.refs_3_ = bf16[3,5120]{1,0:T(4,128)(2,1)S(1)} collective-permute-done((bf16[3,5120]{1,0:T(4,128)(2,1)}, bf16[3,5120]{1,0:T(4,128)(2,1)S(1)}, u32[]{:S(2)}, u32[]{:S(2)}) %collective-permute-start.2) | collective-permute-done | bytes 30752 | tf_op jit(solution)/shard_map/ppermute | solution.py:68
  11.6 1.7 %collective-permute-start.3 = (bf16[4,3,5120]{2,1,0:T(4,128)(2,1)S(1)}, bf16[4,3,5120]{2,1,0:T(4,128)(2,1)S(1)}, u32[]{:S(2)}, u32[]{:S(2)}) collective-permute-start(bf16[4,3,5120]{2,1,0:T(4,128)(2,1)S(1)} %shard_map.83.s0), channel_id=1, source_target_pairs={{0,2},{1,3},{2,0},{3,1},{4,6},{5,7},{6,4},{7,5},{8,10},{9,11},{10,... | collective-permute-start | bytes 368648 | tf_op jit(solution)/shard_map/ppermute | solution.py:68
  13.8 3.9 %collective-permute-start.4 = (bf16[2,3,2,2560]{3,2,1,0:T(2,128)(2,1)}, bf16[2,3,2,2560]{3,2,1,0:T(2,128)(2,1)S(1)}, u32[]{:S(2)}, u32[]{:S(2)}) collective-permute-start(bf16[2,3,2,2560]{3,2,1,0:T(2,128)(2,1)} %bitcast.12), channel_id=1, source_target_pairs={{0,4},{1,5},{2,6},{3,7},{4,0},{5,1},{6,2},{7,3},{8,12},{9,13},{10,... | collective-permute-start | bytes 184328 | tf_op jit(solution)/shard_map/ppermute | solution.py:68
  17.7 1.9 %collective-permute-done.6.refs_3_ = bf16[2,3,2,2560]{3,2,1,0:T(2,128)(2,1)S(1)} collective-permute-done((bf16[2,3,2,2560]{3,2,1,0:T(2,128)(2,1)}, bf16[2,3,2,2560]{3,2,1,0:T(2,128)(2,1)S(1)}, u32[]{:S(2)}, u32[]{:S(2)}) %collective-permute-start.6) | collective-permute-done | bytes 61472 | tf_op jit(solution)/shard_map/ppermute | solution.py:68
  21.9 1.9 %shard_map.85 = (bf16[48,5120]{1,0:T(8,128)(2,1)S(1)}, bf16[48,480]{1,0:T(8,128)(2,1)S(1)}) custom-call(bf16[4,3,5120]{2,1,0:T(4,128)(2,1)S(1)} %shard_map.83.s0, bf16[4,3,5120]{2,1,0:T(4,128)(2,1)S(1)} %collective-permute-done.3.s1, bf16[4,3,5120]{2,1,0:T(4,128)(2,1)S(1)} %collective-permute-done.7.s2, bf16[4,3,5120]{2,1,0:T(4,128)(2,1)S(1)} %collective-permute-done.8.s3, ...), custom_call_target="tpu_custom_call" | custom-call | tf_op jit(solution)/shard_map/pallas_call | solution.py:30
  23.8 2.2 %collective-permute-start.11 = (bf16[48,480]{1,0:T(8,128)(2,1)S(1)}, bf16[48,480]{1,0:T(8,128)(2,1)S(1)}, u32[]{:S(2)}, u32[]{:S(2)}) collective-permute-start(bf16[48,480]{1,0:T(8,128)(2,1)S(1)} %get-tuple-element.49.refs_0_), channel_id=1, source_target_pairs={{0,12},{1,13},{2,14},{3,15},{4,8},{5,9},{6,10},{7,11},{8,4},{9,5},... | collective-permute-start | bytes 138248 | tf_op jit(solution)/shard_map/ppermute | solution.py:68
  28.3 1.4 %shard_map.86.weights = bf16[320,2560]{1,0:T(8,128)(2,1)S(1)} custom-call(bf16[320,2560]{1,0:T(8,128)(2,1)} %bitcast.8), custom_call_target="tpu_custom_call" | custom-call | tf_op jit(solution)/shard_map/pallas_call | solution.py:30
  30.1 2.1 %collective-permute-done.10.refs_2_ = bf16[48,480]{1,0:T(8,128)(2,1)S(1)} collective-permute-done((bf16[48,480]{1,0:T(8,128)(2,1)S(1)}, bf16[48,480]{1,0:T(8,128)(2,1)S(1)}, u32[]{:S(2)}, u32[]{:S(2)}) %collective-permute-start.10) | collective-permute-done | bytes 46112 | tf_op jit(solution)/shard_map/ppermute | solution.py:68
  33.6 3.6 %shard_map.88.w_up = bf16[864,5120]{1,0:T(8,128)(2,1)S(1)} custom-call(bf16[864,5120]{1,0:T(8,128)(2,1)} %bitcast.6), custom_call_target="tpu_custom_call" | custom-call | tf_op jit(solution)/shard_map/pallas_call | solution.py:30
  37.2 1.5 %collective-permute-done.12.s1 = bf16[4,48,480]{2,1,0:T(8,128)(2,1)S(1)} collective-permute-done((bf16[4,48,480]{2,1,0:T(8,128)(2,1)S(1)}, bf16[4,48,480]{2,1,0:T(8,128)(2,1)S(1)}, u32[]{:S(2)}, u32[]{:S(2)}) %collective-permute-start.12) | collective-permute-done | bytes 184352 | tf_op jit(solution)/shard_map/ppermute | solution.py:68
  40.1 5.6 %shard_map.90.refs_0_ = bf16[48,320]{1,0:T(8,128)(2,1)S(1)} custom-call(bf16[4,48,480]{2,1,0:T(8,128)(2,1)S(1)} %shard_map.87.s0, bf16[4,48,480]{2,1,0:T(8,128)(2,1)S(1)} %collective-permute-done.12.s1, bf16[4,48,480]{2,1,0:T(8,128)(2,1)S(1)} %collective-permute-done.13.s2, bf16[4,48,480]{2,1,0:T(8,128)(2,1)S(1)} %collective-permute-done.14.s3, ...), custom_call_target="tpu_custom_call" | custom-call | tf_op jit(solution)/shard_map/pallas_call | solution.py:30
  45.7 1.5 %collective-permute-start.20 = (bf16[48,320]{1,0:T(8,128)(2,1)S(1)}, bf16[48,320]{1,0:T(8,128)(2,1)S(1)}, u32[]{:S(2)}, u32[]{:S(2)}) collective-permute-start(bf16[48,320]{1,0:T(8,128)(2,1)S(1)} %shard_map.90.refs_0_), channel_id=1, source_target_pairs={{0,12},{1,13},{2,14},{3,15},{4,8},{5,9},{6,10},{7,11},{8,4},{9,5},... | collective-permute-start | bytes 92168 | tf_op jit(solution)/shard_map/ppermute | solution.py:68
  47.3 2.9 %collective-permute-start.18 = (bf16[48,320]{1,0:T(8,128)(2,1)S(1)}, bf16[48,320]{1,0:T(8,128)(2,1)S(1)}, u32[]{:S(2)}, u32[]{:S(2)}) collective-permute-start(bf16[48,320]{1,0:T(8,128)(2,1)S(1)} %shard_map.90.refs_0_), channel_id=1, source_target_pairs={{0,4},{1,5},{2,6},{3,7},{4,0},{5,1},{6,2},{7,3},{8,12},{9,13},{10,... | collective-permute-start | bytes 92168 | tf_op jit(solution)/shard_map/ppermute | solution.py:68
  50.2 1.4 %collective-permute-done.20.refs_3_ = bf16[48,320]{1,0:T(8,128)(2,1)S(1)} collective-permute-done((bf16[48,320]{1,0:T(8,128)(2,1)S(1)}, bf16[48,320]{1,0:T(8,128)(2,1)S(1)}, u32[]{:S(2)}, u32[]{:S(2)}) %collective-permute-start.20) | collective-permute-done | bytes 30752 | tf_op jit(solution)/shard_map/ppermute | solution.py:68
  53.6 3.6 %shard_map.92.w_down = bf16[864,5120]{1,0:T(8,128)(2,1)S(1)} custom-call(bf16[864,5120]{1,0:T(8,128)(2,1)} %refs_0_.2), custom_call_target="tpu_custom_call" | custom-call | tf_op jit(solution)/shard_map/pallas_call | solution.py:30
  58.6 1.4 %collective-permute-done.23.s3 = bf16[4,48,320]{2,1,0:T(8,128)(2,1)S(1)} collective-permute-done((bf16[4,48,320]{2,1,0:T(8,128)(2,1)S(1)}, bf16[4,48,320]{2,1,0:T(8,128)(2,1)S(1)}, u32[]{:S(2)}, u32[]{:S(2)}) %collective-permute-start.23) | collective-permute-done | bytes 122912 | tf_op jit(solution)/shard_map/ppermute | solution.py:68
  59.9 5.5 %shard_map.93 = (f32[24,5120]{1,0:T(8,128)S(1)}, bf16[24,5120]{1,0:T(8,128)(2,1)S(1)}, f32[3,5120]{1,0:T(4,128)S(1)}) custom-call(bf16[4,48,320]{2,1,0:T(8,128)(2,1)S(1)} %shard_map.91.s0, bf16[4,48,320]{2,1,0:T(8,128)(2,1)S(1)} %collective-permute-done.21.s1, bf16[4,48,320]{2,1,0:T(8,128)(2,1)S(1)} %collective-permute-done.22.s2, ...), custom_call_target="tpu_custom_call" | custom-call | tf_op jit(solution)/shard_map/pallas_call | solution.py:30
  65.6 1.4 %collective-permute-done.24.got = bf16[24,5120]{1,0:T(8,128)(2,1)S(1)} collective-permute-done((bf16[24,5120]{1,0:T(8,128)(2,1)S(1)}, bf16[24,5120]{1,0:T(8,128)(2,1)S(1)}, u32[]{:S(2)}, u32[]{:S(2)}) %collective-permute-start.24) | collective-permute-done | bytes 245792 | tf_op jit(solution)/shard_map/ppermute | solution.py:68
  67.9 5.5 %collective-permute-done.25.got = bf16[12,5120]{1,0:T(8,128)(2,1)S(1)} collective-permute-done((bf16[12,5120]{1,0:T(8,128)(2,1)S(1)}, bf16[12,5120]{1,0:T(8,128)(2,1)S(1)}, u32[]{:S(2)}, u32[]{:S(2)}) %collective-permute-start.25) | collective-permute-done | bytes 122912 | tf_op jit(solution)/shard_map/ppermute | solution.py:68
  75.3 2.7 %collective-permute-start.28 = (bf16[3,5120]{1,0:T(4,128)(2,1)S(1)}, bf16[3,5120]{1,0:T(4,128)(2,1)S(1)}, u32[]{:S(2)}, u32[]{:S(2)}) collective-permute-start(bf16[3,5120]{1,0:T(4,128)(2,1)S(1)} %get-tuple-element.73), channel_id=1, source_target_pairs={{0,12},{1,13},{2,14},{3,15},{4,8},{5,9},{6,10},{7,11},{8,4},{9,5},... | collective-permute-start | bytes 92168 | tf_op jit(solution)/shard_map/ppermute | solution.py:68
  79.3 1.8 %collective-permute-done.28.got3 = bf16[3,5120]{1,0:T(4,128)(2,1)S(1)} collective-permute-done((bf16[3,5120]{1,0:T(4,128)(2,1)S(1)}, bf16[3,5120]{1,0:T(4,128)(2,1)S(1)}, u32[]{:S(2)}, u32[]{:S(2)}) %collective-permute-start.28) | collective-permute-done | bytes 30752 | tf_op jit(solution)/shard_map/ppermute | solution.py:68
  (49 shorter events, 16.4 us)
Async XLA Ops:
  0.0 8.3 %collective-permute-start.1 = (bf16[3,5120]{1,0:T(4,128)(2,1)}, bf16[3,5120]{1,0:T(4,128)(2,1)S(1)}, u32[]{:S(2)}, u32[]{:S(2)}) collective-permute-start(bf16[3,5120]{1,0:T(4,128)(2,1)} %refs_0_.1), channel_id=1, source_target_pairs={{0,8},{1,9},{2,10},{3,11},{4,12},{5,13},{6,14},{7,15},{8,0},{9,1},... | collective-permute-start | bytes 92168 | tf_op jit(solution)/shard_map/ppermute | solution.py:68
  4.0 4.2 %collective-permute-start = (bf16[3,5120]{1,0:T(4,128)(2,1)}, bf16[3,5120]{1,0:T(4,128)(2,1)S(1)}, u32[]{:S(2)}, u32[]{:S(2)}) collective-permute-start(bf16[3,5120]{1,0:T(4,128)(2,1)} %refs_0_.1), channel_id=1, source_target_pairs={{0,4},{1,5},{2,6},{3,7},{4,0},{5,1},{6,2},{7,3},{8,12},{9,13},{10,... | collective-permute-start | bytes 92168 | tf_op jit(solution)/shard_map/ppermute | solution.py:68
  5.6 6.0 %collective-permute-start.2 = (bf16[3,5120]{1,0:T(4,128)(2,1)}, bf16[3,5120]{1,0:T(4,128)(2,1)S(1)}, u32[]{:S(2)}, u32[]{:S(2)}) collective-permute-start(bf16[3,5120]{1,0:T(4,128)(2,1)} %refs_0_.1), channel_id=1, source_target_pairs={{0,12},{1,13},{2,14},{3,15},{4,8},{5,9},{6,10},{7,11},{8,4},{9,5},... | collective-permute-start | bytes 92168 | tf_op jit(solution)/shard_map/ppermute | solution.py:68
  11.6 8.8 %collective-permute-start.3 = (bf16[4,3,5120]{2,1,0:T(4,128)(2,1)S(1)}, bf16[4,3,5120]{2,1,0:T(4,128)(2,1)S(1)}, u32[]{:S(2)}, u32[]{:S(2)}) collective-permute-start(bf16[4,3,5120]{2,1,0:T(4,128)(2,1)S(1)} %shard_map.83.s0), channel_id=1, source_target_pairs={{0,2},{1,3},{2,0},{3,1},{4,6},{5,7},{6,4},{7,5},{8,10},{9,11},{10,... | collective-permute-start | bytes 368648 | tf_op jit(solution)/shard_map/ppermute | solution.py:68
  13.3 6.3 %collective-permute-start.6 = (bf16[2,3,2,2560]{3,2,1,0:T(2,128)(2,1)}, bf16[2,3,2,2560]{3,2,1,0:T(2,128)(2,1)S(1)}, u32[]{:S(2)}, u32[]{:S(2)}) collective-permute-start(bf16[2,3,2,2560]{3,2,1,0:T(2,128)(2,1)} %bitcast.10), channel_id=1, source_target_pairs={{0,12},{1,13},{2,14},{3,15},{4,8},{5,9},{6,10},{7,11},{8,4},{9,5},... | collective-permute-start | bytes 184328 | tf_op jit(solution)/shard_map/ppermute | solution.py:68
  13.7 6.6 %collective-permute-start.5 = (bf16[2,3,2,2560]{3,2,1,0:T(2,128)(2,1)}, bf16[2,3,2,2560]{3,2,1,0:T(2,128)(2,1)S(1)}, u32[]{:S(2)}, u32[]{:S(2)}) collective-permute-start(bf16[2,3,2,2560]{3,2,1,0:T(2,128)(2,1)} %bitcast.11), channel_id=1, source_target_pairs={{0,8},{1,9},{2,10},{3,11},{4,12},{5,13},{6,14},{7,15},{8,0},{9,1},... | collective-permute-start | bytes 184328 | tf_op jit(solution)/shard_map/ppermute | solution.py:68
  13.8 6.6 %collective-permute-start.4 = (bf16[2,3,2,2560]{3,2,1,0:T(2,128)(2,1)}, bf16[2,3,2,2560]{3,2,1,0:T(2,128)(2,1)S(1)}, u32[]{:S(2)}, u32[]{:S(2)}) collective-permute-start(bf16[2,3,2,2560]{3,2,1,0:T(2,128)(2,1)} %bitcast.12), channel_id=1, source_target_pairs={{0,4},{1,5},{2,6},{3,7},{4,0},{5,1},{6,2},{7,3},{8,12},{9,13},{10,... | collective-permute-start | bytes 184328 | tf_op jit(solution)/shard_map/ppermute | solution.py:68
  20.5 12.6 %collective-permute-start.15 = (bf16[4,2,3,2,2560]{4,3,2,1,0:T(2,128)(2,1)S(1)}, bf16[4,2,3,2,2560]{4,3,2,1,0:T(2,128)(2,1)S(1)}, u32[]{:S(2)}, u32[]{:S(2)}) collective-permute-start(bf16[4,2,3,2,2560]{4,3,2,1,0:T(2,128)(2,1)S(1)} %shard_map.84.s0), channel_id=1, source_target_pairs={{0,2},{1,3},{2,0},{3,1},{4,6},{5,7},{6,4},{7,5},{8,10},{9,11},{10,... | collective-permute-start | bytes 737288 | tf_op jit(solution)/shard_map/ppermute | solution.py:68
  23.8 6.3 %collective-permute-start.11 = (bf16[48,480]{1,0:T(8,128)(2,1)S(1)}, bf16[48,480]{1,0:T(8,128)(2,1)S(1)}, u32[]{:S(2)}, u32[]{:S(2)}) collective-permute-start(bf16[48,480]{1,0:T(8,128)(2,1)S(1)} %get-tuple-element.49.refs_0_), channel_id=1, source_target_pairs={{0,12},{1,13},{2,14},{3,15},{4,8},{5,9},{6,10},{7,11},{8,4},{9,5},... | collective-permute-start | bytes 138248 | tf_op jit(solution)/shard_map/ppermute | solution.py:68
  26.0 6.2 %collective-permute-start.10 = (bf16[48,480]{1,0:T(8,128)(2,1)S(1)}, bf16[48,480]{1,0:T(8,128)(2,1)S(1)}, u32[]{:S(2)}, u32[]{:S(2)}) collective-permute-start(bf16[48,480]{1,0:T(8,128)(2,1)S(1)} %get-tuple-element.49.refs_0_), channel_id=1, source_target_pairs={{0,8},{1,9},{2,10},{3,11},{4,12},{5,13},{6,14},{7,15},{8,0},{9,1},... | collective-permute-start | bytes 138248 | tf_op jit(solution)/shard_map/ppermute | solution.py:68
  27.1 5.1 %collective-permute-start.9 = (bf16[48,480]{1,0:T(8,128)(2,1)S(1)}, bf16[48,480]{1,0:T(8,128)(2,1)S(1)}, u32[]{:S(2)}, u32[]{:S(2)}) collective-permute-start(bf16[48,480]{1,0:T(8,128)(2,1)S(1)} %get-tuple-element.49.refs_0_), channel_id=1, source_target_pairs={{0,4},{1,5},{2,6},{3,7},{4,0},{5,1},{6,2},{7,3},{8,12},{9,13},{10,... | collective-permute-start | bytes 138248 | tf_op jit(solution)/shard_map/ppermute | solution.py:68
  32.3 6.4 %collective-permute-start.12 = (bf16[4,48,480]{2,1,0:T(8,128)(2,1)S(1)}, bf16[4,48,480]{2,1,0:T(8,128)(2,1)S(1)}, u32[]{:S(2)}, u32[]{:S(2)}) collective-permute-start(bf16[4,48,480]{2,1,0:T(8,128)(2,1)S(1)} %shard_map.87.s0), channel_id=1, source_target_pairs={{0,2},{1,3},{2,0},{3,1},{4,6},{5,7},{6,4},{7,5},{8,10},{9,11},{10,... | collective-permute-start | bytes 552968 | tf_op jit(solution)/shard_map/ppermute | solution.py:68
  33.1 5.6 %collective-permute-start.16 = (bf16[4,2,3,2,2560]{4,3,2,1,0:T(2,128)(2,1)S(1)}, bf16[4,2,3,2,2560]{4,3,2,1,0:T(2,128)(2,1)S(1)}, u32[]{:S(2)}, u32[]{:S(2)}) collective-permute-start(bf16[4,2,3,2,2560]{4,3,2,1,0:T(2,128)(2,1)S(1)} %shard_map.84.s0), channel_id=1, source_target_pairs={{0,1},{1,0},{2,3},{3,2},{4,5},{5,4},{6,7},{7,6},{8,9},{9,8},{10,11... | collective-permute-start | bytes 737288 | tf_op jit(solution)/shard_map/ppermute | solution.py:68
  33.1 5.6 %collective-permute-start.17 = (bf16[4,2,3,2,2560]{4,3,2,1,0:T(2,128)(2,1)S(1)}, bf16[4,2,3,2,2560]{4,3,2,1,0:T(2,128)(2,1)S(1)}, u32[]{:S(2)}, u32[]{:S(2)}) collective-permute-start(bf16[4,2,3,2,2560]{4,3,2,1,0:T(2,128)(2,1)S(1)} %collective-permute-done.15.s1), channel_id=1, source_target_pairs={{0,1},{1,0},{2,3},{3,2},{4,5},{5,4},{6,7},{7,6},{8,9},{9,8},{10,11... | collective-permute-start | bytes 737288 | tf_op jit(solution)/shard_map/ppermute | solution.py:68
  33.6 5.8 %collective-permute-start.13 = (bf16[4,48,480]{2,1,0:T(8,128)(2,1)S(1)}, bf16[4,48,480]{2,1,0:T(8,128)(2,1)S(1)}, u32[]{:S(2)}, u32[]{:S(2)}) collective-permute-start(bf16[4,48,480]{2,1,0:T(8,128)(2,1)S(1)} %shard_map.87.s0), channel_id=1, source_target_pairs={{0,1},{1,0},{2,3},{3,2},{4,5},{5,4},{6,7},{7,6},{8,9},{9,8},{10,11... | collective-permute-start | bytes 552968 | tf_op jit(solution)/shard_map/ppermute | solution.py:68
  45.7 5.9 %collective-permute-start.20 = (bf16[48,320]{1,0:T(8,128)(2,1)S(1)}, bf16[48,320]{1,0:T(8,128)(2,1)S(1)}, u32[]{:S(2)}, u32[]{:S(2)}) collective-permute-start(bf16[48,320]{1,0:T(8,128)(2,1)S(1)} %shard_map.90.refs_0_), channel_id=1, source_target_pairs={{0,12},{1,13},{2,14},{3,15},{4,8},{5,9},{6,10},{7,11},{8,4},{9,5},... | collective-permute-start | bytes 92168 | tf_op jit(solution)/shard_map/ppermute | solution.py:68
  47.2 5.5 %collective-permute-start.19 = (bf16[48,320]{1,0:T(8,128)(2,1)S(1)}, bf16[48,320]{1,0:T(8,128)(2,1)S(1)}, u32[]{:S(2)}, u32[]{:S(2)}) collective-permute-start(bf16[48,320]{1,0:T(8,128)(2,1)S(1)} %shard_map.90.refs_0_), channel_id=1, source_target_pairs={{0,8},{1,9},{2,10},{3,11},{4,12},{5,13},{6,14},{7,15},{8,0},{9,1},... | collective-permute-start | bytes 92168 | tf_op jit(solution)/shard_map/ppermute | solution.py:68
  47.3 5.5 %collective-permute-start.18 = (bf16[48,320]{1,0:T(8,128)(2,1)S(1)}, bf16[48,320]{1,0:T(8,128)(2,1)S(1)}, u32[]{:S(2)}, u32[]{:S(2)}) collective-permute-start(bf16[48,320]{1,0:T(8,128)(2,1)S(1)} %shard_map.90.refs_0_), channel_id=1, source_target_pairs={{0,4},{1,5},{2,6},{3,7},{4,0},{5,1},{6,2},{7,3},{8,12},{9,13},{10,... | collective-permute-start | bytes 92168 | tf_op jit(solution)/shard_map/ppermute | solution.py:68
  52.8 5.7 %collective-permute-start.21 = (bf16[4,48,320]{2,1,0:T(8,128)(2,1)S(1)}, bf16[4,48,320]{2,1,0:T(8,128)(2,1)S(1)}, u32[]{:S(2)}, u32[]{:S(2)}) collective-permute-start(bf16[4,48,320]{2,1,0:T(8,128)(2,1)S(1)} %shard_map.91.s0), channel_id=1, source_target_pairs={{0,2},{1,3},{2,0},{3,1},{4,6},{5,7},{6,4},{7,5},{8,10},{9,11},{10,... | collective-permute-start | bytes 368648 | tf_op jit(solution)/shard_map/ppermute | solution.py:68
  53.6 4.9 %collective-permute-start.22 = (bf16[4,48,320]{2,1,0:T(8,128)(2,1)S(1)}, bf16[4,48,320]{2,1,0:T(8,128)(2,1)S(1)}, u32[]{:S(2)}, u32[]{:S(2)}) collective-permute-start(bf16[4,48,320]{2,1,0:T(8,128)(2,1)S(1)} %shard_map.91.s0), channel_id=1, source_target_pairs={{0,1},{1,0},{2,3},{3,2},{4,5},{5,4},{6,7},{7,6},{8,9},{9,8},{10,11... | collective-permute-start | bytes 368648 | tf_op jit(solution)/shard_map/ppermute | solution.py:68
  67.1 6.3 %collective-permute-start.25 = (bf16[12,5120]{1,0:T(8,128)(2,1)S(1)}, bf16[12,5120]{1,0:T(8,128)(2,1)S(1)}, u32[]{:S(2)}, u32[]{:S(2)}) collective-permute-start(bf16[12,5120]{1,0:T(8,128)(2,1)S(1)} %get-tuple-element.69), channel_id=1, source_target_pairs={{0,2},{1,3},{2,0},{3,1},{4,6},{5,7},{6,4},{7,5},{8,10},{9,11},{10,... | collective-permute-start | bytes 368648 | tf_op jit(solution)/shard_map/ppermute | solution.py:68
  73.5 4.5 %collective-permute-start.26 = (bf16[3,5120]{1,0:T(4,128)(2,1)S(1)}, bf16[3,5120]{1,0:T(4,128)(2,1)S(1)}, u32[]{:S(2)}, u32[]{:S(2)}) collective-permute-start(bf16[3,5120]{1,0:T(4,128)(2,1)S(1)} %get-tuple-element.71), channel_id=1, source_target_pairs={{0,4},{1,5},{2,6},{3,7},{4,0},{5,1},{6,2},{7,3},{8,12},{9,13},{10,... | collective-permute-start | bytes 92168 | tf_op jit(solution)/shard_map/ppermute | solution.py:68
  74.4 4.9 %collective-permute-start.27 = (bf16[3,5120]{1,0:T(4,128)(2,1)S(1)}, bf16[3,5120]{1,0:T(4,128)(2,1)S(1)}, u32[]{:S(2)}, u32[]{:S(2)}) collective-permute-start(bf16[3,5120]{1,0:T(4,128)(2,1)S(1)} %get-tuple-element.72), channel_id=1, source_target_pairs={{0,8},{1,9},{2,10},{3,11},{4,12},{5,13},{6,14},{7,15},{8,0},{9,1},... | collective-permute-start | bytes 92168 | tf_op jit(solution)/shard_map/ppermute | solution.py:68
  75.3 5.8 %collective-permute-start.28 = (bf16[3,5120]{1,0:T(4,128)(2,1)S(1)}, bf16[3,5120]{1,0:T(4,128)(2,1)S(1)}, u32[]{:S(2)}, u32[]{:S(2)}) collective-permute-start(bf16[3,5120]{1,0:T(4,128)(2,1)S(1)} %get-tuple-element.73), channel_id=1, source_target_pairs={{0,12},{1,13},{2,14},{3,15},{4,8},{5,9},{6,10},{7,11},{8,4},{9,5},... | collective-permute-start | bytes 92168 | tf_op jit(solution)/shard_map/ppermute | solution.py:68
  (5 other events, 9.2 us)

commit v4 on v3

--- a/solution.py
+++ b/solution.py
@@ -92,29 +92,43 @@
     return [planes, across, swap(planes, 1), swap(across, 1)], load_z, load_y
 
 
-def apart(slot, z):
-    return 4 * z + 2 * (slot & 1) + (slot >> 1)
+def pack_tokens(own, got1, got2, got3, out, rows):
+    for z, ref in enumerate((own, got1, got2, got3)):
+        for half in range(2):
+            row = 12 * half + 3 * z
+            rows[row : row + 3, :] = ref[:, 2560 * half : 2560 * half + 2560].astype(jnp.float32)
+    out[...] = rows[...].astype(jnp.bfloat16)
 
 
 def place(stacks, target):
     me = lax.axis_index("seq")
     for slot, ref in enumerate(stacks):
         for z in range(4):
-            target[me ^ apart(slot, z)] = ref[z]
+            target[me ^ (4 * z + 2 * (slot & 1) + (slot >> 1))] = ref[z]
+
+
+def order(near_axis):
+    near = lax.broadcasted_iota(jnp.int32, (48, 48), near_axis)
+    token = lax.broadcasted_iota(jnp.int32, (48, 48), 1 - near_axis)
+    block = (near * 171) >> 9
+    device = lax.axis_index("seq") ^ (4 * (block & 3) + 2 * ((block >> 2) & 1) + (block >> 3))
+    return (token == 3 * device + near - 3 * block).astype(jnp.bfloat16)
 
 
 def normalize(values, shift, gain):
     return (layer_norm(values) * (1.0 + gain) + shift).astype(jnp.bfloat16)
 
 
-def project_qkv(s0, s1, s2, s3, mod, weights, tokens_out, qkv_out, slots, flat):
-    place((s0, s1, s2, s3), slots)
-    for j in range(16):
-        flat[3 * j : 3 * j + 3, :] = slots[j].astype(jnp.float32)
+def project_qkv(s0, s1, s2, s3, mod, weights, tokens_out, qkv_out, flat):
+    for slot, ref in enumerate((s0, s1, s2, s3)):
+        for half in range(2):
+            piece = ref[12 * half : 12 * half + 12, :].astype(jnp.float32)
+            flat[12 * slot : 12 * slot + 12, 2560 * half : 2560 * half + 2560] = piece
     tokens = flat[...]
     tokens_out[...] = tokens.astype(jnp.bfloat16)
     normed = normalize(tokens, mod[0:1, :], mod[1:2, :])
-    qkv_out[...] = lax.dot_general(normed, weights[...], NT, preferred_element_type=jnp.float32).astype(jnp.bfloat16)
+    qkv = lax.dot_general(normed, weights[...], NT, preferred_element_type=jnp.float32).astype(jnp.bfloat16)
+    qkv_out[...] = jnp.dot(order(1), qkv, preferred_element_type=jnp.float32).astype(jnp.bfloat16)
 
 
 def line_up(s0, s1, s2, s3, keys_out, values_out, keys, values):
@@ -128,65 +142,74 @@
     values_out[...] = values[...].astype(jnp.bfloat16)
 
 
-def attend(s0, s1, s2, s3, old_keys, old_values, gains, weights, out, slots, attended):
+def attend(s0, s1, s2, s3, old_keys, old_values, gains, weights, out, slots, scores, expos, attended):
     place((s0, s1, s2, s3), slots)
-    pieces = [slots[j].astype(jnp.float32) for j in range(16)]
+    pieces = [slots[j] for j in range(16)]
     queries, keys, values = (
         jnp.concatenate([piece[:, 160 * i : 160 * i + 160] for piece in pieces], axis=1) for i in range(3)
     )
-    queries = rms_norm(queries, gains[0:1, :]).astype(jnp.bfloat16)
-    keys = jnp.concatenate([old_keys[...], rms_norm(keys, gains[1:2, :]).astype(jnp.bfloat16)], axis=0)
-    values = jnp.concatenate([old_values[...], values.astype(jnp.bfloat16)], axis=0)
-    for head in range(HEADS):
-        cols = slice(HEAD_DIM * head, HEAD_DIM * (head + 1))
-        scores = lax.dot_general(queries[:, cols], keys[:, cols], NT, preferred_element_type=jnp.float32)
-        scores = scores * (1.0 / math.sqrt(HEAD_DIM))
-        expo = jnp.exp(scores - jnp.max(scores, axis=-1, keepdims=True))
-        total = jnp.sum(expo, axis=-1, keepdims=True)
-        summed = jnp.dot(expo.astype(jnp.bfloat16), values[:, cols], preferred_element_type=jnp.float32)
-        attended[:, cols] = (summed / total).astype(jnp.bfloat16)
-    out[...] = lax.dot_general(attended[...], weights[...], NT, preferred_element_type=jnp.float32).astype(jnp.bfloat16)
-
-
-def feed_forward(s0, s1, s2, s3, tokens, own, mod, w_up, w_down, keep, send, residual_out, slots):
+    queries = rms_norm(queries.astype(jnp.float32), gains[0:1, :]).astype(jnp.bfloat16)
+    keys = rms_norm(keys.astype(jnp.float32), gains[1:2, :]).astype(jnp.bfloat16)
+    keys = jnp.concatenate([old_keys[...], keys], axis=0)
+    values = jnp.concatenate([old_values[...], values], axis=0)
+    none = jnp.zeros((48, HEAD_DIM), jnp.bfloat16)
+    pairs = []
+    for head in range(0, HEADS, 2):
+        first, second = (slice(HEAD_DIM * h, HEAD_DIM * (h + 1)) for h in (head, head + 1))
+        pairs.append((slice(48 * head, 48 * (head + 2)), first, second, slice(HEAD_DIM * head, HEAD_DIM * (head + 2))))
+    for rows, first, second, both in pairs:
+        upper = jnp.concatenate([queries[:, first], none], axis=1)
+        lower = jnp.concatenate([none, queries[:, second]], axis=1)
+        diagonal = jnp.concatenate([upper, lower], axis=0)
+        scores[rows, :] = lax.dot_general(diagonal, keys[:, both], NT, preferred_element_type=jnp.float32)
+    scaled = scores[...] * (1.0 / math.sqrt(HEAD_DIM))
+    expo = jnp.exp(scaled - jnp.max(scaled, axis=-1, keepdims=True))
+    total = jnp.sum(expo, axis=-1, keepdims=True)
+    expos[...] = expo.astype(jnp.bfloat16)
+    for rows, first, second, both in pairs:
+        summed = jnp.dot(expos[rows, :], values[:, both], preferred_element_type=jnp.float32) / total[rows]
+        attended[:, first] = summed[:48, :HEAD_DIM].astype(jnp.bfloat16)
+        attended[:, second] = summed[48:, HEAD_DIM:].astype(jnp.bfloat16)
+    projected = lax.dot_general(attended[...], weights[...], NT, preferred_element_type=jnp.float32)
+    out[...] = jnp.concatenate([projected[:24], projected[24:]], axis=1).astype(jnp.bfloat16)
+
+
+def feed_forward(s0, s1, s2, s3, tokens, mod, w_up, w_down, keep, send, residual_out, slots):
     place((s0, s1, s2, s3), slots)
-    projected = jnp.concatenate([slots[j] for j in range(16)], axis=1)
-    gate = mod[2:3, :]
-    residual = tokens[...].astype(jnp.float32) + gate * projected.astype(jnp.float32)
+    pieces = [slots[j] for j in range(16)]
+    upper = jnp.concatenate([piece[:, :320] for piece in pieces], axis=1)
+    lower = jnp.concatenate([piece[:, 320:] for piece in pieces], axis=1)
+    projected = jnp.concatenate([upper, lower], axis=0)
+    projected = jnp.dot(order(0), projected, preferred_element_type=jnp.float32)
+    residual = tokens[...].astype(jnp.float32) + mod[2:3, :] * projected
+    residual_out[...] = residual[0:3]
     normed = normalize(residual, mod[3:4, :], mod[4:5, :])
     hidden = lax.dot_general(normed, w_up[...], NT, preferred_element_type=jnp.float32)
     hidden = jax.nn.gelu(hidden, approximate=True).astype(jnp.bfloat16)
-    me = lax.axis_index("seq")
-    row = lax.broadcasted_iota(jnp.int32, (48, 48), 0)
-    token = lax.broadcasted_iota(jnp.int32, (48, 48), 1)
-    block = (row * 171) >> 9
-    device = me ^ (4 * (block & 3) + 2 * ((block >> 2) & 1) + (block >> 3))
-    pick = (token == 3 * device + row - 3 * block).astype(jnp.bfloat16)
-    hidden = jnp.dot(pick, hidden, preferred_element_type=jnp.float32).astype(jnp.bfloat16)
     partial = jnp.dot(hidden, w_down[...], preferred_element_type=jnp.float32)
     keep[...] = partial[:24]
     send[...] = partial[24:].astype(jnp.bfloat16)
-    mine = jnp.dot(pick[0:16], projected, preferred_element_type=jnp.float32)[0:3]
-    residual_out[...] = own[...].astype(jnp.float32) + gate * mine
 
 
 def add_near(keep, got, keep_out, send_out):
     total = keep[...] + got[...].astype(jnp.float32)
     keep_out[...] = total[:12]
-    send_out[...] = total[12:].astype(jnp.bfloat16)
+    send_out[...] = jnp.concatenate([total[12:, :2560], total[12:, 2560:]], axis=0).astype(jnp.bfloat16)
 
 
 def add_plane(keep, got, keep_out, send1, send2, send3):
-    total = keep[...] + got[...].astype(jnp.float32)
+    got = got[...].astype(jnp.float32)
+    total = keep[...] + jnp.concatenate([got[:12], got[12:]], axis=1)
     keep_out[...] = total[0:3]
     for z, send in ((1, send1), (2, send2), (3, send3)):
-        send[...] = total[3 * z : 3 * z + 3].astype(jnp.bfloat16)
+        rows = [total[3 * z + i : 3 * z + i + 1, 640 * g : 640 * g + 640] for i in range(3) for g in range(8)]
+        send[...] = jnp.concatenate(rows, axis=0).astype(jnp.bfloat16)
 
 
 def finish(keep, got1, got2, got3, residual, mod, out):
-    total = keep[...]
-    for got in (got1, got2, got3):
-        total = total + got[...].astype(jnp.float32)
+    total = got1[...].astype(jnp.float32) + got2[...].astype(jnp.float32) + got3[...].astype(jnp.float32)
+    rows = [jnp.concatenate([total[8 * i + g : 8 * i + g + 1] for g in range(8)], axis=1) for i in range(3)]
+    total = keep[...] + jnp.concatenate(rows, axis=0)
     out[...] = (residual[...] + mod[5:6, :] * total).astype(jnp.bfloat16)
 
 
@@ -198,12 +221,12 @@
     cache_pieces = tuple(swap(cache_kv, 4 * z) for z in (1, 2, 3))
     tokens, modulation, norm_gains, cache_kv, w_qkv = load(tokens, modulation, norm_gains, cache_kv, w_qkv)
     pieces, tokens = lax.optimization_barrier((pieces, tokens))
-    planes = stack([tokens, *pieces])
+    planes = call(pack_tokens, [((24, 2560), bf16)], tokens, *pieces, scratch=[pltpu.VMEM((24, 2560), f32)])[0]
     across = swap(planes, 2)
     cache_planes = stack([cache_kv, *cache_pieces])
     across, cache_planes = lax.optimization_barrier((across, cache_planes))
     cache_across = swap(cache_planes, 2)
-    all_tokens, qkv = call(
+    near_tokens, qkv = call(
         project_qkv,
         [((48, 5120), bf16), ((48, 480), bf16)],
         planes,
@@ -212,7 +235,7 @@
         swap(across, 1),
         modulation,
         w_qkv,
-        scratch=[pltpu.VMEM((16, 3, 5120), bf16), pltpu.VMEM((48, 5120), f32)],
+        scratch=[pltpu.VMEM((48, 5120), f32)],
     )
     qkv_stacks, w_out, w_up = gather(qkv, w_out.T, w_up.T)
     old_keys, old_values = call(
@@ -226,28 +249,32 @@
     )
     projected = call(
         attend,
-        [((48, 320), bf16)],
+        [((24, 640), bf16)],
         *qkv_stacks,
         old_keys,
         old_values,
         norm_gains,
         w_out,
-        scratch=[pltpu.VMEM((16, 48, 480), bf16), pltpu.VMEM((48, 2560), bf16)],
+        scratch=[
+            pltpu.VMEM((16, 48, 480), bf16),
+            pltpu.VMEM((48 * HEADS, 144), f32),
+            pltpu.VMEM((48 * HEADS, 144), bf16),
+            pltpu.VMEM((48, 2560), bf16),
+        ],
     )[0]
     projected_stacks, _, w_down = gather(projected, None, w_down)
     keep, send, residual = call(
         feed_forward,
         [((24, 5120), f32), ((24, 5120), bf16), ((3, 5120), f32)],
         *projected_stacks,
-        all_tokens,
-        tokens,
+        near_tokens,
         modulation,
         w_up,
         w_down,
-        scratch=[pltpu.VMEM((16, 48, 320), bf16)],
-    )
-    keep, send = call(add_near, [((12, 5120), f32), ((12, 5120), bf16)], keep, swap(send, 1))
-    keep, *sends = call(add_plane, [((3, 5120), f32)] + [((3, 5120), bf16)] * 3, keep, swap(send, 2))
+        scratch=[pltpu.VMEM((16, 24, 640), bf16)],
+    )
+    keep, send = call(add_near, [((12, 5120), f32), ((24, 2560), bf16)], keep, swap(send, 1))
+    keep, *sends = call(add_plane, [((3, 5120), f32)] + [((24, 640), bf16)] * 3, keep, swap(send, 2))
     got = [swap(send, 4 * z) for z, send in zip((1, 2, 3), sends)]
     return call(finish, [((3, 5120), bf16)], keep, *got, residual, modulation)[0]
 

time: 81.9 us -> 76.6 us (0.935)
  Pallas kernels: 25.9 us -> 22.2 us
  waiting for transfers between devices: 26.8 us -> 25 us
    pallas_call x15, Pallas kernels: 25.9 us -> 22.2 us  [call(): pl.pallas_call(body, out_shape=[jax.ShapeDtypeStruct(shape, dtype) for sh...]
    ppermute x29, waiting for transfers between devices: 26.8 us -> 25 us  [swap(): return lax.ppermute(values, 'seq', [(i, i ^ offset) for i in range(16)])]
  transfers between devices with their start and end apart: 29 -> 29, of which waited for: 17 -> 17; matrix products, arithmetic and copies ran while one was open for 0% -> 0% of each run, Pallas kernels for 17% -> 18%
where the time goes in v4:
time: 76.6 us; the launch traced here: 76.5 us
  starting transfers between devices  29.2 us (38%)
  waiting for transfers between devices  25 us (33%)
  Pallas kernels  22.2 us (29%)
    ppermute x29, starting transfers between devices, swap(): return lax.ppermute(values, 'seq', [(i, i ^ offset) for i in range(16)])  29.2 us
    ppermute x29, waiting for transfers between devices, swap(): return lax.ppermute(values, 'seq', [(i, i ^ offset) for i in range(16)])  25 us
    pallas_call x15, Pallas kernels, call(): pl.pallas_call(body, out_shape=[jax.ShapeDtypeStruct(shape, dtype) for sh...  22.2 us
  transfers between devices with their start and end apart: 29, of which 17 were waited for; matrix products, arithmetic and copies ran while one was open for 0% of the time, Pallas kernels for 18%

profile of v4, /device:TPU:0, one launch (start us, length us, event | category | flops | bytes accessed | tf_op | source)
XLA Modules:
  0.0 76.5 jit_solution(13099991021622863100)
XLA Ops:
  0.0 4.0 %collective-permute-start.1 = (bf16[3,5120]{1,0:T(4,128)(2,1)}, bf16[3,5120]{1,0:T(4,128)(2,1)S(1)}, u32[]{:S(2)}, u32[]{:S(2)}) collective-permute-start(bf16[3,5120]{1,0:T(4,128)(2,1)} %refs_0_.1), channel_id=1, source_target_pairs={{0,8},{1,9},{2,10},{3,11},{4,12},{5,13},{6,14},{7,15},{8,0},{9,1},... | collective-permute-start | bytes 92168 | tf_op jit(solution)/shard_map/ppermute | solution.py:68
  4.0 1.6 %collective-permute-start = (bf16[3,5120]{1,0:T(4,128)(2,1)}, bf16[3,5120]{1,0:T(4,128)(2,1)S(1)}, u32[]{:S(2)}, u32[]{:S(2)}) collective-permute-start(bf16[3,5120]{1,0:T(4,128)(2,1)} %refs_0_.1), channel_id=1, source_target_pairs={{0,4},{1,5},{2,6},{3,7},{4,0},{5,1},{6,2},{7,3},{8,12},{9,13},{10,... | collective-permute-start | bytes 92168 | tf_op jit(solution)/shard_map/ppermute | solution.py:68
  5.6 2.6 %shard_map.82 = (bf16[3,5120]{1,0:T(4,128)(2,1)S(1)}, f32[6,5120]{1,0:T(8,128)S(1)}, f32[2,2560]{1,0:T(2,128)S(1)}, bf16[2,3,2,2560]{3,2,1,0:T(2,128)(2,1)S(1)}, bf16[480,5120]{1,0:T(8,128)(2,1)S(1)}) custom-call(bf16[3,5120]{1,0:T(4,128)(2,1)} %refs_0_.1, f32[6,5120]{1,0:T(8,128)} %refs_1_.1, f32[2,2560]{1,0:T(2,128)} %refs_2_.1, ...), custom_call_target="tpu_custom_call" | custom-call | tf_op jit(solution)/shard_map/pallas_call | solution.py:30
  8.3 3.3 %collective-permute-done.2.got3 = bf16[3,5120]{1,0:T(4,128)(2,1)S(1)} collective-permute-done((bf16[3,5120]{1,0:T(4,128)(2,1)}, bf16[3,5120]{1,0:T(4,128)(2,1)S(1)}, u32[]{:S(2)}, u32[]{:S(2)}) %collective-permute-start.2) | collective-permute-done | bytes 30752 | tf_op jit(solution)/shard_map/ppermute | solution.py:68
  11.7 1.7 %collective-permute-start.3 = (bf16[24,2560]{1,0:T(8,128)(2,1)S(1)}, bf16[24,2560]{1,0:T(8,128)(2,1)S(1)}, u32[]{:S(2)}, u32[]{:S(2)}) collective-permute-start(bf16[24,2560]{1,0:T(8,128)(2,1)S(1)} %shard_map.83.s0), channel_id=1, source_target_pairs={{0,2},{1,3},{2,0},{3,1},{4,6},{5,7},{6,4},{7,5},{8,10},{9,11},{10,... | collective-permute-start | bytes 368648 | tf_op jit(solution)/shard_map/ppermute | solution.py:68
  13.8 3.9 %collective-permute-start.4 = (bf16[2,3,2,2560]{3,2,1,0:T(2,128)(2,1)}, bf16[2,3,2,2560]{3,2,1,0:T(2,128)(2,1)S(1)}, u32[]{:S(2)}, u32[]{:S(2)}) collective-permute-start(bf16[2,3,2,2560]{3,2,1,0:T(2,128)(2,1)} %bitcast.12), channel_id=1, source_target_pairs={{0,4},{1,5},{2,6},{3,7},{4,0},{5,1},{6,2},{7,3},{8,12},{9,13},{10,... | collective-permute-start | bytes 184328 | tf_op jit(solution)/shard_map/ppermute | solution.py:68
  17.8 2.0 %collective-permute-done.6.refs_3_ = bf16[2,3,2,2560]{3,2,1,0:T(2,128)(2,1)S(1)} collective-permute-done((bf16[2,3,2,2560]{3,2,1,0:T(2,128)(2,1)}, bf16[2,3,2,2560]{3,2,1,0:T(2,128)(2,1)S(1)}, u32[]{:S(2)}, u32[]{:S(2)}) %collective-permute-start.6) | collective-permute-done | bytes 61472 | tf_op jit(solution)/shard_map/ppermute | solution.py:68
  21.9 1.9 %shard_map.85 = (bf16[48,5120]{1,0:T(8,128)(2,1)S(1)}, bf16[48,480]{1,0:T(8,128)(2,1)S(1)}) custom-call(bf16[24,2560]{1,0:T(8,128)(2,1)S(1)} %shard_map.83.s0, bf16[24,2560]{1,0:T(8,128)(2,1)S(1)} %collective-permute-done.3.s1, bf16[24,2560]{1,0:T(8,128)(2,1)S(1)} %collective-permute-done.7.s2, bf16[24,2560]{1,0:T(8,128)(2,1)S(1)} %collective-permute-done.8.s3, ...), custom_call_target="tpu_custom_call" | custom-call | tf_op jit(solution)/shard_map/pallas_call | solution.py:30
  23.8 2.2 %collective-permute-start.11 = (bf16[48,480]{1,0:T(8,128)(2,1)S(1)}, bf16[48,480]{1,0:T(8,128)(2,1)S(1)}, u32[]{:S(2)}, u32[]{:S(2)}) collective-permute-start(bf16[48,480]{1,0:T(8,128)(2,1)S(1)} %get-tuple-element.49.refs_0_), channel_id=1, source_target_pairs={{0,12},{1,13},{2,14},{3,15},{4,8},{5,9},{6,10},{7,11},{8,4},{9,5},... | collective-permute-start | bytes 138248 | tf_op jit(solution)/shard_map/ppermute | solution.py:68
  28.2 1.4 %shard_map.86.weights = bf16[320,2560]{1,0:T(8,128)(2,1)S(1)} custom-call(bf16[320,2560]{1,0:T(8,128)(2,1)} %bitcast.8), custom_call_target="tpu_custom_call" | custom-call | tf_op jit(solution)/shard_map/pallas_call | solution.py:30
  30.1 2.1 %collective-permute-done.10.refs_2_ = bf16[48,480]{1,0:T(8,128)(2,1)S(1)} collective-permute-done((bf16[48,480]{1,0:T(8,128)(2,1)S(1)}, bf16[48,480]{1,0:T(8,128)(2,1)S(1)}, u32[]{:S(2)}, u32[]{:S(2)}) %collective-permute-start.10) | collective-permute-done | bytes 46112 | tf_op jit(solution)/shard_map/ppermute | solution.py:68
  33.5 3.6 %shard_map.88.w_up = bf16[864,5120]{1,0:T(8,128)(2,1)S(1)} custom-call(bf16[864,5120]{1,0:T(8,128)(2,1)} %bitcast.6), custom_call_target="tpu_custom_call" | custom-call | tf_op jit(solution)/shard_map/pallas_call | solution.py:30
  37.2 1.4 %collective-permute-done.12.s1 = bf16[4,48,480]{2,1,0:T(8,128)(2,1)S(1)} collective-permute-done((bf16[4,48,480]{2,1,0:T(8,128)(2,1)S(1)}, bf16[4,48,480]{2,1,0:T(8,128)(2,1)S(1)}, u32[]{:S(2)}, u32[]{:S(2)}) %collective-permute-start.12) | collective-permute-done | bytes 184352 | tf_op jit(solution)/shard_map/ppermute | solution.py:68
  40.0 1.8 %shard_map.90.refs_0_ = bf16[24,640]{1,0:T(8,128)(2,1)S(1)} custom-call(bf16[4,48,480]{2,1,0:T(8,128)(2,1)S(1)} %shard_map.87.s0, bf16[4,48,480]{2,1,0:T(8,128)(2,1)S(1)} %collective-permute-done.12.s1, bf16[4,48,480]{2,1,0:T(8,128)(2,1)S(1)} %collective-permute-done.13.s2, bf16[4,48,480]{2,1,0:T(8,128)(2,1)S(1)} %collective-permute-done.14.s3, ...), custom_call_target="tpu_custom_call" | custom-call | tf_op jit(solution)/shard_map/pallas_call | solution.py:30
  41.8 1.5 %collective-permute-start.20 = (bf16[24,640]{1,0:T(8,128)(2,1)S(1)}, bf16[24,640]{1,0:T(8,128)(2,1)S(1)}, u32[]{:S(2)}, u32[]{:S(2)}) collective-permute-start(bf16[24,640]{1,0:T(8,128)(2,1)S(1)} %shard_map.90.refs_0_), channel_id=1, source_target_pairs={{0,12},{1,13},{2,14},{3,15},{4,8},{5,9},{6,10},{7,11},{8,4},{9,5},... | collective-permute-start | bytes 92168 | tf_op jit(solution)/shard_map/ppermute | solution.py:68
  43.3 2.9 %collective-permute-start.18 = (bf16[24,640]{1,0:T(8,128)(2,1)S(1)}, bf16[24,640]{1,0:T(8,128)(2,1)S(1)}, u32[]{:S(2)}, u32[]{:S(2)}) collective-permute-start(bf16[24,640]{1,0:T(8,128)(2,1)S(1)} %shard_map.90.refs_0_), channel_id=1, source_target_pairs={{0,4},{1,5},{2,6},{3,7},{4,0},{5,1},{6,2},{7,3},{8,12},{9,13},{10,... | collective-permute-start | bytes 92168 | tf_op jit(solution)/shard_map/ppermute | solution.py:68
  49.4 3.6 %shard_map.92.w_down = bf16[864,5120]{1,0:T(8,128)(2,1)S(1)} custom-call(bf16[864,5120]{1,0:T(8,128)(2,1)} %refs_0_.2), custom_call_target="tpu_custom_call" | custom-call | tf_op jit(solution)/shard_map/pallas_call | solution.py:30
  54.9 5.6 %shard_map.93 = (f32[24,5120]{1,0:T(8,128)S(1)}, bf16[24,5120]{1,0:T(8,128)(2,1)S(1)}, f32[3,5120]{1,0:T(4,128)S(1)}) custom-call(bf16[4,24,640]{2,1,0:T(8,128)(2,1)S(1)} %shard_map.91.s0, bf16[4,24,640]{2,1,0:T(8,128)(2,1)S(1)} %collective-permute-done.21.s1, bf16[4,24,640]{2,1,0:T(8,128)(2,1)S(1)} %collective-permute-done.22.s2, ...), custom_call_target="tpu_custom_call" | custom-call | tf_op jit(solution)/shard_map/pallas_call | solution.py:30
  60.7 1.4 %collective-permute-done.24.got = bf16[24,5120]{1,0:T(8,128)(2,1)S(1)} collective-permute-done((bf16[24,5120]{1,0:T(8,128)(2,1)S(1)}, bf16[24,5120]{1,0:T(8,128)(2,1)S(1)}, u32[]{:S(2)}, u32[]{:S(2)}) %collective-permute-start.24) | collective-permute-done | bytes 245792 | tf_op jit(solution)/shard_map/ppermute | solution.py:68
  63.1 4.4 %collective-permute-done.25.got = bf16[24,2560]{1,0:T(8,128)(2,1)S(1)} collective-permute-done((bf16[24,2560]{1,0:T(8,128)(2,1)S(1)}, bf16[24,2560]{1,0:T(8,128)(2,1)S(1)}, u32[]{:S(2)}, u32[]{:S(2)}) %collective-permute-start.25) | collective-permute-done | bytes 122912 | tf_op jit(solution)/shard_map/ppermute | solution.py:68
  67.7 1.6 %collective-permute-start.26 = (bf16[24,640]{1,0:T(8,128)(2,1)S(1)}, bf16[24,640]{1,0:T(8,128)(2,1)S(1)}, u32[]{:S(2)}, u32[]{:S(2)}) collective-permute-start(bf16[24,640]{1,0:T(8,128)(2,1)S(1)} %get-tuple-element.71), channel_id=1, source_target_pairs={{0,4},{1,5},{2,6},{3,7},{4,0},{5,1},{6,2},{7,3},{8,12},{9,13},{10,... | collective-permute-start | bytes 92168 | tf_op jit(solution)/shard_map/ppermute | solution.py:68
  70.1 2.0 %collective-permute-start.28 = (bf16[24,640]{1,0:T(8,128)(2,1)S(1)}, bf16[24,640]{1,0:T(8,128)(2,1)S(1)}, u32[]{:S(2)}, u32[]{:S(2)}) collective-permute-start(bf16[24,640]{1,0:T(8,128)(2,1)S(1)} %get-tuple-element.73), channel_id=1, source_target_pairs={{0,12},{1,13},{2,14},{3,15},{4,8},{5,9},{6,10},{7,11},{8,4},{9,5},... | collective-permute-start | bytes 92168 | tf_op jit(solution)/shard_map/ppermute | solution.py:68
  72.1 2.2 %collective-permute-done.27.got2 = bf16[24,640]{1,0:T(8,128)(2,1)S(1)} collective-permute-done((bf16[24,640]{1,0:T(8,128)(2,1)S(1)}, bf16[24,640]{1,0:T(8,128)(2,1)S(1)}, u32[]{:S(2)}, u32[]{:S(2)}) %collective-permute-start.27) | collective-permute-done | bytes 30752 | tf_op jit(solution)/shard_map/ppermute | solution.py:68
  74.3 1.5 %collective-permute-done.28.got3 = bf16[24,640]{1,0:T(8,128)(2,1)S(1)} collective-permute-done((bf16[24,640]{1,0:T(8,128)(2,1)S(1)}, bf16[24,640]{1,0:T(8,128)(2,1)S(1)}, u32[]{:S(2)}, u32[]{:S(2)}) %collective-permute-start.28) | collective-permute-done | bytes 30752 | tf_op jit(solution)/shard_map/ppermute | solution.py:68
  (49 shorter events, 16.2 us)
Async XLA Ops:
  0.0 8.3 %collective-permute-start.1 = (bf16[3,5120]{1,0:T(4,128)(2,1)}, bf16[3,5120]{1,0:T(4,128)(2,1)S(1)}, u32[]{:S(2)}, u32[]{:S(2)}) collective-permute-start(bf16[3,5120]{1,0:T(4,128)(2,1)} %refs_0_.1), channel_id=1, source_target_pairs={{0,8},{1,9},{2,10},{3,11},{4,12},{5,13},{6,14},{7,15},{8,0},{9,1},... | collective-permute-start | bytes 92168 | tf_op jit(solution)/shard_map/ppermute | solution.py:68
  4.0 4.2 %collective-permute-start = (bf16[3,5120]{1,0:T(4,128)(2,1)}, bf16[3,5120]{1,0:T(4,128)(2,1)S(1)}, u32[]{:S(2)}, u32[]{:S(2)}) collective-permute-start(bf16[3,5120]{1,0:T(4,128)(2,1)} %refs_0_.1), channel_id=1, source_target_pairs={{0,4},{1,5},{2,6},{3,7},{4,0},{5,1},{6,2},{7,3},{8,12},{9,13},{10,... | collective-permute-start | bytes 92168 | tf_op jit(solution)/shard_map/ppermute | solution.py:68
  5.6 6.0 %collective-permute-start.2 = (bf16[3,5120]{1,0:T(4,128)(2,1)}, bf16[3,5120]{1,0:T(4,128)(2,1)S(1)}, u32[]{:S(2)}, u32[]{:S(2)}) collective-permute-start(bf16[3,5120]{1,0:T(4,128)(2,1)} %refs_0_.1), channel_id=1, source_target_pairs={{0,12},{1,13},{2,14},{3,15},{4,8},{5,9},{6,10},{7,11},{8,4},{9,5},... | collective-permute-start | bytes 92168 | tf_op jit(solution)/shard_map/ppermute | solution.py:68
  11.7 8.8 %collective-permute-start.3 = (bf16[24,2560]{1,0:T(8,128)(2,1)S(1)}, bf16[24,2560]{1,0:T(8,128)(2,1)S(1)}, u32[]{:S(2)}, u32[]{:S(2)}) collective-permute-start(bf16[24,2560]{1,0:T(8,128)(2,1)S(1)} %shard_map.83.s0), channel_id=1, source_target_pairs={{0,2},{1,3},{2,0},{3,1},{4,6},{5,7},{6,4},{7,5},{8,10},{9,11},{10,... | collective-permute-start | bytes 368648 | tf_op jit(solution)/shard_map/ppermute | solution.py:68
  13.4 6.4 %collective-permute-start.6 = (bf16[2,3,2,2560]{3,2,1,0:T(2,128)(2,1)}, bf16[2,3,2,2560]{3,2,1,0:T(2,128)(2,1)S(1)}, u32[]{:S(2)}, u32[]{:S(2)}) collective-permute-start(bf16[2,3,2,2560]{3,2,1,0:T(2,128)(2,1)} %bitcast.10), channel_id=1, source_target_pairs={{0,12},{1,13},{2,14},{3,15},{4,8},{5,9},{6,10},{7,11},{8,4},{9,5},... | collective-permute-start | bytes 184328 | tf_op jit(solution)/shard_map/ppermute | solution.py:68
  13.8 6.6 %collective-permute-start.5 = (bf16[2,3,2,2560]{3,2,1,0:T(2,128)(2,1)}, bf16[2,3,2,2560]{3,2,1,0:T(2,128)(2,1)S(1)}, u32[]{:S(2)}, u32[]{:S(2)}) collective-permute-start(bf16[2,3,2,2560]{3,2,1,0:T(2,128)(2,1)} %bitcast.11), channel_id=1, source_target_pairs={{0,8},{1,9},{2,10},{3,11},{4,12},{5,13},{6,14},{7,15},{8,0},{9,1},... | collective-permute-start | bytes 184328 | tf_op jit(solution)/shard_map/ppermute | solution.py:68
  13.8 6.6 %collective-permute-start.4 = (bf16[2,3,2,2560]{3,2,1,0:T(2,128)(2,1)}, bf16[2,3,2,2560]{3,2,1,0:T(2,128)(2,1)S(1)}, u32[]{:S(2)}, u32[]{:S(2)}) collective-permute-start(bf16[2,3,2,2560]{3,2,1,0:T(2,128)(2,1)} %bitcast.12), channel_id=1, source_target_pairs={{0,4},{1,5},{2,6},{3,7},{4,0},{5,1},{6,2},{7,3},{8,12},{9,13},{10,... | collective-permute-start | bytes 184328 | tf_op jit(solution)/shard_map/ppermute | solution.py:68
  20.5 12.5 %collective-permute-start.15 = (bf16[4,2,3,2,2560]{4,3,2,1,0:T(2,128)(2,1)S(1)}, bf16[4,2,3,2,2560]{4,3,2,1,0:T(2,128)(2,1)S(1)}, u32[]{:S(2)}, u32[]{:S(2)}) collective-permute-start(bf16[4,2,3,2,2560]{4,3,2,1,0:T(2,128)(2,1)S(1)} %shard_map.84.s0), channel_id=1, source_target_pairs={{0,2},{1,3},{2,0},{3,1},{4,6},{5,7},{6,4},{7,5},{8,10},{9,11},{10,... | collective-permute-start | bytes 737288 | tf_op jit(solution)/shard_map/ppermute | solution.py:68
  23.8 6.3 %collective-permute-start.11 = (bf16[48,480]{1,0:T(8,128)(2,1)S(1)}, bf16[48,480]{1,0:T(8,128)(2,1)S(1)}, u32[]{:S(2)}, u32[]{:S(2)}) collective-permute-start(bf16[48,480]{1,0:T(8,128)(2,1)S(1)} %get-tuple-element.49.refs_0_), channel_id=1, source_target_pairs={{0,12},{1,13},{2,14},{3,15},{4,8},{5,9},{6,10},{7,11},{8,4},{9,5},... | collective-permute-start | bytes 138248 | tf_op jit(solution)/shard_map/ppermute | solution.py:68
  25.9 6.2 %collective-permute-start.10 = (bf16[48,480]{1,0:T(8,128)(2,1)S(1)}, bf16[48,480]{1,0:T(8,128)(2,1)S(1)}, u32[]{:S(2)}, u32[]{:S(2)}) collective-permute-start(bf16[48,480]{1,0:T(8,128)(2,1)S(1)} %get-tuple-element.49.refs_0_), channel_id=1, source_target_pairs={{0,8},{1,9},{2,10},{3,11},{4,12},{5,13},{6,14},{7,15},{8,0},{9,1},... | collective-permute-start | bytes 138248 | tf_op jit(solution)/shard_map/ppermute | solution.py:68
  27.1 5.1 %collective-permute-start.9 = (bf16[48,480]{1,0:T(8,128)(2,1)S(1)}, bf16[48,480]{1,0:T(8,128)(2,1)S(1)}, u32[]{:S(2)}, u32[]{:S(2)}) collective-permute-start(bf16[48,480]{1,0:T(8,128)(2,1)S(1)} %get-tuple-element.49.refs_0_), channel_id=1, source_target_pairs={{0,4},{1,5},{2,6},{3,7},{4,0},{5,1},{6,2},{7,3},{8,12},{9,13},{10,... | collective-permute-start | bytes 138248 | tf_op jit(solution)/shard_map/ppermute | solution.py:68
  32.2 6.4 %collective-permute-start.12 = (bf16[4,48,480]{2,1,0:T(8,128)(2,1)S(1)}, bf16[4,48,480]{2,1,0:T(8,128)(2,1)S(1)}, u32[]{:S(2)}, u32[]{:S(2)}) collective-permute-start(bf16[4,48,480]{2,1,0:T(8,128)(2,1)S(1)} %shard_map.87.s0), channel_id=1, source_target_pairs={{0,2},{1,3},{2,0},{3,1},{4,6},{5,7},{6,4},{7,5},{8,10},{9,11},{10,... | collective-permute-start | bytes 552968 | tf_op jit(solution)/shard_map/ppermute | solution.py:68
  33.0 5.6 %collective-permute-start.16 = (bf16[4,2,3,2,2560]{4,3,2,1,0:T(2,128)(2,1)S(1)}, bf16[4,2,3,2,2560]{4,3,2,1,0:T(2,128)(2,1)S(1)}, u32[]{:S(2)}, u32[]{:S(2)}) collective-permute-start(bf16[4,2,3,2,2560]{4,3,2,1,0:T(2,128)(2,1)S(1)} %shard_map.84.s0), channel_id=1, source_target_pairs={{0,1},{1,0},{2,3},{3,2},{4,5},{5,4},{6,7},{7,6},{8,9},{9,8},{10,11... | collective-permute-start | bytes 737288 | tf_op jit(solution)/shard_map/ppermute | solution.py:68
  33.0 5.6 %collective-permute-start.17 = (bf16[4,2,3,2,2560]{4,3,2,1,0:T(2,128)(2,1)S(1)}, bf16[4,2,3,2,2560]{4,3,2,1,0:T(2,128)(2,1)S(1)}, u32[]{:S(2)}, u32[]{:S(2)}) collective-permute-start(bf16[4,2,3,2,2560]{4,3,2,1,0:T(2,128)(2,1)S(1)} %collective-permute-done.15.s1), channel_id=1, source_target_pairs={{0,1},{1,0},{2,3},{3,2},{4,5},{5,4},{6,7},{7,6},{8,9},{9,8},{10,11... | collective-permute-start | bytes 737288 | tf_op jit(solution)/shard_map/ppermute | solution.py:68
  33.5 5.7 %collective-permute-start.13 = (bf16[4,48,480]{2,1,0:T(8,128)(2,1)S(1)}, bf16[4,48,480]{2,1,0:T(8,128)(2,1)S(1)}, u32[]{:S(2)}, u32[]{:S(2)}) collective-permute-start(bf16[4,48,480]{2,1,0:T(8,128)(2,1)S(1)} %shard_map.87.s0), channel_id=1, source_target_pairs={{0,1},{1,0},{2,3},{3,2},{4,5},{5,4},{6,7},{7,6},{8,9},{9,8},{10,11... | collective-permute-start | bytes 552968 | tf_op jit(solution)/shard_map/ppermute | solution.py:68
  41.8 5.7 %collective-permute-start.20 = (bf16[24,640]{1,0:T(8,128)(2,1)S(1)}, bf16[24,640]{1,0:T(8,128)(2,1)S(1)}, u32[]{:S(2)}, u32[]{:S(2)}) collective-permute-start(bf16[24,640]{1,0:T(8,128)(2,1)S(1)} %shard_map.90.refs_0_), channel_id=1, source_target_pairs={{0,12},{1,13},{2,14},{3,15},{4,8},{5,9},{6,10},{7,11},{8,4},{9,5},... | collective-permute-start | bytes 92168 | tf_op jit(solution)/shard_map/ppermute | solution.py:68
  43.3 5.1 %collective-permute-start.19 = (bf16[24,640]{1,0:T(8,128)(2,1)S(1)}, bf16[24,640]{1,0:T(8,128)(2,1)S(1)}, u32[]{:S(2)}, u32[]{:S(2)}) collective-permute-start(bf16[24,640]{1,0:T(8,128)(2,1)S(1)} %shard_map.90.refs_0_), channel_id=1, source_target_pairs={{0,8},{1,9},{2,10},{3,11},{4,12},{5,13},{6,14},{7,15},{8,0},{9,1},... | collective-permute-start | bytes 92168 | tf_op jit(solution)/shard_map/ppermute | solution.py:68
  43.3 5.2 %collective-permute-start.18 = (bf16[24,640]{1,0:T(8,128)(2,1)S(1)}, bf16[24,640]{1,0:T(8,128)(2,1)S(1)}, u32[]{:S(2)}, u32[]{:S(2)}) collective-permute-start(bf16[24,640]{1,0:T(8,128)(2,1)S(1)} %shard_map.90.refs_0_), channel_id=1, source_target_pairs={{0,4},{1,5},{2,6},{3,7},{4,0},{5,1},{6,2},{7,3},{8,12},{9,13},{10,... | collective-permute-start | bytes 92168 | tf_op jit(solution)/shard_map/ppermute | solution.py:68
  48.6 5.0 %collective-permute-start.21 = (bf16[4,24,640]{2,1,0:T(8,128)(2,1)S(1)}, bf16[4,24,640]{2,1,0:T(8,128)(2,1)S(1)}, u32[]{:S(2)}, u32[]{:S(2)}) collective-permute-start(bf16[4,24,640]{2,1,0:T(8,128)(2,1)S(1)} %shard_map.91.s0), channel_id=1, source_target_pairs={{0,2},{1,3},{2,0},{3,1},{4,6},{5,7},{6,4},{7,5},{8,10},{9,11},{10,... | collective-permute-start | bytes 368648 | tf_op jit(solution)/shard_map/ppermute | solution.py:68
  49.4 4.2 %collective-permute-start.22 = (bf16[4,24,640]{2,1,0:T(8,128)(2,1)S(1)}, bf16[4,24,640]{2,1,0:T(8,128)(2,1)S(1)}, u32[]{:S(2)}, u32[]{:S(2)}) collective-permute-start(bf16[4,24,640]{2,1,0:T(8,128)(2,1)S(1)} %shard_map.91.s0), channel_id=1, source_target_pairs={{0,1},{1,0},{2,3},{3,2},{4,5},{5,4},{6,7},{7,6},{8,9},{9,8},{10,11... | collective-permute-start | bytes 368648 | tf_op jit(solution)/shard_map/ppermute | solution.py:68
  62.1 5.4 %collective-permute-start.25 = (bf16[24,2560]{1,0:T(8,128)(2,1)S(1)}, bf16[24,2560]{1,0:T(8,128)(2,1)S(1)}, u32[]{:S(2)}, u32[]{:S(2)}) collective-permute-start(bf16[24,2560]{1,0:T(8,128)(2,1)S(1)} %get-tuple-element.69), channel_id=1, source_target_pairs={{0,2},{1,3},{2,0},{3,1},{4,6},{5,7},{6,4},{7,5},{8,10},{9,11},{10,... | collective-permute-start | bytes 368648 | tf_op jit(solution)/shard_map/ppermute | solution.py:68
  67.7 4.5 %collective-permute-start.26 = (bf16[24,640]{1,0:T(8,128)(2,1)S(1)}, bf16[24,640]{1,0:T(8,128)(2,1)S(1)}, u32[]{:S(2)}, u32[]{:S(2)}) collective-permute-start(bf16[24,640]{1,0:T(8,128)(2,1)S(1)} %get-tuple-element.71), channel_id=1, source_target_pairs={{0,4},{1,5},{2,6},{3,7},{4,0},{5,1},{6,2},{7,3},{8,12},{9,13},{10,... | collective-permute-start | bytes 92168 | tf_op jit(solution)/shard_map/ppermute | solution.py:68
  69.2 5.1 %collective-permute-start.27 = (bf16[24,640]{1,0:T(8,128)(2,1)S(1)}, bf16[24,640]{1,0:T(8,128)(2,1)S(1)}, u32[]{:S(2)}, u32[]{:S(2)}) collective-permute-start(bf16[24,640]{1,0:T(8,128)(2,1)S(1)} %get-tuple-element.72), channel_id=1, source_target_pairs={{0,8},{1,9},{2,10},{3,11},{4,12},{5,13},{6,14},{7,15},{8,0},{9,1},... | collective-permute-start | bytes 92168 | tf_op jit(solution)/shard_map/ppermute | solution.py:68
  70.1 5.7 %collective-permute-start.28 = (bf16[24,640]{1,0:T(8,128)(2,1)S(1)}, bf16[24,640]{1,0:T(8,128)(2,1)S(1)}, u32[]{:S(2)}, u32[]{:S(2)}) collective-permute-start(bf16[24,640]{1,0:T(8,128)(2,1)S(1)} %get-tuple-element.73), channel_id=1, source_target_pairs={{0,12},{1,13},{2,14},{3,15},{4,8},{5,9},{6,10},{7,11},{8,4},{9,5},... | collective-permute-start | bytes 92168 | tf_op jit(solution)/shard_map/ppermute | solution.py:68
  (5 other events, 9.1 us)

commit v5 on v4

--- a/solution.py
+++ b/solution.py
@@ -218,13 +218,13 @@
     w_qkv = jnp.swapaxes(w_qkv, 1, 2).reshape(480, 5120)
     cache_kv = cache_kv.transpose(0, 2, 1, 3)
     pieces = tuple(swap(tokens, 4 * z) for z in (1, 2, 3))
-    cache_pieces = tuple(swap(cache_kv, 4 * z) for z in (1, 2, 3))
+    cache_far = swap(cache_kv, 8)
     tokens, modulation, norm_gains, cache_kv, w_qkv = load(tokens, modulation, norm_gains, cache_kv, w_qkv)
     pieces, tokens = lax.optimization_barrier((pieces, tokens))
     planes = call(pack_tokens, [((24, 2560), bf16)], tokens, *pieces, scratch=[pltpu.VMEM((24, 2560), f32)])[0]
     across = swap(planes, 2)
-    cache_planes = stack([cache_kv, *cache_pieces])
-    across, cache_planes = lax.optimization_barrier((across, cache_planes))
+    pair = stack([cache_kv, cache_far])
+    cache_planes = stack([pair, swap(pair, 4)]).reshape(4, *cache_kv.shape)
     cache_across = swap(cache_planes, 2)
     near_tokens, qkv = call(
         project_qkv,
@@ -275,7 +275,7 @@
     )
     keep, send = call(add_near, [((12, 5120), f32), ((24, 2560), bf16)], keep, swap(send, 1))
     keep, *sends = call(add_plane, [((3, 5120), f32)] + [((24, 640), bf16)] * 3, keep, swap(send, 2))
-    got = [swap(send, 4 * z) for z, send in zip((1, 2, 3), sends)]
+    got = [swap(send, 4 * z) for z, send in zip((3, 2, 1), sends[::-1])]
     return call(finish, [((3, 5120), bf16)], keep, *got, residual, modulation)[0]
 
 

time: 76.6 us -> 71.6 us (0.935)
  waiting for transfers between devices: 25 us -> 20 us
    ppermute x29 -> x28, waiting for transfers between devices: 25 us -> 20 us  [swap(): return lax.ppermute(values, 'seq', [(i, i ^ offset) for i in range(16)])]
    ppermute x29 -> x28, starting transfers between devices: 29.2 us -> 29.2 us  [swap(): return lax.ppermute(values, 'seq', [(i, i ^ offset) for i in range(16)])]
    pallas_call x15 -> x16, Pallas kernels: 22.2 us -> 22.2 us  [call(): pl.pallas_call(body, out_shape=[jax.ShapeDtypeStruct(shape, dtype) for sh...]
  transfers between devices with their start and end apart: 29 -> 28, of which waited for: 17 -> 15; matrix products, arithmetic and copies ran while one was open for 0% -> 0% of each run, Pallas kernels for 18% -> 20%
where the time goes in v5:
time: 71.6 us; the launch traced here: 71.5 us
  starting transfers between devices  29.2 us (41%)
  Pallas kernels  22.2 us (31%)
  waiting for transfers between devices  20 us (28%)
    ppermute x28, starting transfers between devices, swap(): return lax.ppermute(values, 'seq', [(i, i ^ offset) for i in range(16)])  29.2 us
    pallas_call x16, Pallas kernels, call(): pl.pallas_call(body, out_shape=[jax.ShapeDtypeStruct(shape, dtype) for sh...  22.2 us
    ppermute x28, waiting for transfers between devices, swap(): return lax.ppermute(values, 'seq', [(i, i ^ offset) for i in range(16)])  20 us
  transfers between devices with their start and end apart: 28, of which 15 were waited for; matrix products, arithmetic and copies ran while one was open for 0% of the time, Pallas kernels for 20%

profile of v5, /device:TPU:0, one launch (start us, length us, event | category | flops | bytes accessed | tf_op | source)
XLA Modules:
  0.0 71.5 jit_solution(8325908892395474833)
XLA Ops:
  0.0 4.0 %collective-permute-start.1 = (bf16[3,5120]{1,0:T(4,128)(2,1)}, bf16[3,5120]{1,0:T(4,128)(2,1)S(1)}, u32[]{:S(2)}, u32[]{:S(2)}) collective-permute-start(bf16[3,5120]{1,0:T(4,128)(2,1)} %refs_0_.1), channel_id=1, source_target_pairs={{0,8},{1,9},{2,10},{3,11},{4,12},{5,13},{6,14},{7,15},{8,0},{9,1},... | collective-permute-start | bytes 92168 | tf_op jit(solution)/shard_map/ppermute | solution.py:68
  4.0 1.6 %collective-permute-start = (bf16[3,5120]{1,0:T(4,128)(2,1)}, bf16[3,5120]{1,0:T(4,128)(2,1)S(1)}, u32[]{:S(2)}, u32[]{:S(2)}) collective-permute-start(bf16[3,5120]{1,0:T(4,128)(2,1)} %refs_0_.1), channel_id=1, source_target_pairs={{0,4},{1,5},{2,6},{3,7},{4,0},{5,1},{6,2},{7,3},{8,12},{9,13},{10,... | collective-permute-start | bytes 92168 | tf_op jit(solution)/shard_map/ppermute | solution.py:68
  5.6 1.9 %collective-permute-start.12 = (bf16[2,3,2,2560]{3,2,1,0:T(2,128)(2,1)}, bf16[2,3,2,2560]{3,2,1,0:T(2,128)(2,1)S(1)}, u32[]{:S(2)}, u32[]{:S(2)}) collective-permute-start(bf16[2,3,2,2560]{3,2,1,0:T(2,128)(2,1)} %bitcast.13), channel_id=1, source_target_pairs={{0,8},{1,9},{2,10},{3,11},{4,12},{5,13},{6,14},{7,15},{8,0},{9,1},... | collective-permute-start | bytes 184328 | tf_op jit(solution)/shard_map/ppermute | solution.py:68
  7.5 2.6 %shard_map.82 = (bf16[3,5120]{1,0:T(4,128)(2,1)S(1)}, f32[6,5120]{1,0:T(8,128)S(1)}, f32[2,2560]{1,0:T(2,128)S(1)}, bf16[2,3,2,2560]{3,2,1,0:T(2,128)(2,1)S(1)}, bf16[480,5120]{1,0:T(8,128)(2,1)S(1)}) custom-call(bf16[3,5120]{1,0:T(4,128)(2,1)} %refs_0_.1, f32[6,5120]{1,0:T(8,128)} %refs_1_.1, f32[2,2560]{1,0:T(2,128)} %refs_2_.1, ...), custom_call_target="tpu_custom_call" | custom-call | tf_op jit(solution)/shard_map/pallas_call | solution.py:30
  10.2 1.5 %collective-permute-done.2.got3 = bf16[3,5120]{1,0:T(4,128)(2,1)S(1)} collective-permute-done((bf16[3,5120]{1,0:T(4,128)(2,1)}, bf16[3,5120]{1,0:T(4,128)(2,1)S(1)}, u32[]{:S(2)}, u32[]{:S(2)}) %collective-permute-start.2) | collective-permute-done | bytes 30752 | tf_op jit(solution)/shard_map/ppermute | solution.py:68
  11.8 1.6 %collective-permute-start.3 = (bf16[24,2560]{1,0:T(8,128)(2,1)S(1)}, bf16[24,2560]{1,0:T(8,128)(2,1)S(1)}, u32[]{:S(2)}, u32[]{:S(2)}) collective-permute-start(bf16[24,2560]{1,0:T(8,128)(2,1)S(1)} %shard_map.83.s0), channel_id=1, source_target_pairs={{0,2},{1,3},{2,0},{3,1},{4,6},{5,7},{6,4},{7,5},{8,10},{9,11},{10,... | collective-permute-start | bytes 368648 | tf_op jit(solution)/shard_map/ppermute | solution.py:68
  14.4 2.3 %collective-permute-done.3.s1 = bf16[24,2560]{1,0:T(8,128)(2,1)S(1)} collective-permute-done((bf16[24,2560]{1,0:T(8,128)(2,1)S(1)}, bf16[24,2560]{1,0:T(8,128)(2,1)S(1)}, u32[]{:S(2)}, u32[]{:S(2)}) %collective-permute-start.3) | collective-permute-done | bytes 122912 | tf_op jit(solution)/shard_map/ppermute | solution.py:68
  16.7 1.6 %collective-permute-done.13.refs_1_ = bf16[2,2,3,2,2560]{4,3,2,1,0:T(2,128)(2,1)S(1)} collective-permute-done((bf16[2,2,3,2,2560]{4,3,2,1,0:T(2,128)(2,1)S(1)}, bf16[2,2,3,2,2560]{4,3,2,1,0:T(2,128)(2,1)S(1)}, u32[]{:S(2)}, u32[]{:S(2)}) %collective-permute-start.13) | collective-permute-done | bytes 122912 | tf_op jit(solution)/shard_map/ppermute | solution.py:68
  19.1 1.9 %shard_map.84 = (bf16[48,5120]{1,0:T(8,128)(2,1)S(1)}, bf16[48,480]{1,0:T(8,128)(2,1)S(1)}) custom-call(bf16[24,2560]{1,0:T(8,128)(2,1)S(1)} %shard_map.83.s0, bf16[24,2560]{1,0:T(8,128)(2,1)S(1)} %collective-permute-done.3.s1, bf16[24,2560]{1,0:T(8,128)(2,1)S(1)} %collective-permute-done.4.s2, bf16[24,2560]{1,0:T(8,128)(2,1)S(1)} %collective-permute-done.5.s3, ...), custom_call_target="tpu_custom_call" | custom-call | tf_op jit(solution)/shard_map/pallas_call | solution.py:30
  21.0 2.3 %collective-permute-start.8 = (bf16[48,480]{1,0:T(8,128)(2,1)S(1)}, bf16[48,480]{1,0:T(8,128)(2,1)S(1)}, u32[]{:S(2)}, u32[]{:S(2)}) collective-permute-start(bf16[48,480]{1,0:T(8,128)(2,1)S(1)} %get-tuple-element.45.refs_0_), channel_id=1, source_target_pairs={{0,12},{1,13},{2,14},{3,15},{4,8},{5,9},{6,10},{7,11},{8,4},{9,5},... | collective-permute-start | bytes 138248 | tf_op jit(solution)/shard_map/ppermute | solution.py:68
  23.3 2.2 %collective-permute-start.6 = (bf16[48,480]{1,0:T(8,128)(2,1)S(1)}, bf16[48,480]{1,0:T(8,128)(2,1)S(1)}, u32[]{:S(2)}, u32[]{:S(2)}) collective-permute-start(bf16[48,480]{1,0:T(8,128)(2,1)S(1)} %get-tuple-element.45.refs_0_), channel_id=1, source_target_pairs={{0,4},{1,5},{2,6},{3,7},{4,0},{5,1},{6,2},{7,3},{8,12},{9,13},{10,... | collective-permute-start | bytes 138248 | tf_op jit(solution)/shard_map/ppermute | solution.py:68
  25.5 1.4 %shard_map.85.weights = bf16[320,2560]{1,0:T(8,128)(2,1)S(1)} custom-call(bf16[320,2560]{1,0:T(8,128)(2,1)} %bitcast.12), custom_call_target="tpu_custom_call" | custom-call | tf_op jit(solution)/shard_map/pallas_call | solution.py:30
  27.1 1.3 %collective-permute-done.7.refs_2_ = bf16[48,480]{1,0:T(8,128)(2,1)S(1)} collective-permute-done((bf16[48,480]{1,0:T(8,128)(2,1)S(1)}, bf16[48,480]{1,0:T(8,128)(2,1)S(1)}, u32[]{:S(2)}, u32[]{:S(2)}) %collective-permute-start.7) | collective-permute-done | bytes 46112 | tf_op jit(solution)/shard_map/ppermute | solution.py:68
  30.1 3.6 %shard_map.87.w_up = bf16[864,5120]{1,0:T(8,128)(2,1)S(1)} custom-call(bf16[864,5120]{1,0:T(8,128)(2,1)} %bitcast.10), custom_call_target="tpu_custom_call" | custom-call | tf_op jit(solution)/shard_map/pallas_call | solution.py:30
  35.8 1.8 %shard_map.91.refs_0_ = bf16[24,640]{1,0:T(8,128)(2,1)S(1)} custom-call(bf16[4,48,480]{2,1,0:T(8,128)(2,1)S(1)} %shard_map.86.s0, bf16[4,48,480]{2,1,0:T(8,128)(2,1)S(1)} %collective-permute-done.9.s1, bf16[4,48,480]{2,1,0:T(8,128)(2,1)S(1)} %collective-permute-done.10.s2, bf16[4,48,480]{2,1,0:T(8,128)(2,1)S(1)} %collective-permute-done.11.s3, ...), custom_call_target="tpu_custom_call" | custom-call | tf_op jit(solution)/shard_map/pallas_call | solution.py:30
  37.6 1.9 %collective-permute-start.19 = (bf16[24,640]{1,0:T(8,128)(2,1)S(1)}, bf16[24,640]{1,0:T(8,128)(2,1)S(1)}, u32[]{:S(2)}, u32[]{:S(2)}) collective-permute-start(bf16[24,640]{1,0:T(8,128)(2,1)S(1)} %shard_map.91.refs_0_), channel_id=1, source_target_pairs={{0,12},{1,13},{2,14},{3,15},{4,8},{5,9},{6,10},{7,11},{8,4},{9,5},... | collective-permute-start | bytes 92168 | tf_op jit(solution)/shard_map/ppermute | solution.py:68
  40.1 1.9 %collective-permute-start.17 = (bf16[24,640]{1,0:T(8,128)(2,1)S(1)}, bf16[24,640]{1,0:T(8,128)(2,1)S(1)}, u32[]{:S(2)}, u32[]{:S(2)}) collective-permute-start(bf16[24,640]{1,0:T(8,128)(2,1)S(1)} %shard_map.91.refs_0_), channel_id=1, source_target_pairs={{0,4},{1,5},{2,6},{3,7},{4,0},{5,1},{6,2},{7,3},{8,12},{9,13},{10,... | collective-permute-start | bytes 92168 | tf_op jit(solution)/shard_map/ppermute | solution.py:68
  42.0 1.3 %collective-permute-done.19.refs_3_ = bf16[24,640]{1,0:T(8,128)(2,1)S(1)} collective-permute-done((bf16[24,640]{1,0:T(8,128)(2,1)S(1)}, bf16[24,640]{1,0:T(8,128)(2,1)S(1)}, u32[]{:S(2)}, u32[]{:S(2)}) %collective-permute-start.19) | collective-permute-done | bytes 30752 | tf_op jit(solution)/shard_map/ppermute | solution.py:68
  45.7 3.6 %shard_map.93.w_down = bf16[864,5120]{1,0:T(8,128)(2,1)S(1)} custom-call(bf16[864,5120]{1,0:T(8,128)(2,1)} %refs_0_.2), custom_call_target="tpu_custom_call" | custom-call | tf_op jit(solution)/shard_map/pallas_call | solution.py:30
  50.9 5.6 %shard_map.94 = (f32[24,5120]{1,0:T(8,128)S(1)}, bf16[24,5120]{1,0:T(8,128)(2,1)S(1)}, f32[3,5120]{1,0:T(4,128)S(1)}) custom-call(bf16[4,24,640]{2,1,0:T(8,128)(2,1)S(1)} %shard_map.92.s0, bf16[4,24,640]{2,1,0:T(8,128)(2,1)S(1)} %collective-permute-done.20.s1, bf16[4,24,640]{2,1,0:T(8,128)(2,1)S(1)} %collective-permute-done.21.s2, ...), custom_call_target="tpu_custom_call" | custom-call | tf_op jit(solution)/shard_map/pallas_call | solution.py:30
  59.1 4.6 %collective-permute-done.24.got = bf16[24,2560]{1,0:T(8,128)(2,1)S(1)} collective-permute-done((bf16[24,2560]{1,0:T(8,128)(2,1)S(1)}, bf16[24,2560]{1,0:T(8,128)(2,1)S(1)}, u32[]{:S(2)}, u32[]{:S(2)}) %collective-permute-start.24) | collective-permute-done | bytes 122912 | tf_op jit(solution)/shard_map/ppermute | solution.py:68
  63.8 1.9 %collective-permute-start.25 = (bf16[24,640]{1,0:T(8,128)(2,1)S(1)}, bf16[24,640]{1,0:T(8,128)(2,1)S(1)}, u32[]{:S(2)}, u32[]{:S(2)}) collective-permute-start(bf16[24,640]{1,0:T(8,128)(2,1)S(1)} %get-tuple-element.67), channel_id=1, source_target_pairs={{0,12},{1,13},{2,14},{3,15},{4,8},{5,9},{6,10},{7,11},{8,4},{9,5},... | collective-permute-start | bytes 92168 | tf_op jit(solution)/shard_map/ppermute | solution.py:68
  66.6 1.7 %collective-permute-start.27 = (bf16[24,640]{1,0:T(8,128)(2,1)S(1)}, bf16[24,640]{1,0:T(8,128)(2,1)S(1)}, u32[]{:S(2)}, u32[]{:S(2)}) collective-permute-start(bf16[24,640]{1,0:T(8,128)(2,1)S(1)} %get-tuple-element.69), channel_id=1, source_target_pairs={{0,4},{1,5},{2,6},{3,7},{4,0},{5,1},{6,2},{7,3},{8,12},{9,13},{10,... | collective-permute-start | bytes 92168 | tf_op jit(solution)/shard_map/ppermute | solution.py:68
  68.3 1.4 %collective-permute-done.25.got1 = bf16[24,640]{1,0:T(8,128)(2,1)S(1)} collective-permute-done((bf16[24,640]{1,0:T(8,128)(2,1)S(1)}, bf16[24,640]{1,0:T(8,128)(2,1)S(1)}, u32[]{:S(2)}, u32[]{:S(2)}) %collective-permute-start.25) | collective-permute-done | bytes 30752 | tf_op jit(solution)/shard_map/ppermute | solution.py:68
  (48 shorter events, 15.8 us)
Async XLA Ops:
  0.0 10.2 %collective-permute-start.1 = (bf16[3,5120]{1,0:T(4,128)(2,1)}, bf16[3,5120]{1,0:T(4,128)(2,1)S(1)}, u32[]{:S(2)}, u32[]{:S(2)}) collective-permute-start(bf16[3,5120]{1,0:T(4,128)(2,1)} %refs_0_.1), channel_id=1, source_target_pairs={{0,8},{1,9},{2,10},{3,11},{4,12},{5,13},{6,14},{7,15},{8,0},{9,1},... | collective-permute-start | bytes 92168 | tf_op jit(solution)/shard_map/ppermute | solution.py:68
  4.0 6.1 %collective-permute-start = (bf16[3,5120]{1,0:T(4,128)(2,1)}, bf16[3,5120]{1,0:T(4,128)(2,1)S(1)}, u32[]{:S(2)}, u32[]{:S(2)}) collective-permute-start(bf16[3,5120]{1,0:T(4,128)(2,1)} %refs_0_.1), channel_id=1, source_target_pairs={{0,4},{1,5},{2,6},{3,7},{4,0},{5,1},{6,2},{7,3},{8,12},{9,13},{10,... | collective-permute-start | bytes 92168 | tf_op jit(solution)/shard_map/ppermute | solution.py:68
  5.6 6.1 %collective-permute-start.2 = (bf16[3,5120]{1,0:T(4,128)(2,1)}, bf16[3,5120]{1,0:T(4,128)(2,1)S(1)}, u32[]{:S(2)}, u32[]{:S(2)}) collective-permute-start(bf16[3,5120]{1,0:T(4,128)(2,1)} %refs_0_.1), channel_id=1, source_target_pairs={{0,12},{1,13},{2,14},{3,15},{4,8},{5,9},{6,10},{7,11},{8,4},{9,5},... | collective-permute-start | bytes 92168 | tf_op jit(solution)/shard_map/ppermute | solution.py:68
  5.6 7.8 %collective-permute-start.12 = (bf16[2,3,2,2560]{3,2,1,0:T(2,128)(2,1)}, bf16[2,3,2,2560]{3,2,1,0:T(2,128)(2,1)S(1)}, u32[]{:S(2)}, u32[]{:S(2)}) collective-permute-start(bf16[2,3,2,2560]{3,2,1,0:T(2,128)(2,1)} %bitcast.13), channel_id=1, source_target_pairs={{0,8},{1,9},{2,10},{3,11},{4,12},{5,13},{6,14},{7,15},{8,0},{9,1},... | collective-permute-start | bytes 184328 | tf_op jit(solution)/shard_map/ppermute | solution.py:68
  11.8 4.9 %collective-permute-start.3 = (bf16[24,2560]{1,0:T(8,128)(2,1)S(1)}, bf16[24,2560]{1,0:T(8,128)(2,1)S(1)}, u32[]{:S(2)}, u32[]{:S(2)}) collective-permute-start(bf16[24,2560]{1,0:T(8,128)(2,1)S(1)} %shard_map.83.s0), channel_id=1, source_target_pairs={{0,2},{1,3},{2,0},{3,1},{4,6},{5,7},{6,4},{7,5},{8,10},{9,11},{10,... | collective-permute-start | bytes 368648 | tf_op jit(solution)/shard_map/ppermute | solution.py:68
  13.4 4.9 %collective-permute-start.13 = (bf16[2,2,3,2,2560]{4,3,2,1,0:T(2,128)(2,1)S(1)}, bf16[2,2,3,2,2560]{4,3,2,1,0:T(2,128)(2,1)S(1)}, u32[]{:S(2)}, u32[]{:S(2)}) collective-permute-start(bf16[2,2,3,2,2560]{4,3,2,1,0:T(2,128)(2,1)S(1)} %shard_map.88.refs_0_), channel_id=1, source_target_pairs={{0,4},{1,5},{2,6},{3,7},{4,0},{5,1},{6,2},{7,3},{8,12},{9,13},{10,... | collective-permute-start | bytes 368648 | tf_op jit(solution)/shard_map/ppermute | solution.py:68
  14.4 4.7 %collective-permute-start.4 = (bf16[24,2560]{1,0:T(8,128)(2,1)S(1)}, bf16[24,2560]{1,0:T(8,128)(2,1)S(1)}, u32[]{:S(2)}, u32[]{:S(2)}) collective-permute-start(bf16[24,2560]{1,0:T(8,128)(2,1)S(1)} %shard_map.83.s0), channel_id=1, source_target_pairs={{0,1},{1,0},{2,3},{3,2},{4,5},{5,4},{6,7},{7,6},{8,9},{9,8},{10,11... | collective-permute-start | bytes 368648 | tf_op jit(solution)/shard_map/ppermute | solution.py:68
  18.4 11.3 %collective-permute-start.14 = (bf16[4,2,3,2,2560]{4,3,2,1,0:T(2,128)(2,1)S(1)}, bf16[4,2,3,2,2560]{4,3,2,1,0:T(2,128)(2,1)S(1)}, u32[]{:S(2)}, u32[]{:S(2)}) collective-permute-start(bf16[4,2,3,2,2560]{4,3,2,1,0:T(2,128)(2,1)S(1)} %bitcast.7), channel_id=1, source_target_pairs={{0,2},{1,3},{2,0},{3,1},{4,6},{5,7},{6,4},{7,5},{8,10},{9,11},{10,... | collective-permute-start | bytes 737288 | tf_op jit(solution)/shard_map/ppermute | solution.py:68
  21.0 6.1 %collective-permute-start.8 = (bf16[48,480]{1,0:T(8,128)(2,1)S(1)}, bf16[48,480]{1,0:T(8,128)(2,1)S(1)}, u32[]{:S(2)}, u32[]{:S(2)}) collective-permute-start(bf16[48,480]{1,0:T(8,128)(2,1)S(1)} %get-tuple-element.45.refs_0_), channel_id=1, source_target_pairs={{0,12},{1,13},{2,14},{3,15},{4,8},{5,9},{6,10},{7,11},{8,4},{9,5},... | collective-permute-start | bytes 138248 | tf_op jit(solution)/shard_map/ppermute | solution.py:68
  23.3 5.1 %collective-permute-start.7 = (bf16[48,480]{1,0:T(8,128)(2,1)S(1)}, bf16[48,480]{1,0:T(8,128)(2,1)S(1)}, u32[]{:S(2)}, u32[]{:S(2)}) collective-permute-start(bf16[48,480]{1,0:T(8,128)(2,1)S(1)} %get-tuple-element.45.refs_0_), channel_id=1, source_target_pairs={{0,8},{1,9},{2,10},{3,11},{4,12},{5,13},{6,14},{7,15},{8,0},{9,1},... | collective-permute-start | bytes 138248 | tf_op jit(solution)/shard_map/ppermute | solution.py:68
  23.3 5.1 %collective-permute-start.6 = (bf16[48,480]{1,0:T(8,128)(2,1)S(1)}, bf16[48,480]{1,0:T(8,128)(2,1)S(1)}, u32[]{:S(2)}, u32[]{:S(2)}) collective-permute-start(bf16[48,480]{1,0:T(8,128)(2,1)S(1)} %get-tuple-element.45.refs_0_), channel_id=1, source_target_pairs={{0,4},{1,5},{2,6},{3,7},{4,0},{5,1},{6,2},{7,3},{8,12},{9,13},{10,... | collective-permute-start | bytes 138248 | tf_op jit(solution)/shard_map/ppermute | solution.py:68
  28.4 6.0 %collective-permute-start.9 = (bf16[4,48,480]{2,1,0:T(8,128)(2,1)S(1)}, bf16[4,48,480]{2,1,0:T(8,128)(2,1)S(1)}, u32[]{:S(2)}, u32[]{:S(2)}) collective-permute-start(bf16[4,48,480]{2,1,0:T(8,128)(2,1)S(1)} %shard_map.86.s0), channel_id=1, source_target_pairs={{0,2},{1,3},{2,0},{3,1},{4,6},{5,7},{6,4},{7,5},{8,10},{9,11},{10,... | collective-permute-start | bytes 552968 | tf_op jit(solution)/shard_map/ppermute | solution.py:68
  29.6 4.8 %collective-permute-start.15 = (bf16[4,2,3,2,2560]{4,3,2,1,0:T(2,128)(2,1)S(1)}, bf16[4,2,3,2,2560]{4,3,2,1,0:T(2,128)(2,1)S(1)}, u32[]{:S(2)}, u32[]{:S(2)}) collective-permute-start(bf16[4,2,3,2,2560]{4,3,2,1,0:T(2,128)(2,1)S(1)} %bitcast.8), channel_id=1, source_target_pairs={{0,1},{1,0},{2,3},{3,2},{4,5},{5,4},{6,7},{7,6},{8,9},{9,8},{10,11... | collective-permute-start | bytes 737288 | tf_op jit(solution)/shard_map/ppermute | solution.py:68
  29.6 4.8 %collective-permute-start.16 = (bf16[4,2,3,2,2560]{4,3,2,1,0:T(2,128)(2,1)S(1)}, bf16[4,2,3,2,2560]{4,3,2,1,0:T(2,128)(2,1)S(1)}, u32[]{:S(2)}, u32[]{:S(2)}) collective-permute-start(bf16[4,2,3,2,2560]{4,3,2,1,0:T(2,128)(2,1)S(1)} %collective-permute-done.14.s1), channel_id=1, source_target_pairs={{0,1},{1,0},{2,3},{3,2},{4,5},{5,4},{6,7},{7,6},{8,9},{9,8},{10,11... | collective-permute-start | bytes 737288 | tf_op jit(solution)/shard_map/ppermute | solution.py:68
  30.1 4.9 %collective-permute-start.10 = (bf16[4,48,480]{2,1,0:T(8,128)(2,1)S(1)}, bf16[4,48,480]{2,1,0:T(8,128)(2,1)S(1)}, u32[]{:S(2)}, u32[]{:S(2)}) collective-permute-start(bf16[4,48,480]{2,1,0:T(8,128)(2,1)S(1)} %shard_map.86.s0), channel_id=1, source_target_pairs={{0,1},{1,0},{2,3},{3,2},{4,5},{5,4},{6,7},{7,6},{8,9},{9,8},{10,11... | collective-permute-start | bytes 552968 | tf_op jit(solution)/shard_map/ppermute | solution.py:68
  37.6 5.8 %collective-permute-start.19 = (bf16[24,640]{1,0:T(8,128)(2,1)S(1)}, bf16[24,640]{1,0:T(8,128)(2,1)S(1)}, u32[]{:S(2)}, u32[]{:S(2)}) collective-permute-start(bf16[24,640]{1,0:T(8,128)(2,1)S(1)} %shard_map.91.refs_0_), channel_id=1, source_target_pairs={{0,12},{1,13},{2,14},{3,15},{4,8},{5,9},{6,10},{7,11},{8,4},{9,5},... | collective-permute-start | bytes 92168 | tf_op jit(solution)/shard_map/ppermute | solution.py:68
  39.5 4.9 %collective-permute-start.18 = (bf16[24,640]{1,0:T(8,128)(2,1)S(1)}, bf16[24,640]{1,0:T(8,128)(2,1)S(1)}, u32[]{:S(2)}, u32[]{:S(2)}) collective-permute-start(bf16[24,640]{1,0:T(8,128)(2,1)S(1)} %shard_map.91.refs_0_), channel_id=1, source_target_pairs={{0,8},{1,9},{2,10},{3,11},{4,12},{5,13},{6,14},{7,15},{8,0},{9,1},... | collective-permute-start | bytes 92168 | tf_op jit(solution)/shard_map/ppermute | solution.py:68
  40.1 4.4 %collective-permute-start.17 = (bf16[24,640]{1,0:T(8,128)(2,1)S(1)}, bf16[24,640]{1,0:T(8,128)(2,1)S(1)}, u32[]{:S(2)}, u32[]{:S(2)}) collective-permute-start(bf16[24,640]{1,0:T(8,128)(2,1)S(1)} %shard_map.91.refs_0_), channel_id=1, source_target_pairs={{0,4},{1,5},{2,6},{3,7},{4,0},{5,1},{6,2},{7,3},{8,12},{9,13},{10,... | collective-permute-start | bytes 92168 | tf_op jit(solution)/shard_map/ppermute | solution.py:68
  44.4 4.9 %collective-permute-start.20 = (bf16[4,24,640]{2,1,0:T(8,128)(2,1)S(1)}, bf16[4,24,640]{2,1,0:T(8,128)(2,1)S(1)}, u32[]{:S(2)}, u32[]{:S(2)}) collective-permute-start(bf16[4,24,640]{2,1,0:T(8,128)(2,1)S(1)} %shard_map.92.s0), channel_id=1, source_target_pairs={{0,2},{1,3},{2,0},{3,1},{4,6},{5,7},{6,4},{7,5},{8,10},{9,11},{10,... | collective-permute-start | bytes 368648 | tf_op jit(solution)/shard_map/ppermute | solution.py:68
  45.7 4.2 %collective-permute-start.21 = (bf16[4,24,640]{2,1,0:T(8,128)(2,1)S(1)}, bf16[4,24,640]{2,1,0:T(8,128)(2,1)S(1)}, u32[]{:S(2)}, u32[]{:S(2)}) collective-permute-start(bf16[4,24,640]{2,1,0:T(8,128)(2,1)S(1)} %shard_map.92.s0), channel_id=1, source_target_pairs={{0,1},{1,0},{2,3},{3,2},{4,5},{5,4},{6,7},{7,6},{8,9},{9,8},{10,11... | collective-permute-start | bytes 368648 | tf_op jit(solution)/shard_map/ppermute | solution.py:68
  58.0 5.7 %collective-permute-start.24 = (bf16[24,2560]{1,0:T(8,128)(2,1)S(1)}, bf16[24,2560]{1,0:T(8,128)(2,1)S(1)}, u32[]{:S(2)}, u32[]{:S(2)}) collective-permute-start(bf16[24,2560]{1,0:T(8,128)(2,1)S(1)} %get-tuple-element.65), channel_id=1, source_target_pairs={{0,2},{1,3},{2,0},{3,1},{4,6},{5,7},{6,4},{7,5},{8,10},{9,11},{10,... | collective-permute-start | bytes 368648 | tf_op jit(solution)/shard_map/ppermute | solution.py:68
  63.8 5.9 %collective-permute-start.25 = (bf16[24,640]{1,0:T(8,128)(2,1)S(1)}, bf16[24,640]{1,0:T(8,128)(2,1)S(1)}, u32[]{:S(2)}, u32[]{:S(2)}) collective-permute-start(bf16[24,640]{1,0:T(8,128)(2,1)S(1)} %get-tuple-element.67), channel_id=1, source_target_pairs={{0,12},{1,13},{2,14},{3,15},{4,8},{5,9},{6,10},{7,11},{8,4},{9,5},... | collective-permute-start | bytes 92168 | tf_op jit(solution)/shard_map/ppermute | solution.py:68
  65.7 5.1 %collective-permute-start.26 = (bf16[24,640]{1,0:T(8,128)(2,1)S(1)}, bf16[24,640]{1,0:T(8,128)(2,1)S(1)}, u32[]{:S(2)}, u32[]{:S(2)}) collective-permute-start(bf16[24,640]{1,0:T(8,128)(2,1)S(1)} %get-tuple-element.68), channel_id=1, source_target_pairs={{0,8},{1,9},{2,10},{3,11},{4,12},{5,13},{6,14},{7,15},{8,0},{9,1},... | collective-permute-start | bytes 92168 | tf_op jit(solution)/shard_map/ppermute | solution.py:68
  66.6 4.2 %collective-permute-start.27 = (bf16[24,640]{1,0:T(8,128)(2,1)S(1)}, bf16[24,640]{1,0:T(8,128)(2,1)S(1)}, u32[]{:S(2)}, u32[]{:S(2)}) collective-permute-start(bf16[24,640]{1,0:T(8,128)(2,1)S(1)} %get-tuple-element.69), channel_id=1, source_target_pairs={{0,4},{1,5},{2,6},{3,7},{4,0},{5,1},{6,2},{7,3},{8,12},{9,13},{10,... | collective-permute-start | bytes 92168 | tf_op jit(solution)/shard_map/ppermute | solution.py:68
  (4 other events, 6.9 us)

commit v6 on v5

--- a/solution.py
+++ b/solution.py
@@ -111,7 +111,7 @@
     near = lax.broadcasted_iota(jnp.int32, (48, 48), near_axis)
     token = lax.broadcasted_iota(jnp.int32, (48, 48), 1 - near_axis)
     block = (near * 171) >> 9
-    device = lax.axis_index("seq") ^ (4 * (block & 3) + 2 * ((block >> 2) & 1) + (block >> 3))
+    device = lax.axis_index("seq") ^ (4 * (block & 3) + ((block >> 2) & 1) + 2 * (block >> 3))
     return (token == 3 * device + near - 3 * block).astype(jnp.bfloat16)
 
 
@@ -120,7 +120,7 @@
 
 
 def project_qkv(s0, s1, s2, s3, mod, weights, tokens_out, qkv_out, flat):
-    for slot, ref in enumerate((s0, s1, s2, s3)):
+    for slot, ref in enumerate((s0, s2, s1, s3)):
         for half in range(2):
             piece = ref[12 * half : 12 * half + 12, :].astype(jnp.float32)
             flat[12 * slot : 12 * slot + 12, 2560 * half : 2560 * half + 2560] = piece
@@ -187,30 +187,35 @@
     hidden = lax.dot_general(normed, w_up[...], NT, preferred_element_type=jnp.float32)
     hidden = jax.nn.gelu(hidden, approximate=True).astype(jnp.bfloat16)
     partial = jnp.dot(hidden, w_down[...], preferred_element_type=jnp.float32)
-    keep[...] = partial[:24]
-    send[...] = partial[24:].astype(jnp.bfloat16)
-
-
-def add_near(keep, got, keep_out, send_out):
-    total = keep[...] + got[...].astype(jnp.float32)
-    keep_out[...] = total[:12]
-    send_out[...] = jnp.concatenate([total[12:, :2560], total[12:, 2560:]], axis=0).astype(jnp.bfloat16)
-
-
-def add_plane(keep, got, keep_out, send1, send2, send3):
+    first = lax.axis_index("seq") & 1 == 0
+    keep[...] = jnp.where(first, partial[:24], partial[24:])
+    send[...] = jnp.where(first, partial[24:], partial[:24]).astype(jnp.bfloat16)
+
+
+def add_cores(keep, got, own_out, send0, send1, send2, send3):
     got = got[...].astype(jnp.float32)
-    total = keep[...] + jnp.concatenate([got[:12], got[12:]], axis=1)
-    keep_out[...] = total[0:3]
-    for z, send in ((1, send1), (2, send2), (3, send3)):
-        rows = [total[3 * z + i : 3 * z + i + 1, 640 * g : 640 * g + 640] for i in range(3) for g in range(8)]
-        send[...] = jnp.concatenate(rows, axis=0).astype(jnp.bfloat16)
-
-
-def finish(keep, got1, got2, got3, residual, mod, out):
-    total = got1[...].astype(jnp.float32) + got2[...].astype(jnp.float32) + got3[...].astype(jnp.float32)
-    rows = [jnp.concatenate([total[8 * i + g : 8 * i + g + 1] for g in range(8)], axis=1) for i in range(3)]
-    total = keep[...] + jnp.concatenate(rows, axis=0)
-    out[...] = (residual[...] + mod[5:6, :] * total).astype(jnp.bfloat16)
+    total = keep[...] + jnp.concatenate([got[12:], got[:12]], axis=0)
+    for z, send in enumerate((send0, send1, send2, send3)):
+        block = jnp.concatenate([total[3 * z : 3 * z + 3], total[12 + 3 * z : 15 + 3 * z]], axis=0)
+        if z == 0:
+            own_out[...] = block
+        quarters = [block[:, 1280 * q : 1280 * q + 1280] for q in range(4)]
+        send[...] = jnp.concatenate(quarters, axis=0).astype(jnp.bfloat16)
+
+
+def add_chips(own, got0, got1, got2, got3, keep, send):
+    def whole(got):
+        got = got[...].astype(jnp.float32)
+        return jnp.concatenate([got[6 * q : 6 * q + 6] for q in range(4)], axis=1)
+
+    first = lax.axis_index("seq") & 1 == 0
+    total = jnp.where(first, own[...], whole(got0)) + whole(got1) + whole(got2) + whole(got3)
+    keep[...] = total[:3]
+    send[...] = total[3:]
+
+
+def finish(keep, got, residual, mod, out):
+    out[...] = (residual[...] + mod[5:6, :] * (keep[...] + got[...])).astype(jnp.bfloat16)
 
 
 def staged(tokens, modulation, w_qkv, norm_gains, cache_kv, w_out, w_up, w_down):
@@ -273,10 +278,13 @@
         w_down,
         scratch=[pltpu.VMEM((16, 24, 640), bf16)],
     )
-    keep, send = call(add_near, [((12, 5120), f32), ((24, 2560), bf16)], keep, swap(send, 1))
-    keep, *sends = call(add_plane, [((3, 5120), f32)] + [((24, 640), bf16)] * 3, keep, swap(send, 2))
-    got = [swap(send, 4 * z) for z, send in zip((3, 2, 1), sends[::-1])]
-    return call(finish, [((3, 5120), bf16)], keep, *got, residual, modulation)[0]
+    own, *sends = call(add_cores, [((6, 5120), f32)] + [((24, 1280), bf16)] * 4, keep, swap(send, 1))
+    got = []
+    for z, send in enumerate(sends):
+        pairs = [(i, i ^ 4 * z ^ 2 * (i & 1)) for i in range(16)]
+        got.append(lax.ppermute(send, "seq", [(i, j) for i, j in pairs if i != j]))
+    keep, send = call(add_chips, [((3, 5120), f32)] * 2, own, got[0], *[got[k] for k in (3, 2, 1)])
+    return call(finish, [((3, 5120), bf16)], keep, swap(send, 1), residual, modulation)[0]
 
 
 def general(tokens, modulation, w_qkv, norm_gains, cache_kv, w_out, w_up, w_down):

time: 71.6 us -> 71.3 us (level)
  waiting for transfers between devices: 20 us -> 19.2 us
    ppermute x28 -> x25, waiting for transfers between devices: 20 us -> 13.8 us  [swap(): return lax.ppermute(values, 'seq', [(i, i ^ offset) for i in range(16)])]
    ppermute x0 -> x4, waiting for transfers between devices: none -> 5.35 us  [staged(): got.append(lax.ppermute(send, 'seq', [(i, j) for i, j in pairs if i != j]))]
    ppermute x0 -> x4, starting transfers between devices: none -> 5.12 us  [staged(): got.append(lax.ppermute(send, 'seq', [(i, j) for i, j in pairs if i != j]))]
    ppermute x28 -> x25, starting transfers between devices: 29.2 us -> 24.4 us  [swap(): return lax.ppermute(values, 'seq', [(i, i ^ offset) for i in range(16)])]
  transfers between devices with their start and end apart: 28 -> 29, of which waited for: 15 -> 15; matrix products, arithmetic and copies ran while one was open for 0% -> 0% of each run, Pallas kernels for 20% -> 20%
where the time goes in v6:
time: 71.3 us; the launch traced here: 71.1 us
  starting transfers between devices  29.5 us (41%)
  Pallas kernels  22.3 us (31%)
  waiting for transfers between devices  19.2 us (27%)
    ppermute x25, starting transfers between devices, swap(): return lax.ppermute(values, 'seq', [(i, i ^ offset) for i in range(16)])  24.4 us
    pallas_call x16, Pallas kernels, call(): pl.pallas_call(body, out_shape=[jax.ShapeDtypeStruct(shape, dtype) for sh...  22.3 us
    ppermute x25, waiting for transfers between devices, swap(): return lax.ppermute(values, 'seq', [(i, i ^ offset) for i in range(16)])  13.8 us
    ppermute x4, waiting for transfers between devices, staged(): got.append(lax.ppermute(send, 'seq', [(i, j) for i, j in pairs if i != j]))  5.35 us
    ppermute x4, starting transfers between devices, staged(): got.append(lax.ppermute(send, 'seq', [(i, j) for i, j in pairs if i != j]))  5.12 us
  transfers between devices with their start and end apart: 29, of which 15 were waited for; matrix products, arithmetic and copies ran while one was open for 0% of the time, Pallas kernels for 20%

profile of v6, /device:TPU:0, one launch (start us, length us, event | category | flops | bytes accessed | tf_op | source)
XLA Modules:
  0.0 71.1 jit_solution(1943520459601567254)
XLA Ops:
  0.0 4.0 %collective-permute-start.1 = (bf16[3,5120]{1,0:T(4,128)(2,1)}, bf16[3,5120]{1,0:T(4,128)(2,1)S(1)}, u32[]{:S(2)}, u32[]{:S(2)}) collective-permute-start(bf16[3,5120]{1,0:T(4,128)(2,1)} %refs_0_.1), channel_id=1, source_target_pairs={{0,8},{1,9},{2,10},{3,11},{4,12},{5,13},{6,14},{7,15},{8,0},{9,1},... | collective-permute-start | bytes 92168 | tf_op jit(solution)/shard_map/ppermute | solution.py:68
  4.0 1.6 %collective-permute-start = (bf16[3,5120]{1,0:T(4,128)(2,1)}, bf16[3,5120]{1,0:T(4,128)(2,1)S(1)}, u32[]{:S(2)}, u32[]{:S(2)}) collective-permute-start(bf16[3,5120]{1,0:T(4,128)(2,1)} %refs_0_.1), channel_id=1, source_target_pairs={{0,4},{1,5},{2,6},{3,7},{4,0},{5,1},{6,2},{7,3},{8,12},{9,13},{10,... | collective-permute-start | bytes 92168 | tf_op jit(solution)/shard_map/ppermute | solution.py:68
  5.6 1.9 %collective-permute-start.12 = (bf16[2,3,2,2560]{3,2,1,0:T(2,128)(2,1)}, bf16[2,3,2,2560]{3,2,1,0:T(2,128)(2,1)S(1)}, u32[]{:S(2)}, u32[]{:S(2)}) collective-permute-start(bf16[2,3,2,2560]{3,2,1,0:T(2,128)(2,1)} %bitcast.13), channel_id=1, source_target_pairs={{0,8},{1,9},{2,10},{3,11},{4,12},{5,13},{6,14},{7,15},{8,0},{9,1},... | collective-permute-start | bytes 184328 | tf_op jit(solution)/shard_map/ppermute | solution.py:68
  7.5 2.6 %shard_map.82 = (bf16[3,5120]{1,0:T(4,128)(2,1)S(1)}, f32[6,5120]{1,0:T(8,128)S(1)}, f32[2,2560]{1,0:T(2,128)S(1)}, bf16[2,3,2,2560]{3,2,1,0:T(2,128)(2,1)S(1)}, bf16[480,5120]{1,0:T(8,128)(2,1)S(1)}) custom-call(bf16[3,5120]{1,0:T(4,128)(2,1)} %refs_0_.1, f32[6,5120]{1,0:T(8,128)} %refs_1_.1, f32[2,2560]{1,0:T(2,128)} %refs_2_.1, ...), custom_call_target="tpu_custom_call" | custom-call | tf_op jit(solution)/shard_map/pallas_call | solution.py:30
  10.2 1.5 %collective-permute-done.2.got3 = bf16[3,5120]{1,0:T(4,128)(2,1)S(1)} collective-permute-done((bf16[3,5120]{1,0:T(4,128)(2,1)}, bf16[3,5120]{1,0:T(4,128)(2,1)S(1)}, u32[]{:S(2)}, u32[]{:S(2)}) %collective-permute-start.2) | collective-permute-done | bytes 30752 | tf_op jit(solution)/shard_map/ppermute | solution.py:68
  11.8 1.6 %collective-permute-start.3 = (bf16[24,2560]{1,0:T(8,128)(2,1)S(1)}, bf16[24,2560]{1,0:T(8,128)(2,1)S(1)}, u32[]{:S(2)}, u32[]{:S(2)}) collective-permute-start(bf16[24,2560]{1,0:T(8,128)(2,1)S(1)} %shard_map.83.s0), channel_id=1, source_target_pairs={{0,2},{1,3},{2,0},{3,1},{4,6},{5,7},{6,4},{7,5},{8,10},{9,11},{10,... | collective-permute-start | bytes 368648 | tf_op jit(solution)/shard_map/ppermute | solution.py:68
  14.4 2.3 %collective-permute-done.3.s1 = bf16[24,2560]{1,0:T(8,128)(2,1)S(1)} collective-permute-done((bf16[24,2560]{1,0:T(8,128)(2,1)S(1)}, bf16[24,2560]{1,0:T(8,128)(2,1)S(1)}, u32[]{:S(2)}, u32[]{:S(2)}) %collective-permute-start.3) | collective-permute-done | bytes 122912 | tf_op jit(solution)/shard_map/ppermute | solution.py:68
  16.7 1.6 %collective-permute-done.13.refs_1_ = bf16[2,2,3,2,2560]{4,3,2,1,0:T(2,128)(2,1)S(1)} collective-permute-done((bf16[2,2,3,2,2560]{4,3,2,1,0:T(2,128)(2,1)S(1)}, bf16[2,2,3,2,2560]{4,3,2,1,0:T(2,128)(2,1)S(1)}, u32[]{:S(2)}, u32[]{:S(2)}) %collective-permute-start.13) | collective-permute-done | bytes 122912 | tf_op jit(solution)/shard_map/ppermute | solution.py:68
  19.1 1.9 %shard_map.84 = (bf16[48,5120]{1,0:T(8,128)(2,1)S(1)}, bf16[48,480]{1,0:T(8,128)(2,1)S(1)}) custom-call(bf16[24,2560]{1,0:T(8,128)(2,1)S(1)} %shard_map.83.s0, bf16[24,2560]{1,0:T(8,128)(2,1)S(1)} %collective-permute-done.3.s1, bf16[24,2560]{1,0:T(8,128)(2,1)S(1)} %collective-permute-done.4.s2, bf16[24,2560]{1,0:T(8,128)(2,1)S(1)} %collective-permute-done.5.s3, ...), custom_call_target="tpu_custom_call" | custom-call | tf_op jit(solution)/shard_map/pallas_call | solution.py:30
  21.0 2.3 %collective-permute-start.8 = (bf16[48,480]{1,0:T(8,128)(2,1)S(1)}, bf16[48,480]{1,0:T(8,128)(2,1)S(1)}, u32[]{:S(2)}, u32[]{:S(2)}) collective-permute-start(bf16[48,480]{1,0:T(8,128)(2,1)S(1)} %get-tuple-element.46.refs_0_), channel_id=1, source_target_pairs={{0,12},{1,13},{2,14},{3,15},{4,8},{5,9},{6,10},{7,11},{8,4},{9,5},... | collective-permute-start | bytes 138248 | tf_op jit(solution)/shard_map/ppermute | solution.py:68
  23.3 2.2 %collective-permute-start.6 = (bf16[48,480]{1,0:T(8,128)(2,1)S(1)}, bf16[48,480]{1,0:T(8,128)(2,1)S(1)}, u32[]{:S(2)}, u32[]{:S(2)}) collective-permute-start(bf16[48,480]{1,0:T(8,128)(2,1)S(1)} %get-tuple-element.46.refs_0_), channel_id=1, source_target_pairs={{0,4},{1,5},{2,6},{3,7},{4,0},{5,1},{6,2},{7,3},{8,12},{9,13},{10,... | collective-permute-start | bytes 138248 | tf_op jit(solution)/shard_map/ppermute | solution.py:68
  25.5 1.4 %shard_map.85.weights = bf16[320,2560]{1,0:T(8,128)(2,1)S(1)} custom-call(bf16[320,2560]{1,0:T(8,128)(2,1)} %bitcast.12), custom_call_target="tpu_custom_call" | custom-call | tf_op jit(solution)/shard_map/pallas_call | solution.py:30
  27.1 1.3 %collective-permute-done.7.refs_2_ = bf16[48,480]{1,0:T(8,128)(2,1)S(1)} collective-permute-done((bf16[48,480]{1,0:T(8,128)(2,1)S(1)}, bf16[48,480]{1,0:T(8,128)(2,1)S(1)}, u32[]{:S(2)}, u32[]{:S(2)}) %collective-permute-start.7) | collective-permute-done | bytes 46112 | tf_op jit(solution)/shard_map/ppermute | solution.py:68
  30.1 3.6 %shard_map.87.w_up = bf16[864,5120]{1,0:T(8,128)(2,1)S(1)} custom-call(bf16[864,5120]{1,0:T(8,128)(2,1)} %bitcast.10), custom_call_target="tpu_custom_call" | custom-call | tf_op jit(solution)/shard_map/pallas_call | solution.py:30
  35.8 1.8 %shard_map.91.refs_0_ = bf16[24,640]{1,0:T(8,128)(2,1)S(1)} custom-call(bf16[4,48,480]{2,1,0:T(8,128)(2,1)S(1)} %shard_map.86.s0, bf16[4,48,480]{2,1,0:T(8,128)(2,1)S(1)} %collective-permute-done.9.s1, bf16[4,48,480]{2,1,0:T(8,128)(2,1)S(1)} %collective-permute-done.10.s2, bf16[4,48,480]{2,1,0:T(8,128)(2,1)S(1)} %collective-permute-done.11.s3, ...), custom_call_target="tpu_custom_call" | custom-call | tf_op jit(solution)/shard_map/pallas_call | solution.py:30
  37.6 2.0 %collective-permute-start.19 = (bf16[24,640]{1,0:T(8,128)(2,1)S(1)}, bf16[24,640]{1,0:T(8,128)(2,1)S(1)}, u32[]{:S(2)}, u32[]{:S(2)}) collective-permute-start(bf16[24,640]{1,0:T(8,128)(2,1)S(1)} %shard_map.91.refs_0_), channel_id=1, source_target_pairs={{0,12},{1,13},{2,14},{3,15},{4,8},{5,9},{6,10},{7,11},{8,4},{9,5},... | collective-permute-start | bytes 92168 | tf_op jit(solution)/shard_map/ppermute | solution.py:68
  40.1 2.0 %collective-permute-start.17 = (bf16[24,640]{1,0:T(8,128)(2,1)S(1)}, bf16[24,640]{1,0:T(8,128)(2,1)S(1)}, u32[]{:S(2)}, u32[]{:S(2)}) collective-permute-start(bf16[24,640]{1,0:T(8,128)(2,1)S(1)} %shard_map.91.refs_0_), channel_id=1, source_target_pairs={{0,4},{1,5},{2,6},{3,7},{4,0},{5,1},{6,2},{7,3},{8,12},{9,13},{10,... | collective-permute-start | bytes 92168 | tf_op jit(solution)/shard_map/ppermute | solution.py:68
  42.0 1.3 %collective-permute-done.19.refs_3_ = bf16[24,640]{1,0:T(8,128)(2,1)S(1)} collective-permute-done((bf16[24,640]{1,0:T(8,128)(2,1)S(1)}, bf16[24,640]{1,0:T(8,128)(2,1)S(1)}, u32[]{:S(2)}, u32[]{:S(2)}) %collective-permute-start.19) | collective-permute-done | bytes 30752 | tf_op jit(solution)/shard_map/ppermute | solution.py:68
  45.7 3.6 %shard_map.93.w_down = bf16[864,5120]{1,0:T(8,128)(2,1)S(1)} custom-call(bf16[864,5120]{1,0:T(8,128)(2,1)} %refs_0_.2), custom_call_target="tpu_custom_call" | custom-call | tf_op jit(solution)/shard_map/pallas_call | solution.py:30
  50.9 5.5 %shard_map.94 = (f32[24,5120]{1,0:T(8,128)S(1)}, bf16[24,5120]{1,0:T(8,128)(2,1)S(1)}, f32[3,5120]{1,0:T(4,128)S(1)}) custom-call(bf16[4,24,640]{2,1,0:T(8,128)(2,1)S(1)} %shard_map.92.s0, bf16[4,24,640]{2,1,0:T(8,128)(2,1)S(1)} %collective-permute-done.20.s1, bf16[4,24,640]{2,1,0:T(8,128)(2,1)S(1)} %collective-permute-done.21.s2, ...), custom_call_target="tpu_custom_call" | custom-call | tf_op jit(solution)/shard_map/pallas_call | solution.py:30
  58.9 2.0 %collective-permute-start.25 = (bf16[24,1280]{1,0:T(8,128)(2,1)S(1)}, bf16[24,1280]{1,0:T(8,128)(2,1)S(1)}, u32[]{:S(2)}, u32[]{:S(2)}) collective-permute-start(bf16[24,1280]{1,0:T(8,128)(2,1)S(1)} %get-tuple-element.67), channel_id=1, source_target_pairs={{0,12},{1,15},{2,14},{3,13},{4,8},{5,11},{6,10},{7,9},{8,4},{9,7},... | collective-permute-start | bytes 184328 | tf_op jit(solution)/shard_map/ppermute | solution.py:285
  61.7 1.6 %collective-permute-start.27 = (bf16[24,1280]{1,0:T(8,128)(2,1)S(1)}, bf16[24,1280]{1,0:T(8,128)(2,1)S(1)}, u32[]{:S(2)}, u32[]{:S(2)}) collective-permute-start(bf16[24,1280]{1,0:T(8,128)(2,1)S(1)} %get-tuple-element.69), channel_id=1, source_target_pairs={{0,4},{1,7},{2,6},{3,5},{4,0},{5,3},{6,2},{7,1},{8,12},{9,15},{10,... | collective-permute-start | bytes 184328 | tf_op jit(solution)/shard_map/ppermute | solution.py:285
  63.3 1.6 %collective-permute-done.25.got1 = bf16[24,1280]{1,0:T(8,128)(2,1)S(1)} collective-permute-done((bf16[24,1280]{1,0:T(8,128)(2,1)S(1)}, bf16[24,1280]{1,0:T(8,128)(2,1)S(1)}, u32[]{:S(2)}, u32[]{:S(2)}) %collective-permute-start.25) | collective-permute-done | bytes 61472 | tf_op jit(solution)/shard_map/ppermute | solution.py:285
  65.0 3.7 %collective-permute-done.26.got2 = bf16[24,1280]{1,0:T(8,128)(2,1)S(1)} collective-permute-done((bf16[24,1280]{1,0:T(8,128)(2,1)S(1)}, bf16[24,1280]{1,0:T(8,128)(2,1)S(1)}, u32[]{:S(2)}, u32[]{:S(2)}) %collective-permute-start.26) | collective-permute-done | bytes 61472 | tf_op jit(solution)/shard_map/ppermute | solution.py:285
  (50 shorter events, 16.0 us)
Async XLA Ops:
  0.0 10.2 %collective-permute-start.1 = (bf16[3,5120]{1,0:T(4,128)(2,1)}, bf16[3,5120]{1,0:T(4,128)(2,1)S(1)}, u32[]{:S(2)}, u32[]{:S(2)}) collective-permute-start(bf16[3,5120]{1,0:T(4,128)(2,1)} %refs_0_.1), channel_id=1, source_target_pairs={{0,8},{1,9},{2,10},{3,11},{4,12},{5,13},{6,14},{7,15},{8,0},{9,1},... | collective-permute-start | bytes 92168 | tf_op jit(solution)/shard_map/ppermute | solution.py:68
  4.0 6.1 %collective-permute-start = (bf16[3,5120]{1,0:T(4,128)(2,1)}, bf16[3,5120]{1,0:T(4,128)(2,1)S(1)}, u32[]{:S(2)}, u32[]{:S(2)}) collective-permute-start(bf16[3,5120]{1,0:T(4,128)(2,1)} %refs_0_.1), channel_id=1, source_target_pairs={{0,4},{1,5},{2,6},{3,7},{4,0},{5,1},{6,2},{7,3},{8,12},{9,13},{10,... | collective-permute-start | bytes 92168 | tf_op jit(solution)/shard_map/ppermute | solution.py:68
  5.6 6.1 %collective-permute-start.2 = (bf16[3,5120]{1,0:T(4,128)(2,1)}, bf16[3,5120]{1,0:T(4,128)(2,1)S(1)}, u32[]{:S(2)}, u32[]{:S(2)}) collective-permute-start(bf16[3,5120]{1,0:T(4,128)(2,1)} %refs_0_.1), channel_id=1, source_target_pairs={{0,12},{1,13},{2,14},{3,15},{4,8},{5,9},{6,10},{7,11},{8,4},{9,5},... | collective-permute-start | bytes 92168 | tf_op jit(solution)/shard_map/ppermute | solution.py:68
  5.6 7.8 %collective-permute-start.12 = (bf16[2,3,2,2560]{3,2,1,0:T(2,128)(2,1)}, bf16[2,3,2,2560]{3,2,1,0:T(2,128)(2,1)S(1)}, u32[]{:S(2)}, u32[]{:S(2)}) collective-permute-start(bf16[2,3,2,2560]{3,2,1,0:T(2,128)(2,1)} %bitcast.13), channel_id=1, source_target_pairs={{0,8},{1,9},{2,10},{3,11},{4,12},{5,13},{6,14},{7,15},{8,0},{9,1},... | collective-permute-start | bytes 184328 | tf_op jit(solution)/shard_map/ppermute | solution.py:68
  11.8 4.9 %collective-permute-start.3 = (bf16[24,2560]{1,0:T(8,128)(2,1)S(1)}, bf16[24,2560]{1,0:T(8,128)(2,1)S(1)}, u32[]{:S(2)}, u32[]{:S(2)}) collective-permute-start(bf16[24,2560]{1,0:T(8,128)(2,1)S(1)} %shard_map.83.s0), channel_id=1, source_target_pairs={{0,2},{1,3},{2,0},{3,1},{4,6},{5,7},{6,4},{7,5},{8,10},{9,11},{10,... | collective-permute-start | bytes 368648 | tf_op jit(solution)/shard_map/ppermute | solution.py:68
  13.4 4.9 %collective-permute-start.13 = (bf16[2,2,3,2,2560]{4,3,2,1,0:T(2,128)(2,1)S(1)}, bf16[2,2,3,2,2560]{4,3,2,1,0:T(2,128)(2,1)S(1)}, u32[]{:S(2)}, u32[]{:S(2)}) collective-permute-start(bf16[2,2,3,2,2560]{4,3,2,1,0:T(2,128)(2,1)S(1)} %shard_map.88.refs_0_), channel_id=1, source_target_pairs={{0,4},{1,5},{2,6},{3,7},{4,0},{5,1},{6,2},{7,3},{8,12},{9,13},{10,... | collective-permute-start | bytes 368648 | tf_op jit(solution)/shard_map/ppermute | solution.py:68
  14.4 4.7 %collective-permute-start.4 = (bf16[24,2560]{1,0:T(8,128)(2,1)S(1)}, bf16[24,2560]{1,0:T(8,128)(2,1)S(1)}, u32[]{:S(2)}, u32[]{:S(2)}) collective-permute-start(bf16[24,2560]{1,0:T(8,128)(2,1)S(1)} %shard_map.83.s0), channel_id=1, source_target_pairs={{0,1},{1,0},{2,3},{3,2},{4,5},{5,4},{6,7},{7,6},{8,9},{9,8},{10,11... | collective-permute-start | bytes 368648 | tf_op jit(solution)/shard_map/ppermute | solution.py:68
  18.4 11.3 %collective-permute-start.14 = (bf16[4,2,3,2,2560]{4,3,2,1,0:T(2,128)(2,1)S(1)}, bf16[4,2,3,2,2560]{4,3,2,1,0:T(2,128)(2,1)S(1)}, u32[]{:S(2)}, u32[]{:S(2)}) collective-permute-start(bf16[4,2,3,2,2560]{4,3,2,1,0:T(2,128)(2,1)S(1)} %bitcast.7), channel_id=1, source_target_pairs={{0,2},{1,3},{2,0},{3,1},{4,6},{5,7},{6,4},{7,5},{8,10},{9,11},{10,... | collective-permute-start | bytes 737288 | tf_op jit(solution)/shard_map/ppermute | solution.py:68
  21.0 6.1 %collective-permute-start.8 = (bf16[48,480]{1,0:T(8,128)(2,1)S(1)}, bf16[48,480]{1,0:T(8,128)(2,1)S(1)}, u32[]{:S(2)}, u32[]{:S(2)}) collective-permute-start(bf16[48,480]{1,0:T(8,128)(2,1)S(1)} %get-tuple-element.46.refs_0_), channel_id=1, source_target_pairs={{0,12},{1,13},{2,14},{3,15},{4,8},{5,9},{6,10},{7,11},{8,4},{9,5},... | collective-permute-start | bytes 138248 | tf_op jit(solution)/shard_map/ppermute | solution.py:68
  23.3 5.1 %collective-permute-start.7 = (bf16[48,480]{1,0:T(8,128)(2,1)S(1)}, bf16[48,480]{1,0:T(8,128)(2,1)S(1)}, u32[]{:S(2)}, u32[]{:S(2)}) collective-permute-start(bf16[48,480]{1,0:T(8,128)(2,1)S(1)} %get-tuple-element.46.refs_0_), channel_id=1, source_target_pairs={{0,8},{1,9},{2,10},{3,11},{4,12},{5,13},{6,14},{7,15},{8,0},{9,1},... | collective-permute-start | bytes 138248 | tf_op jit(solution)/shard_map/ppermute | solution.py:68
  23.3 5.1 %collective-permute-start.6 = (bf16[48,480]{1,0:T(8,128)(2,1)S(1)}, bf16[48,480]{1,0:T(8,128)(2,1)S(1)}, u32[]{:S(2)}, u32[]{:S(2)}) collective-permute-start(bf16[48,480]{1,0:T(8,128)(2,1)S(1)} %get-tuple-element.46.refs_0_), channel_id=1, source_target_pairs={{0,4},{1,5},{2,6},{3,7},{4,0},{5,1},{6,2},{7,3},{8,12},{9,13},{10,... | collective-permute-start | bytes 138248 | tf_op jit(solution)/shard_map/ppermute | solution.py:68
  28.4 6.0 %collective-permute-start.9 = (bf16[4,48,480]{2,1,0:T(8,128)(2,1)S(1)}, bf16[4,48,480]{2,1,0:T(8,128)(2,1)S(1)}, u32[]{:S(2)}, u32[]{:S(2)}) collective-permute-start(bf16[4,48,480]{2,1,0:T(8,128)(2,1)S(1)} %shard_map.86.s0), channel_id=1, source_target_pairs={{0,2},{1,3},{2,0},{3,1},{4,6},{5,7},{6,4},{7,5},{8,10},{9,11},{10,... | collective-permute-start | bytes 552968 | tf_op jit(solution)/shard_map/ppermute | solution.py:68
  29.6 4.8 %collective-permute-start.15 = (bf16[4,2,3,2,2560]{4,3,2,1,0:T(2,128)(2,1)S(1)}, bf16[4,2,3,2,2560]{4,3,2,1,0:T(2,128)(2,1)S(1)}, u32[]{:S(2)}, u32[]{:S(2)}) collective-permute-start(bf16[4,2,3,2,2560]{4,3,2,1,0:T(2,128)(2,1)S(1)} %bitcast.8), channel_id=1, source_target_pairs={{0,1},{1,0},{2,3},{3,2},{4,5},{5,4},{6,7},{7,6},{8,9},{9,8},{10,11... | collective-permute-start | bytes 737288 | tf_op jit(solution)/shard_map/ppermute | solution.py:68
  29.6 4.8 %collective-permute-start.16 = (bf16[4,2,3,2,2560]{4,3,2,1,0:T(2,128)(2,1)S(1)}, bf16[4,2,3,2,2560]{4,3,2,1,0:T(2,128)(2,1)S(1)}, u32[]{:S(2)}, u32[]{:S(2)}) collective-permute-start(bf16[4,2,3,2,2560]{4,3,2,1,0:T(2,128)(2,1)S(1)} %collective-permute-done.14.s1), channel_id=1, source_target_pairs={{0,1},{1,0},{2,3},{3,2},{4,5},{5,4},{6,7},{7,6},{8,9},{9,8},{10,11... | collective-permute-start | bytes 737288 | tf_op jit(solution)/shard_map/ppermute | solution.py:68
  30.1 4.9 %collective-permute-start.10 = (bf16[4,48,480]{2,1,0:T(8,128)(2,1)S(1)}, bf16[4,48,480]{2,1,0:T(8,128)(2,1)S(1)}, u32[]{:S(2)}, u32[]{:S(2)}) collective-permute-start(bf16[4,48,480]{2,1,0:T(8,128)(2,1)S(1)} %shard_map.86.s0), channel_id=1, source_target_pairs={{0,1},{1,0},{2,3},{3,2},{4,5},{5,4},{6,7},{7,6},{8,9},{9,8},{10,11... | collective-permute-start | bytes 552968 | tf_op jit(solution)/shard_map/ppermute | solution.py:68
  37.6 5.8 %collective-permute-start.19 = (bf16[24,640]{1,0:T(8,128)(2,1)S(1)}, bf16[24,640]{1,0:T(8,128)(2,1)S(1)}, u32[]{:S(2)}, u32[]{:S(2)}) collective-permute-start(bf16[24,640]{1,0:T(8,128)(2,1)S(1)} %shard_map.91.refs_0_), channel_id=1, source_target_pairs={{0,12},{1,13},{2,14},{3,15},{4,8},{5,9},{6,10},{7,11},{8,4},{9,5},... | collective-permute-start | bytes 92168 | tf_op jit(solution)/shard_map/ppermute | solution.py:68
  39.6 4.9 %collective-permute-start.18 = (bf16[24,640]{1,0:T(8,128)(2,1)S(1)}, bf16[24,640]{1,0:T(8,128)(2,1)S(1)}, u32[]{:S(2)}, u32[]{:S(2)}) collective-permute-start(bf16[24,640]{1,0:T(8,128)(2,1)S(1)} %shard_map.91.refs_0_), channel_id=1, source_target_pairs={{0,8},{1,9},{2,10},{3,11},{4,12},{5,13},{6,14},{7,15},{8,0},{9,1},... | collective-permute-start | bytes 92168 | tf_op jit(solution)/shard_map/ppermute | solution.py:68
  40.1 4.4 %collective-permute-start.17 = (bf16[24,640]{1,0:T(8,128)(2,1)S(1)}, bf16[24,640]{1,0:T(8,128)(2,1)S(1)}, u32[]{:S(2)}, u32[]{:S(2)}) collective-permute-start(bf16[24,640]{1,0:T(8,128)(2,1)S(1)} %shard_map.91.refs_0_), channel_id=1, source_target_pairs={{0,4},{1,5},{2,6},{3,7},{4,0},{5,1},{6,2},{7,3},{8,12},{9,13},{10,... | collective-permute-start | bytes 92168 | tf_op jit(solution)/shard_map/ppermute | solution.py:68
  44.4 4.9 %collective-permute-start.20 = (bf16[4,24,640]{2,1,0:T(8,128)(2,1)S(1)}, bf16[4,24,640]{2,1,0:T(8,128)(2,1)S(1)}, u32[]{:S(2)}, u32[]{:S(2)}) collective-permute-start(bf16[4,24,640]{2,1,0:T(8,128)(2,1)S(1)} %shard_map.92.s0), channel_id=1, source_target_pairs={{0,2},{1,3},{2,0},{3,1},{4,6},{5,7},{6,4},{7,5},{8,10},{9,11},{10,... | collective-permute-start | bytes 368648 | tf_op jit(solution)/shard_map/ppermute | solution.py:68
  45.7 4.2 %collective-permute-start.21 = (bf16[4,24,640]{2,1,0:T(8,128)(2,1)S(1)}, bf16[4,24,640]{2,1,0:T(8,128)(2,1)S(1)}, u32[]{:S(2)}, u32[]{:S(2)}) collective-permute-start(bf16[4,24,640]{2,1,0:T(8,128)(2,1)S(1)} %shard_map.92.s0), channel_id=1, source_target_pairs={{0,1},{1,0},{2,3},{3,2},{4,5},{5,4},{6,7},{7,6},{8,9},{9,8},{10,11... | collective-permute-start | bytes 368648 | tf_op jit(solution)/shard_map/ppermute | solution.py:68
  58.2 5.1 %collective-permute-start.24 = (bf16[24,1280]{1,0:T(8,128)(2,1)S(1)}, bf16[24,1280]{1,0:T(8,128)(2,1)S(1)}, u32[]{:S(2)}, u32[]{:S(2)}) collective-permute-start(bf16[24,1280]{1,0:T(8,128)(2,1)S(1)} %get-tuple-element.66), channel_id=1, source_target_pairs={{1,3},{3,1},{5,7},{7,5},{9,11},{11,9},{13,15},{15,13},{17,19},{19,... | collective-permute-start | bytes 184328 | tf_op jit(solution)/shard_map/ppermute | solution.py:285
  58.9 6.1 %collective-permute-start.25 = (bf16[24,1280]{1,0:T(8,128)(2,1)S(1)}, bf16[24,1280]{1,0:T(8,128)(2,1)S(1)}, u32[]{:S(2)}, u32[]{:S(2)}) collective-permute-start(bf16[24,1280]{1,0:T(8,128)(2,1)S(1)} %get-tuple-element.67), channel_id=1, source_target_pairs={{0,12},{1,15},{2,14},{3,13},{4,8},{5,11},{6,10},{7,9},{8,4},{9,7},... | collective-permute-start | bytes 184328 | tf_op jit(solution)/shard_map/ppermute | solution.py:285
  60.9 7.8 %collective-permute-start.26 = (bf16[24,1280]{1,0:T(8,128)(2,1)S(1)}, bf16[24,1280]{1,0:T(8,128)(2,1)S(1)}, u32[]{:S(2)}, u32[]{:S(2)}) collective-permute-start(bf16[24,1280]{1,0:T(8,128)(2,1)S(1)} %get-tuple-element.68), channel_id=1, source_target_pairs={{0,8},{1,11},{2,10},{3,9},{4,12},{5,15},{6,14},{7,13},{8,0},{9,3},... | collective-permute-start | bytes 184328 | tf_op jit(solution)/shard_map/ppermute | solution.py:285
  61.7 6.9 %collective-permute-start.27 = (bf16[24,1280]{1,0:T(8,128)(2,1)S(1)}, bf16[24,1280]{1,0:T(8,128)(2,1)S(1)}, u32[]{:S(2)}, u32[]{:S(2)}) collective-permute-start(bf16[24,1280]{1,0:T(8,128)(2,1)S(1)} %get-tuple-element.69), channel_id=1, source_target_pairs={{0,4},{1,7},{2,6},{3,5},{4,0},{5,3},{6,2},{7,1},{8,12},{9,15},{10,... | collective-permute-start | bytes 184328 | tf_op jit(solution)/shard_map/ppermute | solution.py:285
  (5 other events, 8.6 us)

commit v7 on v6

--- a/solution.py
+++ b/solution.py
@@ -9,6 +9,7 @@
 
 HEAD_DIM = 128
 HEADS = 20
+QKV_CUT, UP_CUT, DOWN_CUT = 2560, 2560, 2560
 
 
 def layer_norm(values):
@@ -38,30 +39,40 @@
     )(*operands)
 
 
-def load(*arrays):
-    parts = []
-    for i, array in enumerate(arrays):
-        rows = array.shape[0]
-        if array.size < 1 << 20:
-            parts.append((i, None))
-        else:
-            cuts = [rows * k // 4 // 16 * 16 for k in range(4)] + [rows]
-            parts += [(i, pl.ds(lo, hi - lo)) for lo, hi in zip(cuts, cuts[1:])]
+def load(*parts):
+    parts = [part if isinstance(part, tuple) else (part, None, None, False) for part in parts]
+    arrays = [pltpu.with_memory_space_constraint(array, pltpu.HBM) for array, *_ in parts]
+    outs, buffers, pieces = [], [], []
+    for i, (array, lo, hi, turn) in enumerate(parts):
+        if lo is None:
+            outs.append((array.shape, array.dtype))
+            pieces.append((i, None, None, None))
+            continue
+        shape = (array.shape[0], hi - lo)
+        outs.append((shape[::-1] if turn else shape, array.dtype))
+        if turn:
+            buffers.append(pltpu.VMEM(shape, array.dtype))
+        size = min(640, hi - lo)
+        for start in range(0, hi - lo, size):
+            pieces.append((i, pl.ds(lo + start, size), pl.ds(start, size), len(buffers) - 1 if turn else None))
 
     def body(*refs):
-        sources, targets, sems = refs[: len(arrays)], refs[len(arrays) : -1], refs[-1]
+        sources, targets = refs[: len(arrays)], refs[len(arrays) : 2 * len(arrays)]
+        sems, *held = refs[2 * len(arrays) :]
         copies = []
-        for n, (i, cut) in enumerate(parts):
-            source, target = (sources[i], targets[i]) if cut is None else (sources[i].at[cut], targets[i].at[cut])
+        for n, (i, cut, into, buffer) in enumerate(pieces):
+            target = targets[i] if buffer is None else held[buffer]
+            source = sources[i] if cut is None else sources[i].at[:, cut]
+            target = target if cut is None else target.at[:, into]
             copies.append(pltpu.make_async_copy(source, target, sems.at[n]))
         for copy in copies:
             copy.start()
-        for copy in copies:
+        for copy, (i, _, into, buffer) in zip(copies, pieces):
             copy.wait()
-
-    outs = [(array.shape, array.dtype) for array in arrays]
-    arrays = [pltpu.with_memory_space_constraint(array, pltpu.HBM) for array in arrays]
-    return call(body, outs, *arrays, spec=HBM, scratch=[pltpu.SemaphoreType.DMA((len(parts),))])
+            if buffer is not None:
+                targets[i][into, :] = held[buffer][:, into].T
+
+    return call(body, outs, *arrays, spec=HBM, scratch=[pltpu.SemaphoreType.DMA((len(pieces),)), *buffers])
 
 
 def swap(values, offset):
@@ -76,20 +87,18 @@
     return call(body, [((len(pieces), *pieces[0].shape), pieces[0].dtype)], *pieces)[0]
 
 
-def load_beside(weights, before, beside):
-    weights, _ = lax.optimization_barrier((weights, before))
-    return lax.optimization_barrier((load(weights)[0], beside))
-
-
-def gather(block, load_z=None, load_y=None):
+def load_beside(parts, before, beside):
+    arrays, _ = lax.optimization_barrier(([array for array, *_ in parts], before))
+    return lax.optimization_barrier((load(*[(array, *part[1:]) for array, part in zip(arrays, parts)]), beside))
+
+
+def gather(block, load_z, load_y):
     pieces = tuple(swap(block, 4 * z) for z in (1, 2, 3))
-    if load_z is not None:
-        load_z, pieces = load_beside(load_z, block, pieces)
+    loaded_z, pieces = load_beside(load_z, block, pieces)
     planes = stack([block, *pieces])
     across = swap(planes, 2)
-    if load_y is not None:
-        load_y, across = load_beside(load_y, planes, across)
-    return [planes, across, swap(planes, 1), swap(across, 1)], load_z, load_y
+    loaded_y, across = load_beside(load_y, planes, across)
+    return [planes, across, swap(planes, 1), swap(across, 1)], loaded_z + loaded_y
 
 
 def pack_tokens(own, got1, got2, got3, out, rows):
@@ -119,7 +128,16 @@
     return (layer_norm(values) * (1.0 + gain) + shift).astype(jnp.bfloat16)
 
 
-def project_qkv(s0, s1, s2, s3, mod, weights, tokens_out, qkv_out, flat):
+def matmul(values, *weights):
+    total, row = None, 0
+    for part in weights:
+        rows = part.shape[0]
+        product = jnp.dot(values[:, row : row + rows], part[...], preferred_element_type=jnp.float32)
+        total, row = product if total is None else total + product, row + rows
+    return total
+
+
+def project_qkv(s0, s1, s2, s3, mod, weights1, weights2, tokens_out, qkv_out, flat):
     for slot, ref in enumerate((s0, s2, s1, s3)):
         for half in range(2):
             piece = ref[12 * half : 12 * half + 12, :].astype(jnp.float32)
@@ -127,7 +145,7 @@
     tokens = flat[...]
     tokens_out[...] = tokens.astype(jnp.bfloat16)
     normed = normalize(tokens, mod[0:1, :], mod[1:2, :])
-    qkv = lax.dot_general(normed, weights[...], NT, preferred_element_type=jnp.float32).astype(jnp.bfloat16)
+    qkv = matmul(normed, weights1, weights2).astype(jnp.bfloat16)
     qkv_out[...] = jnp.dot(order(1), qkv, preferred_element_type=jnp.float32).astype(jnp.bfloat16)
 
 
@@ -174,7 +192,7 @@
     out[...] = jnp.concatenate([projected[:24], projected[24:]], axis=1).astype(jnp.bfloat16)
 
 
-def feed_forward(s0, s1, s2, s3, tokens, mod, w_up, w_down, keep, send, residual_out, slots):
+def feed_forward(s0, s1, s2, s3, tokens, mod, w_up1, w_up2, w_down1, w_down2, keep, send, residual_out, slots):
     place((s0, s1, s2, s3), slots)
     pieces = [slots[j] for j in range(16)]
     upper = jnp.concatenate([piece[:, :320] for piece in pieces], axis=1)
@@ -184,12 +202,14 @@
     residual = tokens[...].astype(jnp.float32) + mod[2:3, :] * projected
     residual_out[...] = residual[0:3]
     normed = normalize(residual, mod[3:4, :], mod[4:5, :])
-    hidden = lax.dot_general(normed, w_up[...], NT, preferred_element_type=jnp.float32)
+    hidden = matmul(normed, w_up1, w_up2)
     hidden = jax.nn.gelu(hidden, approximate=True).astype(jnp.bfloat16)
-    partial = jnp.dot(hidden, w_down[...], preferred_element_type=jnp.float32)
     first = lax.axis_index("seq") & 1 == 0
-    keep[...] = jnp.where(first, partial[:24], partial[24:])
-    send[...] = jnp.where(first, partial[24:], partial[:24]).astype(jnp.bfloat16)
+    middle = w_down1.shape[1]
+    for cols, weights in ((slice(0, middle), w_down1), (slice(middle, None), w_down2)):
+        partial = jnp.dot(hidden, weights[...], preferred_element_type=jnp.float32)
+        keep[:, cols] = jnp.where(first, partial[:24], partial[24:])
+        send[:, cols] = jnp.where(first, partial[24:], partial[:24]).astype(jnp.bfloat16)
 
 
 def add_cores(keep, got, own_out, send0, send1, send2, send3):
@@ -224,10 +244,13 @@
     cache_kv = cache_kv.transpose(0, 2, 1, 3)
     pieces = tuple(swap(tokens, 4 * z) for z in (1, 2, 3))
     cache_far = swap(cache_kv, 8)
-    tokens, modulation, norm_gains, cache_kv, w_qkv = load(tokens, modulation, norm_gains, cache_kv, w_qkv)
+    tokens, modulation, norm_gains, cache_kv, w_qkv1 = load(
+        tokens, modulation, norm_gains, cache_kv, (w_qkv, 0, QKV_CUT, True)
+    )
     pieces, tokens = lax.optimization_barrier((pieces, tokens))
     planes = call(pack_tokens, [((24, 2560), bf16)], tokens, *pieces, scratch=[pltpu.VMEM((24, 2560), f32)])[0]
     across = swap(planes, 2)
+    (w_qkv2,), across = load_beside([(w_qkv, QKV_CUT, 5120, True)], planes, across)
     pair = stack([cache_kv, cache_far])
     cache_planes = stack([pair, swap(pair, 4)]).reshape(4, *cache_kv.shape)
     cache_across = swap(cache_planes, 2)
@@ -239,10 +262,14 @@
         swap(planes, 1),
         swap(across, 1),
         modulation,
-        w_qkv,
+        w_qkv1,
+        w_qkv2,
         scratch=[pltpu.VMEM((48, 5120), f32)],
     )
-    qkv_stacks, w_out, w_up = gather(qkv, w_out.T, w_up.T)
+    w_up, w_out = w_up.T, w_out.T
+    qkv_stacks, (w_up1, w_up2, w_out) = gather(
+        qkv, [(w_up, 0, UP_CUT, True)], [(w_up, UP_CUT, 5120, True), (w_out, 0, 2560, False)]
+    )
     old_keys, old_values = call(
         line_up,
         [((96, 2560), bf16)] * 2,
@@ -267,15 +294,19 @@
             pltpu.VMEM((48, 2560), bf16),
         ],
     )[0]
-    projected_stacks, _, w_down = gather(projected, None, w_down)
+    projected_stacks, (w_down1, w_down2) = gather(
+        projected, [(w_down, 0, DOWN_CUT, False)], [(w_down, DOWN_CUT, 5120, False)]
+    )
     keep, send, residual = call(
         feed_forward,
         [((24, 5120), f32), ((24, 5120), bf16), ((3, 5120), f32)],
         *projected_stacks,
         near_tokens,
         modulation,
-        w_up,
-        w_down,
+        w_up1,
+        w_up2,
+        w_down1,
+        w_down2,
         scratch=[pltpu.VMEM((16, 24, 640), bf16)],
     )
     own, *sends = call(add_cores, [((6, 5120), f32)] + [((24, 1280), bf16)] * 4, keep, swap(send, 1))

time: 71.3 us -> 69.2 us (0.971)
  waiting for transfers between devices: 19.2 us -> 17.1 us
  starting transfers between devices: 29.5 us -> 28.4 us
  Pallas kernels: 22.3 us -> 23.4 us
    ppermute x25, waiting for transfers between devices: 13.8 us -> 11.8 us  [swap(): return lax.ppermute(values, 'seq', [(i, i ^ offset) for i in range(16)])]
    pallas_call x16 -> x18, Pallas kernels: 22.3 us -> 23.4 us  [call(): pl.pallas_call(body, out_shape=[jax.ShapeDtypeStruct(shape, dtype) for sh...]
    ppermute x25, starting transfers between devices: 24.4 us -> 23.3 us  [swap(): return lax.ppermute(values, 'seq', [(i, i ^ offset) for i in range(16)])]
  transfers between devices with their start and end apart: 29 -> 29, of which waited for: 15 -> 13; matrix products, arithmetic and copies ran while one was open for 0% -> 0% of each run, Pallas kernels for 20% -> 24%
where the time goes in v7:
time: 69.2 us; the launch traced here: 69.1 us
  starting transfers between devices  28.4 us (41%)
  Pallas kernels  23.4 us (34%)
  waiting for transfers between devices  17.1 us (25%)
    pallas_call x18, Pallas kernels, call(): pl.pallas_call(body, out_shape=[jax.ShapeDtypeStruct(shape, dtype) for sh...  23.4 us
    ppermute x25, starting transfers between devices, swap(): return lax.ppermute(values, 'seq', [(i, i ^ offset) for i in range(16)])  23.3 us
    ppermute x25, waiting for transfers between devices, swap(): return lax.ppermute(values, 'seq', [(i, i ^ offset) for i in range(16)])  11.8 us
    ppermute x4, waiting for transfers between devices, staged(): got.append(lax.ppermute(send, 'seq', [(i, j) for i, j in pairs if i != j]))  5.31 us
    ppermute x4, starting transfers between devices, staged(): got.append(lax.ppermute(send, 'seq', [(i, j) for i, j in pairs if i != j]))  5.12 us
  transfers between devices with their start and end apart: 29, of which 13 were waited for; matrix products, arithmetic and copies ran while one was open for 0% of the time, Pallas kernels for 24%

profile of v7, /device:TPU:0, one launch (start us, length us, event | category | flops | bytes accessed | tf_op | source)
XLA Modules:
  0.0 69.1 jit_solution(11170104124613483867)
XLA Ops:
  0.0 4.0 %collective-permute-start.1 = (bf16[3,5120]{1,0:T(4,128)(2,1)}, bf16[3,5120]{1,0:T(4,128)(2,1)S(1)}, u32[]{:S(2)}, u32[]{:S(2)}) collective-permute-start(bf16[3,5120]{1,0:T(4,128)(2,1)} %refs_0_.1), channel_id=1, source_target_pairs={{0,8},{1,9},{2,10},{3,11},{4,12},{5,13},{6,14},{7,15},{8,0},{9,1},... | collective-permute-start | bytes 92168 | tf_op jit(solution)/shard_map/ppermute | solution.py:79
  4.0 1.6 %collective-permute-start = (bf16[3,5120]{1,0:T(4,128)(2,1)}, bf16[3,5120]{1,0:T(4,128)(2,1)S(1)}, u32[]{:S(2)}, u32[]{:S(2)}) collective-permute-start(bf16[3,5120]{1,0:T(4,128)(2,1)} %refs_0_.1), channel_id=1, source_target_pairs={{0,4},{1,5},{2,6},{3,7},{4,0},{5,1},{6,2},{7,3},{8,12},{9,13},{10,... | collective-permute-start | bytes 92168 | tf_op jit(solution)/shard_map/ppermute | solution.py:79
  5.6 1.9 %collective-permute-start.12 = (bf16[2,3,2,2560]{3,2,1,0:T(2,128)(2,1)}, bf16[2,3,2,2560]{3,2,1,0:T(2,128)(2,1)S(1)}, u32[]{:S(2)}, u32[]{:S(2)}) collective-permute-start(bf16[2,3,2,2560]{3,2,1,0:T(2,128)(2,1)} %bitcast.15), channel_id=1, source_target_pairs={{0,8},{1,9},{2,10},{3,11},{4,12},{5,13},{6,14},{7,15},{8,0},{9,1},... | collective-permute-start | bytes 184328 | tf_op jit(solution)/shard_map/ppermute | solution.py:79
  7.5 2.2 %shard_map.82 = (bf16[3,5120]{1,0:T(4,128)(2,1)S(1)}, f32[6,5120]{1,0:T(8,128)S(1)}, f32[2,2560]{1,0:T(2,128)S(1)}, bf16[2,3,2,2560]{3,2,1,0:T(2,128)(2,1)S(1)}, bf16[2560,480]{1,0:T(8,128)(2,1)S(1)}) custom-call(bf16[3,5120]{1,0:T(4,128)(2,1)} %refs_0_.1, f32[6,5120]{1,0:T(8,128)} %refs_1_.1, f32[2,2560]{1,0:T(2,128)} %refs_2_.1, ...), custom_call_target="tpu_custom_call" | custom-call | tf_op jit(solution)/shard_map/pallas_call | solution.py:31
  9.8 2.0 %collective-permute-done.2.got3 = bf16[3,5120]{1,0:T(4,128)(2,1)S(1)} collective-permute-done((bf16[3,5120]{1,0:T(4,128)(2,1)}, bf16[3,5120]{1,0:T(4,128)(2,1)S(1)}, u32[]{:S(2)}, u32[]{:S(2)}) %collective-permute-start.2) | collective-permute-done | bytes 30752 | tf_op jit(solution)/shard_map/ppermute | solution.py:79
  11.8 1.6 %collective-permute-start.3 = (bf16[24,2560]{1,0:T(8,128)(2,1)S(1)}, bf16[24,2560]{1,0:T(8,128)(2,1)S(1)}, u32[]{:S(2)}, u32[]{:S(2)}) collective-permute-start(bf16[24,2560]{1,0:T(8,128)(2,1)S(1)} %shard_map.83.s0), channel_id=1, source_target_pairs={{0,2},{1,3},{2,0},{3,1},{4,6},{5,7},{6,4},{7,5},{8,10},{9,11},{10,... | collective-permute-start | bytes 368648 | tf_op jit(solution)/shard_map/ppermute | solution.py:79
  14.0 2.0 %shard_map.84.weights2 = bf16[2560,480]{1,0:T(8,128)(2,1)S(1)} custom-call(bf16[480,5120]{1,0:T(8,128)(2,1)} %bitcast.13), custom_call_target="tpu_custom_call" | custom-call | tf_op jit(solution)/shard_map/pallas_call | solution.py:31
  16.7 1.6 %collective-permute-done.13.refs_1_ = bf16[2,2,3,2,2560]{4,3,2,1,0:T(2,128)(2,1)S(1)} collective-permute-done((bf16[2,2,3,2,2560]{4,3,2,1,0:T(2,128)(2,1)S(1)}, bf16[2,2,3,2,2560]{4,3,2,1,0:T(2,128)(2,1)S(1)}, u32[]{:S(2)}, u32[]{:S(2)}) %collective-permute-start.13) | collective-permute-done | bytes 122912 | tf_op jit(solution)/shard_map/ppermute | solution.py:79
  19.1 1.5 %shard_map.85 = (bf16[48,5120]{1,0:T(8,128)(2,1)S(1)}, bf16[48,480]{1,0:T(8,128)(2,1)S(1)}) custom-call(bf16[24,2560]{1,0:T(8,128)(2,1)S(1)} %shard_map.83.s0, bf16[24,2560]{1,0:T(8,128)(2,1)S(1)} %collective-permute-done.3.s1, bf16[24,2560]{1,0:T(8,128)(2,1)S(1)} %collective-permute-done.4.s2, bf16[24,2560]{1,0:T(8,128)(2,1)S(1)} %collective-permute-done.5.s3, ...), custom_call_target="tpu_custom_call" | custom-call | tf_op jit(solution)/shard_map/pallas_call | solution.py:31
  20.6 2.3 %collective-permute-start.8 = (bf16[48,480]{1,0:T(8,128)(2,1)S(1)}, bf16[48,480]{1,0:T(8,128)(2,1)S(1)}, u32[]{:S(2)}, u32[]{:S(2)}) collective-permute-start(bf16[48,480]{1,0:T(8,128)(2,1)S(1)} %get-tuple-element.61.refs_0_), channel_id=1, source_target_pairs={{0,12},{1,13},{2,14},{3,15},{4,8},{5,9},{6,10},{7,11},{8,4},{9,5},... | collective-permute-start | bytes 138248 | tf_op jit(solution)/shard_map/ppermute | solution.py:79
  22.9 2.2 %collective-permute-start.6 = (bf16[48,480]{1,0:T(8,128)(2,1)S(1)}, bf16[48,480]{1,0:T(8,128)(2,1)S(1)}, u32[]{:S(2)}, u32[]{:S(2)}) collective-permute-start(bf16[48,480]{1,0:T(8,128)(2,1)S(1)} %get-tuple-element.61.refs_0_), channel_id=1, source_target_pairs={{0,4},{1,5},{2,6},{3,7},{4,0},{5,1},{6,2},{7,3},{8,12},{9,13},{10,... | collective-permute-start | bytes 138248 | tf_op jit(solution)/shard_map/ppermute | solution.py:79
  25.1 2.7 %shard_map.86.w_up1 = bf16[2560,864]{1,0:T(8,128)(2,1)S(1)} custom-call(bf16[864,5120]{1,0:T(8,128)(2,1)} %bitcast.10), custom_call_target="tpu_custom_call" | custom-call | tf_op jit(solution)/shard_map/pallas_call | solution.py:31
  29.8 2.8 %shard_map.88 = (bf16[2560,864]{1,0:T(8,128)(2,1)S(1)}, bf16[320,2560]{1,0:T(8,128)(2,1)S(1)}) custom-call(bf16[864,5120]{1,0:T(8,128)(2,1)} %bitcast.11, bf16[320,2560]{1,0:T(8,128)(2,1)} %bitcast.14), custom_call_target="tpu_custom_call" | custom-call | tf_op jit(solution)/shard_map/pallas_call | solution.py:31
  35.4 1.8 %shard_map.92.refs_0_ = bf16[24,640]{1,0:T(8,128)(2,1)S(1)} custom-call(bf16[4,48,480]{2,1,0:T(8,128)(2,1)S(1)} %shard_map.87.s0, bf16[4,48,480]{2,1,0:T(8,128)(2,1)S(1)} %collective-permute-done.9.s1, bf16[4,48,480]{2,1,0:T(8,128)(2,1)S(1)} %collective-permute-done.10.s2, bf16[4,48,480]{2,1,0:T(8,128)(2,1)S(1)} %collective-permute-done.11.s3, ...), custom_call_target="tpu_custom_call" | custom-call | tf_op jit(solution)/shard_map/pallas_call | solution.py:31
  37.2 2.0 %collective-permute-start.19 = (bf16[24,640]{1,0:T(8,128)(2,1)S(1)}, bf16[24,640]{1,0:T(8,128)(2,1)S(1)}, u32[]{:S(2)}, u32[]{:S(2)}) collective-permute-start(bf16[24,640]{1,0:T(8,128)(2,1)S(1)} %shard_map.92.refs_0_), channel_id=1, source_target_pairs={{0,12},{1,13},{2,14},{3,15},{4,8},{5,9},{6,10},{7,11},{8,4},{9,5},... | collective-permute-start | bytes 92168 | tf_op jit(solution)/shard_map/ppermute | solution.py:79
  39.6 1.9 %collective-permute-start.17 = (bf16[24,640]{1,0:T(8,128)(2,1)S(1)}, bf16[24,640]{1,0:T(8,128)(2,1)S(1)}, u32[]{:S(2)}, u32[]{:S(2)}) collective-permute-start(bf16[24,640]{1,0:T(8,128)(2,1)S(1)} %shard_map.92.refs_0_), channel_id=1, source_target_pairs={{0,4},{1,5},{2,6},{3,7},{4,0},{5,1},{6,2},{7,3},{8,12},{9,13},{10,... | collective-permute-start | bytes 92168 | tf_op jit(solution)/shard_map/ppermute | solution.py:79
  41.6 2.3 %shard_map.93.w_down1 = bf16[864,2560]{1,0:T(8,128)(2,1)S(1)} custom-call(bf16[864,5120]{1,0:T(8,128)(2,1)} %refs_0_.3), custom_call_target="tpu_custom_call" | custom-call | tf_op jit(solution)/shard_map/pallas_call | solution.py:31
  45.2 2.3 %shard_map.95.w_down2 = bf16[864,2560]{1,0:T(8,128)(2,1)S(1)} custom-call(bf16[864,5120]{1,0:T(8,128)(2,1)} %refs_0_.3), custom_call_target="tpu_custom_call" | custom-call | tf_op jit(solution)/shard_map/pallas_call | solution.py:31
  47.5 1.5 %collective-permute-done.20.s1 = bf16[4,24,640]{2,1,0:T(8,128)(2,1)S(1)} collective-permute-done((bf16[4,24,640]{2,1,0:T(8,128)(2,1)S(1)}, bf16[4,24,640]{2,1,0:T(8,128)(2,1)S(1)}, u32[]{:S(2)}, u32[]{:S(2)}) %collective-permute-start.20) | collective-permute-done | bytes 122912 | tf_op jit(solution)/shard_map/ppermute | solution.py:79
  50.3 4.1 %shard_map.96 = (f32[24,5120]{1,0:T(8,128)S(1)}, bf16[24,5120]{1,0:T(8,128)(2,1)S(1)}, f32[3,5120]{1,0:T(4,128)S(1)}) custom-call(bf16[4,24,640]{2,1,0:T(8,128)(2,1)S(1)} %shard_map.94.s0, bf16[4,24,640]{2,1,0:T(8,128)(2,1)S(1)} %collective-permute-done.20.s1, bf16[4,24,640]{2,1,0:T(8,128)(2,1)S(1)} %collective-permute-done.21.s2, ...), custom_call_target="tpu_custom_call" | custom-call | tf_op jit(solution)/shard_map/pallas_call | solution.py:31
  56.9 2.1 %collective-permute-start.25 = (bf16[24,1280]{1,0:T(8,128)(2,1)S(1)}, bf16[24,1280]{1,0:T(8,128)(2,1)S(1)}, u32[]{:S(2)}, u32[]{:S(2)}) collective-permute-start(bf16[24,1280]{1,0:T(8,128)(2,1)S(1)} %get-tuple-element.91), channel_id=1, source_target_pairs={{0,12},{1,15},{2,14},{3,13},{4,8},{5,11},{6,10},{7,9},{8,4},{9,7},... | collective-permute-start | bytes 184328 | tf_op jit(solution)/shard_map/ppermute | solution.py:316
  59.9 1.5 %collective-permute-start.27 = (bf16[24,1280]{1,0:T(8,128)(2,1)S(1)}, bf16[24,1280]{1,0:T(8,128)(2,1)S(1)}, u32[]{:S(2)}, u32[]{:S(2)}) collective-permute-start(bf16[24,1280]{1,0:T(8,128)(2,1)S(1)} %get-tuple-element.93), channel_id=1, source_target_pairs={{0,4},{1,7},{2,6},{3,5},{4,0},{5,3},{6,2},{7,1},{8,12},{9,15},{10,... | collective-permute-start | bytes 184328 | tf_op jit(solution)/shard_map/ppermute | solution.py:316
  61.4 1.6 %collective-permute-done.25.got1 = bf16[24,1280]{1,0:T(8,128)(2,1)S(1)} collective-permute-done((bf16[24,1280]{1,0:T(8,128)(2,1)S(1)}, bf16[24,1280]{1,0:T(8,128)(2,1)S(1)}, u32[]{:S(2)}, u32[]{:S(2)}) %collective-permute-start.25) | collective-permute-done | bytes 61472 | tf_op jit(solution)/shard_map/ppermute | solution.py:316
  63.0 3.7 %collective-permute-done.26.got2 = bf16[24,1280]{1,0:T(8,128)(2,1)S(1)} collective-permute-done((bf16[24,1280]{1,0:T(8,128)(2,1)S(1)}, bf16[24,1280]{1,0:T(8,128)(2,1)S(1)}, u32[]{:S(2)}, u32[]{:S(2)}) %collective-permute-start.26) | collective-permute-done | bytes 61472 | tf_op jit(solution)/shard_map/ppermute | solution.py:316
  (52 shorter events, 15.7 us)
Async XLA Ops:
  0.0 9.7 %collective-permute-start.1 = (bf16[3,5120]{1,0:T(4,128)(2,1)}, bf16[3,5120]{1,0:T(4,128)(2,1)S(1)}, u32[]{:S(2)}, u32[]{:S(2)}) collective-permute-start(bf16[3,5120]{1,0:T(4,128)(2,1)} %refs_0_.1), channel_id=1, source_target_pairs={{0,8},{1,9},{2,10},{3,11},{4,12},{5,13},{6,14},{7,15},{8,0},{9,1},... | collective-permute-start | bytes 92168 | tf_op jit(solution)/shard_map/ppermute | solution.py:79
  4.0 5.7 %collective-permute-start = (bf16[3,5120]{1,0:T(4,128)(2,1)}, bf16[3,5120]{1,0:T(4,128)(2,1)S(1)}, u32[]{:S(2)}, u32[]{:S(2)}) collective-permute-start(bf16[3,5120]{1,0:T(4,128)(2,1)} %refs_0_.1), channel_id=1, source_target_pairs={{0,4},{1,5},{2,6},{3,7},{4,0},{5,1},{6,2},{7,3},{8,12},{9,13},{10,... | collective-permute-start | bytes 92168 | tf_op jit(solution)/shard_map/ppermute | solution.py:79
  5.6 6.1 %collective-permute-start.2 = (bf16[3,5120]{1,0:T(4,128)(2,1)}, bf16[3,5120]{1,0:T(4,128)(2,1)S(1)}, u32[]{:S(2)}, u32[]{:S(2)}) collective-permute-start(bf16[3,5120]{1,0:T(4,128)(2,1)} %refs_0_.1), channel_id=1, source_target_pairs={{0,12},{1,13},{2,14},{3,15},{4,8},{5,9},{6,10},{7,11},{8,4},{9,5},... | collective-permute-start | bytes 92168 | tf_op jit(solution)/shard_map/ppermute | solution.py:79
  5.6 7.8 %collective-permute-start.12 = (bf16[2,3,2,2560]{3,2,1,0:T(2,128)(2,1)}, bf16[2,3,2,2560]{3,2,1,0:T(2,128)(2,1)S(1)}, u32[]{:S(2)}, u32[]{:S(2)}) collective-permute-start(bf16[2,3,2,2560]{3,2,1,0:T(2,128)(2,1)} %bitcast.15), channel_id=1, source_target_pairs={{0,8},{1,9},{2,10},{3,11},{4,12},{5,13},{6,14},{7,15},{8,0},{9,1},... | collective-permute-start | bytes 184328 | tf_op jit(solution)/shard_map/ppermute | solution.py:79
  11.8 4.9 %collective-permute-start.3 = (bf16[24,2560]{1,0:T(8,128)(2,1)S(1)}, bf16[24,2560]{1,0:T(8,128)(2,1)S(1)}, u32[]{:S(2)}, u32[]{:S(2)}) collective-permute-start(bf16[24,2560]{1,0:T(8,128)(2,1)S(1)} %shard_map.83.s0), channel_id=1, source_target_pairs={{0,2},{1,3},{2,0},{3,1},{4,6},{5,7},{6,4},{7,5},{8,10},{9,11},{10,... | collective-permute-start | bytes 368648 | tf_op jit(solution)/shard_map/ppermute | solution.py:79
  13.4 4.9 %collective-permute-start.13 = (bf16[2,2,3,2,2560]{4,3,2,1,0:T(2,128)(2,1)S(1)}, bf16[2,2,3,2,2560]{4,3,2,1,0:T(2,128)(2,1)S(1)}, u32[]{:S(2)}, u32[]{:S(2)}) collective-permute-start(bf16[2,2,3,2,2560]{4,3,2,1,0:T(2,128)(2,1)S(1)} %shard_map.89.refs_0_), channel_id=1, source_target_pairs={{0,4},{1,5},{2,6},{3,7},{4,0},{5,1},{6,2},{7,3},{8,12},{9,13},{10,... | collective-permute-start | bytes 368648 | tf_op jit(solution)/shard_map/ppermute | solution.py:79
  14.0 5.2 %collective-permute-start.4 = (bf16[24,2560]{1,0:T(8,128)(2,1)S(1)}, bf16[24,2560]{1,0:T(8,128)(2,1)S(1)}, u32[]{:S(2)}, u32[]{:S(2)}) collective-permute-start(bf16[24,2560]{1,0:T(8,128)(2,1)S(1)} %shard_map.83.s0), channel_id=1, source_target_pairs={{0,1},{1,0},{2,3},{3,2},{4,5},{5,4},{6,7},{7,6},{8,9},{9,8},{10,11... | collective-permute-start | bytes 368648 | tf_op jit(solution)/shard_map/ppermute | solution.py:79
  18.4 10.9 %collective-permute-start.14 = (bf16[4,2,3,2,2560]{4,3,2,1,0:T(2,128)(2,1)S(1)}, bf16[4,2,3,2,2560]{4,3,2,1,0:T(2,128)(2,1)S(1)}, u32[]{:S(2)}, u32[]{:S(2)}) collective-permute-start(bf16[4,2,3,2,2560]{4,3,2,1,0:T(2,128)(2,1)S(1)} %bitcast.7), channel_id=1, source_target_pairs={{0,2},{1,3},{2,0},{3,1},{4,6},{5,7},{6,4},{7,5},{8,10},{9,11},{10,... | collective-permute-start | bytes 737288 | tf_op jit(solution)/shard_map/ppermute | solution.py:79
  20.6 7.2 %collective-permute-start.8 = (bf16[48,480]{1,0:T(8,128)(2,1)S(1)}, bf16[48,480]{1,0:T(8,128)(2,1)S(1)}, u32[]{:S(2)}, u32[]{:S(2)}) collective-permute-start(bf16[48,480]{1,0:T(8,128)(2,1)S(1)} %get-tuple-element.61.refs_0_), channel_id=1, source_target_pairs={{0,12},{1,13},{2,14},{3,15},{4,8},{5,9},{6,10},{7,11},{8,4},{9,5},... | collective-permute-start | bytes 138248 | tf_op jit(solution)/shard_map/ppermute | solution.py:79
  22.9 5.0 %collective-permute-start.7 = (bf16[48,480]{1,0:T(8,128)(2,1)S(1)}, bf16[48,480]{1,0:T(8,128)(2,1)S(1)}, u32[]{:S(2)}, u32[]{:S(2)}) collective-permute-start(bf16[48,480]{1,0:T(8,128)(2,1)S(1)} %get-tuple-element.61.refs_0_), channel_id=1, source_target_pairs={{0,8},{1,9},{2,10},{3,11},{4,12},{5,13},{6,14},{7,15},{8,0},{9,1},... | collective-permute-start | bytes 138248 | tf_op jit(solution)/shard_map/ppermute | solution.py:79
  22.9 5.0 %collective-permute-start.6 = (bf16[48,480]{1,0:T(8,128)(2,1)S(1)}, bf16[48,480]{1,0:T(8,128)(2,1)S(1)}, u32[]{:S(2)}, u32[]{:S(2)}) collective-permute-start(bf16[48,480]{1,0:T(8,128)(2,1)S(1)} %get-tuple-element.61.refs_0_), channel_id=1, source_target_pairs={{0,4},{1,5},{2,6},{3,7},{4,0},{5,1},{6,2},{7,3},{8,12},{9,13},{10,... | collective-permute-start | bytes 138248 | tf_op jit(solution)/shard_map/ppermute | solution.py:79
  27.9 6.0 %collective-permute-start.9 = (bf16[4,48,480]{2,1,0:T(8,128)(2,1)S(1)}, bf16[4,48,480]{2,1,0:T(8,128)(2,1)S(1)}, u32[]{:S(2)}, u32[]{:S(2)}) collective-permute-start(bf16[4,48,480]{2,1,0:T(8,128)(2,1)S(1)} %shard_map.87.s0), channel_id=1, source_target_pairs={{0,2},{1,3},{2,0},{3,1},{4,6},{5,7},{6,4},{7,5},{8,10},{9,11},{10,... | collective-permute-start | bytes 552968 | tf_op jit(solution)/shard_map/ppermute | solution.py:79
  29.3 4.7 %collective-permute-start.15 = (bf16[4,2,3,2,2560]{4,3,2,1,0:T(2,128)(2,1)S(1)}, bf16[4,2,3,2,2560]{4,3,2,1,0:T(2,128)(2,1)S(1)}, u32[]{:S(2)}, u32[]{:S(2)}) collective-permute-start(bf16[4,2,3,2,2560]{4,3,2,1,0:T(2,128)(2,1)S(1)} %bitcast.8), channel_id=1, source_target_pairs={{0,1},{1,0},{2,3},{3,2},{4,5},{5,4},{6,7},{7,6},{8,9},{9,8},{10,11... | collective-permute-start | bytes 737288 | tf_op jit(solution)/shard_map/ppermute | solution.py:79
  29.3 4.7 %collective-permute-start.16 = (bf16[4,2,3,2,2560]{4,3,2,1,0:T(2,128)(2,1)S(1)}, bf16[4,2,3,2,2560]{4,3,2,1,0:T(2,128)(2,1)S(1)}, u32[]{:S(2)}, u32[]{:S(2)}) collective-permute-start(bf16[4,2,3,2,2560]{4,3,2,1,0:T(2,128)(2,1)S(1)} %collective-permute-done.14.s1), channel_id=1, source_target_pairs={{0,1},{1,0},{2,3},{3,2},{4,5},{5,4},{6,7},{7,6},{8,9},{9,8},{10,11... | collective-permute-start | bytes 737288 | tf_op jit(solution)/shard_map/ppermute | solution.py:79
  29.8 4.8 %collective-permute-start.10 = (bf16[4,48,480]{2,1,0:T(8,128)(2,1)S(1)}, bf16[4,48,480]{2,1,0:T(8,128)(2,1)S(1)}, u32[]{:S(2)}, u32[]{:S(2)}) collective-permute-start(bf16[4,48,480]{2,1,0:T(8,128)(2,1)S(1)} %shard_map.87.s0), channel_id=1, source_target_pairs={{0,1},{1,0},{2,3},{3,2},{4,5},{5,4},{6,7},{7,6},{8,9},{9,8},{10,11... | collective-permute-start | bytes 552968 | tf_op jit(solution)/shard_map/ppermute | solution.py:79
  37.2 6.7 %collective-permute-start.19 = (bf16[24,640]{1,0:T(8,128)(2,1)S(1)}, bf16[24,640]{1,0:T(8,128)(2,1)S(1)}, u32[]{:S(2)}, u32[]{:S(2)}) collective-permute-start(bf16[24,640]{1,0:T(8,128)(2,1)S(1)} %shard_map.92.refs_0_), channel_id=1, source_target_pairs={{0,12},{1,13},{2,14},{3,15},{4,8},{5,9},{6,10},{7,11},{8,4},{9,5},... | collective-permute-start | bytes 92168 | tf_op jit(solution)/shard_map/ppermute | solution.py:79
  39.1 4.9 %collective-permute-start.18 = (bf16[24,640]{1,0:T(8,128)(2,1)S(1)}, bf16[24,640]{1,0:T(8,128)(2,1)S(1)}, u32[]{:S(2)}, u32[]{:S(2)}) collective-permute-start(bf16[24,640]{1,0:T(8,128)(2,1)S(1)} %shard_map.92.refs_0_), channel_id=1, source_target_pairs={{0,8},{1,9},{2,10},{3,11},{4,12},{5,13},{6,14},{7,15},{8,0},{9,1},... | collective-permute-start | bytes 92168 | tf_op jit(solution)/shard_map/ppermute | solution.py:79
  39.6 4.4 %collective-permute-start.17 = (bf16[24,640]{1,0:T(8,128)(2,1)S(1)}, bf16[24,640]{1,0:T(8,128)(2,1)S(1)}, u32[]{:S(2)}, u32[]{:S(2)}) collective-permute-start(bf16[24,640]{1,0:T(8,128)(2,1)S(1)} %shard_map.92.refs_0_), channel_id=1, source_target_pairs={{0,4},{1,5},{2,6},{3,7},{4,0},{5,1},{6,2},{7,3},{8,12},{9,13},{10,... | collective-permute-start | bytes 92168 | tf_op jit(solution)/shard_map/ppermute | solution.py:79
  44.0 4.9 %collective-permute-start.20 = (bf16[4,24,640]{2,1,0:T(8,128)(2,1)S(1)}, bf16[4,24,640]{2,1,0:T(8,128)(2,1)S(1)}, u32[]{:S(2)}, u32[]{:S(2)}) collective-permute-start(bf16[4,24,640]{2,1,0:T(8,128)(2,1)S(1)} %shard_map.94.s0), channel_id=1, source_target_pairs={{0,2},{1,3},{2,0},{3,1},{4,6},{5,7},{6,4},{7,5},{8,10},{9,11},{10,... | collective-permute-start | bytes 368648 | tf_op jit(solution)/shard_map/ppermute | solution.py:79
  45.2 3.8 %collective-permute-start.21 = (bf16[4,24,640]{2,1,0:T(8,128)(2,1)S(1)}, bf16[4,24,640]{2,1,0:T(8,128)(2,1)S(1)}, u32[]{:S(2)}, u32[]{:S(2)}) collective-permute-start(bf16[4,24,640]{2,1,0:T(8,128)(2,1)S(1)} %shard_map.94.s0), channel_id=1, source_target_pairs={{0,1},{1,0},{2,3},{3,2},{4,5},{5,4},{6,7},{7,6},{8,9},{9,8},{10,11... | collective-permute-start | bytes 368648 | tf_op jit(solution)/shard_map/ppermute | solution.py:79
  56.2 5.1 %collective-permute-start.24 = (bf16[24,1280]{1,0:T(8,128)(2,1)S(1)}, bf16[24,1280]{1,0:T(8,128)(2,1)S(1)}, u32[]{:S(2)}, u32[]{:S(2)}) collective-permute-start(bf16[24,1280]{1,0:T(8,128)(2,1)S(1)} %get-tuple-element.90), channel_id=1, source_target_pairs={{1,3},{3,1},{5,7},{7,5},{9,11},{11,9},{13,15},{15,13},{17,19},{19,... | collective-permute-start | bytes 184328 | tf_op jit(solution)/shard_map/ppermute | solution.py:316
  56.9 6.1 %collective-permute-start.25 = (bf16[24,1280]{1,0:T(8,128)(2,1)S(1)}, bf16[24,1280]{1,0:T(8,128)(2,1)S(1)}, u32[]{:S(2)}, u32[]{:S(2)}) collective-permute-start(bf16[24,1280]{1,0:T(8,128)(2,1)S(1)} %get-tuple-element.91), channel_id=1, source_target_pairs={{0,12},{1,15},{2,14},{3,13},{4,8},{5,11},{6,10},{7,9},{8,4},{9,7},... | collective-permute-start | bytes 184328 | tf_op jit(solution)/shard_map/ppermute | solution.py:316
  59.0 7.7 %collective-permute-start.26 = (bf16[24,1280]{1,0:T(8,128)(2,1)S(1)}, bf16[24,1280]{1,0:T(8,128)(2,1)S(1)}, u32[]{:S(2)}, u32[]{:S(2)}) collective-permute-start(bf16[24,1280]{1,0:T(8,128)(2,1)S(1)} %get-tuple-element.92), channel_id=1, source_target_pairs={{0,8},{1,11},{2,10},{3,9},{4,12},{5,15},{6,14},{7,13},{8,0},{9,3},... | collective-permute-start | bytes 184328 | tf_op jit(solution)/shard_map/ppermute | solution.py:316
  59.9 6.8 %collective-permute-start.27 = (bf16[24,1280]{1,0:T(8,128)(2,1)S(1)}, bf16[24,1280]{1,0:T(8,128)(2,1)S(1)}, u32[]{:S(2)}, u32[]{:S(2)}) collective-permute-start(bf16[24,1280]{1,0:T(8,128)(2,1)S(1)} %get-tuple-element.93), channel_id=1, source_target_pairs={{0,4},{1,7},{2,6},{3,5},{4,0},{5,3},{6,2},{7,1},{8,12},{9,15},{10,... | collective-permute-start | bytes 184328 | tf_op jit(solution)/shard_map/ppermute | solution.py:316
  (5 other events, 8.4 us)

commit v8 on v7

--- a/solution.py
+++ b/solution.py
@@ -137,16 +137,24 @@
     return total
 
 
-def project_qkv(s0, s1, s2, s3, mod, weights1, weights2, tokens_out, qkv_out, flat):
-    for slot, ref in enumerate((s0, s2, s1, s3)):
+def unpack_tokens(stacks, rows):
+    for slot, ref in enumerate(stacks):
         for half in range(2):
             piece = ref[12 * half : 12 * half + 12, :].astype(jnp.float32)
-            flat[12 * slot : 12 * slot + 12, 2560 * half : 2560 * half + 2560] = piece
-    tokens = flat[...]
-    tokens_out[...] = tokens.astype(jnp.bfloat16)
-    normed = normalize(tokens, mod[0:1, :], mod[1:2, :])
+            rows[12 * slot : 12 * slot + 12, 2560 * half : 2560 * half + 2560] = piece
+
+
+def project_qkv(s0, s2, s1, s3, mod, weights1, weights2, qkv_out, rows):
+    unpack_tokens((s0, s2, s1, s3), rows)
+    normed = normalize(rows[...], mod[0:1, :], mod[1:2, :])
     qkv = matmul(normed, weights1, weights2).astype(jnp.bfloat16)
     qkv_out[...] = jnp.dot(order(1), qkv, preferred_element_type=jnp.float32).astype(jnp.bfloat16)
+
+
+def order_tokens(s0, s2, s1, s3, out, rows):
+    unpack_tokens((s0, s2, s1, s3), rows)
+    tokens = rows[...].astype(jnp.bfloat16)
+    out[...] = jnp.dot(order(1), tokens, preferred_element_type=jnp.float32).astype(jnp.bfloat16)
 
 
 def line_up(s0, s1, s2, s3, keys_out, values_out, keys, values):
@@ -192,18 +200,27 @@
     out[...] = jnp.concatenate([projected[:24], projected[24:]], axis=1).astype(jnp.bfloat16)
 
 
-def feed_forward(s0, s1, s2, s3, tokens, mod, w_up1, w_up2, w_down1, w_down2, keep, send, residual_out, slots):
-    place((s0, s1, s2, s3), slots)
+def line_up_projected(stacks, slots):
+    place(stacks, slots)
     pieces = [slots[j] for j in range(16)]
     upper = jnp.concatenate([piece[:, :320] for piece in pieces], axis=1)
     lower = jnp.concatenate([piece[:, 320:] for piece in pieces], axis=1)
-    projected = jnp.concatenate([upper, lower], axis=0)
-    projected = jnp.dot(order(0), projected, preferred_element_type=jnp.float32)
-    residual = tokens[...].astype(jnp.float32) + mod[2:3, :] * projected
-    residual_out[...] = residual[0:3]
+    return jnp.concatenate([upper, lower], axis=0)
+
+
+def own_residual(s0, s1, s2, s3, tokens, mod, out, slots):
+    projected = line_up_projected((s0, s1, s2, s3), slots)
+    own = jnp.dot(order(0)[0:16], projected, preferred_element_type=jnp.float32)[0:3]
+    out[...] = tokens[...].astype(jnp.float32) + mod[2:3, :] * own
+
+
+def feed_forward(s0, s1, s2, s3, tokens, mod, w_up1, w_up2, w_down1, w_down2, keep, send, slots):
+    projected = line_up_projected((s0, s1, s2, s3), slots)
+    residual = tokens[...].astype(jnp.float32) + mod[2:3, :] * projected.astype(jnp.float32)
     normed = normalize(residual, mod[3:4, :], mod[4:5, :])
     hidden = matmul(normed, w_up1, w_up2)
     hidden = jax.nn.gelu(hidden, approximate=True).astype(jnp.bfloat16)
+    hidden = jnp.dot(order(0), hidden, preferred_element_type=jnp.float32).astype(jnp.bfloat16)
     first = lax.axis_index("seq") & 1 == 0
     middle = w_down1.shape[1]
     for cols, weights in ((slice(0, middle), w_down1), (slice(middle, None), w_down2)):
@@ -254,18 +271,17 @@
     pair = stack([cache_kv, cache_far])
     cache_planes = stack([pair, swap(pair, 4)]).reshape(4, *cache_kv.shape)
     cache_across = swap(cache_planes, 2)
-    near_tokens, qkv = call(
+    token_stacks = [planes, swap(planes, 1), across, swap(across, 1)]
+    qkv = call(
         project_qkv,
-        [((48, 5120), bf16), ((48, 480), bf16)],
-        planes,
-        across,
-        swap(planes, 1),
-        swap(across, 1),
+        [((48, 480), bf16)],
+        *token_stacks,
         modulation,
         w_qkv1,
         w_qkv2,
         scratch=[pltpu.VMEM((48, 5120), f32)],
-    )
+    )[0]
+    all_tokens = call(order_tokens, [((48, 5120), bf16)], *token_stacks, scratch=[pltpu.VMEM((48, 5120), f32)])[0]
     w_up, w_out = w_up.T, w_out.T
     qkv_stacks, (w_up1, w_up2, w_out) = gather(
         qkv, [(w_up, 0, UP_CUT, True)], [(w_up, UP_CUT, 5120, True), (w_out, 0, 2560, False)]
@@ -297,11 +313,11 @@
     projected_stacks, (w_down1, w_down2) = gather(
         projected, [(w_down, 0, DOWN_CUT, False)], [(w_down, DOWN_CUT, 5120, False)]
     )
-    keep, send, residual = call(
+    keep, send = call(
         feed_forward,
-        [((24, 5120), f32), ((24, 5120), bf16), ((3, 5120), f32)],
+        [((24, 5120), f32), ((24, 5120), bf16)],
         *projected_stacks,
-        near_tokens,
+        all_tokens,
         modulation,
         w_up1,
         w_up2,
@@ -309,6 +325,9 @@
         w_down2,
         scratch=[pltpu.VMEM((16, 24, 640), bf16)],
     )
+    keep, projected_stacks = lax.optimization_barrier((keep, projected_stacks))
+    slots = pltpu.VMEM((16, 24, 640), bf16)
+    residual = call(own_residual, [((3, 5120), f32)], *projected_stacks, tokens, modulation, scratch=[slots])[0]
     own, *sends = call(add_cores, [((6, 5120), f32)] + [((24, 1280), bf16)] * 4, keep, swap(send, 1))
     got = []
     for z, send in enumerate(sends):

time: 69.2 us -> 69 us (level)
  waiting for transfers between devices: 17.1 us -> 16.4 us
    pallas_call x18 -> x20, Pallas kernels: 23.4 us -> 23.9 us  [call(): pl.pallas_call(body, out_shape=[jax.ShapeDtypeStruct(shape, dtype) for sh...]
  transfers between devices with their start and end apart: 29 -> 29, of which waited for: 13 -> 13; matrix products, arithmetic and copies ran while one was open for 0% -> 0% of each run, Pallas kernels for 24% -> 25%
where the time goes in v8:
time: 69 us; the launch traced here: 68.8 us
  starting transfers between devices  28.4 us (41%)
  Pallas kernels  23.9 us (35%)
  waiting for transfers between devices  16.4 us (24%)
    pallas_call x20, Pallas kernels, call(): pl.pallas_call(body, out_shape=[jax.ShapeDtypeStruct(shape, dtype) for sh...  23.9 us
    ppermute x25, starting transfers between devices, swap(): return lax.ppermute(values, 'seq', [(i, i ^ offset) for i in range(16)])  23.3 us
    ppermute x25, waiting for transfers between devices, swap(): return lax.ppermute(values, 'seq', [(i, i ^ offset) for i in range(16)])  11.1 us
    ppermute x4, waiting for transfers between devices, staged(): got.append(lax.ppermute(send, 'seq', [(i, j) for i, j in pairs if i != j]))  5.29 us
    ppermute x4, starting transfers between devices, staged(): got.append(lax.ppermute(send, 'seq', [(i, j) for i, j in pairs if i != j]))  5.12 us
  transfers between devices with their start and end apart: 29, of which 13 were waited for; matrix products, arithmetic and copies ran while one was open for 0% of the time, Pallas kernels for 25%

profile of v8, /device:TPU:0, one launch (start us, length us, event | category | flops | bytes accessed | tf_op | source)
XLA Modules:
  0.0 68.8 jit_solution(3761051001890460360)
XLA Ops:
  0.0 4.0 %collective-permute-start.1 = (bf16[3,5120]{1,0:T(4,128)(2,1)}, bf16[3,5120]{1,0:T(4,128)(2,1)S(1)}, u32[]{:S(2)}, u32[]{:S(2)}) collective-permute-start(bf16[3,5120]{1,0:T(4,128)(2,1)} %refs_0_.1), channel_id=1, source_target_pairs={{0,8},{1,9},{2,10},{3,11},{4,12},{5,13},{6,14},{7,15},{8,0},{9,1},... | collective-permute-start | bytes 92168 | tf_op jit(solution)/shard_map/ppermute | solution.py:79
  4.0 1.6 %collective-permute-start = (bf16[3,5120]{1,0:T(4,128)(2,1)}, bf16[3,5120]{1,0:T(4,128)(2,1)S(1)}, u32[]{:S(2)}, u32[]{:S(2)}) collective-permute-start(bf16[3,5120]{1,0:T(4,128)(2,1)} %refs_0_.1), channel_id=1, source_target_pairs={{0,4},{1,5},{2,6},{3,7},{4,0},{5,1},{6,2},{7,3},{8,12},{9,13},{10,... | collective-permute-start | bytes 92168 | tf_op jit(solution)/shard_map/ppermute | solution.py:79
  5.6 1.9 %collective-permute-start.12 = (bf16[2,3,2,2560]{3,2,1,0:T(2,128)(2,1)}, bf16[2,3,2,2560]{3,2,1,0:T(2,128)(2,1)S(1)}, u32[]{:S(2)}, u32[]{:S(2)}) collective-permute-start(bf16[2,3,2,2560]{3,2,1,0:T(2,128)(2,1)} %bitcast.15), channel_id=1, source_target_pairs={{0,8},{1,9},{2,10},{3,11},{4,12},{5,13},{6,14},{7,15},{8,0},{9,1},... | collective-permute-start | bytes 184328 | tf_op jit(solution)/shard_map/ppermute | solution.py:79
  7.5 2.2 %shard_map.82 = (bf16[3,5120]{1,0:T(4,128)(2,1)S(1)}, f32[6,5120]{1,0:T(8,128)S(1)}, f32[2,2560]{1,0:T(2,128)S(1)}, bf16[2,3,2,2560]{3,2,1,0:T(2,128)(2,1)S(1)}, bf16[2560,480]{1,0:T(8,128)(2,1)S(1)}) custom-call(bf16[3,5120]{1,0:T(4,128)(2,1)} %refs_0_.1, f32[6,5120]{1,0:T(8,128)} %refs_1_.1, f32[2,2560]{1,0:T(2,128)} %refs_2_.1, ...), custom_call_target="tpu_custom_call" | custom-call | tf_op jit(solution)/shard_map/pallas_call | solution.py:31
  9.8 2.0 %collective-permute-done.2.got3 = bf16[3,5120]{1,0:T(4,128)(2,1)S(1)} collective-permute-done((bf16[3,5120]{1,0:T(4,128)(2,1)}, bf16[3,5120]{1,0:T(4,128)(2,1)S(1)}, u32[]{:S(2)}, u32[]{:S(2)}) %collective-permute-start.2) | collective-permute-done | bytes 30752 | tf_op jit(solution)/shard_map/ppermute | solution.py:79
  11.8 1.6 %collective-permute-start.4 = (bf16[24,2560]{1,0:T(8,128)(2,1)S(1)}, bf16[24,2560]{1,0:T(8,128)(2,1)S(1)}, u32[]{:S(2)}, u32[]{:S(2)}) collective-permute-start(bf16[24,2560]{1,0:T(8,128)(2,1)S(1)} %shard_map.83.s0), channel_id=1, source_target_pairs={{0,2},{1,3},{2,0},{3,1},{4,6},{5,7},{6,4},{7,5},{8,10},{9,11},{10,... | collective-permute-start | bytes 368648 | tf_op jit(solution)/shard_map/ppermute | solution.py:79
  14.0 2.0 %shard_map.84.weights2 = bf16[2560,480]{1,0:T(8,128)(2,1)S(1)} custom-call(bf16[480,5120]{1,0:T(8,128)(2,1)} %bitcast.13), custom_call_target="tpu_custom_call" | custom-call | tf_op jit(solution)/shard_map/pallas_call | solution.py:31
  16.7 1.6 %collective-permute-done.13.refs_1_ = bf16[2,2,3,2,2560]{4,3,2,1,0:T(2,128)(2,1)S(1)} collective-permute-done((bf16[2,2,3,2,2560]{4,3,2,1,0:T(2,128)(2,1)S(1)}, bf16[2,2,3,2,2560]{4,3,2,1,0:T(2,128)(2,1)S(1)}, u32[]{:S(2)}, u32[]{:S(2)}) %collective-permute-start.13) | collective-permute-done | bytes 122912 | tf_op jit(solution)/shard_map/ppermute | solution.py:79
  19.1 1.5 %shard_map.85.refs_0_ = bf16[48,480]{1,0:T(8,128)(2,1)S(1)} custom-call(bf16[24,2560]{1,0:T(8,128)(2,1)S(1)} %shard_map.83.s0, bf16[24,2560]{1,0:T(8,128)(2,1)S(1)} %collective-permute-done.3.s2, bf16[24,2560]{1,0:T(8,128)(2,1)S(1)} %collective-permute-done.4.s1, bf16[24,2560]{1,0:T(8,128)(2,1)S(1)} %collective-permute-done.5.s3, ...), custom_call_target="tpu_custom_call" | custom-call | tf_op jit(solution)/shard_map/pallas_call | solution.py:31
  20.6 2.3 %collective-permute-start.8 = (bf16[48,480]{1,0:T(8,128)(2,1)S(1)}, bf16[48,480]{1,0:T(8,128)(2,1)S(1)}, u32[]{:S(2)}, u32[]{:S(2)}) collective-permute-start(bf16[48,480]{1,0:T(8,128)(2,1)S(1)} %shard_map.85.refs_0_), channel_id=1, source_target_pairs={{0,12},{1,13},{2,14},{3,15},{4,8},{5,9},{6,10},{7,11},{8,4},{9,5},... | collective-permute-start | bytes 138248 | tf_op jit(solution)/shard_map/ppermute | solution.py:79
  22.9 2.2 %collective-permute-start.6 = (bf16[48,480]{1,0:T(8,128)(2,1)S(1)}, bf16[48,480]{1,0:T(8,128)(2,1)S(1)}, u32[]{:S(2)}, u32[]{:S(2)}) collective-permute-start(bf16[48,480]{1,0:T(8,128)(2,1)S(1)} %shard_map.85.refs_0_), channel_id=1, source_target_pairs={{0,4},{1,5},{2,6},{3,7},{4,0},{5,1},{6,2},{7,3},{8,12},{9,13},{10,... | collective-permute-start | bytes 138248 | tf_op jit(solution)/shard_map/ppermute | solution.py:79
  25.1 2.7 %shard_map.86.w_up1 = bf16[2560,864]{1,0:T(8,128)(2,1)S(1)} custom-call(bf16[864,5120]{1,0:T(8,128)(2,1)} %bitcast.10), custom_call_target="tpu_custom_call" | custom-call | tf_op jit(solution)/shard_map/pallas_call | solution.py:31
  29.8 2.8 %shard_map.88 = (bf16[2560,864]{1,0:T(8,128)(2,1)S(1)}, bf16[320,2560]{1,0:T(8,128)(2,1)S(1)}) custom-call(bf16[864,5120]{1,0:T(8,128)(2,1)} %bitcast.11, bf16[320,2560]{1,0:T(8,128)(2,1)} %bitcast.14), custom_call_target="tpu_custom_call" | custom-call | tf_op jit(solution)/shard_map/pallas_call | solution.py:31
  35.4 1.8 %shard_map.92.refs_0_ = bf16[24,640]{1,0:T(8,128)(2,1)S(1)} custom-call(bf16[4,48,480]{2,1,0:T(8,128)(2,1)S(1)} %shard_map.87.s0, bf16[4,48,480]{2,1,0:T(8,128)(2,1)S(1)} %collective-permute-done.9.s1, bf16[4,48,480]{2,1,0:T(8,128)(2,1)S(1)} %collective-permute-done.10.s2, bf16[4,48,480]{2,1,0:T(8,128)(2,1)S(1)} %collective-permute-done.11.s3, ...), custom_call_target="tpu_custom_call" | custom-call | tf_op jit(solution)/shard_map/pallas_call | solution.py:31
  37.1 2.0 %collective-permute-start.19 = (bf16[24,640]{1,0:T(8,128)(2,1)S(1)}, bf16[24,640]{1,0:T(8,128)(2,1)S(1)}, u32[]{:S(2)}, u32[]{:S(2)}) collective-permute-start(bf16[24,640]{1,0:T(8,128)(2,1)S(1)} %shard_map.92.refs_0_), channel_id=1, source_target_pairs={{0,12},{1,13},{2,14},{3,15},{4,8},{5,9},{6,10},{7,11},{8,4},{9,5},... | collective-permute-start | bytes 92168 | tf_op jit(solution)/shard_map/ppermute | solution.py:79
  39.6 1.9 %collective-permute-start.17 = (bf16[24,640]{1,0:T(8,128)(2,1)S(1)}, bf16[24,640]{1,0:T(8,128)(2,1)S(1)}, u32[]{:S(2)}, u32[]{:S(2)}) collective-permute-start(bf16[24,640]{1,0:T(8,128)(2,1)S(1)} %shard_map.92.refs_0_), channel_id=1, source_target_pairs={{0,4},{1,5},{2,6},{3,7},{4,0},{5,1},{6,2},{7,3},{8,12},{9,13},{10,... | collective-permute-start | bytes 92168 | tf_op jit(solution)/shard_map/ppermute | solution.py:79
  41.5 2.3 %shard_map.93.w_down1 = bf16[864,2560]{1,0:T(8,128)(2,1)S(1)} custom-call(bf16[864,5120]{1,0:T(8,128)(2,1)} %refs_0_.3), custom_call_target="tpu_custom_call" | custom-call | tf_op jit(solution)/shard_map/pallas_call | solution.py:31
  45.2 2.3 %shard_map.95.w_down2 = bf16[864,2560]{1,0:T(8,128)(2,1)S(1)} custom-call(bf16[864,5120]{1,0:T(8,128)(2,1)} %refs_0_.3), custom_call_target="tpu_custom_call" | custom-call | tf_op jit(solution)/shard_map/pallas_call | solution.py:31
  47.5 1.5 %collective-permute-done.20.s1 = bf16[4,24,640]{2,1,0:T(8,128)(2,1)S(1)} collective-permute-done((bf16[4,24,640]{2,1,0:T(8,128)(2,1)S(1)}, bf16[4,24,640]{2,1,0:T(8,128)(2,1)S(1)}, u32[]{:S(2)}, u32[]{:S(2)}) %collective-permute-start.20) | collective-permute-done | bytes 122912 | tf_op jit(solution)/shard_map/ppermute | solution.py:79
  50.3 3.9 %shard_map.97 = (f32[24,5120]{1,0:T(8,128)S(1)}, bf16[24,5120]{1,0:T(8,128)(2,1)S(1)}) custom-call(bf16[4,24,640]{2,1,0:T(8,128)(2,1)S(1)} %shard_map.94.s0, bf16[4,24,640]{2,1,0:T(8,128)(2,1)S(1)} %collective-permute-done.20.s1, bf16[4,24,640]{2,1,0:T(8,128)(2,1)S(1)} %collective-permute-done.21.s2, bf16[4,24,640]{2,1,0:T(8,128)(2,1)S(1)} %collective-permute-done.22.s3, ...), custom_call_target="tpu_custom_call" | custom-call | tf_op jit(solution)/shard_map/pallas_call | solution.py:31
  56.7 2.1 %collective-permute-start.25 = (bf16[24,1280]{1,0:T(8,128)(2,1)S(1)}, bf16[24,1280]{1,0:T(8,128)(2,1)S(1)}, u32[]{:S(2)}, u32[]{:S(2)}) collective-permute-start(bf16[24,1280]{1,0:T(8,128)(2,1)S(1)} %get-tuple-element.92), channel_id=1, source_target_pairs={{0,12},{1,15},{2,14},{3,13},{4,8},{5,11},{6,10},{7,9},{8,4},{9,7},... | collective-permute-start | bytes 184328 | tf_op jit(solution)/shard_map/ppermute | solution.py:335
  59.7 1.5 %collective-permute-start.27 = (bf16[24,1280]{1,0:T(8,128)(2,1)S(1)}, bf16[24,1280]{1,0:T(8,128)(2,1)S(1)}, u32[]{:S(2)}, u32[]{:S(2)}) collective-permute-start(bf16[24,1280]{1,0:T(8,128)(2,1)S(1)} %get-tuple-element.94), channel_id=1, source_target_pairs={{0,4},{1,7},{2,6},{3,5},{4,0},{5,3},{6,2},{7,1},{8,12},{9,15},{10,... | collective-permute-start | bytes 184328 | tf_op jit(solution)/shard_map/ppermute | solution.py:335
  61.1 1.6 %collective-permute-done.25.got1 = bf16[24,1280]{1,0:T(8,128)(2,1)S(1)} collective-permute-done((bf16[24,1280]{1,0:T(8,128)(2,1)S(1)}, bf16[24,1280]{1,0:T(8,128)(2,1)S(1)}, u32[]{:S(2)}, u32[]{:S(2)}) %collective-permute-start.25) | collective-permute-done | bytes 61472 | tf_op jit(solution)/shard_map/ppermute | solution.py:335
  62.8 3.7 %collective-permute-done.26.got2 = bf16[24,1280]{1,0:T(8,128)(2,1)S(1)} collective-permute-done((bf16[24,1280]{1,0:T(8,128)(2,1)S(1)}, bf16[24,1280]{1,0:T(8,128)(2,1)S(1)}, u32[]{:S(2)}, u32[]{:S(2)}) %collective-permute-start.26) | collective-permute-done | bytes 61472 | tf_op jit(solution)/shard_map/ppermute | solution.py:335
  (54 shorter events, 15.8 us)
Async XLA Ops:
  0.0 9.7 %collective-permute-start.1 = (bf16[3,5120]{1,0:T(4,128)(2,1)}, bf16[3,5120]{1,0:T(4,128)(2,1)S(1)}, u32[]{:S(2)}, u32[]{:S(2)}) collective-permute-start(bf16[3,5120]{1,0:T(4,128)(2,1)} %refs_0_.1), channel_id=1, source_target_pairs={{0,8},{1,9},{2,10},{3,11},{4,12},{5,13},{6,14},{7,15},{8,0},{9,1},... | collective-permute-start | bytes 92168 | tf_op jit(solution)/shard_map/ppermute | solution.py:79
  4.0 5.7 %collective-permute-start = (bf16[3,5120]{1,0:T(4,128)(2,1)}, bf16[3,5120]{1,0:T(4,128)(2,1)S(1)}, u32[]{:S(2)}, u32[]{:S(2)}) collective-permute-start(bf16[3,5120]{1,0:T(4,128)(2,1)} %refs_0_.1), channel_id=1, source_target_pairs={{0,4},{1,5},{2,6},{3,7},{4,0},{5,1},{6,2},{7,3},{8,12},{9,13},{10,... | collective-permute-start | bytes 92168 | tf_op jit(solution)/shard_map/ppermute | solution.py:79
  5.6 6.1 %collective-permute-start.2 = (bf16[3,5120]{1,0:T(4,128)(2,1)}, bf16[3,5120]{1,0:T(4,128)(2,1)S(1)}, u32[]{:S(2)}, u32[]{:S(2)}) collective-permute-start(bf16[3,5120]{1,0:T(4,128)(2,1)} %refs_0_.1), channel_id=1, source_target_pairs={{0,12},{1,13},{2,14},{3,15},{4,8},{5,9},{6,10},{7,11},{8,4},{9,5},... | collective-permute-start | bytes 92168 | tf_op jit(solution)/shard_map/ppermute | solution.py:79
  5.6 7.8 %collective-permute-start.12 = (bf16[2,3,2,2560]{3,2,1,0:T(2,128)(2,1)}, bf16[2,3,2,2560]{3,2,1,0:T(2,128)(2,1)S(1)}, u32[]{:S(2)}, u32[]{:S(2)}) collective-permute-start(bf16[2,3,2,2560]{3,2,1,0:T(2,128)(2,1)} %bitcast.15), channel_id=1, source_target_pairs={{0,8},{1,9},{2,10},{3,11},{4,12},{5,13},{6,14},{7,15},{8,0},{9,1},... | collective-permute-start | bytes 184328 | tf_op jit(solution)/shard_map/ppermute | solution.py:79
  11.8 4.9 %collective-permute-start.4 = (bf16[24,2560]{1,0:T(8,128)(2,1)S(1)}, bf16[24,2560]{1,0:T(8,128)(2,1)S(1)}, u32[]{:S(2)}, u32[]{:S(2)}) collective-permute-start(bf16[24,2560]{1,0:T(8,128)(2,1)S(1)} %shard_map.83.s0), channel_id=1, source_target_pairs={{0,2},{1,3},{2,0},{3,1},{4,6},{5,7},{6,4},{7,5},{8,10},{9,11},{10,... | collective-permute-start | bytes 368648 | tf_op jit(solution)/shard_map/ppermute | solution.py:79
  13.4 4.9 %collective-permute-start.13 = (bf16[2,2,3,2,2560]{4,3,2,1,0:T(2,128)(2,1)S(1)}, bf16[2,2,3,2,2560]{4,3,2,1,0:T(2,128)(2,1)S(1)}, u32[]{:S(2)}, u32[]{:S(2)}) collective-permute-start(bf16[2,2,3,2,2560]{4,3,2,1,0:T(2,128)(2,1)S(1)} %shard_map.89.refs_0_), channel_id=1, source_target_pairs={{0,4},{1,5},{2,6},{3,7},{4,0},{5,1},{6,2},{7,3},{8,12},{9,13},{10,... | collective-permute-start | bytes 368648 | tf_op jit(solution)/shard_map/ppermute | solution.py:79
  14.0 5.2 %collective-permute-start.3 = (bf16[24,2560]{1,0:T(8,128)(2,1)S(1)}, bf16[24,2560]{1,0:T(8,128)(2,1)S(1)}, u32[]{:S(2)}, u32[]{:S(2)}) collective-permute-start(bf16[24,2560]{1,0:T(8,128)(2,1)S(1)} %shard_map.83.s0), channel_id=1, source_target_pairs={{0,1},{1,0},{2,3},{3,2},{4,5},{5,4},{6,7},{7,6},{8,9},{9,8},{10,11... | collective-permute-start | bytes 368648 | tf_op jit(solution)/shard_map/ppermute | solution.py:79
  18.4 10.9 %collective-permute-start.14 = (bf16[4,2,3,2,2560]{4,3,2,1,0:T(2,128)(2,1)S(1)}, bf16[4,2,3,2,2560]{4,3,2,1,0:T(2,128)(2,1)S(1)}, u32[]{:S(2)}, u32[]{:S(2)}) collective-permute-start(bf16[4,2,3,2,2560]{4,3,2,1,0:T(2,128)(2,1)S(1)} %bitcast.7), channel_id=1, source_target_pairs={{0,2},{1,3},{2,0},{3,1},{4,6},{5,7},{6,4},{7,5},{8,10},{9,11},{10,... | collective-permute-start | bytes 737288 | tf_op jit(solution)/shard_map/ppermute | solution.py:79
  20.6 7.2 %collective-permute-start.8 = (bf16[48,480]{1,0:T(8,128)(2,1)S(1)}, bf16[48,480]{1,0:T(8,128)(2,1)S(1)}, u32[]{:S(2)}, u32[]{:S(2)}) collective-permute-start(bf16[48,480]{1,0:T(8,128)(2,1)S(1)} %shard_map.85.refs_0_), channel_id=1, source_target_pairs={{0,12},{1,13},{2,14},{3,15},{4,8},{5,9},{6,10},{7,11},{8,4},{9,5},... | collective-permute-start | bytes 138248 | tf_op jit(solution)/shard_map/ppermute | solution.py:79
  22.9 5.0 %collective-permute-start.7 = (bf16[48,480]{1,0:T(8,128)(2,1)S(1)}, bf16[48,480]{1,0:T(8,128)(2,1)S(1)}, u32[]{:S(2)}, u32[]{:S(2)}) collective-permute-start(bf16[48,480]{1,0:T(8,128)(2,1)S(1)} %shard_map.85.refs_0_), channel_id=1, source_target_pairs={{0,8},{1,9},{2,10},{3,11},{4,12},{5,13},{6,14},{7,15},{8,0},{9,1},... | collective-permute-start | bytes 138248 | tf_op jit(solution)/shard_map/ppermute | solution.py:79
  22.9 5.0 %collective-permute-start.6 = (bf16[48,480]{1,0:T(8,128)(2,1)S(1)}, bf16[48,480]{1,0:T(8,128)(2,1)S(1)}, u32[]{:S(2)}, u32[]{:S(2)}) collective-permute-start(bf16[48,480]{1,0:T(8,128)(2,1)S(1)} %shard_map.85.refs_0_), channel_id=1, source_target_pairs={{0,4},{1,5},{2,6},{3,7},{4,0},{5,1},{6,2},{7,3},{8,12},{9,13},{10,... | collective-permute-start | bytes 138248 | tf_op jit(solution)/shard_map/ppermute | solution.py:79
  27.9 6.0 %collective-permute-start.9 = (bf16[4,48,480]{2,1,0:T(8,128)(2,1)S(1)}, bf16[4,48,480]{2,1,0:T(8,128)(2,1)S(1)}, u32[]{:S(2)}, u32[]{:S(2)}) collective-permute-start(bf16[4,48,480]{2,1,0:T(8,128)(2,1)S(1)} %shard_map.87.s0), channel_id=1, source_target_pairs={{0,2},{1,3},{2,0},{3,1},{4,6},{5,7},{6,4},{7,5},{8,10},{9,11},{10,... | collective-permute-start | bytes 552968 | tf_op jit(solution)/shard_map/ppermute | solution.py:79
  29.2 4.7 %collective-permute-start.15 = (bf16[4,2,3,2,2560]{4,3,2,1,0:T(2,128)(2,1)S(1)}, bf16[4,2,3,2,2560]{4,3,2,1,0:T(2,128)(2,1)S(1)}, u32[]{:S(2)}, u32[]{:S(2)}) collective-permute-start(bf16[4,2,3,2,2560]{4,3,2,1,0:T(2,128)(2,1)S(1)} %bitcast.8), channel_id=1, source_target_pairs={{0,1},{1,0},{2,3},{3,2},{4,5},{5,4},{6,7},{7,6},{8,9},{9,8},{10,11... | collective-permute-start | bytes 737288 | tf_op jit(solution)/shard_map/ppermute | solution.py:79
  29.2 4.7 %collective-permute-start.16 = (bf16[4,2,3,2,2560]{4,3,2,1,0:T(2,128)(2,1)S(1)}, bf16[4,2,3,2,2560]{4,3,2,1,0:T(2,128)(2,1)S(1)}, u32[]{:S(2)}, u32[]{:S(2)}) collective-permute-start(bf16[4,2,3,2,2560]{4,3,2,1,0:T(2,128)(2,1)S(1)} %collective-permute-done.14.s1), channel_id=1, source_target_pairs={{0,1},{1,0},{2,3},{3,2},{4,5},{5,4},{6,7},{7,6},{8,9},{9,8},{10,11... | collective-permute-start | bytes 737288 | tf_op jit(solution)/shard_map/ppermute | solution.py:79
  29.7 4.8 %collective-permute-start.10 = (bf16[4,48,480]{2,1,0:T(8,128)(2,1)S(1)}, bf16[4,48,480]{2,1,0:T(8,128)(2,1)S(1)}, u32[]{:S(2)}, u32[]{:S(2)}) collective-permute-start(bf16[4,48,480]{2,1,0:T(8,128)(2,1)S(1)} %shard_map.87.s0), channel_id=1, source_target_pairs={{0,1},{1,0},{2,3},{3,2},{4,5},{5,4},{6,7},{7,6},{8,9},{9,8},{10,11... | collective-permute-start | bytes 552968 | tf_op jit(solution)/shard_map/ppermute | solution.py:79
  37.1 6.7 %collective-permute-start.19 = (bf16[24,640]{1,0:T(8,128)(2,1)S(1)}, bf16[24,640]{1,0:T(8,128)(2,1)S(1)}, u32[]{:S(2)}, u32[]{:S(2)}) collective-permute-start(bf16[24,640]{1,0:T(8,128)(2,1)S(1)} %shard_map.92.refs_0_), channel_id=1, source_target_pairs={{0,12},{1,13},{2,14},{3,15},{4,8},{5,9},{6,10},{7,11},{8,4},{9,5},... | collective-permute-start | bytes 92168 | tf_op jit(solution)/shard_map/ppermute | solution.py:79
  39.1 4.9 %collective-permute-start.18 = (bf16[24,640]{1,0:T(8,128)(2,1)S(1)}, bf16[24,640]{1,0:T(8,128)(2,1)S(1)}, u32[]{:S(2)}, u32[]{:S(2)}) collective-permute-start(bf16[24,640]{1,0:T(8,128)(2,1)S(1)} %shard_map.92.refs_0_), channel_id=1, source_target_pairs={{0,8},{1,9},{2,10},{3,11},{4,12},{5,13},{6,14},{7,15},{8,0},{9,1},... | collective-permute-start | bytes 92168 | tf_op jit(solution)/shard_map/ppermute | solution.py:79
  39.6 4.4 %collective-permute-start.17 = (bf16[24,640]{1,0:T(8,128)(2,1)S(1)}, bf16[24,640]{1,0:T(8,128)(2,1)S(1)}, u32[]{:S(2)}, u32[]{:S(2)}) collective-permute-start(bf16[24,640]{1,0:T(8,128)(2,1)S(1)} %shard_map.92.refs_0_), channel_id=1, source_target_pairs={{0,4},{1,5},{2,6},{3,7},{4,0},{5,1},{6,2},{7,3},{8,12},{9,13},{10,... | collective-permute-start | bytes 92168 | tf_op jit(solution)/shard_map/ppermute | solution.py:79
  44.0 4.9 %collective-permute-start.20 = (bf16[4,24,640]{2,1,0:T(8,128)(2,1)S(1)}, bf16[4,24,640]{2,1,0:T(8,128)(2,1)S(1)}, u32[]{:S(2)}, u32[]{:S(2)}) collective-permute-start(bf16[4,24,640]{2,1,0:T(8,128)(2,1)S(1)} %shard_map.94.s0), channel_id=1, source_target_pairs={{0,2},{1,3},{2,0},{3,1},{4,6},{5,7},{6,4},{7,5},{8,10},{9,11},{10,... | collective-permute-start | bytes 368648 | tf_op jit(solution)/shard_map/ppermute | solution.py:79
  45.2 4.1 %collective-permute-start.21 = (bf16[4,24,640]{2,1,0:T(8,128)(2,1)S(1)}, bf16[4,24,640]{2,1,0:T(8,128)(2,1)S(1)}, u32[]{:S(2)}, u32[]{:S(2)}) collective-permute-start(bf16[4,24,640]{2,1,0:T(8,128)(2,1)S(1)} %shard_map.94.s0), channel_id=1, source_target_pairs={{0,1},{1,0},{2,3},{3,2},{4,5},{5,4},{6,7},{7,6},{8,9},{9,8},{10,11... | collective-permute-start | bytes 368648 | tf_op jit(solution)/shard_map/ppermute | solution.py:79
  56.0 5.1 %collective-permute-start.24 = (bf16[24,1280]{1,0:T(8,128)(2,1)S(1)}, bf16[24,1280]{1,0:T(8,128)(2,1)S(1)}, u32[]{:S(2)}, u32[]{:S(2)}) collective-permute-start(bf16[24,1280]{1,0:T(8,128)(2,1)S(1)} %get-tuple-element.91), channel_id=1, source_target_pairs={{1,3},{3,1},{5,7},{7,5},{9,11},{11,9},{13,15},{15,13},{17,19},{19,... | collective-permute-start | bytes 184328 | tf_op jit(solution)/shard_map/ppermute | solution.py:335
  56.7 6.1 %collective-permute-start.25 = (bf16[24,1280]{1,0:T(8,128)(2,1)S(1)}, bf16[24,1280]{1,0:T(8,128)(2,1)S(1)}, u32[]{:S(2)}, u32[]{:S(2)}) collective-permute-start(bf16[24,1280]{1,0:T(8,128)(2,1)S(1)} %get-tuple-element.92), channel_id=1, source_target_pairs={{0,12},{1,15},{2,14},{3,13},{4,8},{5,11},{6,10},{7,9},{8,4},{9,7},... | collective-permute-start | bytes 184328 | tf_op jit(solution)/shard_map/ppermute | solution.py:335
  58.8 7.7 %collective-permute-start.26 = (bf16[24,1280]{1,0:T(8,128)(2,1)S(1)}, bf16[24,1280]{1,0:T(8,128)(2,1)S(1)}, u32[]{:S(2)}, u32[]{:S(2)}) collective-permute-start(bf16[24,1280]{1,0:T(8,128)(2,1)S(1)} %get-tuple-element.93), channel_id=1, source_target_pairs={{0,8},{1,11},{2,10},{3,9},{4,12},{5,15},{6,14},{7,13},{8,0},{9,3},... | collective-permute-start | bytes 184328 | tf_op jit(solution)/shard_map/ppermute | solution.py:335
  59.7 6.8 %collective-permute-start.27 = (bf16[24,1280]{1,0:T(8,128)(2,1)S(1)}, bf16[24,1280]{1,0:T(8,128)(2,1)S(1)}, u32[]{:S(2)}, u32[]{:S(2)}) collective-permute-start(bf16[24,1280]{1,0:T(8,128)(2,1)S(1)} %get-tuple-element.94), channel_id=1, source_target_pairs={{0,4},{1,7},{2,6},{3,5},{4,0},{5,3},{6,2},{7,1},{8,12},{9,15},{10,... | collective-permute-start | bytes 184328 | tf_op jit(solution)/shard_map/ppermute | solution.py:335
  (5 other events, 8.4 us)

commit v9 on v8

--- a/solution.py
+++ b/solution.py
@@ -240,7 +240,7 @@
         send[...] = jnp.concatenate(quarters, axis=0).astype(jnp.bfloat16)
 
 
-def add_chips(own, got0, got1, got2, got3, keep, send):
+def add_chips(own, got3, got2, got1, got0, keep, send):
     def whole(got):
         got = got[...].astype(jnp.float32)
         return jnp.concatenate([got[6 * q : 6 * q + 6] for q in range(4)], axis=1)
@@ -333,7 +333,7 @@
     for z, send in enumerate(sends):
         pairs = [(i, i ^ 4 * z ^ 2 * (i & 1)) for i in range(16)]
         got.append(lax.ppermute(send, "seq", [(i, j) for i, j in pairs if i != j]))
-    keep, send = call(add_chips, [((3, 5120), f32)] * 2, own, got[0], *[got[k] for k in (3, 2, 1)])
+    keep, send = call(add_chips, [((3, 5120), f32)] * 2, own, *[got[k] for k in (3, 2, 1, 0)])
     return call(finish, [((3, 5120), bf16)], keep, swap(send, 1), residual, modulation)[0]
 
 

time: 69 us -> 68.1 us (0.987)
  waiting for transfers between devices: 16.4 us -> 15.4 us
    ppermute x4, waiting for transfers between devices: 5.29 us -> 4.25 us  [staged(): got.append(lax.ppermute(send, 'seq', [(i, j) for i, j in pairs if i != j]))]
where the time goes in v9:
time: 68.1 us; the launch traced here: 67.9 us
  starting transfers between devices  28.5 us (42%)
  Pallas kernels  23.9 us (35%)
  waiting for transfers between devices  15.4 us (23%)
    pallas_call x20, Pallas kernels, call(): pl.pallas_call(body, out_shape=[jax.ShapeDtypeStruct(shape, dtype) for sh...  23.9 us
    ppermute x25, starting transfers between devices, swap(): return lax.ppermute(values, 'seq', [(i, i ^ offset) for i in range(16)])  23.4 us
    ppermute x25, waiting for transfers between devices, swap(): return lax.ppermute(values, 'seq', [(i, i ^ offset) for i in range(16)])  11.1 us
    ppermute x4, starting transfers between devices, staged(): got.append(lax.ppermute(send, 'seq', [(i, j) for i, j in pairs if i != j]))  5.11 us
    ppermute x4, waiting for transfers between devices, staged(): got.append(lax.ppermute(send, 'seq', [(i, j) for i, j in pairs if i != j]))  4.25 us
  transfers between devices with their start and end apart: 29, of which 13 were waited for; matrix products, arithmetic and copies ran while one was open for 0% of the time, Pallas kernels for 25%

profile of v9, /device:TPU:0, one launch (start us, length us, event | category | flops | bytes accessed | tf_op | source)
XLA Modules:
  0.0 67.9 jit_solution(415823809048813225)
XLA Ops:
  0.0 4.0 %collective-permute-start.1 = (bf16[3,5120]{1,0:T(4,128)(2,1)}, bf16[3,5120]{1,0:T(4,128)(2,1)S(1)}, u32[]{:S(2)}, u32[]{:S(2)}) collective-permute-start(bf16[3,5120]{1,0:T(4,128)(2,1)} %refs_0_.1), channel_id=1, source_target_pairs={{0,8},{1,9},{2,10},{3,11},{4,12},{5,13},{6,14},{7,15},{8,0},{9,1},... | collective-permute-start | bytes 92168 | tf_op jit(solution)/shard_map/ppermute | solution.py:79
  4.0 1.6 %collective-permute-start = (bf16[3,5120]{1,0:T(4,128)(2,1)}, bf16[3,5120]{1,0:T(4,128)(2,1)S(1)}, u32[]{:S(2)}, u32[]{:S(2)}) collective-permute-start(bf16[3,5120]{1,0:T(4,128)(2,1)} %refs_0_.1), channel_id=1, source_target_pairs={{0,4},{1,5},{2,6},{3,7},{4,0},{5,1},{6,2},{7,3},{8,12},{9,13},{10,... | collective-permute-start | bytes 92168 | tf_op jit(solution)/shard_map/ppermute | solution.py:79
  5.6 1.9 %collective-permute-start.12 = (bf16[2,3,2,2560]{3,2,1,0:T(2,128)(2,1)}, bf16[2,3,2,2560]{3,2,1,0:T(2,128)(2,1)S(1)}, u32[]{:S(2)}, u32[]{:S(2)}) collective-permute-start(bf16[2,3,2,2560]{3,2,1,0:T(2,128)(2,1)} %bitcast.15), channel_id=1, source_target_pairs={{0,8},{1,9},{2,10},{3,11},{4,12},{5,13},{6,14},{7,15},{8,0},{9,1},... | collective-permute-start | bytes 184328 | tf_op jit(solution)/shard_map/ppermute | solution.py:79
  7.5 2.2 %shard_map.82 = (bf16[3,5120]{1,0:T(4,128)(2,1)S(1)}, f32[6,5120]{1,0:T(8,128)S(1)}, f32[2,2560]{1,0:T(2,128)S(1)}, bf16[2,3,2,2560]{3,2,1,0:T(2,128)(2,1)S(1)}, bf16[2560,480]{1,0:T(8,128)(2,1)S(1)}) custom-call(bf16[3,5120]{1,0:T(4,128)(2,1)} %refs_0_.1, f32[6,5120]{1,0:T(8,128)} %refs_1_.1, f32[2,2560]{1,0:T(2,128)} %refs_2_.1, ...), custom_call_target="tpu_custom_call" | custom-call | tf_op jit(solution)/shard_map/pallas_call | solution.py:31
  9.8 2.0 %collective-permute-done.2.got3 = bf16[3,5120]{1,0:T(4,128)(2,1)S(1)} collective-permute-done((bf16[3,5120]{1,0:T(4,128)(2,1)}, bf16[3,5120]{1,0:T(4,128)(2,1)S(1)}, u32[]{:S(2)}, u32[]{:S(2)}) %collective-permute-start.2) | collective-permute-done | bytes 30752 | tf_op jit(solution)/shard_map/ppermute | solution.py:79
  11.8 1.6 %collective-permute-start.4 = (bf16[24,2560]{1,0:T(8,128)(2,1)S(1)}, bf16[24,2560]{1,0:T(8,128)(2,1)S(1)}, u32[]{:S(2)}, u32[]{:S(2)}) collective-permute-start(bf16[24,2560]{1,0:T(8,128)(2,1)S(1)} %shard_map.83.s0), channel_id=1, source_target_pairs={{0,2},{1,3},{2,0},{3,1},{4,6},{5,7},{6,4},{7,5},{8,10},{9,11},{10,... | collective-permute-start | bytes 368648 | tf_op jit(solution)/shard_map/ppermute | solution.py:79
  14.0 2.0 %shard_map.84.weights2 = bf16[2560,480]{1,0:T(8,128)(2,1)S(1)} custom-call(bf16[480,5120]{1,0:T(8,128)(2,1)} %bitcast.13), custom_call_target="tpu_custom_call" | custom-call | tf_op jit(solution)/shard_map/pallas_call | solution.py:31
  16.7 1.6 %collective-permute-done.13.refs_1_ = bf16[2,2,3,2,2560]{4,3,2,1,0:T(2,128)(2,1)S(1)} collective-permute-done((bf16[2,2,3,2,2560]{4,3,2,1,0:T(2,128)(2,1)S(1)}, bf16[2,2,3,2,2560]{4,3,2,1,0:T(2,128)(2,1)S(1)}, u32[]{:S(2)}, u32[]{:S(2)}) %collective-permute-start.13) | collective-permute-done | bytes 122912 | tf_op jit(solution)/shard_map/ppermute | solution.py:79
  19.1 1.5 %shard_map.85.refs_0_ = bf16[48,480]{1,0:T(8,128)(2,1)S(1)} custom-call(bf16[24,2560]{1,0:T(8,128)(2,1)S(1)} %shard_map.83.s0, bf16[24,2560]{1,0:T(8,128)(2,1)S(1)} %collective-permute-done.3.s2, bf16[24,2560]{1,0:T(8,128)(2,1)S(1)} %collective-permute-done.4.s1, bf16[24,2560]{1,0:T(8,128)(2,1)S(1)} %collective-permute-done.5.s3, ...), custom_call_target="tpu_custom_call" | custom-call | tf_op jit(solution)/shard_map/pallas_call | solution.py:31
  20.6 2.3 %collective-permute-start.8 = (bf16[48,480]{1,0:T(8,128)(2,1)S(1)}, bf16[48,480]{1,0:T(8,128)(2,1)S(1)}, u32[]{:S(2)}, u32[]{:S(2)}) collective-permute-start(bf16[48,480]{1,0:T(8,128)(2,1)S(1)} %shard_map.85.refs_0_), channel_id=1, source_target_pairs={{0,12},{1,13},{2,14},{3,15},{4,8},{5,9},{6,10},{7,11},{8,4},{9,5},... | collective-permute-start | bytes 138248 | tf_op jit(solution)/shard_map/ppermute | solution.py:79
  22.9 2.2 %collective-permute-start.6 = (bf16[48,480]{1,0:T(8,128)(2,1)S(1)}, bf16[48,480]{1,0:T(8,128)(2,1)S(1)}, u32[]{:S(2)}, u32[]{:S(2)}) collective-permute-start(bf16[48,480]{1,0:T(8,128)(2,1)S(1)} %shard_map.85.refs_0_), channel_id=1, source_target_pairs={{0,4},{1,5},{2,6},{3,7},{4,0},{5,1},{6,2},{7,3},{8,12},{9,13},{10,... | collective-permute-start | bytes 138248 | tf_op jit(solution)/shard_map/ppermute | solution.py:79
  25.1 2.7 %shard_map.86.w_up1 = bf16[2560,864]{1,0:T(8,128)(2,1)S(1)} custom-call(bf16[864,5120]{1,0:T(8,128)(2,1)} %bitcast.10), custom_call_target="tpu_custom_call" | custom-call | tf_op jit(solution)/shard_map/pallas_call | solution.py:31
  29.8 2.8 %shard_map.88 = (bf16[2560,864]{1,0:T(8,128)(2,1)S(1)}, bf16[320,2560]{1,0:T(8,128)(2,1)S(1)}) custom-call(bf16[864,5120]{1,0:T(8,128)(2,1)} %bitcast.11, bf16[320,2560]{1,0:T(8,128)(2,1)} %bitcast.14), custom_call_target="tpu_custom_call" | custom-call | tf_op jit(solution)/shard_map/pallas_call | solution.py:31
  35.4 1.8 %shard_map.92.refs_0_ = bf16[24,640]{1,0:T(8,128)(2,1)S(1)} custom-call(bf16[4,48,480]{2,1,0:T(8,128)(2,1)S(1)} %shard_map.87.s0, bf16[4,48,480]{2,1,0:T(8,128)(2,1)S(1)} %collective-permute-done.9.s1, bf16[4,48,480]{2,1,0:T(8,128)(2,1)S(1)} %collective-permute-done.10.s2, bf16[4,48,480]{2,1,0:T(8,128)(2,1)S(1)} %collective-permute-done.11.s3, ...), custom_call_target="tpu_custom_call" | custom-call | tf_op jit(solution)/shard_map/pallas_call | solution.py:31
  37.1 2.0 %collective-permute-start.19 = (bf16[24,640]{1,0:T(8,128)(2,1)S(1)}, bf16[24,640]{1,0:T(8,128)(2,1)S(1)}, u32[]{:S(2)}, u32[]{:S(2)}) collective-permute-start(bf16[24,640]{1,0:T(8,128)(2,1)S(1)} %shard_map.92.refs_0_), channel_id=1, source_target_pairs={{0,12},{1,13},{2,14},{3,15},{4,8},{5,9},{6,10},{7,11},{8,4},{9,5},... | collective-permute-start | bytes 92168 | tf_op jit(solution)/shard_map/ppermute | solution.py:79
  39.6 1.9 %collective-permute-start.17 = (bf16[24,640]{1,0:T(8,128)(2,1)S(1)}, bf16[24,640]{1,0:T(8,128)(2,1)S(1)}, u32[]{:S(2)}, u32[]{:S(2)}) collective-permute-start(bf16[24,640]{1,0:T(8,128)(2,1)S(1)} %shard_map.92.refs_0_), channel_id=1, source_target_pairs={{0,4},{1,5},{2,6},{3,7},{4,0},{5,1},{6,2},{7,3},{8,12},{9,13},{10,... | collective-permute-start | bytes 92168 | tf_op jit(solution)/shard_map/ppermute | solution.py:79
  41.5 2.3 %shard_map.93.w_down1 = bf16[864,2560]{1,0:T(8,128)(2,1)S(1)} custom-call(bf16[864,5120]{1,0:T(8,128)(2,1)} %refs_0_.3), custom_call_target="tpu_custom_call" | custom-call | tf_op jit(solution)/shard_map/pallas_call | solution.py:31
  45.2 2.3 %shard_map.95.w_down2 = bf16[864,2560]{1,0:T(8,128)(2,1)S(1)} custom-call(bf16[864,5120]{1,0:T(8,128)(2,1)} %refs_0_.3), custom_call_target="tpu_custom_call" | custom-call | tf_op jit(solution)/shard_map/pallas_call | solution.py:31
  47.5 1.5 %collective-permute-done.20.s1 = bf16[4,24,640]{2,1,0:T(8,128)(2,1)S(1)} collective-permute-done((bf16[4,24,640]{2,1,0:T(8,128)(2,1)S(1)}, bf16[4,24,640]{2,1,0:T(8,128)(2,1)S(1)}, u32[]{:S(2)}, u32[]{:S(2)}) %collective-permute-start.20) | collective-permute-done | bytes 122912 | tf_op jit(solution)/shard_map/ppermute | solution.py:79
  50.3 3.9 %shard_map.97 = (f32[24,5120]{1,0:T(8,128)S(1)}, bf16[24,5120]{1,0:T(8,128)(2,1)S(1)}) custom-call(bf16[4,24,640]{2,1,0:T(8,128)(2,1)S(1)} %shard_map.94.s0, bf16[4,24,640]{2,1,0:T(8,128)(2,1)S(1)} %collective-permute-done.20.s1, bf16[4,24,640]{2,1,0:T(8,128)(2,1)S(1)} %collective-permute-done.21.s2, bf16[4,24,640]{2,1,0:T(8,128)(2,1)S(1)} %collective-permute-done.22.s3, ...), custom_call_target="tpu_custom_call" | custom-call | tf_op jit(solution)/shard_map/pallas_call | solution.py:31
  56.0 2.1 %collective-permute-start.24 = (bf16[24,1280]{1,0:T(8,128)(2,1)S(1)}, bf16[24,1280]{1,0:T(8,128)(2,1)S(1)}, u32[]{:S(2)}, u32[]{:S(2)}) collective-permute-start(bf16[24,1280]{1,0:T(8,128)(2,1)S(1)} %get-tuple-element.91), channel_id=1, source_target_pairs={{0,12},{1,15},{2,14},{3,13},{4,8},{5,11},{6,10},{7,9},{8,4},{9,7},... | collective-permute-start | bytes 184328 | tf_op jit(solution)/shard_map/ppermute | solution.py:335
  59.0 1.5 %collective-permute-start.26 = (bf16[24,1280]{1,0:T(8,128)(2,1)S(1)}, bf16[24,1280]{1,0:T(8,128)(2,1)S(1)}, u32[]{:S(2)}, u32[]{:S(2)}) collective-permute-start(bf16[24,1280]{1,0:T(8,128)(2,1)S(1)} %get-tuple-element.93), channel_id=1, source_target_pairs={{0,4},{1,7},{2,6},{3,5},{4,0},{5,3},{6,2},{7,1},{8,12},{9,15},{10,... | collective-permute-start | bytes 184328 | tf_op jit(solution)/shard_map/ppermute | solution.py:335
  61.1 1.7 %collective-permute-done.24.got3 = bf16[24,1280]{1,0:T(8,128)(2,1)S(1)} collective-permute-done((bf16[24,1280]{1,0:T(8,128)(2,1)S(1)}, bf16[24,1280]{1,0:T(8,128)(2,1)S(1)}, u32[]{:S(2)}, u32[]{:S(2)}) %collective-permute-start.24) | collective-permute-done | bytes 61472 | tf_op jit(solution)/shard_map/ppermute | solution.py:335
  62.8 2.6 %collective-permute-done.25.got2 = bf16[24,1280]{1,0:T(8,128)(2,1)S(1)} collective-permute-done((bf16[24,1280]{1,0:T(8,128)(2,1)S(1)}, bf16[24,1280]{1,0:T(8,128)(2,1)S(1)}, u32[]{:S(2)}, u32[]{:S(2)}) %collective-permute-start.25) | collective-permute-done | bytes 61472 | tf_op jit(solution)/shard_map/ppermute | solution.py:335
  (54 shorter events, 15.9 us)
Async XLA Ops:
  0.0 9.7 %collective-permute-start.1 = (bf16[3,5120]{1,0:T(4,128)(2,1)}, bf16[3,5120]{1,0:T(4,128)(2,1)S(1)}, u32[]{:S(2)}, u32[]{:S(2)}) collective-permute-start(bf16[3,5120]{1,0:T(4,128)(2,1)} %refs_0_.1), channel_id=1, source_target_pairs={{0,8},{1,9},{2,10},{3,11},{4,12},{5,13},{6,14},{7,15},{8,0},{9,1},... | collective-permute-start | bytes 92168 | tf_op jit(solution)/shard_map/ppermute | solution.py:79
  4.0 5.7 %collective-permute-start = (bf16[3,5120]{1,0:T(4,128)(2,1)}, bf16[3,5120]{1,0:T(4,128)(2,1)S(1)}, u32[]{:S(2)}, u32[]{:S(2)}) collective-permute-start(bf16[3,5120]{1,0:T(4,128)(2,1)} %refs_0_.1), channel_id=1, source_target_pairs={{0,4},{1,5},{2,6},{3,7},{4,0},{5,1},{6,2},{7,3},{8,12},{9,13},{10,... | collective-permute-start | bytes 92168 | tf_op jit(solution)/shard_map/ppermute | solution.py:79
  5.6 6.1 %collective-permute-start.2 = (bf16[3,5120]{1,0:T(4,128)(2,1)}, bf16[3,5120]{1,0:T(4,128)(2,1)S(1)}, u32[]{:S(2)}, u32[]{:S(2)}) collective-permute-start(bf16[3,5120]{1,0:T(4,128)(2,1)} %refs_0_.1), channel_id=1, source_target_pairs={{0,12},{1,13},{2,14},{3,15},{4,8},{5,9},{6,10},{7,11},{8,4},{9,5},... | collective-permute-start | bytes 92168 | tf_op jit(solution)/shard_map/ppermute | solution.py:79
  5.6 7.8 %collective-permute-start.12 = (bf16[2,3,2,2560]{3,2,1,0:T(2,128)(2,1)}, bf16[2,3,2,2560]{3,2,1,0:T(2,128)(2,1)S(1)}, u32[]{:S(2)}, u32[]{:S(2)}) collective-permute-start(bf16[2,3,2,2560]{3,2,1,0:T(2,128)(2,1)} %bitcast.15), channel_id=1, source_target_pairs={{0,8},{1,9},{2,10},{3,11},{4,12},{5,13},{6,14},{7,15},{8,0},{9,1},... | collective-permute-start | bytes 184328 | tf_op jit(solution)/shard_map/ppermute | solution.py:79
  11.8 4.9 %collective-permute-start.4 = (bf16[24,2560]{1,0:T(8,128)(2,1)S(1)}, bf16[24,2560]{1,0:T(8,128)(2,1)S(1)}, u32[]{:S(2)}, u32[]{:S(2)}) collective-permute-start(bf16[24,2560]{1,0:T(8,128)(2,1)S(1)} %shard_map.83.s0), channel_id=1, source_target_pairs={{0,2},{1,3},{2,0},{3,1},{4,6},{5,7},{6,4},{7,5},{8,10},{9,11},{10,... | collective-permute-start | bytes 368648 | tf_op jit(solution)/shard_map/ppermute | solution.py:79
  13.4 4.9 %collective-permute-start.13 = (bf16[2,2,3,2,2560]{4,3,2,1,0:T(2,128)(2,1)S(1)}, bf16[2,2,3,2,2560]{4,3,2,1,0:T(2,128)(2,1)S(1)}, u32[]{:S(2)}, u32[]{:S(2)}) collective-permute-start(bf16[2,2,3,2,2560]{4,3,2,1,0:T(2,128)(2,1)S(1)} %shard_map.89.refs_0_), channel_id=1, source_target_pairs={{0,4},{1,5},{2,6},{3,7},{4,0},{5,1},{6,2},{7,3},{8,12},{9,13},{10,... | collective-permute-start | bytes 368648 | tf_op jit(solution)/shard_map/ppermute | solution.py:79
  14.0 5.2 %collective-permute-start.3 = (bf16[24,2560]{1,0:T(8,128)(2,1)S(1)}, bf16[24,2560]{1,0:T(8,128)(2,1)S(1)}, u32[]{:S(2)}, u32[]{:S(2)}) collective-permute-start(bf16[24,2560]{1,0:T(8,128)(2,1)S(1)} %shard_map.83.s0), channel_id=1, source_target_pairs={{0,1},{1,0},{2,3},{3,2},{4,5},{5,4},{6,7},{7,6},{8,9},{9,8},{10,11... | collective-permute-start | bytes 368648 | tf_op jit(solution)/shard_map/ppermute | solution.py:79
  18.4 10.9 %collective-permute-start.14 = (bf16[4,2,3,2,2560]{4,3,2,1,0:T(2,128)(2,1)S(1)}, bf16[4,2,3,2,2560]{4,3,2,1,0:T(2,128)(2,1)S(1)}, u32[]{:S(2)}, u32[]{:S(2)}) collective-permute-start(bf16[4,2,3,2,2560]{4,3,2,1,0:T(2,128)(2,1)S(1)} %bitcast.7), channel_id=1, source_target_pairs={{0,2},{1,3},{2,0},{3,1},{4,6},{5,7},{6,4},{7,5},{8,10},{9,11},{10,... | collective-permute-start | bytes 737288 | tf_op jit(solution)/shard_map/ppermute | solution.py:79
  20.6 7.2 %collective-permute-start.8 = (bf16[48,480]{1,0:T(8,128)(2,1)S(1)}, bf16[48,480]{1,0:T(8,128)(2,1)S(1)}, u32[]{:S(2)}, u32[]{:S(2)}) collective-permute-start(bf16[48,480]{1,0:T(8,128)(2,1)S(1)} %shard_map.85.refs_0_), channel_id=1, source_target_pairs={{0,12},{1,13},{2,14},{3,15},{4,8},{5,9},{6,10},{7,11},{8,4},{9,5},... | collective-permute-start | bytes 138248 | tf_op jit(solution)/shard_map/ppermute | solution.py:79
  22.9 5.0 %collective-permute-start.7 = (bf16[48,480]{1,0:T(8,128)(2,1)S(1)}, bf16[48,480]{1,0:T(8,128)(2,1)S(1)}, u32[]{:S(2)}, u32[]{:S(2)}) collective-permute-start(bf16[48,480]{1,0:T(8,128)(2,1)S(1)} %shard_map.85.refs_0_), channel_id=1, source_target_pairs={{0,8},{1,9},{2,10},{3,11},{4,12},{5,13},{6,14},{7,15},{8,0},{9,1},... | collective-permute-start | bytes 138248 | tf_op jit(solution)/shard_map/ppermute | solution.py:79
  22.9 5.0 %collective-permute-start.6 = (bf16[48,480]{1,0:T(8,128)(2,1)S(1)}, bf16[48,480]{1,0:T(8,128)(2,1)S(1)}, u32[]{:S(2)}, u32[]{:S(2)}) collective-permute-start(bf16[48,480]{1,0:T(8,128)(2,1)S(1)} %shard_map.85.refs_0_), channel_id=1, source_target_pairs={{0,4},{1,5},{2,6},{3,7},{4,0},{5,1},{6,2},{7,3},{8,12},{9,13},{10,... | collective-permute-start | bytes 138248 | tf_op jit(solution)/shard_map/ppermute | solution.py:79
  27.9 6.0 %collective-permute-start.9 = (bf16[4,48,480]{2,1,0:T(8,128)(2,1)S(1)}, bf16[4,48,480]{2,1,0:T(8,128)(2,1)S(1)}, u32[]{:S(2)}, u32[]{:S(2)}) collective-permute-start(bf16[4,48,480]{2,1,0:T(8,128)(2,1)S(1)} %shard_map.87.s0), channel_id=1, source_target_pairs={{0,2},{1,3},{2,0},{3,1},{4,6},{5,7},{6,4},{7,5},{8,10},{9,11},{10,... | collective-permute-start | bytes 552968 | tf_op jit(solution)/shard_map/ppermute | solution.py:79
  29.2 4.7 %collective-permute-start.15 = (bf16[4,2,3,2,2560]{4,3,2,1,0:T(2,128)(2,1)S(1)}, bf16[4,2,3,2,2560]{4,3,2,1,0:T(2,128)(2,1)S(1)}, u32[]{:S(2)}, u32[]{:S(2)}) collective-permute-start(bf16[4,2,3,2,2560]{4,3,2,1,0:T(2,128)(2,1)S(1)} %bitcast.8), channel_id=1, source_target_pairs={{0,1},{1,0},{2,3},{3,2},{4,5},{5,4},{6,7},{7,6},{8,9},{9,8},{10,11... | collective-permute-start | bytes 737288 | tf_op jit(solution)/shard_map/ppermute | solution.py:79
  29.2 4.7 %collective-permute-start.16 = (bf16[4,2,3,2,2560]{4,3,2,1,0:T(2,128)(2,1)S(1)}, bf16[4,2,3,2,2560]{4,3,2,1,0:T(2,128)(2,1)S(1)}, u32[]{:S(2)}, u32[]{:S(2)}) collective-permute-start(bf16[4,2,3,2,2560]{4,3,2,1,0:T(2,128)(2,1)S(1)} %collective-permute-done.14.s1), channel_id=1, source_target_pairs={{0,1},{1,0},{2,3},{3,2},{4,5},{5,4},{6,7},{7,6},{8,9},{9,8},{10,11... | collective-permute-start | bytes 737288 | tf_op jit(solution)/shard_map/ppermute | solution.py:79
  29.7 4.8 %collective-permute-start.10 = (bf16[4,48,480]{2,1,0:T(8,128)(2,1)S(1)}, bf16[4,48,480]{2,1,0:T(8,128)(2,1)S(1)}, u32[]{:S(2)}, u32[]{:S(2)}) collective-permute-start(bf16[4,48,480]{2,1,0:T(8,128)(2,1)S(1)} %shard_map.87.s0), channel_id=1, source_target_pairs={{0,1},{1,0},{2,3},{3,2},{4,5},{5,4},{6,7},{7,6},{8,9},{9,8},{10,11... | collective-permute-start | bytes 552968 | tf_op jit(solution)/shard_map/ppermute | solution.py:79
  37.1 6.7 %collective-permute-start.19 = (bf16[24,640]{1,0:T(8,128)(2,1)S(1)}, bf16[24,640]{1,0:T(8,128)(2,1)S(1)}, u32[]{:S(2)}, u32[]{:S(2)}) collective-permute-start(bf16[24,640]{1,0:T(8,128)(2,1)S(1)} %shard_map.92.refs_0_), channel_id=1, source_target_pairs={{0,12},{1,13},{2,14},{3,15},{4,8},{5,9},{6,10},{7,11},{8,4},{9,5},... | collective-permute-start | bytes 92168 | tf_op jit(solution)/shard_map/ppermute | solution.py:79
  39.1 4.9 %collective-permute-start.18 = (bf16[24,640]{1,0:T(8,128)(2,1)S(1)}, bf16[24,640]{1,0:T(8,128)(2,1)S(1)}, u32[]{:S(2)}, u32[]{:S(2)}) collective-permute-start(bf16[24,640]{1,0:T(8,128)(2,1)S(1)} %shard_map.92.refs_0_), channel_id=1, source_target_pairs={{0,8},{1,9},{2,10},{3,11},{4,12},{5,13},{6,14},{7,15},{8,0},{9,1},... | collective-permute-start | bytes 92168 | tf_op jit(solution)/shard_map/ppermute | solution.py:79
  39.6 4.4 %collective-permute-start.17 = (bf16[24,640]{1,0:T(8,128)(2,1)S(1)}, bf16[24,640]{1,0:T(8,128)(2,1)S(1)}, u32[]{:S(2)}, u32[]{:S(2)}) collective-permute-start(bf16[24,640]{1,0:T(8,128)(2,1)S(1)} %shard_map.92.refs_0_), channel_id=1, source_target_pairs={{0,4},{1,5},{2,6},{3,7},{4,0},{5,1},{6,2},{7,3},{8,12},{9,13},{10,... | collective-permute-start | bytes 92168 | tf_op jit(solution)/shard_map/ppermute | solution.py:79
  44.0 4.9 %collective-permute-start.20 = (bf16[4,24,640]{2,1,0:T(8,128)(2,1)S(1)}, bf16[4,24,640]{2,1,0:T(8,128)(2,1)S(1)}, u32[]{:S(2)}, u32[]{:S(2)}) collective-permute-start(bf16[4,24,640]{2,1,0:T(8,128)(2,1)S(1)} %shard_map.94.s0), channel_id=1, source_target_pairs={{0,2},{1,3},{2,0},{3,1},{4,6},{5,7},{6,4},{7,5},{8,10},{9,11},{10,... | collective-permute-start | bytes 368648 | tf_op jit(solution)/shard_map/ppermute | solution.py:79
  45.2 4.1 %collective-permute-start.21 = (bf16[4,24,640]{2,1,0:T(8,128)(2,1)S(1)}, bf16[4,24,640]{2,1,0:T(8,128)(2,1)S(1)}, u32[]{:S(2)}, u32[]{:S(2)}) collective-permute-start(bf16[4,24,640]{2,1,0:T(8,128)(2,1)S(1)} %shard_map.94.s0), channel_id=1, source_target_pairs={{0,1},{1,0},{2,3},{3,2},{4,5},{5,4},{6,7},{7,6},{8,9},{9,8},{10,11... | collective-permute-start | bytes 368648 | tf_op jit(solution)/shard_map/ppermute | solution.py:79
  56.0 6.8 %collective-permute-start.24 = (bf16[24,1280]{1,0:T(8,128)(2,1)S(1)}, bf16[24,1280]{1,0:T(8,128)(2,1)S(1)}, u32[]{:S(2)}, u32[]{:S(2)}) collective-permute-start(bf16[24,1280]{1,0:T(8,128)(2,1)S(1)} %get-tuple-element.91), channel_id=1, source_target_pairs={{0,12},{1,15},{2,14},{3,13},{4,8},{5,11},{6,10},{7,9},{8,4},{9,7},... | collective-permute-start | bytes 184328 | tf_op jit(solution)/shard_map/ppermute | solution.py:335
  58.1 7.3 %collective-permute-start.25 = (bf16[24,1280]{1,0:T(8,128)(2,1)S(1)}, bf16[24,1280]{1,0:T(8,128)(2,1)S(1)}, u32[]{:S(2)}, u32[]{:S(2)}) collective-permute-start(bf16[24,1280]{1,0:T(8,128)(2,1)S(1)} %get-tuple-element.92), channel_id=1, source_target_pairs={{0,8},{1,11},{2,10},{3,9},{4,12},{5,15},{6,14},{7,13},{8,0},{9,3},... | collective-permute-start | bytes 184328 | tf_op jit(solution)/shard_map/ppermute | solution.py:335
  59.0 6.4 %collective-permute-start.26 = (bf16[24,1280]{1,0:T(8,128)(2,1)S(1)}, bf16[24,1280]{1,0:T(8,128)(2,1)S(1)}, u32[]{:S(2)}, u32[]{:S(2)}) collective-permute-start(bf16[24,1280]{1,0:T(8,128)(2,1)S(1)} %get-tuple-element.93), channel_id=1, source_target_pairs={{0,4},{1,7},{2,6},{3,5},{4,0},{5,3},{6,2},{7,1},{8,12},{9,15},{10,... | collective-permute-start | bytes 184328 | tf_op jit(solution)/shard_map/ppermute | solution.py:335
  60.5 4.9 %collective-permute-start.27 = (bf16[24,1280]{1,0:T(8,128)(2,1)S(1)}, bf16[24,1280]{1,0:T(8,128)(2,1)S(1)}, u32[]{:S(2)}, u32[]{:S(2)}) collective-permute-start(bf16[24,1280]{1,0:T(8,128)(2,1)S(1)} %get-tuple-element.94), channel_id=1, source_target_pairs={{1,3},{3,1},{5,7},{7,5},{9,11},{11,9},{13,15},{15,13},{17,19},{19,... | collective-permute-start | bytes 184328 | tf_op jit(solution)/shard_map/ppermute | solution.py:335
  (5 other events, 8.5 us)

commit v10 on v9

--- a/solution.py
+++ b/solution.py
@@ -9,7 +9,7 @@
 
 HEAD_DIM = 128
 HEADS = 20
-QKV_CUT, UP_CUT, DOWN_CUT = 2560, 2560, 2560
+QKV_CUT, UP_CUT, DOWN_CUT = 1920, 1920, 1920
 
 
 def layer_norm(values):
@@ -106,7 +106,7 @@
         for half in range(2):
             row = 12 * half + 3 * z
             rows[row : row + 3, :] = ref[:, 2560 * half : 2560 * half + 2560].astype(jnp.float32)
-    out[...] = rows[...].astype(jnp.bfloat16)
+    out[...] = rows[:24, :].astype(jnp.bfloat16)
 
 
 def place(stacks, target):
@@ -139,21 +139,22 @@
 
 def unpack_tokens(stacks, rows):
     for slot, ref in enumerate(stacks):
+        values = ref[...].astype(jnp.float32)
         for half in range(2):
-            piece = ref[12 * half : 12 * half + 12, :].astype(jnp.float32)
+            piece = values[12 * half : 12 * half + 12]
             rows[12 * slot : 12 * slot + 12, 2560 * half : 2560 * half + 2560] = piece
 
 
 def project_qkv(s0, s2, s1, s3, mod, weights1, weights2, qkv_out, rows):
     unpack_tokens((s0, s2, s1, s3), rows)
-    normed = normalize(rows[...], mod[0:1, :], mod[1:2, :])
+    normed = normalize(rows[:48, :], mod[0:1, :], mod[1:2, :])
     qkv = matmul(normed, weights1, weights2).astype(jnp.bfloat16)
     qkv_out[...] = jnp.dot(order(1), qkv, preferred_element_type=jnp.float32).astype(jnp.bfloat16)
 
 
 def order_tokens(s0, s2, s1, s3, out, rows):
     unpack_tokens((s0, s2, s1, s3), rows)
-    tokens = rows[...].astype(jnp.bfloat16)
+    tokens = rows[:48, :].astype(jnp.bfloat16)
     out[...] = jnp.dot(order(1), tokens, preferred_element_type=jnp.float32).astype(jnp.bfloat16)
 
 
@@ -164,8 +165,8 @@
                 row = 6 * (4 * slot + z) + 2 * token
                 keys[row : row + 2, :] = ref[z, 0, token].astype(jnp.float32)
                 values[row : row + 2, :] = ref[z, 1, token].astype(jnp.float32)
-    keys_out[...] = keys[...].astype(jnp.bfloat16)
-    values_out[...] = values[...].astype(jnp.bfloat16)
+    keys_out[...] = keys[:96, :].astype(jnp.bfloat16)
+    values_out[...] = values[:96, :].astype(jnp.bfloat16)
 
 
 def attend(s0, s1, s2, s3, old_keys, old_values, gains, weights, out, slots, scores, expos, attended):
@@ -265,7 +266,7 @@
         tokens, modulation, norm_gains, cache_kv, (w_qkv, 0, QKV_CUT, True)
     )
     pieces, tokens = lax.optimization_barrier((pieces, tokens))
-    planes = call(pack_tokens, [((24, 2560), bf16)], tokens, *pieces, scratch=[pltpu.VMEM((24, 2560), f32)])[0]
+    planes = call(pack_tokens, [((24, 2560), bf16)], tokens, *pieces, scratch=[pltpu.VMEM((32, 2560), f32)])[0]
     across = swap(planes, 2)
     (w_qkv2,), across = load_beside([(w_qkv, QKV_CUT, 5120, True)], planes, across)
     pair = stack([cache_kv, cache_far])
@@ -279,9 +280,9 @@
         modulation,
         w_qkv1,
         w_qkv2,
-        scratch=[pltpu.VMEM((48, 5120), f32)],
+        scratch=[pltpu.VMEM((56, 5120), f32)],
     )[0]
-    all_tokens = call(order_tokens, [((48, 5120), bf16)], *token_stacks, scratch=[pltpu.VMEM((48, 5120), f32)])[0]
+    all_tokens = call(order_tokens, [((48, 5120), bf16)], *token_stacks, scratch=[pltpu.VMEM((56, 5120), f32)])[0]
     w_up, w_out = w_up.T, w_out.T
     qkv_stacks, (w_up1, w_up2, w_out) = gather(
         qkv, [(w_up, 0, UP_CUT, True)], [(w_up, UP_CUT, 5120, True), (w_out, 0, 2560, False)]
@@ -293,7 +294,7 @@
         cache_across,
         swap(cache_planes, 1),
         swap(cache_across, 1),
-        scratch=[pltpu.VMEM((96, 2560), f32)] * 2,
+        scratch=[pltpu.VMEM((104, 2560), f32)] * 2,
     )
     projected = call(
         attend,

time: 68.1 us -> 67.9 us (level)
  no operation moved by 1% of the time
where the time goes in v10:
time: 67.9 us; the launch traced here: 67.8 us
  starting transfers between devices  28.3 us (42%)
  Pallas kernels  23.6 us (35%)
  waiting for transfers between devices  15.6 us (23%)
    pallas_call x20, Pallas kernels, call(): pl.pallas_call(body, out_shape=[jax.ShapeDtypeStruct(shape, dtype) for sh...  23.6 us
    ppermute x25, starting transfers between devices, swap(): return lax.ppermute(values, 'seq', [(i, i ^ offset) for i in range(16)])  23.2 us
    ppermute x25, waiting for transfers between devices, swap(): return lax.ppermute(values, 'seq', [(i, i ^ offset) for i in range(16)])  11.6 us
    ppermute x4, starting transfers between devices, staged(): got.append(lax.ppermute(send, 'seq', [(i, j) for i, j in pairs if i != j]))  5.11 us
    ppermute x4, waiting for transfers between devices, staged(): got.append(lax.ppermute(send, 'seq', [(i, j) for i, j in pairs if i != j]))  4.07 us
  transfers between devices with their start and end apart: 29, of which 13 were waited for; matrix products, arithmetic and copies ran while one was open for 0% of the time, Pallas kernels for 25%

profile of v10, /device:TPU:0, one launch (start us, length us, event | category | flops | bytes accessed | tf_op | source)
XLA Modules:
  0.0 67.8 jit_solution(14149852433914981325)
XLA Ops:
  0.0 4.0 %collective-permute-start.1 = (bf16[3,5120]{1,0:T(4,128)(2,1)}, bf16[3,5120]{1,0:T(4,128)(2,1)S(1)}, u32[]{:S(2)}, u32[]{:S(2)}) collective-permute-start(bf16[3,5120]{1,0:T(4,128)(2,1)} %refs_0_.1), channel_id=1, source_target_pairs={{0,8},{1,9},{2,10},{3,11},{4,12},{5,13},{6,14},{7,15},{8,0},{9,1},... | collective-permute-start | bytes 92168 | tf_op jit(solution)/shard_map/ppermute | solution.py:79
  4.0 1.6 %collective-permute-start = (bf16[3,5120]{1,0:T(4,128)(2,1)}, bf16[3,5120]{1,0:T(4,128)(2,1)S(1)}, u32[]{:S(2)}, u32[]{:S(2)}) collective-permute-start(bf16[3,5120]{1,0:T(4,128)(2,1)} %refs_0_.1), channel_id=1, source_target_pairs={{0,4},{1,5},{2,6},{3,7},{4,0},{5,1},{6,2},{7,3},{8,12},{9,13},{10,... | collective-permute-start | bytes 92168 | tf_op jit(solution)/shard_map/ppermute | solution.py:79
  5.6 1.9 %collective-permute-start.12 = (bf16[2,3,2,2560]{3,2,1,0:T(2,128)(2,1)}, bf16[2,3,2,2560]{3,2,1,0:T(2,128)(2,1)S(1)}, u32[]{:S(2)}, u32[]{:S(2)}) collective-permute-start(bf16[2,3,2,2560]{3,2,1,0:T(2,128)(2,1)} %bitcast.15), channel_id=1, source_target_pairs={{0,8},{1,9},{2,10},{3,11},{4,12},{5,13},{6,14},{7,15},{8,0},{9,1},... | collective-permute-start | bytes 184328 | tf_op jit(solution)/shard_map/ppermute | solution.py:79
  7.5 2.0 %shard_map.82 = (bf16[3,5120]{1,0:T(4,128)(2,1)S(1)}, f32[6,5120]{1,0:T(8,128)S(1)}, f32[2,2560]{1,0:T(2,128)S(1)}, bf16[2,3,2,2560]{3,2,1,0:T(2,128)(2,1)S(1)}, bf16[1920,480]{1,0:T(8,128)(2,1)S(1)}) custom-call(bf16[3,5120]{1,0:T(4,128)(2,1)} %refs_0_.1, f32[6,5120]{1,0:T(8,128)} %refs_1_.1, f32[2,2560]{1,0:T(2,128)} %refs_2_.1, ...), custom_call_target="tpu_custom_call" | custom-call | tf_op jit(solution)/shard_map/pallas_call | solution.py:31
  9.5 2.2 %collective-permute-done.2.got3 = bf16[3,5120]{1,0:T(4,128)(2,1)S(1)} collective-permute-done((bf16[3,5120]{1,0:T(4,128)(2,1)}, bf16[3,5120]{1,0:T(4,128)(2,1)S(1)}, u32[]{:S(2)}, u32[]{:S(2)}) %collective-permute-start.2) | collective-permute-done | bytes 30752 | tf_op jit(solution)/shard_map/ppermute | solution.py:79
  11.8 1.6 %collective-permute-start.4 = (bf16[24,2560]{1,0:T(8,128)(2,1)S(1)}, bf16[24,2560]{1,0:T(8,128)(2,1)S(1)}, u32[]{:S(2)}, u32[]{:S(2)}) collective-permute-start(bf16[24,2560]{1,0:T(8,128)(2,1)S(1)} %shard_map.83.s0), channel_id=1, source_target_pairs={{0,2},{1,3},{2,0},{3,1},{4,6},{5,7},{6,4},{7,5},{8,10},{9,11},{10,... | collective-permute-start | bytes 368648 | tf_op jit(solution)/shard_map/ppermute | solution.py:79
  13.8 2.3 %shard_map.84.weights2 = bf16[3200,480]{1,0:T(8,128)(2,1)S(1)} custom-call(bf16[480,5120]{1,0:T(8,128)(2,1)} %bitcast.13), custom_call_target="tpu_custom_call" | custom-call | tf_op jit(solution)/shard_map/pallas_call | solution.py:31
  16.7 1.6 %collective-permute-done.13.refs_1_ = bf16[2,2,3,2,2560]{4,3,2,1,0:T(2,128)(2,1)S(1)} collective-permute-done((bf16[2,2,3,2,2560]{4,3,2,1,0:T(2,128)(2,1)S(1)}, bf16[2,2,3,2,2560]{4,3,2,1,0:T(2,128)(2,1)S(1)}, u32[]{:S(2)}, u32[]{:S(2)}) %collective-permute-start.13) | collective-permute-done | bytes 122912 | tf_op jit(solution)/shard_map/ppermute | solution.py:79
  19.1 1.5 %shard_map.85.refs_0_ = bf16[48,480]{1,0:T(8,128)(2,1)S(1)} custom-call(bf16[24,2560]{1,0:T(8,128)(2,1)S(1)} %shard_map.83.s0, bf16[24,2560]{1,0:T(8,128)(2,1)S(1)} %collective-permute-done.3.s2, bf16[24,2560]{1,0:T(8,128)(2,1)S(1)} %collective-permute-done.4.s1, bf16[24,2560]{1,0:T(8,128)(2,1)S(1)} %collective-permute-done.5.s3, ...), custom_call_target="tpu_custom_call" | custom-call | tf_op jit(solution)/shard_map/pallas_call | solution.py:31
  20.6 2.3 %collective-permute-start.8 = (bf16[48,480]{1,0:T(8,128)(2,1)S(1)}, bf16[48,480]{1,0:T(8,128)(2,1)S(1)}, u32[]{:S(2)}, u32[]{:S(2)}) collective-permute-start(bf16[48,480]{1,0:T(8,128)(2,1)S(1)} %shard_map.85.refs_0_), channel_id=1, source_target_pairs={{0,12},{1,13},{2,14},{3,15},{4,8},{5,9},{6,10},{7,11},{8,4},{9,5},... | collective-permute-start | bytes 138248 | tf_op jit(solution)/shard_map/ppermute | solution.py:79
  22.9 2.2 %collective-permute-start.6 = (bf16[48,480]{1,0:T(8,128)(2,1)S(1)}, bf16[48,480]{1,0:T(8,128)(2,1)S(1)}, u32[]{:S(2)}, u32[]{:S(2)}) collective-permute-start(bf16[48,480]{1,0:T(8,128)(2,1)S(1)} %shard_map.85.refs_0_), channel_id=1, source_target_pairs={{0,4},{1,5},{2,6},{3,7},{4,0},{5,1},{6,2},{7,3},{8,12},{9,13},{10,... | collective-permute-start | bytes 138248 | tf_op jit(solution)/shard_map/ppermute | solution.py:79
  25.1 2.4 %shard_map.86.w_up1 = bf16[1920,864]{1,0:T(8,128)(2,1)S(1)} custom-call(bf16[864,5120]{1,0:T(8,128)(2,1)} %bitcast.10), custom_call_target="tpu_custom_call" | custom-call | tf_op jit(solution)/shard_map/pallas_call | solution.py:31
  29.6 3.1 %shard_map.88 = (bf16[3200,864]{1,0:T(8,128)(2,1)S(1)}, bf16[320,2560]{1,0:T(8,128)(2,1)S(1)}) custom-call(bf16[864,5120]{1,0:T(8,128)(2,1)} %bitcast.11, bf16[320,2560]{1,0:T(8,128)(2,1)} %bitcast.14), custom_call_target="tpu_custom_call" | custom-call | tf_op jit(solution)/shard_map/pallas_call | solution.py:31
  35.4 1.8 %shard_map.92.refs_0_ = bf16[24,640]{1,0:T(8,128)(2,1)S(1)} custom-call(bf16[4,48,480]{2,1,0:T(8,128)(2,1)S(1)} %shard_map.87.s0, bf16[4,48,480]{2,1,0:T(8,128)(2,1)S(1)} %collective-permute-done.9.s1, bf16[4,48,480]{2,1,0:T(8,128)(2,1)S(1)} %collective-permute-done.10.s2, bf16[4,48,480]{2,1,0:T(8,128)(2,1)S(1)} %collective-permute-done.11.s3, ...), custom_call_target="tpu_custom_call" | custom-call | tf_op jit(solution)/shard_map/pallas_call | solution.py:31
  37.1 2.0 %collective-permute-start.19 = (bf16[24,640]{1,0:T(8,128)(2,1)S(1)}, bf16[24,640]{1,0:T(8,128)(2,1)S(1)}, u32[]{:S(2)}, u32[]{:S(2)}) collective-permute-start(bf16[24,640]{1,0:T(8,128)(2,1)S(1)} %shard_map.92.refs_0_), channel_id=1, source_target_pairs={{0,12},{1,13},{2,14},{3,15},{4,8},{5,9},{6,10},{7,11},{8,4},{9,5},... | collective-permute-start | bytes 92168 | tf_op jit(solution)/shard_map/ppermute | solution.py:79
  39.6 2.0 %collective-permute-start.17 = (bf16[24,640]{1,0:T(8,128)(2,1)S(1)}, bf16[24,640]{1,0:T(8,128)(2,1)S(1)}, u32[]{:S(2)}, u32[]{:S(2)}) collective-permute-start(bf16[24,640]{1,0:T(8,128)(2,1)S(1)} %shard_map.92.refs_0_), channel_id=1, source_target_pairs={{0,4},{1,5},{2,6},{3,7},{4,0},{5,1},{6,2},{7,3},{8,12},{9,13},{10,... | collective-permute-start | bytes 92168 | tf_op jit(solution)/shard_map/ppermute | solution.py:79
  41.6 1.9 %shard_map.93.w_down1 = bf16[864,1920]{1,0:T(8,128)(2,1)S(1)} custom-call(bf16[864,5120]{1,0:T(8,128)(2,1)} %refs_0_.3), custom_call_target="tpu_custom_call" | custom-call | tf_op jit(solution)/shard_map/pallas_call | solution.py:31
  45.2 2.6 %shard_map.95.w_down2 = bf16[864,3200]{1,0:T(8,128)(2,1)S(1)} custom-call(bf16[864,5120]{1,0:T(8,128)(2,1)} %refs_0_.3), custom_call_target="tpu_custom_call" | custom-call | tf_op jit(solution)/shard_map/pallas_call | solution.py:31
  50.3 3.7 %shard_map.97 = (f32[24,5120]{1,0:T(8,128)S(1)}, bf16[24,5120]{1,0:T(8,128)(2,1)S(1)}) custom-call(bf16[4,24,640]{2,1,0:T(8,128)(2,1)S(1)} %shard_map.94.s0, bf16[4,24,640]{2,1,0:T(8,128)(2,1)S(1)} %collective-permute-done.20.s1, bf16[4,24,640]{2,1,0:T(8,128)(2,1)S(1)} %collective-permute-done.21.s2, bf16[4,24,640]{2,1,0:T(8,128)(2,1)S(1)} %collective-permute-done.22.s3, ...), custom_call_target="tpu_custom_call" | custom-call | tf_op jit(solution)/shard_map/pallas_call | solution.py:31
  54.3 1.4 %collective-permute-done.23.got = bf16[24,5120]{1,0:T(8,128)(2,1)S(1)} collective-permute-done((bf16[24,5120]{1,0:T(8,128)(2,1)S(1)}, bf16[24,5120]{1,0:T(8,128)(2,1)S(1)}, u32[]{:S(2)}, u32[]{:S(2)}) %collective-permute-start.23) | collective-permute-done | bytes 245792 | tf_op jit(solution)/shard_map/ppermute | solution.py:79
  55.8 2.1 %collective-permute-start.24 = (bf16[24,1280]{1,0:T(8,128)(2,1)S(1)}, bf16[24,1280]{1,0:T(8,128)(2,1)S(1)}, u32[]{:S(2)}, u32[]{:S(2)}) collective-permute-start(bf16[24,1280]{1,0:T(8,128)(2,1)S(1)} %get-tuple-element.91), channel_id=1, source_target_pairs={{0,12},{1,15},{2,14},{3,13},{4,8},{5,11},{6,10},{7,9},{8,4},{9,7},... | collective-permute-start | bytes 184328 | tf_op jit(solution)/shard_map/ppermute | solution.py:336
  58.8 1.5 %collective-permute-start.26 = (bf16[24,1280]{1,0:T(8,128)(2,1)S(1)}, bf16[24,1280]{1,0:T(8,128)(2,1)S(1)}, u32[]{:S(2)}, u32[]{:S(2)}) collective-permute-start(bf16[24,1280]{1,0:T(8,128)(2,1)S(1)} %get-tuple-element.93), channel_id=1, source_target_pairs={{0,4},{1,7},{2,6},{3,5},{4,0},{5,3},{6,2},{7,1},{8,12},{9,15},{10,... | collective-permute-start | bytes 184328 | tf_op jit(solution)/shard_map/ppermute | solution.py:336
  60.9 1.7 %collective-permute-done.24.got3 = bf16[24,1280]{1,0:T(8,128)(2,1)S(1)} collective-permute-done((bf16[24,1280]{1,0:T(8,128)(2,1)S(1)}, bf16[24,1280]{1,0:T(8,128)(2,1)S(1)}, u32[]{:S(2)}, u32[]{:S(2)}) %collective-permute-start.24) | collective-permute-done | bytes 61472 | tf_op jit(solution)/shard_map/ppermute | solution.py:336
  62.6 2.4 %collective-permute-done.25.got2 = bf16[24,1280]{1,0:T(8,128)(2,1)S(1)} collective-permute-done((bf16[24,1280]{1,0:T(8,128)(2,1)S(1)}, bf16[24,1280]{1,0:T(8,128)(2,1)S(1)}, u32[]{:S(2)}, u32[]{:S(2)}) %collective-permute-start.25) | collective-permute-done | bytes 61472 | tf_op jit(solution)/shard_map/ppermute | solution.py:336
  (54 shorter events, 16.0 us)
Async XLA Ops:
  0.0 9.5 %collective-permute-start.1 = (bf16[3,5120]{1,0:T(4,128)(2,1)}, bf16[3,5120]{1,0:T(4,128)(2,1)S(1)}, u32[]{:S(2)}, u32[]{:S(2)}) collective-permute-start(bf16[3,5120]{1,0:T(4,128)(2,1)} %refs_0_.1), channel_id=1, source_target_pairs={{0,8},{1,9},{2,10},{3,11},{4,12},{5,13},{6,14},{7,15},{8,0},{9,1},... | collective-permute-start | bytes 92168 | tf_op jit(solution)/shard_map/ppermute | solution.py:79
  4.0 5.5 %collective-permute-start = (bf16[3,5120]{1,0:T(4,128)(2,1)}, bf16[3,5120]{1,0:T(4,128)(2,1)S(1)}, u32[]{:S(2)}, u32[]{:S(2)}) collective-permute-start(bf16[3,5120]{1,0:T(4,128)(2,1)} %refs_0_.1), channel_id=1, source_target_pairs={{0,4},{1,5},{2,6},{3,7},{4,0},{5,1},{6,2},{7,3},{8,12},{9,13},{10,... | collective-permute-start | bytes 92168 | tf_op jit(solution)/shard_map/ppermute | solution.py:79
  5.6 6.1 %collective-permute-start.2 = (bf16[3,5120]{1,0:T(4,128)(2,1)}, bf16[3,5120]{1,0:T(4,128)(2,1)S(1)}, u32[]{:S(2)}, u32[]{:S(2)}) collective-permute-start(bf16[3,5120]{1,0:T(4,128)(2,1)} %refs_0_.1), channel_id=1, source_target_pairs={{0,12},{1,13},{2,14},{3,15},{4,8},{5,9},{6,10},{7,11},{8,4},{9,5},... | collective-permute-start | bytes 92168 | tf_op jit(solution)/shard_map/ppermute | solution.py:79
  5.6 7.8 %collective-permute-start.12 = (bf16[2,3,2,2560]{3,2,1,0:T(2,128)(2,1)}, bf16[2,3,2,2560]{3,2,1,0:T(2,128)(2,1)S(1)}, u32[]{:S(2)}, u32[]{:S(2)}) collective-permute-start(bf16[2,3,2,2560]{3,2,1,0:T(2,128)(2,1)} %bitcast.15), channel_id=1, source_target_pairs={{0,8},{1,9},{2,10},{3,11},{4,12},{5,13},{6,14},{7,15},{8,0},{9,1},... | collective-permute-start | bytes 184328 | tf_op jit(solution)/shard_map/ppermute | solution.py:79
  11.8 4.9 %collective-permute-start.4 = (bf16[24,2560]{1,0:T(8,128)(2,1)S(1)}, bf16[24,2560]{1,0:T(8,128)(2,1)S(1)}, u32[]{:S(2)}, u32[]{:S(2)}) collective-permute-start(bf16[24,2560]{1,0:T(8,128)(2,1)S(1)} %shard_map.83.s0), channel_id=1, source_target_pairs={{0,2},{1,3},{2,0},{3,1},{4,6},{5,7},{6,4},{7,5},{8,10},{9,11},{10,... | collective-permute-start | bytes 368648 | tf_op jit(solution)/shard_map/ppermute | solution.py:79
  13.4 4.9 %collective-permute-start.13 = (bf16[2,2,3,2,2560]{4,3,2,1,0:T(2,128)(2,1)S(1)}, bf16[2,2,3,2,2560]{4,3,2,1,0:T(2,128)(2,1)S(1)}, u32[]{:S(2)}, u32[]{:S(2)}) collective-permute-start(bf16[2,2,3,2,2560]{4,3,2,1,0:T(2,128)(2,1)S(1)} %shard_map.89.refs_0_), channel_id=1, source_target_pairs={{0,4},{1,5},{2,6},{3,7},{4,0},{5,1},{6,2},{7,3},{8,12},{9,13},{10,... | collective-permute-start | bytes 368648 | tf_op jit(solution)/shard_map/ppermute | solution.py:79
  13.8 5.4 %collective-permute-start.3 = (bf16[24,2560]{1,0:T(8,128)(2,1)S(1)}, bf16[24,2560]{1,0:T(8,128)(2,1)S(1)}, u32[]{:S(2)}, u32[]{:S(2)}) collective-permute-start(bf16[24,2560]{1,0:T(8,128)(2,1)S(1)} %shard_map.83.s0), channel_id=1, source_target_pairs={{0,1},{1,0},{2,3},{3,2},{4,5},{5,4},{6,7},{7,6},{8,9},{9,8},{10,11... | collective-permute-start | bytes 368648 | tf_op jit(solution)/shard_map/ppermute | solution.py:79
  18.4 10.7 %collective-permute-start.14 = (bf16[4,2,3,2,2560]{4,3,2,1,0:T(2,128)(2,1)S(1)}, bf16[4,2,3,2,2560]{4,3,2,1,0:T(2,128)(2,1)S(1)}, u32[]{:S(2)}, u32[]{:S(2)}) collective-permute-start(bf16[4,2,3,2,2560]{4,3,2,1,0:T(2,128)(2,1)S(1)} %bitcast.7), channel_id=1, source_target_pairs={{0,2},{1,3},{2,0},{3,1},{4,6},{5,7},{6,4},{7,5},{8,10},{9,11},{10,... | collective-permute-start | bytes 737288 | tf_op jit(solution)/shard_map/ppermute | solution.py:79
  20.6 6.8 %collective-permute-start.8 = (bf16[48,480]{1,0:T(8,128)(2,1)S(1)}, bf16[48,480]{1,0:T(8,128)(2,1)S(1)}, u32[]{:S(2)}, u32[]{:S(2)}) collective-permute-start(bf16[48,480]{1,0:T(8,128)(2,1)S(1)} %shard_map.85.refs_0_), channel_id=1, source_target_pairs={{0,12},{1,13},{2,14},{3,15},{4,8},{5,9},{6,10},{7,11},{8,4},{9,5},... | collective-permute-start | bytes 138248 | tf_op jit(solution)/shard_map/ppermute | solution.py:79
  22.9 5.0 %collective-permute-start.7 = (bf16[48,480]{1,0:T(8,128)(2,1)S(1)}, bf16[48,480]{1,0:T(8,128)(2,1)S(1)}, u32[]{:S(2)}, u32[]{:S(2)}) collective-permute-start(bf16[48,480]{1,0:T(8,128)(2,1)S(1)} %shard_map.85.refs_0_), channel_id=1, source_target_pairs={{0,8},{1,9},{2,10},{3,11},{4,12},{5,13},{6,14},{7,15},{8,0},{9,1},... | collective-permute-start | bytes 138248 | tf_op jit(solution)/shard_map/ppermute | solution.py:79
  22.9 5.0 %collective-permute-start.6 = (bf16[48,480]{1,0:T(8,128)(2,1)S(1)}, bf16[48,480]{1,0:T(8,128)(2,1)S(1)}, u32[]{:S(2)}, u32[]{:S(2)}) collective-permute-start(bf16[48,480]{1,0:T(8,128)(2,1)S(1)} %shard_map.85.refs_0_), channel_id=1, source_target_pairs={{0,4},{1,5},{2,6},{3,7},{4,0},{5,1},{6,2},{7,3},{8,12},{9,13},{10,... | collective-permute-start | bytes 138248 | tf_op jit(solution)/shard_map/ppermute | solution.py:79
  27.9 6.0 %collective-permute-start.9 = (bf16[4,48,480]{2,1,0:T(8,128)(2,1)S(1)}, bf16[4,48,480]{2,1,0:T(8,128)(2,1)S(1)}, u32[]{:S(2)}, u32[]{:S(2)}) collective-permute-start(bf16[4,48,480]{2,1,0:T(8,128)(2,1)S(1)} %shard_map.87.s0), channel_id=1, source_target_pairs={{0,2},{1,3},{2,0},{3,1},{4,6},{5,7},{6,4},{7,5},{8,10},{9,11},{10,... | collective-permute-start | bytes 552968 | tf_op jit(solution)/shard_map/ppermute | solution.py:79
  29.1 4.9 %collective-permute-start.15 = (bf16[4,2,3,2,2560]{4,3,2,1,0:T(2,128)(2,1)S(1)}, bf16[4,2,3,2,2560]{4,3,2,1,0:T(2,128)(2,1)S(1)}, u32[]{:S(2)}, u32[]{:S(2)}) collective-permute-start(bf16[4,2,3,2,2560]{4,3,2,1,0:T(2,128)(2,1)S(1)} %bitcast.8), channel_id=1, source_target_pairs={{0,1},{1,0},{2,3},{3,2},{4,5},{5,4},{6,7},{7,6},{8,9},{9,8},{10,11... | collective-permute-start | bytes 737288 | tf_op jit(solution)/shard_map/ppermute | solution.py:79
  29.1 4.9 %collective-permute-start.16 = (bf16[4,2,3,2,2560]{4,3,2,1,0:T(2,128)(2,1)S(1)}, bf16[4,2,3,2,2560]{4,3,2,1,0:T(2,128)(2,1)S(1)}, u32[]{:S(2)}, u32[]{:S(2)}) collective-permute-start(bf16[4,2,3,2,2560]{4,3,2,1,0:T(2,128)(2,1)S(1)} %collective-permute-done.14.s1), channel_id=1, source_target_pairs={{0,1},{1,0},{2,3},{3,2},{4,5},{5,4},{6,7},{7,6},{8,9},{9,8},{10,11... | collective-permute-start | bytes 737288 | tf_op jit(solution)/shard_map/ppermute | solution.py:79
  29.6 5.0 %collective-permute-start.10 = (bf16[4,48,480]{2,1,0:T(8,128)(2,1)S(1)}, bf16[4,48,480]{2,1,0:T(8,128)(2,1)S(1)}, u32[]{:S(2)}, u32[]{:S(2)}) collective-permute-start(bf16[4,48,480]{2,1,0:T(8,128)(2,1)S(1)} %shard_map.87.s0), channel_id=1, source_target_pairs={{0,1},{1,0},{2,3},{3,2},{4,5},{5,4},{6,7},{7,6},{8,9},{9,8},{10,11... | collective-permute-start | bytes 552968 | tf_op jit(solution)/shard_map/ppermute | solution.py:79
  37.1 6.4 %collective-permute-start.19 = (bf16[24,640]{1,0:T(8,128)(2,1)S(1)}, bf16[24,640]{1,0:T(8,128)(2,1)S(1)}, u32[]{:S(2)}, u32[]{:S(2)}) collective-permute-start(bf16[24,640]{1,0:T(8,128)(2,1)S(1)} %shard_map.92.refs_0_), channel_id=1, source_target_pairs={{0,12},{1,13},{2,14},{3,15},{4,8},{5,9},{6,10},{7,11},{8,4},{9,5},... | collective-permute-start | bytes 92168 | tf_op jit(solution)/shard_map/ppermute | solution.py:79
  39.1 4.9 %collective-permute-start.18 = (bf16[24,640]{1,0:T(8,128)(2,1)S(1)}, bf16[24,640]{1,0:T(8,128)(2,1)S(1)}, u32[]{:S(2)}, u32[]{:S(2)}) collective-permute-start(bf16[24,640]{1,0:T(8,128)(2,1)S(1)} %shard_map.92.refs_0_), channel_id=1, source_target_pairs={{0,8},{1,9},{2,10},{3,11},{4,12},{5,13},{6,14},{7,15},{8,0},{9,1},... | collective-permute-start | bytes 92168 | tf_op jit(solution)/shard_map/ppermute | solution.py:79
  39.6 4.4 %collective-permute-start.17 = (bf16[24,640]{1,0:T(8,128)(2,1)S(1)}, bf16[24,640]{1,0:T(8,128)(2,1)S(1)}, u32[]{:S(2)}, u32[]{:S(2)}) collective-permute-start(bf16[24,640]{1,0:T(8,128)(2,1)S(1)} %shard_map.92.refs_0_), channel_id=1, source_target_pairs={{0,4},{1,5},{2,6},{3,7},{4,0},{5,1},{6,2},{7,3},{8,12},{9,13},{10,... | collective-permute-start | bytes 92168 | tf_op jit(solution)/shard_map/ppermute | solution.py:79
  44.0 4.9 %collective-permute-start.20 = (bf16[4,24,640]{2,1,0:T(8,128)(2,1)S(1)}, bf16[4,24,640]{2,1,0:T(8,128)(2,1)S(1)}, u32[]{:S(2)}, u32[]{:S(2)}) collective-permute-start(bf16[4,24,640]{2,1,0:T(8,128)(2,1)S(1)} %shard_map.94.s0), channel_id=1, source_target_pairs={{0,2},{1,3},{2,0},{3,1},{4,6},{5,7},{6,4},{7,5},{8,10},{9,11},{10,... | collective-permute-start | bytes 368648 | tf_op jit(solution)/shard_map/ppermute | solution.py:79
  45.2 4.1 %collective-permute-start.21 = (bf16[4,24,640]{2,1,0:T(8,128)(2,1)S(1)}, bf16[4,24,640]{2,1,0:T(8,128)(2,1)S(1)}, u32[]{:S(2)}, u32[]{:S(2)}) collective-permute-start(bf16[4,24,640]{2,1,0:T(8,128)(2,1)S(1)} %shard_map.94.s0), channel_id=1, source_target_pairs={{0,1},{1,0},{2,3},{3,2},{4,5},{5,4},{6,7},{7,6},{8,9},{9,8},{10,11... | collective-permute-start | bytes 368648 | tf_op jit(solution)/shard_map/ppermute | solution.py:79
  55.8 6.8 %collective-permute-start.24 = (bf16[24,1280]{1,0:T(8,128)(2,1)S(1)}, bf16[24,1280]{1,0:T(8,128)(2,1)S(1)}, u32[]{:S(2)}, u32[]{:S(2)}) collective-permute-start(bf16[24,1280]{1,0:T(8,128)(2,1)S(1)} %get-tuple-element.91), channel_id=1, source_target_pairs={{0,12},{1,15},{2,14},{3,13},{4,8},{5,11},{6,10},{7,9},{8,4},{9,7},... | collective-permute-start | bytes 184328 | tf_op jit(solution)/shard_map/ppermute | solution.py:336
  57.9 7.1 %collective-permute-start.25 = (bf16[24,1280]{1,0:T(8,128)(2,1)S(1)}, bf16[24,1280]{1,0:T(8,128)(2,1)S(1)}, u32[]{:S(2)}, u32[]{:S(2)}) collective-permute-start(bf16[24,1280]{1,0:T(8,128)(2,1)S(1)} %get-tuple-element.92), channel_id=1, source_target_pairs={{0,8},{1,11},{2,10},{3,9},{4,12},{5,15},{6,14},{7,13},{8,0},{9,3},... | collective-permute-start | bytes 184328 | tf_op jit(solution)/shard_map/ppermute | solution.py:336
  58.8 6.2 %collective-permute-start.26 = (bf16[24,1280]{1,0:T(8,128)(2,1)S(1)}, bf16[24,1280]{1,0:T(8,128)(2,1)S(1)}, u32[]{:S(2)}, u32[]{:S(2)}) collective-permute-start(bf16[24,1280]{1,0:T(8,128)(2,1)S(1)} %get-tuple-element.93), channel_id=1, source_target_pairs={{0,4},{1,7},{2,6},{3,5},{4,0},{5,3},{6,2},{7,1},{8,12},{9,15},{10,... | collective-permute-start | bytes 184328 | tf_op jit(solution)/shard_map/ppermute | solution.py:336
  60.3 4.7 %collective-permute-start.27 = (bf16[24,1280]{1,0:T(8,128)(2,1)S(1)}, bf16[24,1280]{1,0:T(8,128)(2,1)S(1)}, u32[]{:S(2)}, u32[]{:S(2)}) collective-permute-start(bf16[24,1280]{1,0:T(8,128)(2,1)S(1)} %get-tuple-element.94), channel_id=1, source_target_pairs={{1,3},{3,1},{5,7},{7,5},{9,11},{11,9},{13,15},{15,13},{17,19},{19,... | collective-permute-start | bytes 184328 | tf_op jit(solution)/shard_map/ppermute | solution.py:336
  (5 other events, 8.7 us)

commit v11 on v10

--- a/solution.py
+++ b/solution.py
@@ -191,13 +191,13 @@
         scores[rows, :] = lax.dot_general(diagonal, keys[:, both], NT, preferred_element_type=jnp.float32)
     scaled = scores[...] * (1.0 / math.sqrt(HEAD_DIM))
     expo = jnp.exp(scaled - jnp.max(scaled, axis=-1, keepdims=True))
-    total = jnp.sum(expo, axis=-1, keepdims=True)
+    total = 1.0 / jnp.sum(expo, axis=-1, keepdims=True)
     expos[...] = expo.astype(jnp.bfloat16)
     for rows, first, second, both in pairs:
-        summed = jnp.dot(expos[rows, :], values[:, both], preferred_element_type=jnp.float32) / total[rows]
+        summed = jnp.dot(expos[rows, :], values[:, both], preferred_element_type=jnp.float32) * total[rows]
         attended[:, first] = summed[:48, :HEAD_DIM].astype(jnp.bfloat16)
         attended[:, second] = summed[48:, HEAD_DIM:].astype(jnp.bfloat16)
-    projected = lax.dot_general(attended[...], weights[...], NT, preferred_element_type=jnp.float32)
+    projected = matmul(attended[...], weights)
     out[...] = jnp.concatenate([projected[:24], projected[24:]], axis=1).astype(jnp.bfloat16)
 
 
@@ -285,7 +285,7 @@
     all_tokens = call(order_tokens, [((48, 5120), bf16)], *token_stacks, scratch=[pltpu.VMEM((56, 5120), f32)])[0]
     w_up, w_out = w_up.T, w_out.T
     qkv_stacks, (w_up1, w_up2, w_out) = gather(
-        qkv, [(w_up, 0, UP_CUT, True)], [(w_up, UP_CUT, 5120, True), (w_out, 0, 2560, False)]
+        qkv, [(w_up, 0, UP_CUT, True)], [(w_up, UP_CUT, 5120, True), (w_out, 0, 2560, True)]
     )
     old_keys, old_values = call(
         line_up,

time: 67.9 us -> 67.9 us (level)
  waiting for transfers between devices: 15.6 us -> 14.8 us
  Pallas kernels: 23.6 us -> 24.3 us
    ppermute x25, waiting for transfers between devices: 11.6 us -> 10.9 us  [swap(): return lax.ppermute(values, 'seq', [(i, i ^ offset) for i in range(16)])]
  transfers between devices with their start and end apart: 29 -> 29, of which waited for: 13 -> 14; matrix products, arithmetic and copies ran while one was open for 0% -> 0% of each run, Pallas kernels for 25% -> 26%
where the time goes in v11:
time: 67.9 us; the launch traced here: 67.7 us
  starting transfers between devices  28.4 us (42%)
  Pallas kernels  24.3 us (36%)
  waiting for transfers between devices  14.8 us (22%)
    pallas_call x20, Pallas kernels, call(): pl.pallas_call(body, out_shape=[jax.ShapeDtypeStruct(shape, dtype) for sh...  24.3 us
    ppermute x25, starting transfers between devices, swap(): return lax.ppermute(values, 'seq', [(i, i ^ offset) for i in range(16)])  23.3 us
    ppermute x25, waiting for transfers between devices, swap(): return lax.ppermute(values, 'seq', [(i, i ^ offset) for i in range(16)])  10.9 us
    ppermute x4, starting transfers between devices, staged(): got.append(lax.ppermute(send, 'seq', [(i, j) for i, j in pairs if i != j]))  5.11 us
    ppermute x4, waiting for transfers between devices, staged(): got.append(lax.ppermute(send, 'seq', [(i, j) for i, j in pairs if i != j]))  3.95 us
  transfers between devices with their start and end apart: 29, of which 14 were waited for; matrix products, arithmetic and copies ran while one was open for 0% of the time, Pallas kernels for 26%

profile of v11, /device:TPU:0, one launch (start us, length us, event | category | flops | bytes accessed | tf_op | source)
XLA Modules:
  0.0 67.7 jit_solution(7455100384407226979)
XLA Ops:
  0.0 4.0 %collective-permute-start.1 = (bf16[3,5120]{1,0:T(4,128)(2,1)}, bf16[3,5120]{1,0:T(4,128)(2,1)S(1)}, u32[]{:S(2)}, u32[]{:S(2)}) collective-permute-start(bf16[3,5120]{1,0:T(4,128)(2,1)} %refs_0_.1), channel_id=1, source_target_pairs={{0,8},{1,9},{2,10},{3,11},{4,12},{5,13},{6,14},{7,15},{8,0},{9,1},... | collective-permute-start | bytes 92168 | tf_op jit(solution)/shard_map/ppermute | solution.py:79
  4.0 1.6 %collective-permute-start = (bf16[3,5120]{1,0:T(4,128)(2,1)}, bf16[3,5120]{1,0:T(4,128)(2,1)S(1)}, u32[]{:S(2)}, u32[]{:S(2)}) collective-permute-start(bf16[3,5120]{1,0:T(4,128)(2,1)} %refs_0_.1), channel_id=1, source_target_pairs={{0,4},{1,5},{2,6},{3,7},{4,0},{5,1},{6,2},{7,3},{8,12},{9,13},{10,... | collective-permute-start | bytes 92168 | tf_op jit(solution)/shard_map/ppermute | solution.py:79
  5.6 1.9 %collective-permute-start.12 = (bf16[2,3,2,2560]{3,2,1,0:T(2,128)(2,1)}, bf16[2,3,2,2560]{3,2,1,0:T(2,128)(2,1)S(1)}, u32[]{:S(2)}, u32[]{:S(2)}) collective-permute-start(bf16[2,3,2,2560]{3,2,1,0:T(2,128)(2,1)} %bitcast.15), channel_id=1, source_target_pairs={{0,8},{1,9},{2,10},{3,11},{4,12},{5,13},{6,14},{7,15},{8,0},{9,1},... | collective-permute-start | bytes 184328 | tf_op jit(solution)/shard_map/ppermute | solution.py:79
  7.5 2.0 %shard_map.82 = (bf16[3,5120]{1,0:T(4,128)(2,1)S(1)}, f32[6,5120]{1,0:T(8,128)S(1)}, f32[2,2560]{1,0:T(2,128)S(1)}, bf16[2,3,2,2560]{3,2,1,0:T(2,128)(2,1)S(1)}, bf16[1920,480]{1,0:T(8,128)(2,1)S(1)}) custom-call(bf16[3,5120]{1,0:T(4,128)(2,1)} %refs_0_.1, f32[6,5120]{1,0:T(8,128)} %refs_1_.1, f32[2,2560]{1,0:T(2,128)} %refs_2_.1, ...), custom_call_target="tpu_custom_call" | custom-call | tf_op jit(solution)/shard_map/pallas_call | solution.py:31
  9.5 2.2 %collective-permute-done.2.got3 = bf16[3,5120]{1,0:T(4,128)(2,1)S(1)} collective-permute-done((bf16[3,5120]{1,0:T(4,128)(2,1)}, bf16[3,5120]{1,0:T(4,128)(2,1)S(1)}, u32[]{:S(2)}, u32[]{:S(2)}) %collective-permute-start.2) | collective-permute-done | bytes 30752 | tf_op jit(solution)/shard_map/ppermute | solution.py:79
  11.8 1.6 %collective-permute-start.4 = (bf16[24,2560]{1,0:T(8,128)(2,1)S(1)}, bf16[24,2560]{1,0:T(8,128)(2,1)S(1)}, u32[]{:S(2)}, u32[]{:S(2)}) collective-permute-start(bf16[24,2560]{1,0:T(8,128)(2,1)S(1)} %shard_map.83.s0), channel_id=1, source_target_pairs={{0,2},{1,3},{2,0},{3,1},{4,6},{5,7},{6,4},{7,5},{8,10},{9,11},{10,... | collective-permute-start | bytes 368648 | tf_op jit(solution)/shard_map/ppermute | solution.py:79
  13.8 2.3 %shard_map.84.weights2 = bf16[3200,480]{1,0:T(8,128)(2,1)S(1)} custom-call(bf16[480,5120]{1,0:T(8,128)(2,1)} %bitcast.13), custom_call_target="tpu_custom_call" | custom-call | tf_op jit(solution)/shard_map/pallas_call | solution.py:31
  16.7 1.6 %collective-permute-done.13.refs_1_ = bf16[2,2,3,2,2560]{4,3,2,1,0:T(2,128)(2,1)S(1)} collective-permute-done((bf16[2,2,3,2,2560]{4,3,2,1,0:T(2,128)(2,1)S(1)}, bf16[2,2,3,2,2560]{4,3,2,1,0:T(2,128)(2,1)S(1)}, u32[]{:S(2)}, u32[]{:S(2)}) %collective-permute-start.13) | collective-permute-done | bytes 122912 | tf_op jit(solution)/shard_map/ppermute | solution.py:79
  19.1 1.5 %shard_map.85.refs_0_ = bf16[48,480]{1,0:T(8,128)(2,1)S(1)} custom-call(bf16[24,2560]{1,0:T(8,128)(2,1)S(1)} %shard_map.83.s0, bf16[24,2560]{1,0:T(8,128)(2,1)S(1)} %collective-permute-done.3.s2, bf16[24,2560]{1,0:T(8,128)(2,1)S(1)} %collective-permute-done.4.s1, bf16[24,2560]{1,0:T(8,128)(2,1)S(1)} %collective-permute-done.5.s3, ...), custom_call_target="tpu_custom_call" | custom-call | tf_op jit(solution)/shard_map/pallas_call | solution.py:31
  20.6 2.3 %collective-permute-start.8 = (bf16[48,480]{1,0:T(8,128)(2,1)S(1)}, bf16[48,480]{1,0:T(8,128)(2,1)S(1)}, u32[]{:S(2)}, u32[]{:S(2)}) collective-permute-start(bf16[48,480]{1,0:T(8,128)(2,1)S(1)} %shard_map.85.refs_0_), channel_id=1, source_target_pairs={{0,12},{1,13},{2,14},{3,15},{4,8},{5,9},{6,10},{7,11},{8,4},{9,5},... | collective-permute-start | bytes 138248 | tf_op jit(solution)/shard_map/ppermute | solution.py:79
  22.9 2.2 %collective-permute-start.6 = (bf16[48,480]{1,0:T(8,128)(2,1)S(1)}, bf16[48,480]{1,0:T(8,128)(2,1)S(1)}, u32[]{:S(2)}, u32[]{:S(2)}) collective-permute-start(bf16[48,480]{1,0:T(8,128)(2,1)S(1)} %shard_map.85.refs_0_), channel_id=1, source_target_pairs={{0,4},{1,5},{2,6},{3,7},{4,0},{5,1},{6,2},{7,3},{8,12},{9,13},{10,... | collective-permute-start | bytes 138248 | tf_op jit(solution)/shard_map/ppermute | solution.py:79
  25.1 2.4 %shard_map.86.w_up1 = bf16[1920,864]{1,0:T(8,128)(2,1)S(1)} custom-call(bf16[864,5120]{1,0:T(8,128)(2,1)} %bitcast.10), custom_call_target="tpu_custom_call" | custom-call | tf_op jit(solution)/shard_map/pallas_call | solution.py:31
  29.6 3.9 %shard_map.88 = (bf16[3200,864]{1,0:T(8,128)(2,1)S(1)}, bf16[2560,320]{1,0:T(8,128)(2,1)S(1)}) custom-call(bf16[864,5120]{1,0:T(8,128)(2,1)} %bitcast.11, bf16[320,2560]{1,0:T(8,128)(2,1)} %bitcast.14), custom_call_target="tpu_custom_call" | custom-call | tf_op jit(solution)/shard_map/pallas_call | solution.py:31
  35.4 1.7 %shard_map.92.refs_0_ = bf16[24,640]{1,0:T(8,128)(2,1)S(1)} custom-call(bf16[4,48,480]{2,1,0:T(8,128)(2,1)S(1)} %shard_map.87.s0, bf16[4,48,480]{2,1,0:T(8,128)(2,1)S(1)} %collective-permute-done.9.s1, bf16[4,48,480]{2,1,0:T(8,128)(2,1)S(1)} %collective-permute-done.10.s2, bf16[4,48,480]{2,1,0:T(8,128)(2,1)S(1)} %collective-permute-done.11.s3, ...), custom_call_target="tpu_custom_call" | custom-call | tf_op jit(solution)/shard_map/pallas_call | solution.py:31
  37.0 2.0 %collective-permute-start.19 = (bf16[24,640]{1,0:T(8,128)(2,1)S(1)}, bf16[24,640]{1,0:T(8,128)(2,1)S(1)}, u32[]{:S(2)}, u32[]{:S(2)}) collective-permute-start(bf16[24,640]{1,0:T(8,128)(2,1)S(1)} %shard_map.92.refs_0_), channel_id=1, source_target_pairs={{0,12},{1,13},{2,14},{3,15},{4,8},{5,9},{6,10},{7,11},{8,4},{9,5},... | collective-permute-start | bytes 92168 | tf_op jit(solution)/shard_map/ppermute | solution.py:79
  39.8 1.6 %collective-permute-start.17 = (bf16[24,640]{1,0:T(8,128)(2,1)S(1)}, bf16[24,640]{1,0:T(8,128)(2,1)S(1)}, u32[]{:S(2)}, u32[]{:S(2)}) collective-permute-start(bf16[24,640]{1,0:T(8,128)(2,1)S(1)} %shard_map.92.refs_0_), channel_id=1, source_target_pairs={{0,4},{1,5},{2,6},{3,7},{4,0},{5,1},{6,2},{7,3},{8,12},{9,13},{10,... | collective-permute-start | bytes 92168 | tf_op jit(solution)/shard_map/ppermute | solution.py:79
  41.5 1.9 %shard_map.93.w_down1 = bf16[864,1920]{1,0:T(8,128)(2,1)S(1)} custom-call(bf16[864,5120]{1,0:T(8,128)(2,1)} %refs_0_.3), custom_call_target="tpu_custom_call" | custom-call | tf_op jit(solution)/shard_map/pallas_call | solution.py:31
  45.2 2.6 %shard_map.95.w_down2 = bf16[864,3200]{1,0:T(8,128)(2,1)S(1)} custom-call(bf16[864,5120]{1,0:T(8,128)(2,1)} %refs_0_.3), custom_call_target="tpu_custom_call" | custom-call | tf_op jit(solution)/shard_map/pallas_call | solution.py:31
  50.4 3.7 %shard_map.97 = (f32[24,5120]{1,0:T(8,128)S(1)}, bf16[24,5120]{1,0:T(8,128)(2,1)S(1)}) custom-call(bf16[4,24,640]{2,1,0:T(8,128)(2,1)S(1)} %shard_map.94.s0, bf16[4,24,640]{2,1,0:T(8,128)(2,1)S(1)} %collective-permute-done.20.s1, bf16[4,24,640]{2,1,0:T(8,128)(2,1)S(1)} %collective-permute-done.21.s2, bf16[4,24,640]{2,1,0:T(8,128)(2,1)S(1)} %collective-permute-done.22.s3, ...), custom_call_target="tpu_custom_call" | custom-call | tf_op jit(solution)/shard_map/pallas_call | solution.py:31
  54.3 1.4 %collective-permute-done.23.got = bf16[24,5120]{1,0:T(8,128)(2,1)S(1)} collective-permute-done((bf16[24,5120]{1,0:T(8,128)(2,1)S(1)}, bf16[24,5120]{1,0:T(8,128)(2,1)S(1)}, u32[]{:S(2)}, u32[]{:S(2)}) %collective-permute-start.23) | collective-permute-done | bytes 245792 | tf_op jit(solution)/shard_map/ppermute | solution.py:79
  55.9 2.1 %collective-permute-start.24 = (bf16[24,1280]{1,0:T(8,128)(2,1)S(1)}, bf16[24,1280]{1,0:T(8,128)(2,1)S(1)}, u32[]{:S(2)}, u32[]{:S(2)}) collective-permute-start(bf16[24,1280]{1,0:T(8,128)(2,1)S(1)} %get-tuple-element.91), channel_id=1, source_target_pairs={{0,12},{1,15},{2,14},{3,13},{4,8},{5,11},{6,10},{7,9},{8,4},{9,7},... | collective-permute-start | bytes 184328 | tf_op jit(solution)/shard_map/ppermute | solution.py:336
  58.7 1.6 %collective-permute-start.26 = (bf16[24,1280]{1,0:T(8,128)(2,1)S(1)}, bf16[24,1280]{1,0:T(8,128)(2,1)S(1)}, u32[]{:S(2)}, u32[]{:S(2)}) collective-permute-start(bf16[24,1280]{1,0:T(8,128)(2,1)S(1)} %get-tuple-element.93), channel_id=1, source_target_pairs={{0,4},{1,7},{2,6},{3,5},{4,0},{5,3},{6,2},{7,1},{8,12},{9,15},{10,... | collective-permute-start | bytes 184328 | tf_op jit(solution)/shard_map/ppermute | solution.py:336
  61.0 1.6 %collective-permute-done.24.got3 = bf16[24,1280]{1,0:T(8,128)(2,1)S(1)} collective-permute-done((bf16[24,1280]{1,0:T(8,128)(2,1)S(1)}, bf16[24,1280]{1,0:T(8,128)(2,1)S(1)}, u32[]{:S(2)}, u32[]{:S(2)}) %collective-permute-start.24) | collective-permute-done | bytes 61472 | tf_op jit(solution)/shard_map/ppermute | solution.py:336
  62.6 2.3 %collective-permute-done.25.got2 = bf16[24,1280]{1,0:T(8,128)(2,1)S(1)} collective-permute-done((bf16[24,1280]{1,0:T(8,128)(2,1)S(1)}, bf16[24,1280]{1,0:T(8,128)(2,1)S(1)}, u32[]{:S(2)}, u32[]{:S(2)}) %collective-permute-start.25) | collective-permute-done | bytes 61472 | tf_op jit(solution)/shard_map/ppermute | solution.py:336
  (54 shorter events, 15.6 us)
Async XLA Ops:
  0.0 9.5 %collective-permute-start.1 = (bf16[3,5120]{1,0:T(4,128)(2,1)}, bf16[3,5120]{1,0:T(4,128)(2,1)S(1)}, u32[]{:S(2)}, u32[]{:S(2)}) collective-permute-start(bf16[3,5120]{1,0:T(4,128)(2,1)} %refs_0_.1), channel_id=1, source_target_pairs={{0,8},{1,9},{2,10},{3,11},{4,12},{5,13},{6,14},{7,15},{8,0},{9,1},... | collective-permute-start | bytes 92168 | tf_op jit(solution)/shard_map/ppermute | solution.py:79
  4.0 5.5 %collective-permute-start = (bf16[3,5120]{1,0:T(4,128)(2,1)}, bf16[3,5120]{1,0:T(4,128)(2,1)S(1)}, u32[]{:S(2)}, u32[]{:S(2)}) collective-permute-start(bf16[3,5120]{1,0:T(4,128)(2,1)} %refs_0_.1), channel_id=1, source_target_pairs={{0,4},{1,5},{2,6},{3,7},{4,0},{5,1},{6,2},{7,3},{8,12},{9,13},{10,... | collective-permute-start | bytes 92168 | tf_op jit(solution)/shard_map/ppermute | solution.py:79
  5.6 6.1 %collective-permute-start.2 = (bf16[3,5120]{1,0:T(4,128)(2,1)}, bf16[3,5120]{1,0:T(4,128)(2,1)S(1)}, u32[]{:S(2)}, u32[]{:S(2)}) collective-permute-start(bf16[3,5120]{1,0:T(4,128)(2,1)} %refs_0_.1), channel_id=1, source_target_pairs={{0,12},{1,13},{2,14},{3,15},{4,8},{5,9},{6,10},{7,11},{8,4},{9,5},... | collective-permute-start | bytes 92168 | tf_op jit(solution)/shard_map/ppermute | solution.py:79
  5.6 7.8 %collective-permute-start.12 = (bf16[2,3,2,2560]{3,2,1,0:T(2,128)(2,1)}, bf16[2,3,2,2560]{3,2,1,0:T(2,128)(2,1)S(1)}, u32[]{:S(2)}, u32[]{:S(2)}) collective-permute-start(bf16[2,3,2,2560]{3,2,1,0:T(2,128)(2,1)} %bitcast.15), channel_id=1, source_target_pairs={{0,8},{1,9},{2,10},{3,11},{4,12},{5,13},{6,14},{7,15},{8,0},{9,1},... | collective-permute-start | bytes 184328 | tf_op jit(solution)/shard_map/ppermute | solution.py:79
  11.8 4.9 %collective-permute-start.4 = (bf16[24,2560]{1,0:T(8,128)(2,1)S(1)}, bf16[24,2560]{1,0:T(8,128)(2,1)S(1)}, u32[]{:S(2)}, u32[]{:S(2)}) collective-permute-start(bf16[24,2560]{1,0:T(8,128)(2,1)S(1)} %shard_map.83.s0), channel_id=1, source_target_pairs={{0,2},{1,3},{2,0},{3,1},{4,6},{5,7},{6,4},{7,5},{8,10},{9,11},{10,... | collective-permute-start | bytes 368648 | tf_op jit(solution)/shard_map/ppermute | solution.py:79
  13.4 4.9 %collective-permute-start.13 = (bf16[2,2,3,2,2560]{4,3,2,1,0:T(2,128)(2,1)S(1)}, bf16[2,2,3,2,2560]{4,3,2,1,0:T(2,128)(2,1)S(1)}, u32[]{:S(2)}, u32[]{:S(2)}) collective-permute-start(bf16[2,2,3,2,2560]{4,3,2,1,0:T(2,128)(2,1)S(1)} %shard_map.89.refs_0_), channel_id=1, source_target_pairs={{0,4},{1,5},{2,6},{3,7},{4,0},{5,1},{6,2},{7,3},{8,12},{9,13},{10,... | collective-permute-start | bytes 368648 | tf_op jit(solution)/shard_map/ppermute | solution.py:79
  13.8 5.4 %collective-permute-start.3 = (bf16[24,2560]{1,0:T(8,128)(2,1)S(1)}, bf16[24,2560]{1,0:T(8,128)(2,1)S(1)}, u32[]{:S(2)}, u32[]{:S(2)}) collective-permute-start(bf16[24,2560]{1,0:T(8,128)(2,1)S(1)} %shard_map.83.s0), channel_id=1, source_target_pairs={{0,1},{1,0},{2,3},{3,2},{4,5},{5,4},{6,7},{7,6},{8,9},{9,8},{10,11... | collective-permute-start | bytes 368648 | tf_op jit(solution)/shard_map/ppermute | solution.py:79
  18.4 10.7 %collective-permute-start.14 = (bf16[4,2,3,2,2560]{4,3,2,1,0:T(2,128)(2,1)S(1)}, bf16[4,2,3,2,2560]{4,3,2,1,0:T(2,128)(2,1)S(1)}, u32[]{:S(2)}, u32[]{:S(2)}) collective-permute-start(bf16[4,2,3,2,2560]{4,3,2,1,0:T(2,128)(2,1)S(1)} %bitcast.7), channel_id=1, source_target_pairs={{0,2},{1,3},{2,0},{3,1},{4,6},{5,7},{6,4},{7,5},{8,10},{9,11},{10,... | collective-permute-start | bytes 737288 | tf_op jit(solution)/shard_map/ppermute | solution.py:79
  20.6 6.8 %collective-permute-start.8 = (bf16[48,480]{1,0:T(8,128)(2,1)S(1)}, bf16[48,480]{1,0:T(8,128)(2,1)S(1)}, u32[]{:S(2)}, u32[]{:S(2)}) collective-permute-start(bf16[48,480]{1,0:T(8,128)(2,1)S(1)} %shard_map.85.refs_0_), channel_id=1, source_target_pairs={{0,12},{1,13},{2,14},{3,15},{4,8},{5,9},{6,10},{7,11},{8,4},{9,5},... | collective-permute-start | bytes 138248 | tf_op jit(solution)/shard_map/ppermute | solution.py:79
  22.9 5.0 %collective-permute-start.7 = (bf16[48,480]{1,0:T(8,128)(2,1)S(1)}, bf16[48,480]{1,0:T(8,128)(2,1)S(1)}, u32[]{:S(2)}, u32[]{:S(2)}) collective-permute-start(bf16[48,480]{1,0:T(8,128)(2,1)S(1)} %shard_map.85.refs_0_), channel_id=1, source_target_pairs={{0,8},{1,9},{2,10},{3,11},{4,12},{5,13},{6,14},{7,15},{8,0},{9,1},... | collective-permute-start | bytes 138248 | tf_op jit(solution)/shard_map/ppermute | solution.py:79
  22.9 5.0 %collective-permute-start.6 = (bf16[48,480]{1,0:T(8,128)(2,1)S(1)}, bf16[48,480]{1,0:T(8,128)(2,1)S(1)}, u32[]{:S(2)}, u32[]{:S(2)}) collective-permute-start(bf16[48,480]{1,0:T(8,128)(2,1)S(1)} %shard_map.85.refs_0_), channel_id=1, source_target_pairs={{0,4},{1,5},{2,6},{3,7},{4,0},{5,1},{6,2},{7,3},{8,12},{9,13},{10,... | collective-permute-start | bytes 138248 | tf_op jit(solution)/shard_map/ppermute | solution.py:79
  27.9 6.0 %collective-permute-start.9 = (bf16[4,48,480]{2,1,0:T(8,128)(2,1)S(1)}, bf16[4,48,480]{2,1,0:T(8,128)(2,1)S(1)}, u32[]{:S(2)}, u32[]{:S(2)}) collective-permute-start(bf16[4,48,480]{2,1,0:T(8,128)(2,1)S(1)} %shard_map.87.s0), channel_id=1, source_target_pairs={{0,2},{1,3},{2,0},{3,1},{4,6},{5,7},{6,4},{7,5},{8,10},{9,11},{10,... | collective-permute-start | bytes 552968 | tf_op jit(solution)/shard_map/ppermute | solution.py:79
  29.1 5.0 %collective-permute-start.15 = (bf16[4,2,3,2,2560]{4,3,2,1,0:T(2,128)(2,1)S(1)}, bf16[4,2,3,2,2560]{4,3,2,1,0:T(2,128)(2,1)S(1)}, u32[]{:S(2)}, u32[]{:S(2)}) collective-permute-start(bf16[4,2,3,2,2560]{4,3,2,1,0:T(2,128)(2,1)S(1)} %bitcast.8), channel_id=1, source_target_pairs={{0,1},{1,0},{2,3},{3,2},{4,5},{5,4},{6,7},{7,6},{8,9},{9,8},{10,11... | collective-permute-start | bytes 737288 | tf_op jit(solution)/shard_map/ppermute | solution.py:79
  29.1 5.0 %collective-permute-start.16 = (bf16[4,2,3,2,2560]{4,3,2,1,0:T(2,128)(2,1)S(1)}, bf16[4,2,3,2,2560]{4,3,2,1,0:T(2,128)(2,1)S(1)}, u32[]{:S(2)}, u32[]{:S(2)}) collective-permute-start(bf16[4,2,3,2,2560]{4,3,2,1,0:T(2,128)(2,1)S(1)} %collective-permute-done.14.s1), channel_id=1, source_target_pairs={{0,1},{1,0},{2,3},{3,2},{4,5},{5,4},{6,7},{7,6},{8,9},{9,8},{10,11... | collective-permute-start | bytes 737288 | tf_op jit(solution)/shard_map/ppermute | solution.py:79
  29.6 5.1 %collective-permute-start.10 = (bf16[4,48,480]{2,1,0:T(8,128)(2,1)S(1)}, bf16[4,48,480]{2,1,0:T(8,128)(2,1)S(1)}, u32[]{:S(2)}, u32[]{:S(2)}) collective-permute-start(bf16[4,48,480]{2,1,0:T(8,128)(2,1)S(1)} %shard_map.87.s0), channel_id=1, source_target_pairs={{0,1},{1,0},{2,3},{3,2},{4,5},{5,4},{6,7},{7,6},{8,9},{9,8},{10,11... | collective-permute-start | bytes 552968 | tf_op jit(solution)/shard_map/ppermute | solution.py:79
  37.0 6.4 %collective-permute-start.19 = (bf16[24,640]{1,0:T(8,128)(2,1)S(1)}, bf16[24,640]{1,0:T(8,128)(2,1)S(1)}, u32[]{:S(2)}, u32[]{:S(2)}) collective-permute-start(bf16[24,640]{1,0:T(8,128)(2,1)S(1)} %shard_map.92.refs_0_), channel_id=1, source_target_pairs={{0,12},{1,13},{2,14},{3,15},{4,8},{5,9},{6,10},{7,11},{8,4},{9,5},... | collective-permute-start | bytes 92168 | tf_op jit(solution)/shard_map/ppermute | solution.py:79
  39.0 4.9 %collective-permute-start.18 = (bf16[24,640]{1,0:T(8,128)(2,1)S(1)}, bf16[24,640]{1,0:T(8,128)(2,1)S(1)}, u32[]{:S(2)}, u32[]{:S(2)}) collective-permute-start(bf16[24,640]{1,0:T(8,128)(2,1)S(1)} %shard_map.92.refs_0_), channel_id=1, source_target_pairs={{0,8},{1,9},{2,10},{3,11},{4,12},{5,13},{6,14},{7,15},{8,0},{9,1},... | collective-permute-start | bytes 92168 | tf_op jit(solution)/shard_map/ppermute | solution.py:79
  39.8 4.2 %collective-permute-start.17 = (bf16[24,640]{1,0:T(8,128)(2,1)S(1)}, bf16[24,640]{1,0:T(8,128)(2,1)S(1)}, u32[]{:S(2)}, u32[]{:S(2)}) collective-permute-start(bf16[24,640]{1,0:T(8,128)(2,1)S(1)} %shard_map.92.refs_0_), channel_id=1, source_target_pairs={{0,4},{1,5},{2,6},{3,7},{4,0},{5,1},{6,2},{7,3},{8,12},{9,13},{10,... | collective-permute-start | bytes 92168 | tf_op jit(solution)/shard_map/ppermute | solution.py:79
  44.1 4.9 %collective-permute-start.20 = (bf16[4,24,640]{2,1,0:T(8,128)(2,1)S(1)}, bf16[4,24,640]{2,1,0:T(8,128)(2,1)S(1)}, u32[]{:S(2)}, u32[]{:S(2)}) collective-permute-start(bf16[4,24,640]{2,1,0:T(8,128)(2,1)S(1)} %shard_map.94.s0), channel_id=1, source_target_pairs={{0,2},{1,3},{2,0},{3,1},{4,6},{5,7},{6,4},{7,5},{8,10},{9,11},{10,... | collective-permute-start | bytes 368648 | tf_op jit(solution)/shard_map/ppermute | solution.py:79
  45.2 4.2 %collective-permute-start.21 = (bf16[4,24,640]{2,1,0:T(8,128)(2,1)S(1)}, bf16[4,24,640]{2,1,0:T(8,128)(2,1)S(1)}, u32[]{:S(2)}, u32[]{:S(2)}) collective-permute-start(bf16[4,24,640]{2,1,0:T(8,128)(2,1)S(1)} %shard_map.94.s0), channel_id=1, source_target_pairs={{0,1},{1,0},{2,3},{3,2},{4,5},{5,4},{6,7},{7,6},{8,9},{9,8},{10,11... | collective-permute-start | bytes 368648 | tf_op jit(solution)/shard_map/ppermute | solution.py:79
  55.9 6.8 %collective-permute-start.24 = (bf16[24,1280]{1,0:T(8,128)(2,1)S(1)}, bf16[24,1280]{1,0:T(8,128)(2,1)S(1)}, u32[]{:S(2)}, u32[]{:S(2)}) collective-permute-start(bf16[24,1280]{1,0:T(8,128)(2,1)S(1)} %get-tuple-element.91), channel_id=1, source_target_pairs={{0,12},{1,15},{2,14},{3,13},{4,8},{5,11},{6,10},{7,9},{8,4},{9,7},... | collective-permute-start | bytes 184328 | tf_op jit(solution)/shard_map/ppermute | solution.py:336
  58.0 7.0 %collective-permute-start.25 = (bf16[24,1280]{1,0:T(8,128)(2,1)S(1)}, bf16[24,1280]{1,0:T(8,128)(2,1)S(1)}, u32[]{:S(2)}, u32[]{:S(2)}) collective-permute-start(bf16[24,1280]{1,0:T(8,128)(2,1)S(1)} %get-tuple-element.92), channel_id=1, source_target_pairs={{0,8},{1,11},{2,10},{3,9},{4,12},{5,15},{6,14},{7,13},{8,0},{9,3},... | collective-permute-start | bytes 184328 | tf_op jit(solution)/shard_map/ppermute | solution.py:336
  58.7 6.2 %collective-permute-start.26 = (bf16[24,1280]{1,0:T(8,128)(2,1)S(1)}, bf16[24,1280]{1,0:T(8,128)(2,1)S(1)}, u32[]{:S(2)}, u32[]{:S(2)}) collective-permute-start(bf16[24,1280]{1,0:T(8,128)(2,1)S(1)} %get-tuple-element.93), channel_id=1, source_target_pairs={{0,4},{1,7},{2,6},{3,5},{4,0},{5,3},{6,2},{7,1},{8,12},{9,15},{10,... | collective-permute-start | bytes 184328 | tf_op jit(solution)/shard_map/ppermute | solution.py:336
  60.3 4.6 %collective-permute-start.27 = (bf16[24,1280]{1,0:T(8,128)(2,1)S(1)}, bf16[24,1280]{1,0:T(8,128)(2,1)S(1)}, u32[]{:S(2)}, u32[]{:S(2)}) collective-permute-start(bf16[24,1280]{1,0:T(8,128)(2,1)S(1)} %get-tuple-element.94), channel_id=1, source_target_pairs={{1,3},{3,1},{5,7},{7,5},{9,11},{11,9},{13,15},{15,13},{17,19},{19,... | collective-permute-start | bytes 184328 | tf_op jit(solution)/shard_map/ppermute | solution.py:336
  (5 other events, 8.8 us)

commit v12 on v10

--- a/solution.py
+++ b/solution.py
@@ -249,11 +249,11 @@
     first = lax.axis_index("seq") & 1 == 0
     total = jnp.where(first, own[...], whole(got0)) + whole(got1) + whole(got2) + whole(got3)
     keep[...] = total[:3]
-    send[...] = total[3:]
+    send[...] = total[3:].astype(jnp.bfloat16)
 
 
 def finish(keep, got, residual, mod, out):
-    out[...] = (residual[...] + mod[5:6, :] * (keep[...] + got[...])).astype(jnp.bfloat16)
+    out[...] = (residual[...] + mod[5:6, :] * (keep[...] + got[...].astype(jnp.float32))).astype(jnp.bfloat16)
 
 
 def staged(tokens, modulation, w_qkv, norm_gains, cache_kv, w_out, w_up, w_down):
@@ -334,7 +334,7 @@
     for z, send in enumerate(sends):
         pairs = [(i, i ^ 4 * z ^ 2 * (i & 1)) for i in range(16)]
         got.append(lax.ppermute(send, "seq", [(i, j) for i, j in pairs if i != j]))
-    keep, send = call(add_chips, [((3, 5120), f32)] * 2, own, *[got[k] for k in (3, 2, 1, 0)])
+    keep, send = call(add_chips, [((3, 5120), f32), ((3, 5120), bf16)], own, *[got[k] for k in (3, 2, 1, 0)])
     return call(finish, [((3, 5120), bf16)], keep, swap(send, 1), residual, modulation)[0]
 
 

time: 67.9 us -> 67.9 us (level)
  no operation moved by 1% of the time
where the time goes in v12:
time: 67.9 us; the launch traced here: 67.7 us
  starting transfers between devices  28.3 us (42%)
  Pallas kernels  23.6 us (35%)
  waiting for transfers between devices  15.6 us (23%)
    pallas_call x20, Pallas kernels, call(): pl.pallas_call(body, out_shape=[jax.ShapeDtypeStruct(shape, dtype) for sh...  23.6 us
    ppermute x25, starting transfers between devices, swap(): return lax.ppermute(values, 'seq', [(i, i ^ offset) for i in range(16)])  23.2 us
    ppermute x25, waiting for transfers between devices, swap(): return lax.ppermute(values, 'seq', [(i, i ^ offset) for i in range(16)])  11.5 us
    ppermute x4, starting transfers between devices, staged(): got.append(lax.ppermute(send, 'seq', [(i, j) for i, j in pairs if i != j]))  5.11 us
    ppermute x4, waiting for transfers between devices, staged(): got.append(lax.ppermute(send, 'seq', [(i, j) for i, j in pairs if i != j]))  4.07 us
  transfers between devices with their start and end apart: 29, of which 13 were waited for; matrix products, arithmetic and copies ran while one was open for 0% of the time, Pallas kernels for 25%

profile of v12, /device:TPU:0, one launch (start us, length us, event | category | flops | bytes accessed | tf_op | source)
XLA Modules:
  0.0 67.7 jit_solution(1207025112737372736)
XLA Ops:
  0.0 4.0 %collective-permute-start.1 = (bf16[3,5120]{1,0:T(4,128)(2,1)}, bf16[3,5120]{1,0:T(4,128)(2,1)S(1)}, u32[]{:S(2)}, u32[]{:S(2)}) collective-permute-start(bf16[3,5120]{1,0:T(4,128)(2,1)} %refs_0_.1), channel_id=1, source_target_pairs={{0,8},{1,9},{2,10},{3,11},{4,12},{5,13},{6,14},{7,15},{8,0},{9,1},... | collective-permute-start | bytes 92168 | tf_op jit(solution)/shard_map/ppermute | solution.py:79
  4.0 1.6 %collective-permute-start = (bf16[3,5120]{1,0:T(4,128)(2,1)}, bf16[3,5120]{1,0:T(4,128)(2,1)S(1)}, u32[]{:S(2)}, u32[]{:S(2)}) collective-permute-start(bf16[3,5120]{1,0:T(4,128)(2,1)} %refs_0_.1), channel_id=1, source_target_pairs={{0,4},{1,5},{2,6},{3,7},{4,0},{5,1},{6,2},{7,3},{8,12},{9,13},{10,... | collective-permute-start | bytes 92168 | tf_op jit(solution)/shard_map/ppermute | solution.py:79
  5.6 1.9 %collective-permute-start.12 = (bf16[2,3,2,2560]{3,2,1,0:T(2,128)(2,1)}, bf16[2,3,2,2560]{3,2,1,0:T(2,128)(2,1)S(1)}, u32[]{:S(2)}, u32[]{:S(2)}) collective-permute-start(bf16[2,3,2,2560]{3,2,1,0:T(2,128)(2,1)} %bitcast.15), channel_id=1, source_target_pairs={{0,8},{1,9},{2,10},{3,11},{4,12},{5,13},{6,14},{7,15},{8,0},{9,1},... | collective-permute-start | bytes 184328 | tf_op jit(solution)/shard_map/ppermute | solution.py:79
  7.5 2.0 %shard_map.82 = (bf16[3,5120]{1,0:T(4,128)(2,1)S(1)}, f32[6,5120]{1,0:T(8,128)S(1)}, f32[2,2560]{1,0:T(2,128)S(1)}, bf16[2,3,2,2560]{3,2,1,0:T(2,128)(2,1)S(1)}, bf16[1920,480]{1,0:T(8,128)(2,1)S(1)}) custom-call(bf16[3,5120]{1,0:T(4,128)(2,1)} %refs_0_.1, f32[6,5120]{1,0:T(8,128)} %refs_1_.1, f32[2,2560]{1,0:T(2,128)} %refs_2_.1, ...), custom_call_target="tpu_custom_call" | custom-call | tf_op jit(solution)/shard_map/pallas_call | solution.py:31
  9.5 2.2 %collective-permute-done.2.got3 = bf16[3,5120]{1,0:T(4,128)(2,1)S(1)} collective-permute-done((bf16[3,5120]{1,0:T(4,128)(2,1)}, bf16[3,5120]{1,0:T(4,128)(2,1)S(1)}, u32[]{:S(2)}, u32[]{:S(2)}) %collective-permute-start.2) | collective-permute-done | bytes 30752 | tf_op jit(solution)/shard_map/ppermute | solution.py:79
  11.8 1.6 %collective-permute-start.4 = (bf16[24,2560]{1,0:T(8,128)(2,1)S(1)}, bf16[24,2560]{1,0:T(8,128)(2,1)S(1)}, u32[]{:S(2)}, u32[]{:S(2)}) collective-permute-start(bf16[24,2560]{1,0:T(8,128)(2,1)S(1)} %shard_map.83.s0), channel_id=1, source_target_pairs={{0,2},{1,3},{2,0},{3,1},{4,6},{5,7},{6,4},{7,5},{8,10},{9,11},{10,... | collective-permute-start | bytes 368648 | tf_op jit(solution)/shard_map/ppermute | solution.py:79
  13.8 2.3 %shard_map.84.weights2 = bf16[3200,480]{1,0:T(8,128)(2,1)S(1)} custom-call(bf16[480,5120]{1,0:T(8,128)(2,1)} %bitcast.13), custom_call_target="tpu_custom_call" | custom-call | tf_op jit(solution)/shard_map/pallas_call | solution.py:31
  16.7 1.6 %collective-permute-done.13.refs_1_ = bf16[2,2,3,2,2560]{4,3,2,1,0:T(2,128)(2,1)S(1)} collective-permute-done((bf16[2,2,3,2,2560]{4,3,2,1,0:T(2,128)(2,1)S(1)}, bf16[2,2,3,2,2560]{4,3,2,1,0:T(2,128)(2,1)S(1)}, u32[]{:S(2)}, u32[]{:S(2)}) %collective-permute-start.13) | collective-permute-done | bytes 122912 | tf_op jit(solution)/shard_map/ppermute | solution.py:79
  19.1 1.5 %shard_map.85.refs_0_ = bf16[48,480]{1,0:T(8,128)(2,1)S(1)} custom-call(bf16[24,2560]{1,0:T(8,128)(2,1)S(1)} %shard_map.83.s0, bf16[24,2560]{1,0:T(8,128)(2,1)S(1)} %collective-permute-done.3.s2, bf16[24,2560]{1,0:T(8,128)(2,1)S(1)} %collective-permute-done.4.s1, bf16[24,2560]{1,0:T(8,128)(2,1)S(1)} %collective-permute-done.5.s3, ...), custom_call_target="tpu_custom_call" | custom-call | tf_op jit(solution)/shard_map/pallas_call | solution.py:31
  20.6 2.3 %collective-permute-start.8 = (bf16[48,480]{1,0:T(8,128)(2,1)S(1)}, bf16[48,480]{1,0:T(8,128)(2,1)S(1)}, u32[]{:S(2)}, u32[]{:S(2)}) collective-permute-start(bf16[48,480]{1,0:T(8,128)(2,1)S(1)} %shard_map.85.refs_0_), channel_id=1, source_target_pairs={{0,12},{1,13},{2,14},{3,15},{4,8},{5,9},{6,10},{7,11},{8,4},{9,5},... | collective-permute-start | bytes 138248 | tf_op jit(solution)/shard_map/ppermute | solution.py:79
  22.9 2.2 %collective-permute-start.6 = (bf16[48,480]{1,0:T(8,128)(2,1)S(1)}, bf16[48,480]{1,0:T(8,128)(2,1)S(1)}, u32[]{:S(2)}, u32[]{:S(2)}) collective-permute-start(bf16[48,480]{1,0:T(8,128)(2,1)S(1)} %shard_map.85.refs_0_), channel_id=1, source_target_pairs={{0,4},{1,5},{2,6},{3,7},{4,0},{5,1},{6,2},{7,3},{8,12},{9,13},{10,... | collective-permute-start | bytes 138248 | tf_op jit(solution)/shard_map/ppermute | solution.py:79
  25.1 2.4 %shard_map.86.w_up1 = bf16[1920,864]{1,0:T(8,128)(2,1)S(1)} custom-call(bf16[864,5120]{1,0:T(8,128)(2,1)} %bitcast.10), custom_call_target="tpu_custom_call" | custom-call | tf_op jit(solution)/shard_map/pallas_call | solution.py:31
  29.6 3.1 %shard_map.88 = (bf16[3200,864]{1,0:T(8,128)(2,1)S(1)}, bf16[320,2560]{1,0:T(8,128)(2,1)S(1)}) custom-call(bf16[864,5120]{1,0:T(8,128)(2,1)} %bitcast.11, bf16[320,2560]{1,0:T(8,128)(2,1)} %bitcast.14), custom_call_target="tpu_custom_call" | custom-call | tf_op jit(solution)/shard_map/pallas_call | solution.py:31
  35.4 1.8 %shard_map.92.refs_0_ = bf16[24,640]{1,0:T(8,128)(2,1)S(1)} custom-call(bf16[4,48,480]{2,1,0:T(8,128)(2,1)S(1)} %shard_map.87.s0, bf16[4,48,480]{2,1,0:T(8,128)(2,1)S(1)} %collective-permute-done.9.s1, bf16[4,48,480]{2,1,0:T(8,128)(2,1)S(1)} %collective-permute-done.10.s2, bf16[4,48,480]{2,1,0:T(8,128)(2,1)S(1)} %collective-permute-done.11.s3, ...), custom_call_target="tpu_custom_call" | custom-call | tf_op jit(solution)/shard_map/pallas_call | solution.py:31
  37.1 2.0 %collective-permute-start.19 = (bf16[24,640]{1,0:T(8,128)(2,1)S(1)}, bf16[24,640]{1,0:T(8,128)(2,1)S(1)}, u32[]{:S(2)}, u32[]{:S(2)}) collective-permute-start(bf16[24,640]{1,0:T(8,128)(2,1)S(1)} %shard_map.92.refs_0_), channel_id=1, source_target_pairs={{0,12},{1,13},{2,14},{3,15},{4,8},{5,9},{6,10},{7,11},{8,4},{9,5},... | collective-permute-start | bytes 92168 | tf_op jit(solution)/shard_map/ppermute | solution.py:79
  39.6 2.0 %collective-permute-start.17 = (bf16[24,640]{1,0:T(8,128)(2,1)S(1)}, bf16[24,640]{1,0:T(8,128)(2,1)S(1)}, u32[]{:S(2)}, u32[]{:S(2)}) collective-permute-start(bf16[24,640]{1,0:T(8,128)(2,1)S(1)} %shard_map.92.refs_0_), channel_id=1, source_target_pairs={{0,4},{1,5},{2,6},{3,7},{4,0},{5,1},{6,2},{7,3},{8,12},{9,13},{10,... | collective-permute-start | bytes 92168 | tf_op jit(solution)/shard_map/ppermute | solution.py:79
  41.6 1.9 %shard_map.93.w_down1 = bf16[864,1920]{1,0:T(8,128)(2,1)S(1)} custom-call(bf16[864,5120]{1,0:T(8,128)(2,1)} %refs_0_.3), custom_call_target="tpu_custom_call" | custom-call | tf_op jit(solution)/shard_map/pallas_call | solution.py:31
  45.2 2.6 %shard_map.95.w_down2 = bf16[864,3200]{1,0:T(8,128)(2,1)S(1)} custom-call(bf16[864,5120]{1,0:T(8,128)(2,1)} %refs_0_.3), custom_call_target="tpu_custom_call" | custom-call | tf_op jit(solution)/shard_map/pallas_call | solution.py:31
  50.3 3.7 %shard_map.97 = (f32[24,5120]{1,0:T(8,128)S(1)}, bf16[24,5120]{1,0:T(8,128)(2,1)S(1)}) custom-call(bf16[4,24,640]{2,1,0:T(8,128)(2,1)S(1)} %shard_map.94.s0, bf16[4,24,640]{2,1,0:T(8,128)(2,1)S(1)} %collective-permute-done.20.s1, bf16[4,24,640]{2,1,0:T(8,128)(2,1)S(1)} %collective-permute-done.21.s2, bf16[4,24,640]{2,1,0:T(8,128)(2,1)S(1)} %collective-permute-done.22.s3, ...), custom_call_target="tpu_custom_call" | custom-call | tf_op jit(solution)/shard_map/pallas_call | solution.py:31
  54.3 1.4 %collective-permute-done.23.got = bf16[24,5120]{1,0:T(8,128)(2,1)S(1)} collective-permute-done((bf16[24,5120]{1,0:T(8,128)(2,1)S(1)}, bf16[24,5120]{1,0:T(8,128)(2,1)S(1)}, u32[]{:S(2)}, u32[]{:S(2)}) %collective-permute-start.23) | collective-permute-done | bytes 245792 | tf_op jit(solution)/shard_map/ppermute | solution.py:79
  55.8 2.1 %collective-permute-start.24 = (bf16[24,1280]{1,0:T(8,128)(2,1)S(1)}, bf16[24,1280]{1,0:T(8,128)(2,1)S(1)}, u32[]{:S(2)}, u32[]{:S(2)}) collective-permute-start(bf16[24,1280]{1,0:T(8,128)(2,1)S(1)} %get-tuple-element.91), channel_id=1, source_target_pairs={{0,12},{1,15},{2,14},{3,13},{4,8},{5,11},{6,10},{7,9},{8,4},{9,7},... | collective-permute-start | bytes 184328 | tf_op jit(solution)/shard_map/ppermute | solution.py:336
  58.8 1.5 %collective-permute-start.26 = (bf16[24,1280]{1,0:T(8,128)(2,1)S(1)}, bf16[24,1280]{1,0:T(8,128)(2,1)S(1)}, u32[]{:S(2)}, u32[]{:S(2)}) collective-permute-start(bf16[24,1280]{1,0:T(8,128)(2,1)S(1)} %get-tuple-element.93), channel_id=1, source_target_pairs={{0,4},{1,7},{2,6},{3,5},{4,0},{5,3},{6,2},{7,1},{8,12},{9,15},{10,... | collective-permute-start | bytes 184328 | tf_op jit(solution)/shard_map/ppermute | solution.py:336
  60.9 1.7 %collective-permute-done.24.got3 = bf16[24,1280]{1,0:T(8,128)(2,1)S(1)} collective-permute-done((bf16[24,1280]{1,0:T(8,128)(2,1)S(1)}, bf16[24,1280]{1,0:T(8,128)(2,1)S(1)}, u32[]{:S(2)}, u32[]{:S(2)}) %collective-permute-start.24) | collective-permute-done | bytes 61472 | tf_op jit(solution)/shard_map/ppermute | solution.py:336
  62.6 2.4 %collective-permute-done.25.got2 = bf16[24,1280]{1,0:T(8,128)(2,1)S(1)} collective-permute-done((bf16[24,1280]{1,0:T(8,128)(2,1)S(1)}, bf16[24,1280]{1,0:T(8,128)(2,1)S(1)}, u32[]{:S(2)}, u32[]{:S(2)}) %collective-permute-start.25) | collective-permute-done | bytes 61472 | tf_op jit(solution)/shard_map/ppermute | solution.py:336
  (54 shorter events, 16.0 us)
Async XLA Ops:
  0.0 9.5 %collective-permute-start.1 = (bf16[3,5120]{1,0:T(4,128)(2,1)}, bf16[3,5120]{1,0:T(4,128)(2,1)S(1)}, u32[]{:S(2)}, u32[]{:S(2)}) collective-permute-start(bf16[3,5120]{1,0:T(4,128)(2,1)} %refs_0_.1), channel_id=1, source_target_pairs={{0,8},{1,9},{2,10},{3,11},{4,12},{5,13},{6,14},{7,15},{8,0},{9,1},... | collective-permute-start | bytes 92168 | tf_op jit(solution)/shard_map/ppermute | solution.py:79
  4.0 5.5 %collective-permute-start = (bf16[3,5120]{1,0:T(4,128)(2,1)}, bf16[3,5120]{1,0:T(4,128)(2,1)S(1)}, u32[]{:S(2)}, u32[]{:S(2)}) collective-permute-start(bf16[3,5120]{1,0:T(4,128)(2,1)} %refs_0_.1), channel_id=1, source_target_pairs={{0,4},{1,5},{2,6},{3,7},{4,0},{5,1},{6,2},{7,3},{8,12},{9,13},{10,... | collective-permute-start | bytes 92168 | tf_op jit(solution)/shard_map/ppermute | solution.py:79
  5.6 6.1 %collective-permute-start.2 = (bf16[3,5120]{1,0:T(4,128)(2,1)}, bf16[3,5120]{1,0:T(4,128)(2,1)S(1)}, u32[]{:S(2)}, u32[]{:S(2)}) collective-permute-start(bf16[3,5120]{1,0:T(4,128)(2,1)} %refs_0_.1), channel_id=1, source_target_pairs={{0,12},{1,13},{2,14},{3,15},{4,8},{5,9},{6,10},{7,11},{8,4},{9,5},... | collective-permute-start | bytes 92168 | tf_op jit(solution)/shard_map/ppermute | solution.py:79
  5.6 7.8 %collective-permute-start.12 = (bf16[2,3,2,2560]{3,2,1,0:T(2,128)(2,1)}, bf16[2,3,2,2560]{3,2,1,0:T(2,128)(2,1)S(1)}, u32[]{:S(2)}, u32[]{:S(2)}) collective-permute-start(bf16[2,3,2,2560]{3,2,1,0:T(2,128)(2,1)} %bitcast.15), channel_id=1, source_target_pairs={{0,8},{1,9},{2,10},{3,11},{4,12},{5,13},{6,14},{7,15},{8,0},{9,1},... | collective-permute-start | bytes 184328 | tf_op jit(solution)/shard_map/ppermute | solution.py:79
  11.8 4.9 %collective-permute-start.4 = (bf16[24,2560]{1,0:T(8,128)(2,1)S(1)}, bf16[24,2560]{1,0:T(8,128)(2,1)S(1)}, u32[]{:S(2)}, u32[]{:S(2)}) collective-permute-start(bf16[24,2560]{1,0:T(8,128)(2,1)S(1)} %shard_map.83.s0), channel_id=1, source_target_pairs={{0,2},{1,3},{2,0},{3,1},{4,6},{5,7},{6,4},{7,5},{8,10},{9,11},{10,... | collective-permute-start | bytes 368648 | tf_op jit(solution)/shard_map/ppermute | solution.py:79
  13.4 4.9 %collective-permute-start.13 = (bf16[2,2,3,2,2560]{4,3,2,1,0:T(2,128)(2,1)S(1)}, bf16[2,2,3,2,2560]{4,3,2,1,0:T(2,128)(2,1)S(1)}, u32[]{:S(2)}, u32[]{:S(2)}) collective-permute-start(bf16[2,2,3,2,2560]{4,3,2,1,0:T(2,128)(2,1)S(1)} %shard_map.89.refs_0_), channel_id=1, source_target_pairs={{0,4},{1,5},{2,6},{3,7},{4,0},{5,1},{6,2},{7,3},{8,12},{9,13},{10,... | collective-permute-start | bytes 368648 | tf_op jit(solution)/shard_map/ppermute | solution.py:79
  13.8 5.4 %collective-permute-start.3 = (bf16[24,2560]{1,0:T(8,128)(2,1)S(1)}, bf16[24,2560]{1,0:T(8,128)(2,1)S(1)}, u32[]{:S(2)}, u32[]{:S(2)}) collective-permute-start(bf16[24,2560]{1,0:T(8,128)(2,1)S(1)} %shard_map.83.s0), channel_id=1, source_target_pairs={{0,1},{1,0},{2,3},{3,2},{4,5},{5,4},{6,7},{7,6},{8,9},{9,8},{10,11... | collective-permute-start | bytes 368648 | tf_op jit(solution)/shard_map/ppermute | solution.py:79
  18.4 10.7 %collective-permute-start.14 = (bf16[4,2,3,2,2560]{4,3,2,1,0:T(2,128)(2,1)S(1)}, bf16[4,2,3,2,2560]{4,3,2,1,0:T(2,128)(2,1)S(1)}, u32[]{:S(2)}, u32[]{:S(2)}) collective-permute-start(bf16[4,2,3,2,2560]{4,3,2,1,0:T(2,128)(2,1)S(1)} %bitcast.7), channel_id=1, source_target_pairs={{0,2},{1,3},{2,0},{3,1},{4,6},{5,7},{6,4},{7,5},{8,10},{9,11},{10,... | collective-permute-start | bytes 737288 | tf_op jit(solution)/shard_map/ppermute | solution.py:79
  20.6 6.8 %collective-permute-start.8 = (bf16[48,480]{1,0:T(8,128)(2,1)S(1)}, bf16[48,480]{1,0:T(8,128)(2,1)S(1)}, u32[]{:S(2)}, u32[]{:S(2)}) collective-permute-start(bf16[48,480]{1,0:T(8,128)(2,1)S(1)} %shard_map.85.refs_0_), channel_id=1, source_target_pairs={{0,12},{1,13},{2,14},{3,15},{4,8},{5,9},{6,10},{7,11},{8,4},{9,5},... | collective-permute-start | bytes 138248 | tf_op jit(solution)/shard_map/ppermute | solution.py:79
  22.9 5.0 %collective-permute-start.7 = (bf16[48,480]{1,0:T(8,128)(2,1)S(1)}, bf16[48,480]{1,0:T(8,128)(2,1)S(1)}, u32[]{:S(2)}, u32[]{:S(2)}) collective-permute-start(bf16[48,480]{1,0:T(8,128)(2,1)S(1)} %shard_map.85.refs_0_), channel_id=1, source_target_pairs={{0,8},{1,9},{2,10},{3,11},{4,12},{5,13},{6,14},{7,15},{8,0},{9,1},... | collective-permute-start | bytes 138248 | tf_op jit(solution)/shard_map/ppermute | solution.py:79
  22.9 5.0 %collective-permute-start.6 = (bf16[48,480]{1,0:T(8,128)(2,1)S(1)}, bf16[48,480]{1,0:T(8,128)(2,1)S(1)}, u32[]{:S(2)}, u32[]{:S(2)}) collective-permute-start(bf16[48,480]{1,0:T(8,128)(2,1)S(1)} %shard_map.85.refs_0_), channel_id=1, source_target_pairs={{0,4},{1,5},{2,6},{3,7},{4,0},{5,1},{6,2},{7,3},{8,12},{9,13},{10,... | collective-permute-start | bytes 138248 | tf_op jit(solution)/shard_map/ppermute | solution.py:79
  27.9 6.0 %collective-permute-start.9 = (bf16[4,48,480]{2,1,0:T(8,128)(2,1)S(1)}, bf16[4,48,480]{2,1,0:T(8,128)(2,1)S(1)}, u32[]{:S(2)}, u32[]{:S(2)}) collective-permute-start(bf16[4,48,480]{2,1,0:T(8,128)(2,1)S(1)} %shard_map.87.s0), channel_id=1, source_target_pairs={{0,2},{1,3},{2,0},{3,1},{4,6},{5,7},{6,4},{7,5},{8,10},{9,11},{10,... | collective-permute-start | bytes 552968 | tf_op jit(solution)/shard_map/ppermute | solution.py:79
  29.1 4.9 %collective-permute-start.15 = (bf16[4,2,3,2,2560]{4,3,2,1,0:T(2,128)(2,1)S(1)}, bf16[4,2,3,2,2560]{4,3,2,1,0:T(2,128)(2,1)S(1)}, u32[]{:S(2)}, u32[]{:S(2)}) collective-permute-start(bf16[4,2,3,2,2560]{4,3,2,1,0:T(2,128)(2,1)S(1)} %bitcast.8), channel_id=1, source_target_pairs={{0,1},{1,0},{2,3},{3,2},{4,5},{5,4},{6,7},{7,6},{8,9},{9,8},{10,11... | collective-permute-start | bytes 737288 | tf_op jit(solution)/shard_map/ppermute | solution.py:79
  29.1 4.9 %collective-permute-start.16 = (bf16[4,2,3,2,2560]{4,3,2,1,0:T(2,128)(2,1)S(1)}, bf16[4,2,3,2,2560]{4,3,2,1,0:T(2,128)(2,1)S(1)}, u32[]{:S(2)}, u32[]{:S(2)}) collective-permute-start(bf16[4,2,3,2,2560]{4,3,2,1,0:T(2,128)(2,1)S(1)} %collective-permute-done.14.s1), channel_id=1, source_target_pairs={{0,1},{1,0},{2,3},{3,2},{4,5},{5,4},{6,7},{7,6},{8,9},{9,8},{10,11... | collective-permute-start | bytes 737288 | tf_op jit(solution)/shard_map/ppermute | solution.py:79
  29.6 5.0 %collective-permute-start.10 = (bf16[4,48,480]{2,1,0:T(8,128)(2,1)S(1)}, bf16[4,48,480]{2,1,0:T(8,128)(2,1)S(1)}, u32[]{:S(2)}, u32[]{:S(2)}) collective-permute-start(bf16[4,48,480]{2,1,0:T(8,128)(2,1)S(1)} %shard_map.87.s0), channel_id=1, source_target_pairs={{0,1},{1,0},{2,3},{3,2},{4,5},{5,4},{6,7},{7,6},{8,9},{9,8},{10,11... | collective-permute-start | bytes 552968 | tf_op jit(solution)/shard_map/ppermute | solution.py:79
  37.1 6.4 %collective-permute-start.19 = (bf16[24,640]{1,0:T(8,128)(2,1)S(1)}, bf16[24,640]{1,0:T(8,128)(2,1)S(1)}, u32[]{:S(2)}, u32[]{:S(2)}) collective-permute-start(bf16[24,640]{1,0:T(8,128)(2,1)S(1)} %shard_map.92.refs_0_), channel_id=1, source_target_pairs={{0,12},{1,13},{2,14},{3,15},{4,8},{5,9},{6,10},{7,11},{8,4},{9,5},... | collective-permute-start | bytes 92168 | tf_op jit(solution)/shard_map/ppermute | solution.py:79
  39.1 4.9 %collective-permute-start.18 = (bf16[24,640]{1,0:T(8,128)(2,1)S(1)}, bf16[24,640]{1,0:T(8,128)(2,1)S(1)}, u32[]{:S(2)}, u32[]{:S(2)}) collective-permute-start(bf16[24,640]{1,0:T(8,128)(2,1)S(1)} %shard_map.92.refs_0_), channel_id=1, source_target_pairs={{0,8},{1,9},{2,10},{3,11},{4,12},{5,13},{6,14},{7,15},{8,0},{9,1},... | collective-permute-start | bytes 92168 | tf_op jit(solution)/shard_map/ppermute | solution.py:79
  39.6 4.4 %collective-permute-start.17 = (bf16[24,640]{1,0:T(8,128)(2,1)S(1)}, bf16[24,640]{1,0:T(8,128)(2,1)S(1)}, u32[]{:S(2)}, u32[]{:S(2)}) collective-permute-start(bf16[24,640]{1,0:T(8,128)(2,1)S(1)} %shard_map.92.refs_0_), channel_id=1, source_target_pairs={{0,4},{1,5},{2,6},{3,7},{4,0},{5,1},{6,2},{7,3},{8,12},{9,13},{10,... | collective-permute-start | bytes 92168 | tf_op jit(solution)/shard_map/ppermute | solution.py:79
  44.0 4.9 %collective-permute-start.20 = (bf16[4,24,640]{2,1,0:T(8,128)(2,1)S(1)}, bf16[4,24,640]{2,1,0:T(8,128)(2,1)S(1)}, u32[]{:S(2)}, u32[]{:S(2)}) collective-permute-start(bf16[4,24,640]{2,1,0:T(8,128)(2,1)S(1)} %shard_map.94.s0), channel_id=1, source_target_pairs={{0,2},{1,3},{2,0},{3,1},{4,6},{5,7},{6,4},{7,5},{8,10},{9,11},{10,... | collective-permute-start | bytes 368648 | tf_op jit(solution)/shard_map/ppermute | solution.py:79
  45.2 4.1 %collective-permute-start.21 = (bf16[4,24,640]{2,1,0:T(8,128)(2,1)S(1)}, bf16[4,24,640]{2,1,0:T(8,128)(2,1)S(1)}, u32[]{:S(2)}, u32[]{:S(2)}) collective-permute-start(bf16[4,24,640]{2,1,0:T(8,128)(2,1)S(1)} %shard_map.94.s0), channel_id=1, source_target_pairs={{0,1},{1,0},{2,3},{3,2},{4,5},{5,4},{6,7},{7,6},{8,9},{9,8},{10,11... | collective-permute-start | bytes 368648 | tf_op jit(solution)/shard_map/ppermute | solution.py:79
  55.8 6.8 %collective-permute-start.24 = (bf16[24,1280]{1,0:T(8,128)(2,1)S(1)}, bf16[24,1280]{1,0:T(8,128)(2,1)S(1)}, u32[]{:S(2)}, u32[]{:S(2)}) collective-permute-start(bf16[24,1280]{1,0:T(8,128)(2,1)S(1)} %get-tuple-element.91), channel_id=1, source_target_pairs={{0,12},{1,15},{2,14},{3,13},{4,8},{5,11},{6,10},{7,9},{8,4},{9,7},... | collective-permute-start | bytes 184328 | tf_op jit(solution)/shard_map/ppermute | solution.py:336
  57.9 7.1 %collective-permute-start.25 = (bf16[24,1280]{1,0:T(8,128)(2,1)S(1)}, bf16[24,1280]{1,0:T(8,128)(2,1)S(1)}, u32[]{:S(2)}, u32[]{:S(2)}) collective-permute-start(bf16[24,1280]{1,0:T(8,128)(2,1)S(1)} %get-tuple-element.92), channel_id=1, source_target_pairs={{0,8},{1,11},{2,10},{3,9},{4,12},{5,15},{6,14},{7,13},{8,0},{9,3},... | collective-permute-start | bytes 184328 | tf_op jit(solution)/shard_map/ppermute | solution.py:336
  58.8 6.2 %collective-permute-start.26 = (bf16[24,1280]{1,0:T(8,128)(2,1)S(1)}, bf16[24,1280]{1,0:T(8,128)(2,1)S(1)}, u32[]{:S(2)}, u32[]{:S(2)}) collective-permute-start(bf16[24,1280]{1,0:T(8,128)(2,1)S(1)} %get-tuple-element.93), channel_id=1, source_target_pairs={{0,4},{1,7},{2,6},{3,5},{4,0},{5,3},{6,2},{7,1},{8,12},{9,15},{10,... | collective-permute-start | bytes 184328 | tf_op jit(solution)/shard_map/ppermute | solution.py:336
  60.3 4.7 %collective-permute-start.27 = (bf16[24,1280]{1,0:T(8,128)(2,1)S(1)}, bf16[24,1280]{1,0:T(8,128)(2,1)S(1)}, u32[]{:S(2)}, u32[]{:S(2)}) collective-permute-start(bf16[24,1280]{1,0:T(8,128)(2,1)S(1)} %get-tuple-element.94), channel_id=1, source_target_pairs={{1,3},{3,1},{5,7},{7,5},{9,11},{11,9},{13,15},{15,13},{17,19},{19,... | collective-permute-start | bytes 184328 | tf_op jit(solution)/shard_map/ppermute | solution.py:336
  (5 other events, 8.7 us)
